TPU v7x, 256 devices: a whole 4x4x8 slice. The times are simulated.
256 devices in a mesh: group: 8 (over x, core), fsdp: 32 (over z, y).
Axes of the slice: x: 4, y: 4, z: 8, core: 2. Of those that a mesh axis runs over, the one named last changes fastest.
Arguments:
- hidden: bfloat16 [64, 128, 8192], P('group', None, 'fsdp'), may hold values from -6 to 6
- norm_gain: bfloat16 [8192], replicated, may hold values from 0.099609375 to 1.8984375
- w_query: bfloat16 [8192, 8192], P('group', 'fsdp'), may hold values from -0.0625 to 0.0625
- key_projection_weight: bfloat16 [8192, 1024], P('group'), may hold values from -0.0625 to 0.0625
- value_projection_weight: bfloat16 [8192, 1024], P('group'), may hold values from -0.0625 to 0.0625
- prompt_key_cache: bfloat16 [2048, 1024], P('group'), may hold values from -74 to 74
- prompt_value_cache: bfloat16 [2048, 1024], P('group'), may hold values from -6 to 6
- keep_flag: int32 [64], replicated, may hold values from 0 to 1, as said below
- destination: int32 [64], replicated, may hold values from 0 to 31, as said below
- row_counts: int32 [64], replicated, may hold values from 32 to 128
Outputs:
- attended: bfloat16 [32, 128, 8192], P('group', None, 'fsdp')
Inputs may be any that keep to these rules, and one draw needn't show every extreme that they name: `keep_flag`: exactly 32 blocks are kept. `destination`: the kept blocks name the slots 0 to 31, each exactly once. Among the 8 blocks g * 8 to g * 8 + 7, the kept ones that name a slot of d * 4 to d * 4 + 3 number either 0 or exactly 1. Entries of dropped blocks are arbitrary slot numbers.
All inputs are finite; a program needn't handle non-finite values.
Results may differ from a plain program's by a relative error of at most 0.012.
The roundings to bfloat16 on the way count: a program that leaves them out, or rounds other values in their place, can miss the bound.
Values may be sent and summed in bfloat16 or wider, within the bound.
No kernel may reach another device: no remote copies, remote signals or barrier semaphores. Data moves between devices by JAX's collectives and lax.ppermute only.
A program may use at most 128 MiB of HBM per device.

v0:
```python
import jax
import jax.numpy as jnp
from jax import lax
from jax.sharding import PartitionSpec as P

QUERY_HEADS = 64
KEY_VALUE_HEADS = 8
HEAD_SIZE = 128
PROMPT_TOKENS = 2048
IN_DEV = 8
CAP = 1
OUT_DEV = 4


EPSILON = 1e-05
ROPE_THETA = 500000.0
CONTEXT_BASE = 8192.0
STRETCH = 8.0
MASKED_SCORE = -1e30


def rope_tables(length, offset):
    half_dim = HEAD_SIZE // 2
    base_rate = ROPE_THETA ** (-(jnp.arange(half_dim, dtype=jnp.float32) * 2.0 / HEAD_SIZE))
    ratio = CONTEXT_BASE * base_rate / (2.0 * jnp.pi)
    smooth = jnp.clip((ratio - 1.0) / 3.0, 0.0, 1.0)
    inverse_rate = (1.0 - smooth) * base_rate / STRETCH + smooth * base_rate
    token_positions = jnp.arange(length, dtype=jnp.float32) + offset
    angles = token_positions[:, None] * inverse_rate[None, :]
    return (jnp.cos(angles), jnp.sin(angles))


def rotate(values, cosine, sine_table):
    half_dim = values.shape[-1] // 2
    first_half = values[..., :half_dim]
    second = values[..., half_dim:]
    cosine = cosine[:, None, :]
    sine_table = sine_table[:, None, :]
    return jnp.concatenate(
        [first_half * cosine - second * sine_table, second * cosine + first_half * sine_table],
        axis=-1,
    )


def routing(keep_flag, destination):
    block_total = keep_flag.shape[0]
    block_index = jnp.arange(block_total, dtype=jnp.int32)
    block_owner = block_index // IN_DEV
    is_live = keep_flag == 1
    target = destination // OUT_DEV
    earlier = (
        (block_owner[:, None] == block_owner[None, :])
        & (target[:, None] == target[None, :])
        & is_live[None, :]
        & (block_index[None, :] < block_index[:, None])
    )
    order_rank = jnp.sum(earlier.astype(jnp.int32), axis=1)
    return (block_owner, is_live, target, order_rank)


def pack_for_send(values, keep_flag, destination):
    group_count = lax.axis_size("group")
    my_group = lax.axis_index("group")
    block_owner, is_live, target, order_rank = routing(keep_flag, destination)
    local_info = lax.dynamic_slice_in_dim(
        jnp.stack([is_live.astype(jnp.int32), target, order_rank]), my_group * IN_DEV, IN_DEV, 1
    )
    peer_ids = jnp.arange(group_count, dtype=jnp.int32)[:, None, None]
    copies = jnp.arange(CAP, dtype=jnp.int32)[None, :, None]
    select = (
        (local_info[0][None, None, :] == 1)
        & (local_info[1][None, None, :] == peer_ids)
        & (local_info[2][None, None, :] == copies)
    )
    rows_flat = values.reshape(IN_DEV, -1)
    packed = jnp.einsum(
        "dcs,sx->dcx", select.astype(jnp.bfloat16), rows_flat, preferred_element_type=jnp.float32
    ).astype(jnp.bfloat16)
    return packed.reshape((group_count, CAP) + values.shape[1:])


def unpack_received(received, keep_flag, destination):
    group_count = lax.axis_size("group")
    my_group = lax.axis_index("group")
    block_owner, is_live, target, order_rank = routing(keep_flag, destination)
    slot_ids = my_group * OUT_DEV + jnp.arange(OUT_DEV, dtype=jnp.int32)
    matched = is_live[None, :] & (destination[None, :] == slot_ids[:, None])
    pair_code = block_owner * CAP + order_rank
    onehot = pair_code[:, None] == jnp.arange(group_count * CAP, dtype=jnp.int32)[None, :]
    select = jnp.dot(matched.astype(jnp.float32), onehot.astype(jnp.float32)).astype(jnp.bfloat16)
    rows_flat = received.reshape(group_count * CAP, -1)
    picked = jnp.dot(select, rows_flat, preferred_element_type=jnp.float32).astype(jnp.bfloat16)
    return (picked.reshape((OUT_DEV,) + received.shape[2:]), matched)


def attend(
    blocks,
    lengths,
    norm_gain,
    w_query,
    key_projection_weight,
    value_projection_weight,
    prompt_key_cache,
    prompt_value_cache,
):
    block_count = blocks.shape[0]
    span_len = blocks.shape[1]
    row_total = block_count * span_len
    gathered = lax.all_gather(blocks, "fsdp", axis=2, tiled=True)
    rows_wide = gathered.reshape(row_total, -1).astype(jnp.float32)
    normalized_input = (
        rows_wide
        * lax.rsqrt(jnp.mean(rows_wide * rows_wide, axis=1, keepdims=True) + EPSILON)
        * norm_gain.astype(jnp.float32)
    ).astype(jnp.bfloat16)
    local_heads = w_query.shape[1] // HEAD_SIZE
    key_value_index = lax.axis_index("fsdp") * local_heads // (QUERY_HEADS // KEY_VALUE_HEADS)
    key_rows = lax.dynamic_slice_in_dim(
        key_projection_weight, key_value_index * HEAD_SIZE, HEAD_SIZE, 1
    )
    value_rows = lax.dynamic_slice_in_dim(
        value_projection_weight, key_value_index * HEAD_SIZE, HEAD_SIZE, 1
    )
    pieces = (
        lax.all_gather(w_query, "group", axis=0, tiled=True),
        lax.all_gather(key_rows, "group", axis=0, tiled=True),
        lax.all_gather(value_rows, "group", axis=0, tiled=True),
    )
    query_vectors = jnp.dot(normalized_input, pieces[0], preferred_element_type=jnp.float32)
    fresh_keys = jnp.dot(normalized_input, pieces[1], preferred_element_type=jnp.float32)
    fresh_values = jnp.dot(normalized_input, pieces[2], preferred_element_type=jnp.float32)
    cosine, sine_table = rope_tables(span_len, PROMPT_TOKENS)
    query_vectors = rotate(
        query_vectors.reshape(block_count, span_len, local_heads, HEAD_SIZE), cosine, sine_table
    ).astype(jnp.bfloat16)
    fresh_keys = (
        rotate(fresh_keys.reshape(block_count, span_len, 1, HEAD_SIZE), cosine, sine_table)
        .reshape(block_count, span_len, HEAD_SIZE)
        .astype(jnp.bfloat16)
    )
    fresh_values = fresh_values.reshape(block_count, span_len, HEAD_SIZE).astype(jnp.bfloat16)
    score_scale = HEAD_SIZE ** (-0.5)
    query_rows = query_vectors.reshape(row_total, local_heads, HEAD_SIZE)
    prompt_keys = lax.dynamic_slice_in_dim(
        prompt_key_cache, key_value_index * HEAD_SIZE, HEAD_SIZE, 1
    )
    prompt_values = lax.dynamic_slice_in_dim(
        prompt_value_cache, key_value_index * HEAD_SIZE, HEAD_SIZE, 1
    )
    pieces = (
        lax.all_gather(prompt_keys, "group", axis=0, tiled=True),
        lax.all_gather(prompt_values, "group", axis=0, tiled=True),
    )
    row_max = jnp.full((row_total, local_heads), MASKED_SCORE, jnp.float32)
    scores = (
        jnp.einsum("rhd,kd->rhk", query_rows, pieces[0], preferred_element_type=jnp.float32)
        * score_scale
    )
    new_max = jnp.maximum(row_max, jnp.max(scores, axis=2))
    powers = jnp.exp(scores - new_max[:, :, None])
    row_sum = jnp.sum(powers, axis=2)
    weighted = jnp.einsum(
        "rhk,kd->rhd", powers.astype(jnp.bfloat16), pieces[1], preferred_element_type=jnp.float32
    )
    row_max, row_sum, weighted = (new_max, row_sum, weighted)
    row_max = row_max.reshape(block_count, span_len, local_heads)
    row_sum = row_sum.reshape(block_count, span_len, local_heads)
    weighted = weighted.reshape(block_count, span_len, local_heads, HEAD_SIZE)
    scores = (
        jnp.einsum("cupy,cly->cupl", query_vectors, fresh_keys, preferred_element_type=jnp.float32)
        * score_scale
    )
    position = jnp.arange(span_len, dtype=jnp.int32)
    allowed = (position[None, None, :] <= position[None, :, None]) & (
        position[None, None, :] < lengths[:, None, None]
    )
    scores = jnp.where(allowed[:, :, None, :], scores, MASKED_SCORE)
    new_max = jnp.maximum(row_max, jnp.max(scores, axis=3))
    powers = jnp.exp(scores - new_max[..., None])
    rescale = jnp.exp(row_max - new_max)
    row_sum = row_sum * rescale + jnp.sum(powers, axis=3)
    weighted = weighted * rescale[..., None] + jnp.einsum(
        "zcmn,znu->zcmu",
        powers.astype(jnp.bfloat16),
        fresh_values,
        preferred_element_type=jnp.float32,
    )
    mixed_out = weighted / row_sum[..., None]
    live_rows = position[None, :] < lengths[:, None]
    mixed_out = jnp.where(live_rows[:, :, None, None], mixed_out, 0.0)
    return mixed_out.reshape(block_count, span_len, local_heads * HEAD_SIZE).astype(jnp.bfloat16)


def body(
    hidden,
    norm_gain,
    w_query,
    key_projection_weight,
    value_projection_weight,
    prompt_key_cache,
    prompt_value_cache,
    keep_flag,
    destination,
    row_counts,
):
    my_group = lax.axis_index("group")
    lengths = lax.dynamic_slice_in_dim(row_counts, my_group * IN_DEV, IN_DEV)
    results = attend(
        hidden,
        lengths,
        norm_gain,
        w_query,
        key_projection_weight,
        value_projection_weight,
        prompt_key_cache,
        prompt_value_cache,
    )
    packed = pack_for_send(results, keep_flag, destination)
    received = lax.all_to_all(packed, "group", split_axis=0, concat_axis=0, tiled=True)
    blocks, matched = unpack_received(received, keep_flag, destination)
    return blocks


def solution(mesh):
    return jax.shard_map(
        body,
        mesh=mesh,
        in_specs=(
            P("group", None, "fsdp"),
            P(),
            P("group", "fsdp"),
            P("group", None),
            P("group", None),
            P("group", None),
            P("group", None),
            P(),
            P(),
            P(),
        ),
        out_specs=P("group", None, "fsdp"),
        check_vma=False,
    )
```

profile of v0, /device:TPU:8, one launch (start us, length us, event | category | flops | bytes accessed | tf_op | source)
XLA Modules:
  0.0 293.4 jit_solution(16595268362099369970)
XLA Ops:
  6.5 0.7 all-gather.7.cloned.1.call-update
  7.3 0.7 all-gather.5.cloned.1.call-update
  8.1 0.1 copy-done
  8.1 0.1 constant_dynamic-slice_fusion.1
  8.2 0.9 copy.70
  9.1 0.0 all-gather.11.cloned.1.call-start
  9.1 1.7 constant_dynamic-slice_fusion
  10.9 0.7 convert_bitcast_fusion
  11.6 0.7 and_select_fusion
  12.2 0.2 convert_reduce_fusion
  12.4 0.1 constant_dynamic-slice_fusion.4
  12.5 0.9 constant_dynamic-slice_fusion.3
  13.4 13.4 %all_gather.20 = bf16[2048,128]{1,0:T(8,128)(2,1)S(1)} all-gather(bf16[256,128]{1,0:T(8,128)(2,1)S(1)} %constant_dynamic-slice_fusion.3), channel_id=1, replica_groups=mesh['group'=8,'fsdp'=32] {'group'}, dimensions={0}, use_global_device_ids=true | all-gather | bytes 589824 | tf_op jit(solution)/shard_map/all_gather | solution.py:151
  26.8 0.7 convert_element_type.59
  27.5 0.7 dynamic_slice.19
  28.3 0.1 iota_compare_fusion.5
  28.3 0.8 constant_dynamic-slice_fusion.2
  29.2 15.3 %all_gather.21 = bf16[2048,128]{1,0:T(8,128)(2,1)} all-gather(bf16[256,128]{1,0:T(8,128)(2,1)S(1)} %constant_dynamic-slice_fusion.2), channel_id=1, replica_groups=mesh['group'=8,'fsdp'=32] {'group'}, dimensions={0}, use_global_device_ids=true | all-gather | bytes 589824 | tf_op jit(solution)/shard_map/all_gather | solution.py:152
  44.5 0.2 multiply_cosine_fusion
  44.7 0.9 broadcast_and_fusion
  45.5 3.4 %all-gather.7.cloned.1.call-done = bf16[8192,256]{1,0:T(8,128)(2,1)} async-done(((bf16[1024,256]{1,0:T(8,128)(2,1)}), bf16[8192,256]{1,0:T(8,128)(2,1)}) %all-gather.7.cloned.1.call-update) | async-done | bytes 4194320 | tf_op jit(solution)/shard_map/all_gather | solution.py:125
  48.9 6.4 %copy.46 = bf16[256,8192]{1,0:T(8,128)(2,1)} copy(bf16[256,8192]{0,1:T(8,128)(2,1)} %bitcast.87) | data formatting | bytes 8388608 | tf_op jit(solution)/shard_map/dot_general | solution.py:129
  55.3 145.2 %all-gather.5.cloned.1.call-done = bf16[8,128,8192]{2,1,0:T(8,128)(2,1)} async-done(((bf16[8,128,256]{2,1,0:T(8,128)(2,1)}), bf16[8,128,8192]{2,1,0:T(8,128)(2,1)}) %all-gather.5.cloned.1.call-update) | async-done | bytes 16777232 | tf_op jit(solution)/shard_map/all_gather | solution.py:109
  200.5 7.4 %fusion = f32[8,128]{1,0:T(8,128)S(1)} fusion(bf16[8,128,8192]{2,1,0:T(8,128)(2,1)} %all-gather.5.cloned.1.call-done), kind=kLoop, calls=%fused_computation.4 | loop fusion | flops 25164800 | bytes 16781312 | tf_op jit(solution)/shard_map/reduce_sum | solution.py:113
  208.0 3.2 %copy-done.1 = bf16[8,128,8192]{2,1,0:T(8,128)(2,1)S(1)} copy-done((bf16[8,128,8192]{2,1,0:T(8,128)(2,1)S(1)}, bf16[8,128,8192]{2,1,0:T(8,128)(2,1)}, u32[]{:S(2)}) %copy-start.1) | copy-done | bytes 16777240
  211.2 14.0 %fusion.3 = f32[8,128,2,128]{1,3,2,0:T(8,128)S(1)} fusion(bf16[2,128,8192,1]{2,1,0,3:T(8,128)(2,1)} %bitcast.88, bf16[8,128,8192]{2,1,0:T(8,128)(2,1)S(1)} %copy-done.1, f32[8192]{0:T(1024)S(1)} %convert_element_type.59, f32[8,128]{1,0:T(8,128)S(1)} %add_rsqrt_fusion), kind=kOutput, calls=%fused_computation.7 | convolution fusion | flops 4328521728 | bytes 22056960 | tf_op jit(solution)/shard_map/dot_general | solution.py:129
  225.2 0.9 subtract_convert_fusion
  226.1 0.3 copy.64
  226.4 2.0 copy.65
  228.3 0.2 all-gather.9.cloned.1.call-done
  228.5 10.0 %fusion.20 = f32[8,128,1,128]{1,3,0,2:T(8,128)S(1)} fusion(bf16[8192,128]{0,1:T(8,128)(2,1)} %all-gather.9.cloned.1.call-done, bf16[8,128,8192]{2,1,0:T(8,128)(2,1)} %all-gather.5.cloned.1.call-done, f32[8192]{0:T(1024)S(1)} %convert_element_type.59, f32[8,128]{1,0:T(8,128)S(1)} %add_rsqrt_fusion), kind=kOutput, calls=%fused_computation.24 | convolution fusion | flops 2181038080 | bytes 19435520 | tf_op jit(solution)/shard_map/dot_general | solution.py:130
  238.5 0.1 subtract_convert_fusion.1
  238.6 0.4 fusion.81
  239.1 2.5 multiply_reduce_fusion
  241.6 0.2 fusion.39
  241.7 3.5 %fusion.5 = f32[1024,2]{0,1:T(2,128)S(1)} fusion(f32[1024,2,2048]{2,0,1:T(8,128)S(1)} %get-tuple-element.18, f32[1024,2]{0,1:T(2,128)S(1)} %broadcast_maximum_fusion), kind=kLoop, calls=%fused_computation.11 | loop fusion | flops 12580864 | bytes 16793600 | tf_op jit(solution)/shard_map/reduce_sum | solution.py:161
  245.3 4.3 %fusion.12 = f32[1024,2,128]{2,0,1:T(8,128)} fusion(f32[1024,2,2048]{2,0,1:T(8,128)S(1)} %get-tuple-element.18, f32[1024,2]{0,1:T(2,128)S(1)} %broadcast_maximum_fusion, bf16[2048,128]{1,0:T(8,128)(2,1)S(1)} %copy-done.3), kind=kOutput, calls=%fused_computation.15 | convolution fusion | flops 1086324736 | bytes 18358272 | tf_op jit(solution)/shard_map/rhk,kd->rhd/dot_general | solution.py:162
  249.5 8.7 %all-gather.11.cloned.1.call-done = bf16[8192,128]{1,0:T(8,128)(2,1)} async-done(((bf16[1024,128]{1,0:T(8,128)(2,1)}), bf16[8192,128]{1,0:T(8,128)(2,1)}) %all-gather.11.cloned.1.call-update) | async-done | bytes 2097168 | tf_op jit(solution)/shard_map/all_gather | solution.py:127
  258.3 10.1 %fusion.19 = bf16[8,128,2,128]{3,1,2,0:T(8,128)(2,1)} fusion(bf16[8192,128]{1,0:T(8,128)(2,1)} %all-gather.11.cloned.1.call-done, bf16[8,128,8192]{2,1,0:T(8,128)(2,1)} %all-gather.5.cloned.1.call-done, f32[8192]{0:T(1024)S(1)} %convert_element_type.59, f32[8,128]{1,0:T(8,128)S(1)} %add_rsqrt_fusion, f32[8,128,2,128]{3,1,0,2:T(8,128)} %bitcast.95, ...), kind=kOutput, calls=%fused_computation.23 | convolution fusion | flops 2250113024 | bytes 21558272 | tf_op jit(solution)/shard_map/zcmn,znu->zcmu/dot_general | solution.py:182
  268.4 1.6 copy.57
  270.0 0.4 convert_element_type.66
  270.4 0.3 convolution_convert_fusion
  270.7 0.9 copy.58
  271.6 3.5 %all-to-all-start = ((bf16[8,1,128,256]{3,2,1,0:T(8,128)(2,1)}), bf16[8,1,128,256]{3,2,1,0:T(8,128)(2,1)S(1)}, u32[]{:S(2)}, u32[]{:S(2)}) async-start(bf16[8,1,128,256]{3,2,1,0:T(8,128)(2,1)} %copy.58), calls=%async_computation | async-start | bytes 1048576 | tf_op jit(solution)/shard_map/all_to_all | solution.py:219
  275.1 10.2 %all-to-all-done = bf16[8,1,128,256]{3,2,1,0:T(8,128)(2,1)S(1)} async-done(((bf16[8,1,128,256]{3,2,1,0:T(8,128)(2,1)}), bf16[8,1,128,256]{3,2,1,0:T(8,128)(2,1)S(1)}, u32[]{:S(2)}, u32[]{:S(2)}) %all-to-all-start) | async-done | bytes 524320 | tf_op jit(solution)/shard_map/all_to_all | solution.py:219
  285.3 0.3 copy.71
  285.6 0.5 convolution_convert_fusion.1
  286.1 0.7 copy.77
  (33 shorter events, 0.3 us)
Async XLA Ops:
  6.5 1.6 copy-start
  6.5 42.3 %all-gather.7.cloned.1.call-start = ((), (), s32[]{:S(2)}) async-start(), calls=%async_computation.2 | async-start | bytes 4718592 | tf_op jit(solution)/shard_map/all_gather | solution.py:125
  7.3 193.2 %all-gather.5.cloned.1.call-start = ((), (), s32[]{:S(2)}) async-start(), calls=%async_computation.1 | async-start | bytes 17301504 | tf_op jit(solution)/shard_map/all_gather | solution.py:109
  8.0 220.5 %all-gather.9.cloned.1.call-start = ((), (), s32[]{:S(2)}) async-start(), calls=%async_computation.3 | async-start | bytes 2359296 | tf_op jit(solution)/shard_map/all_gather | solution.py:126
  9.1 249.2 %all-gather.11.cloned.1.call-start = ((), (), s32[]{:S(2)}) async-start(), calls=%async_computation.4 | async-start | bytes 2359296 | tf_op jit(solution)/shard_map/all_gather | solution.py:127
  200.5 10.7 %copy-start.1 = (bf16[8,128,8192]{2,1,0:T(8,128)(2,1)S(1)}, bf16[8,128,8192]{2,1,0:T(8,128)(2,1)}, u32[]{:S(2)}) copy-start(bf16[8,128,8192]{2,1,0:T(8,128)(2,1)} %all-gather.5.cloned.1.call-done) | copy-start | bytes 50331652
  228.5 10.1 %copy-start.4 = (bf16[8,128,2,64]{1,3,2,0:T(8,128)(2,1)S(1)}, bf16[8,128,2,64]{1,3,2,0:T(8,128)(2,1)}, u32[]{:S(2)}) copy-start(bf16[8,128,2,64]{1,3,2,0:T(8,128)(2,1)} %get-tuple-element.8) | copy-start | bytes 786436
  228.5 10.2 %copy-start.7 = (pred[8,128,128]{1,2,0:T(8,128)(4,1)S(1)}, pred[8,128,128]{1,2,0:T(8,128)(4,1)}, u32[]{:S(2)}) copy-start(pred[8,128,128]{1,2,0:T(8,128)(4,1)} %broadcast_and_fusion) | copy-start | bytes 393220
  228.5 10.6 %copy-start.2 = (bf16[8,128,2,64]{3,1,0,2:T(8,128)(2,1)S(1)}, bf16[8,128,2,64]{3,1,0,2:T(8,128)(2,1)}, u32[]{:S(2)}) copy-start(bf16[8,128,2,64]{3,1,0,2:T(8,128)(2,1)} %copy.65) | copy-start | bytes 786436
  239.0 6.2 %copy-start.5 = (f32[8,128,2,128]{1,3,2,0:T(8,128)}, f32[8,128,2,128]{1,3,2,0:T(8,128)S(1)}, u32[]{:S(2)}) copy-start(f32[8,128,2,128]{1,3,2,0:T(8,128)S(1)} %get-tuple-element.20) | copy-start | bytes 3145732
  239.0 6.2 %copy-start.3 = (bf16[2048,128]{1,0:T(8,128)(2,1)S(1)}, bf16[2048,128]{1,0:T(8,128)(2,1)}, u32[]{:S(2)}) copy-start(bf16[2048,128]{1,0:T(8,128)(2,1)} %all_gather.21) | copy-start | bytes 1572868
  245.2 13.0 %copy-start.6 = (f32[8,128,2,128]{1,3,2,0:T(8,128)S(1)}, f32[8,128,2,128]{1,3,2,0:T(8,128)}, u32[]{:S(2)}) copy-start(f32[8,128,2,128]{1,3,2,0:T(8,128)} %copy-done.5) | copy-start | bytes 3145732
  258.3 27.4 %copy-start.8 = (s32[64]{0:T(128)S(1)}, s32[64]{0:T(128)}, u32[]{:S(2)}) copy-start(s32[64]{0:T(128)} %param.18) | copy-start | bytes 772
  271.6 13.8 %all-to-all-start = ((bf16[8,1,128,256]{3,2,1,0:T(8,128)(2,1)}), bf16[8,1,128,256]{3,2,1,0:T(8,128)(2,1)S(1)}, u32[]{:S(2)}, u32[]{:S(2)}) async-start(bf16[8,1,128,256]{3,2,1,0:T(8,128)(2,1)} %copy.58), calls=%async_computation | async-start | bytes 1048576 | tf_op jit(solution)/shard_map/all_to_all | solution.py:219
Sparse Core Ops, SparseCore 0:
  9.2 39.6 all-gather.6
  51.3 149.1 all-gather.4
  202.4 26.0 all-gather.8
  230.2 28.0 all-gather.10
where the time goes:
time: 295 us; the launch traced here: 293 us
  waiting for transfers between devices  169 us (57%)
  matrix products  42.1 us (14%)
  blocking collectives  28.7 us (10%)
  local copies, waits for them, and re-layouts  21 us (7%)
  other arithmetic  15.5 us (5%)
  between operations  13.4 us (5%)
  starting transfers between devices  3.61 us (1%)
    all_gather x1, waiting for transfers between devices, attend(): gathered = lax.all_gather(blocks, 'fsdp', axis=2, tiled=True)  145 us
    all_gather x1, blocking collectives, attend(): lax.all_gather(prompt_values, 'group', axis=0, tiled=True)  15.3 us
    dot_general x1, matrix products, attend(): jnp.dot(normalized_input, pieces[0], preferred_element_type=jnp.float32)  14 us
    all_gather x1, blocking collectives, attend(): lax.all_gather(prompt_keys, 'group', axis=0, tiled=True)  13.4 us
    all_to_all x1, waiting for transfers between devices, body(): lax.all_to_all(packed, 'group', split_axis=0, concat_axis=0, tiled=True)  10.2 us
    dot_general x1, matrix products, attend(): jnp.einsum('zcmn,znu->zcmu', powers.astype(jnp.bfloat16), fresh_values, p...  10.1 us
    dot_general x1, matrix products, attend(): jnp.dot(normalized_input, pieces[1], preferred_element_type=jnp.float32)  10 us
    all_gather x1, waiting for transfers between devices, attend(): lax.all_gather(value_rows, 'group', axis=0, tiled=True)  8.71 us
  transfers between devices with their start and end apart: 5, of which 5 were waited for; matrix products, arithmetic and copies ran while one was open for 21% of the time, Pallas kernels for 0%

commit v1 on v0

v1 whole, which is shorter than its diff:
```python
import functools

import jax
import jax.numpy as jnp
from jax import lax
from jax.experimental import pallas as pl
from jax.experimental.pallas import tpu as pltpu
from jax.sharding import PartitionSpec as P

HEAD_SIZE = 128
PROMPT_TOKENS = 2048
IN_DEV = 8
OUT_DEV = 4
ROWS = 128
XS, CORES, ZS, YS = 4, 2, 8, 4
TILE = 256
MODEL_WIDTH = 8192

EPSILON = 1e-05
ROPE_THETA = 500000.0
CONTEXT_BASE = 8192.0
STRETCH = 8.0
MASKED_SCORE = -1e30

RELS = [(dx, dc) for dx in range(XS) for dc in range(CORES)]


def group_perm(dx, dc):
    return [
        (x * CORES + c, ((x + dx) % XS) * CORES + (c ^ dc)) for x in range(XS) for c in range(CORES)
    ]


def z_perm(d):
    return [(z * YS + y, ((z + d) % ZS) * YS + y) for z in range(ZS) for y in range(YS)]


def y_perm(d):
    return [(z * YS + y, z * YS + (y + d) % YS) for z in range(ZS) for y in range(YS)]


def send_group(v, dx, dc):
    return lax.ppermute(v, "group", group_perm(dx, dc))


def send_z(v, d):
    return lax.ppermute(v, "fsdp", z_perm(d))


def send_y(v, d):
    return lax.ppermute(v, "fsdp", y_perm(d))


def rope_tables(length, offset):
    half_dim = HEAD_SIZE // 2
    base_rate = ROPE_THETA ** (-(jnp.arange(half_dim, dtype=jnp.float32) * 2.0 / HEAD_SIZE))
    ratio = CONTEXT_BASE * base_rate / (2.0 * jnp.pi)
    smooth = jnp.clip((ratio - 1.0) / 3.0, 0.0, 1.0)
    inverse_rate = (1.0 - smooth) * base_rate / STRETCH + smooth * base_rate
    token_positions = jnp.arange(length, dtype=jnp.float32) + offset
    angles = token_positions[:, None] * inverse_rate[None, :]
    cosine, sine = jnp.cos(angles), jnp.sin(angles)
    return (
        jnp.concatenate([cosine, cosine], axis=1),
        jnp.concatenate([-sine, sine], axis=1),
    )


def swap_halves(v):
    half = HEAD_SIZE // 2
    return jnp.concatenate([v[:, half:], v[:, :half]], axis=1)


ANY = pl.BlockSpec(memory_space=pl.ANY)
VMEM = pl.BlockSpec(memory_space=pltpu.VMEM)
SMEM = pl.BlockSpec(memory_space=pltpu.SMEM)


def shaped(shape, dtype):
    return jax.ShapeDtypeStruct(shape, dtype)


def pack_kernel(meta, hidden, wq, wk, wv, kc, vc, *rest):
    outs, sems = rest[:-1], rest[-1]
    blocks, own, parts = outs[:8], outs[8], outs[9:12]
    z = meta[8]
    y = meta[9]
    cols = pl.ds(pl.multiple_of(z * HEAD_SIZE, HEAD_SIZE), HEAD_SIZE)
    rows = pl.ds(pl.multiple_of(y * TILE, TILE), TILE)
    copies = [(hidden.at[meta[i]], blocks[i]) for i in range(8)]
    for r in range(1, 4):
        other = lax.rem(y + YS - r, YS)
        copies.append(
            (wq.at[pl.ds(pl.multiple_of(other * TILE, TILE), TILE)], parts[r - 1])
        )
    copies.append((wq.at[rows], own.at[0]))
    copies.append((wk.at[rows, cols], own.at[1, :, pl.ds(0, HEAD_SIZE)]))
    copies.append((wv.at[rows, cols], own.at[1, :, pl.ds(HEAD_SIZE, HEAD_SIZE)]))
    copies.append((kc.at[:, cols], own.at[2, :, pl.ds(0, HEAD_SIZE)]))
    copies.append((vc.at[:, cols], own.at[2, :, pl.ds(HEAD_SIZE, HEAD_SIZE)]))
    started = [pltpu.make_async_copy(s, d, sems.at[i]) for i, (s, d) in enumerate(copies)]
    for copy in started:
        copy.start()
    for copy in started:
        copy.wait()


def pack(meta, hidden, wq, wk, wv, kc, vc):
    bf16 = jnp.bfloat16
    out_shape = (
        [shaped((ROWS, TILE), bf16)] * 8
        + [shaped((3, TILE, TILE), bf16)]
        + [shaped((TILE, TILE), bf16)] * 3
    )
    return pl.pallas_call(
        pack_kernel,
        out_shape=out_shape,
        in_specs=[SMEM] + [ANY] * 6,
        out_specs=[ANY] * 12,
        scratch_shapes=[pltpu.SemaphoreType.DMA((16,))],
        name="pack",
    )(meta, hidden, wq, wk, wv, kc, vc)


def unpack_kernel(source, *refs):
    pieces, x_ref, ss_ref = refs[:8], refs[8], refs[9]
    ones = jnp.ones((8, TILE), jnp.float32)
    for j in range(OUT_DEV):
        rows = pl.ds(j * ROWS, ROWS)
        for i in range(8):

            @pl.when(source[j] == i)
            def _():
                x_ref[rows, :] = pieces[i][...]

        wide = x_ref[rows, :].astype(jnp.float32)
        sums = lax.dot_general(
            ones,
            wide * wide,
            (((1,), (1,)), ((), ())),
            precision=lax.Precision.HIGHEST,
            preferred_element_type=jnp.float32,
        )
        ss_ref[pl.ds(j, 1), :] = sums[0:1, :]


def unpack(source, pieces):
    return pl.pallas_call(
        unpack_kernel,
        out_shape=[
            shaped((OUT_DEV * ROWS, TILE), jnp.bfloat16),
            shaped((OUT_DEV, ROWS), jnp.float32),
        ],
        in_specs=[SMEM] + [VMEM] * 8,
        out_specs=[VMEM] * 2,
        name="unpack",
    )(source, *pieces)


SHARDS = 8


def project_kernel(meta, scale, gain, *refs):
    shards, weights = refs[:9], refs[9:19]
    own_ref, kv_ref, o1, o2, o3 = refs[19:24]
    normed, wide_w, sems = refs[24:]
    copies = []

    def bring(src, first, last, position):
        base = pl.ds(pl.multiple_of(meta[8 + position] * TILE, TILE), TILE)
        for n in range(first, last):
            copies.append(
                pltpu.make_async_copy(
                    src.at[n - first], wide_w.at[n, base], sems.at[len(copies)]
                )
            )
            copies[-1].start()

    for half in range(2):
        own, left, right, far_a, far_b = weights[5 * half : 5 * half + 5]
        bring(own, 0, 5, 4 * half)
        bring(left, 0, 5, 4 * half + 1)
        bring(right, 0, 5, 4 * half + 2)
        bring(far_a, 0, 3, 4 * half + 3)
        bring(far_b, 3, 5, 4 * half + 3)

    def norm(src, rows, position):
        k = meta[position]
        cols = pl.ds(pl.multiple_of(k * TILE, TILE), TILE)
        normed[rows, cols] = (
            src[...].astype(jnp.float32) * scale[rows, :] * gain[pl.ds(k, 1), :]
        ).astype(jnp.bfloat16)

    every = pl.ds(0, OUT_DEV * ROWS)
    for s in range(7):
        norm(shards[s], every, s)
    half_rows = OUT_DEV * ROWS // 2
    norm(shards[7], pl.ds(0, half_rows), 7)
    norm(shards[8], pl.ds(half_rows, half_rows), 7)
    for copy in copies:
        copy.wait()

    def product(n):
        return jnp.dot(normed[...], wide_w[n], preferred_element_type=jnp.float32)

    kv_ref[...] = product(4)
    for n, out in ((1, o1), (2, o2), (3, o3)):
        out[...] = product(n).astype(jnp.bfloat16)
    own_ref[...] = product(0)


def project(meta, scale, gain, shards, weights):
    total = OUT_DEV * ROWS
    return pl.pallas_call(
        project_kernel,
        out_shape=[shaped((total, TILE), jnp.float32)] * 2
        + [shaped((total, TILE), jnp.bfloat16)] * 3,
        in_specs=[SMEM] + [VMEM] * 2 + [VMEM] * 9 + [ANY] * 10,
        out_specs=[VMEM] * 5,
        scratch_shapes=[
            pltpu.VMEM((total, SHARDS * TILE), jnp.bfloat16),
            pltpu.VMEM((5, SHARDS * TILE, TILE), jnp.bfloat16),
            pltpu.SemaphoreType.DMA((40,)),
        ],
        compiler_params=pltpu.CompilerParams(vmem_limit_bytes=40 * 2**20),
        cost_estimate=pl.CostEstimate(
            flops=2 * total * 2048 * 1280, bytes_accessed=10 * 2**20, transcendentals=0
        ),
        name="project",
    )(meta, scale, gain, *shards, *weights)


def attend_kernel(meta, own, o1, o2, o3, cosine, sine, fresh, *refs):
    caches, out_ref, keys, values = refs[:8], refs[8], refs[9], refs[10]
    slot = pl.program_id(0)
    part = TILE

    @pl.when(slot == 0)
    def _():
        for i, cache in enumerate(caches):
            keys[pl.ds(i * part, part), :] = cache[0, :, :HEAD_SIZE]
            values[pl.ds(i * part, part), :] = cache[0, :, HEAD_SIZE:]

    keys[pl.ds(PROMPT_TOKENS, ROWS), :] = fresh[0, :, :HEAD_SIZE]
    values[pl.ds(PROMPT_TOKENS, ROWS), :] = fresh[0, :, HEAD_SIZE:]
    q = own[...] + o1[...].astype(jnp.float32) + o2[...].astype(jnp.float32)
    q = q + o3[...].astype(jnp.float32)
    turned = []
    for h in range(2):
        v = q[:, h * HEAD_SIZE : (h + 1) * HEAD_SIZE]
        turned.append((v * cosine[...] + swap_halves(v) * sine[...]).astype(jnp.bfloat16))
    queries = jnp.concatenate(turned, axis=0)
    scores = lax.dot_general(
        queries, keys[...], (((1,), (1,)), ((), ())), preferred_element_type=jnp.float32
    ) * (HEAD_SIZE**-0.5)
    valid = meta[slot]
    row = lax.broadcasted_iota(jnp.int32, (2 * ROWS, ROWS), 0) % ROWS
    column = lax.broadcasted_iota(jnp.int32, (2 * ROWS, ROWS), 1)
    allowed = (column <= row) & (column < valid)
    old = scores[:, :PROMPT_TOKENS]
    new = jnp.where(allowed, scores[:, PROMPT_TOKENS:], MASKED_SCORE)
    top = jnp.maximum(
        jnp.max(old, axis=1, keepdims=True), jnp.max(new, axis=1, keepdims=True)
    )
    old, new = jnp.exp(old - top), jnp.exp(new - top)
    total = jnp.sum(old, axis=1, keepdims=True) + jnp.sum(new, axis=1, keepdims=True)
    mixed = jnp.dot(
        old.astype(jnp.bfloat16), values[:PROMPT_TOKENS, :], preferred_element_type=jnp.float32
    ) + jnp.dot(
        new.astype(jnp.bfloat16), values[PROMPT_TOKENS:, :], preferred_element_type=jnp.float32
    )
    mixed = jnp.where(row < valid, mixed / total, 0.0).astype(jnp.bfloat16)
    out_ref[0, :, :HEAD_SIZE] = mixed[:ROWS]
    out_ref[0, :, HEAD_SIZE:] = mixed[ROWS:]


def attend(meta, own, others, cosine, sine, fresh, caches, cache_blocks):
    by_slot = pl.BlockSpec((ROWS, TILE), lambda j, m: (j, 0))
    table = pl.BlockSpec((ROWS, HEAD_SIZE), lambda j, m: (0, 0))

    def cache_spec(block):
        return pl.BlockSpec((1, TILE, TILE), lambda j, m: (block, 0, 0))

    return pl.pallas_call(
        attend_kernel,
        out_shape=shaped((OUT_DEV, ROWS, TILE), jnp.bfloat16),
        grid_spec=pltpu.PrefetchScalarGridSpec(
            num_scalar_prefetch=1,
            grid=(OUT_DEV,),
            in_specs=[by_slot] * 4
            + [table] * 2
            + [pl.BlockSpec((1, ROWS, TILE), lambda j, m: (m[4 + j], 0, 0))]
            + [cache_spec(b) for b in cache_blocks],
            out_specs=pl.BlockSpec((1, ROWS, TILE), lambda j, m: (j, 0, 0)),
            scratch_shapes=[
                pltpu.VMEM((PROMPT_TOKENS + ROWS, HEAD_SIZE), jnp.bfloat16),
                pltpu.VMEM((PROMPT_TOKENS + ROWS, HEAD_SIZE), jnp.bfloat16),
            ],
        ),
        compiler_params=pltpu.CompilerParams(vmem_limit_bytes=40 * 2**20),
        cost_estimate=pl.CostEstimate(
            flops=4 * 1024 * 2176 * 128, bytes_accessed=4 * 2**20, transcendentals=1024 * 2176
        ),
        name="attend",
    )(meta, own, *others, cosine, sine, fresh, *caches)


def body(
    hidden,
    norm_gain,
    w_query,
    key_projection_weight,
    value_projection_weight,
    prompt_key_cache,
    prompt_value_cache,
    keep_flag,
    destination,
    row_counts,
):
    g = lax.axis_index("group")
    f = lax.axis_index("fsdp")
    x, c = g // CORES, g % CORES
    z, y = f // YS, f % YS

    block_ids = jnp.arange(keep_flag.shape[0], dtype=jnp.int32)
    live = keep_flag == 1
    targets = jnp.stack([((x + dx) % XS) * CORES + (c ^ dc) for dx, dc in RELS])
    mine = live & (block_ids // IN_DEV == g)
    chosen = jnp.sum(
        jnp.where(
            mine[None, :] & (destination[None, :] // OUT_DEV == targets[:, None]),
            block_ids[None, :] % IN_DEV,
            0,
        ),
        axis=1,
    )
    slots = g * OUT_DEV + jnp.arange(OUT_DEV, dtype=jnp.int32)
    matched = live[None, :] & (destination[None, :] == slots[:, None])
    sources = jnp.sum(jnp.where(matched, block_ids[None, :], 0), axis=1)
    lengths = jnp.sum(jnp.where(matched, row_counts[None, :], 0), axis=1)
    source_group = sources // IN_DEV
    source_rel = ((x - source_group // CORES) % XS) * CORES + (c ^ (source_group % CORES))

    pack_meta = jnp.concatenate([chosen, jnp.stack([z, y])]).astype(jnp.int32)
    packed = pack(
        pack_meta,
        hidden,
        w_query,
        key_projection_weight,
        value_projection_weight,
        prompt_key_cache,
        prompt_value_cache,
    )
    blocks, own_parts, w_parts = packed[:8], packed[8], packed[9:12]

    pieces = [
        blocks[i] if rel == (0, 0) else send_group(blocks[i], *rel) for i, rel in enumerate(RELS)
    ]
    rows, squares = unpack(source_rel.astype(jnp.int32), pieces)

    for bit in (1, 2, 4, 8, 16):
        squares = squares + lax.ppermute(squares, "fsdp", [(i, i ^ bit) for i in range(ZS * YS)])
    scale = lax.rsqrt(squares / MODEL_WIDTH + EPSILON).reshape(OUT_DEV * ROWS, 1)

    fwd, bwd = [rows], [rows]
    for _ in range(3):
        fwd.append(send_z(fwd[-1], 1))
        bwd.append(send_z(bwd[-1], -1))
    half = OUT_DEV * ROWS // 2
    far = [send_z(fwd[3][:half], 1), send_z(bwd[3][half:], -1)]
    shards = fwd + bwd[1:] + far
    shard_ids = [(z - s) % ZS for s in range(4)] + [(z + s) % ZS for s in (1, 2, 3)] + [(z + 4) % ZS]

    arrived = [send_y(w_parts[r - 1], -r) for r in (1, 2, 3)]
    own = jnp.concatenate([own_parts[:1], jnp.stack(arrived), own_parts[1:]], axis=0)
    left, right = send_group(own, 1, 0), send_group(own, -1, 0)
    far_a, far_b = send_group(left[:3], 1, 0), send_group(right[3:], -1, 0)
    same_core = [own, left, right, far_a, far_b]
    other_core = [send_group(v, 0, 1) for v in same_core]
    weights = same_core + other_core
    weight_ids = [
        ((x + dx) % XS) * CORES + cc for cc in (c, 1 - c) for dx in (0, -1, 1, 2)
    ]

    gain = norm_gain.reshape(ZS, YS, TILE)
    gain = lax.dynamic_index_in_dim(gain, y, 1, keepdims=False).astype(jnp.float32)
    meta = jnp.stack(shard_ids + weight_ids).astype(jnp.int32)
    q_own, kv_own, *q_others = project(meta, scale, gain, shards, weights)

    kv_slots = kv_own.reshape(OUT_DEV, ROWS, TILE)
    kv = lax.dynamic_index_in_dim(kv_slots, y, 0, keepdims=False)
    for r in (1, 2, 3):
        part = lax.dynamic_index_in_dim(kv_slots, (y + r) % YS, 0, keepdims=False)
        kv = kv + send_y(part.astype(jnp.bfloat16), r).astype(jnp.float32)
    q_parts = [send_y(v, r) for r, v in zip((1, 2, 3), q_others)]

    cosine, sine = rope_tables(ROWS, PROMPT_TOKENS)
    key = kv[:, :HEAD_SIZE]
    key = (key * cosine + swap_halves(key) * sine).astype(jnp.bfloat16)
    fresh_own = jnp.concatenate([key, kv[:, HEAD_SIZE:].astype(jnp.bfloat16)], axis=1)
    fresh = jnp.stack([fresh_own] + [send_y(fresh_own, r) for r in (1, 2, 3)])
    fresh_ids = (y - jnp.arange(OUT_DEV, dtype=jnp.int32)) % YS

    caches, cache_blocks = [], []
    for part in (same_core, other_core):
        caches += [part[0], part[1], part[2], part[4]]
        cache_blocks += [5, 5, 5, 2]
    return attend(
        jnp.concatenate([lengths, fresh_ids]).astype(jnp.int32),
        q_own,
        q_parts,
        cosine,
        sine,
        fresh,
        caches,
        cache_blocks,
    )


def solution(mesh):
    return jax.shard_map(
        body,
        mesh=mesh,
        in_specs=(
            P("group", None, "fsdp"),
            P(),
            P("group", "fsdp"),
            P("group", None),
            P("group", None),
            P("group", None),
            P("group", None),
            P(),
            P(),
            P(),
        ),
        out_specs=P("group", None, "fsdp"),
        check_vma=False,
    )
```

time: 295 us -> 197 us (0.67)
  waiting for transfers between devices: 169 us -> 49.7 us
  Pallas kernels: 0 us -> 62.9 us
  starting transfers between devices: 3.61 us -> 60.8 us
  matrix products: 42.1 us -> 0 us
  blocking collectives: 28.7 us -> 0 us
  between operations: 13.4 us -> 0.36 us
  other arithmetic: 15.5 us -> 7.23 us
  local copies, waits for them, and re-layouts: 21 us -> 14.3 us
    all_gather x4 -> x0, waiting for transfers between devices: 157 us -> none  [the longest x1 145 us: attend(): gathered = lax.all_gather(blocks, 'fsdp', axis=2, tiled=True)]
    pallas_call x0 -> x4, Pallas kernels: none -> 62.9 us  [the longest x1 41.7 us: pack(): pl.pallas_call(pack_kernel, out_shape=out_shape, in_specs=[SMEM] + [ANY]...]
    ppermute x0 -> x41, starting transfers between devices: none -> 60.8 us  [the longest x12 19.5 us: send_y(): return lax.ppermute(v, 'fsdp', y_perm(d))]
    ppermute x0 -> x41, waiting for transfers between devices: none -> 49.7 us  [the longest x12 22.2 us: send_y(): return lax.ppermute(v, 'fsdp', y_perm(d))]
    dot_general x8 -> x0, matrix products: 42.1 us -> none  [the longest x1 14 us: attend(): jnp.dot(normalized_input, pieces[0], preferred_element_type=jnp.float32)]
    all_gather x2 -> x0, blocking collectives: 28.7 us -> none  [the longest x1 15.3 us: attend(): lax.all_gather(prompt_values, 'group', axis=0, tiled=True)]
    reduce_sum x4 -> x2, other arithmetic: 11.2 us -> 0.88 us  [the longest x1 0.7 us: body(): sources = jnp.sum(jnp.where(matched, block_ids[None, :], 0), axis=1)]
    all_to_all x1 -> x0, waiting for transfers between devices: 10.2 us -> none  [body(): lax.all_to_all(packed, 'group', split_axis=0, concat_axis=0, tiled=True)]
  transfers between devices with their start and end apart: 5 -> 41, of which waited for: 5 -> 15; matrix products, arithmetic and copies ran while one was open for 21% -> 7% of each run, Pallas kernels for 0% -> 2%
where the time goes in v1:
time: 197 us; the launch traced here: 195 us
  Pallas kernels  62.9 us (32%)
  starting transfers between devices  60.8 us (31%)
  waiting for transfers between devices  49.7 us (25%)
  local copies, waits for them, and re-layouts  14.3 us (7%)
  other arithmetic  7.23 us (4%)
    pallas_call x1, Pallas kernels, pack(): pl.pallas_call(pack_kernel, out_shape=out_shape, in_specs=[SMEM] + [ANY]...  41.7 us
    ppermute x12, waiting for transfers between devices, send_y(): return lax.ppermute(v, 'fsdp', y_perm(d))  22.2 us
    ppermute x12, starting transfers between devices, send_y(): return lax.ppermute(v, 'fsdp', y_perm(d))  19.5 us
    ppermute x8, starting transfers between devices, send_z(): return lax.ppermute(v, 'fsdp', z_perm(d))  16.9 us
    ppermute x16, starting transfers between devices, send_group(): return lax.ppermute(v, 'group', group_perm(dx, dc))  14.4 us
    ppermute x5, waiting for transfers between devices, body(): lax.ppermute(squares, 'fsdp', [(i, i ^ bit) for i in range(ZS * YS)])  14.1 us
    pallas_call x1, Pallas kernels, project(): pl.pallas_call(project_kernel, out_shape=[shaped((total, TILE), jnp.float...  10.3 us
    ppermute x5, starting transfers between devices, body(): lax.ppermute(squares, 'fsdp', [(i, i ^ bit) for i in range(ZS * YS)])  10.1 us
  transfers between devices with their start and end apart: 41, of which 15 were waited for; matrix products, arithmetic and copies ran while one was open for 7% of the time, Pallas kernels for 2%

profile of v1, /device:TPU:8, one launch (start us, length us, event | category | flops | bytes accessed | tf_op | source)
XLA Modules:
  0.0 195.3 jit_solution(11341592051177821913)
XLA Ops:
  2.2 41.7 %pack.1 = (bf16[128,256]{1,0:T(8,128)(2,1)}, bf16[128,256]{1,0:T(8,128)(2,1)}, bf16[128,256]{1,0:T(8,128)(2,1)}, bf16[128,256]{1,0:T(8,128)(2,1)}, bf16[128,256]...) custom-call(s32[10]{0:T(128)} %pad_add_fusion.1.meta, ...), custom_call_target="tpu_custom_call" | custom-call | tf_op jit(solution)/shard_map/pack/pallas_call | solution.py:115
  44.1 1.6 collective-permute-start.1
  45.6 1.2 collective-permute-start.2
  46.9 1.7 collective-permute-start.3
  48.6 2.2 %collective-permute-start.20 = (bf16[256,256]{1,0:T(8,128)(2,1)}, bf16[256,256]{1,0:T(8,128)(2,1)S(1)}, u32[]{:S(2)}, u32[]{:S(2)}) collective-permute-start(bf16[256,256]{1,0:T(8,128)(2,1)} %get-tuple-element.35), channel_id=1, source_target_pairs={{0,3},{1,0},{2,1},{3,2},{4,7},{5,4},{6,5},{7,6},{8,11},{9,8},{10,9... | collective-permute-start | bytes 393224 | tf_op jit(solution)/shard_map/ppermute | solution.py:51
  52.4 1.8 collective-permute-done.20
  54.3 3.5 %collective-permute-start.21 = (bf16[256,256]{1,0:T(8,128)(2,1)}, bf16[256,256]{1,0:T(8,128)(2,1)S(1)}, u32[]{:S(2)}, u32[]{:S(2)}) collective-permute-start(bf16[256,256]{1,0:T(8,128)(2,1)} %get-tuple-element.36), channel_id=1, source_target_pairs={{0,2},{1,3},{2,0},{3,1},{4,6},{5,7},{6,4},{7,5},{8,10},{9,11},{10,... | collective-permute-start | bytes 393224 | tf_op jit(solution)/shard_map/ppermute | solution.py:51
  57.8 3.2 %collective-permute-done.21 = bf16[256,256]{1,0:T(8,128)(2,1)S(1)} collective-permute-done((bf16[256,256]{1,0:T(8,128)(2,1)}, bf16[256,256]{1,0:T(8,128)(2,1)S(1)}, u32[]{:S(2)}, u32[]{:S(2)}) %collective-permute-start.21) | collective-permute-done | bytes 131104 | tf_op jit(solution)/shard_map/ppermute | solution.py:51
  61.0 1.6 collective-permute-start.22
  62.5 3.8 %collective-permute-done.22 = bf16[256,256]{1,0:T(8,128)(2,1)S(1)} collective-permute-done((bf16[256,256]{1,0:T(8,128)(2,1)}, bf16[256,256]{1,0:T(8,128)(2,1)S(1)}, u32[]{:S(2)}, u32[]{:S(2)}) %collective-permute-start.22) | collective-permute-done | bytes 131104 | tf_op jit(solution)/shard_map/ppermute | solution.py:51
  66.3 1.0 slice_dynamic-update-slice_fusion.refs_9_.refs_0_
  67.3 2.1 %collective-permute-start.5 = (bf16[128,256]{1,0:T(8,128)(2,1)}, bf16[128,256]{1,0:T(8,128)(2,1)S(1)}, u32[]{:S(2)}, u32[]{:S(2)}) collective-permute-start(bf16[128,256]{1,0:T(8,128)(2,1)} %get-tuple-element.30), channel_id=1, source_target_pairs={{0,192},{32,224},{64,0},{96,32},{128,64},{160,96},{192,128},{224,1... | collective-permute-start | bytes 196616 | tf_op jit(solution)/shard_map/ppermute | solution.py:43
  69.4 1.5 collective-permute-start.6
  70.9 1.3 collective-permute-start.23
  72.3 1.9 collective-permute-start.24
  75.5 3.0 %unpack.1 = (bf16[512,256]{1,0:T(8,128)(2,1)}, f32[4,128]{1,0:T(4,128)}) custom-call(s32[4]{0:T(128)} %fusion.10.source, bf16[128,256]{1,0:T(8,128)(2,1)} %get-tuple-element.24.refs_0_, bf16[128,256]{1,0:T(8,128)(2,1)} %copy-done.6, bf16[128,256]{1,0:T(8,128)(2,1)} %copy-done.7, bf16[128,256]{1,0:T(8,128)(2,1)} %copy-done.8, bf16[128,256]{1,0:T(8,128)(2,1)} %copy-done.9, ...), custom_call_target="tpu_custom_call" | custom-call | tf_op jit(solution)/shard_map/unpack/pallas_call | solution.py:148
  78.5 1.8 collective-permute-start.12
  80.2 3.9 %collective-permute-start.15 = (bf16[512,256]{1,0:T(8,128)(2,1)}, bf16[512,256]{1,0:T(8,128)(2,1)S(1)}, u32[]{:S(2)}, u32[]{:S(2)}) collective-permute-start(bf16[512,256]{1,0:T(8,128)(2,1)} %get-tuple-element.33.refs_0_), channel_id=1, source_target_pairs={{0,28},{1,29},{2,30},{3,31},{4,0},{5,1},{6,2},{7,3},{8,4},{9,5},{1... | collective-permute-start | bytes 786440 | tf_op jit(solution)/shard_map/ppermute | solution.py:47
  84.2 7.2 %collective-permute-done.12.refs_1_ = bf16[512,256]{1,0:T(8,128)(2,1)S(1)} collective-permute-done((bf16[512,256]{1,0:T(8,128)(2,1)}, bf16[512,256]{1,0:T(8,128)(2,1)S(1)}, u32[]{:S(2)}, u32[]{:S(2)}) %collective-permute-start.12) | collective-permute-done | bytes 262176 | tf_op jit(solution)/shard_map/ppermute | solution.py:47
  92.1 3.2 %collective-permute-start.16 = (bf16[512,256]{1,0:T(8,128)(2,1)S(1)}, bf16[512,256]{1,0:T(8,128)(2,1)}, u32[]{:S(2)}, u32[]{:S(2)}) collective-permute-start(bf16[512,256]{1,0:T(8,128)(2,1)S(1)} %collective-permute-done.15.refs_4_), channel_id=1, source_target_pairs={{0,28},{1,29},{2,30},{3,31},{4,0},{5,1},{6,2},{7,3},{8,4},{9,5},{1... | collective-permute-start | bytes 786440 | tf_op jit(solution)/shard_map/ppermute | solution.py:47
  96.0 2.7 %collective-permute-start.7 = (f32[4,128]{1,0:T(4,128)}, f32[4,128]{1,0:T(4,128)S(1)}, u32[]{:S(2)}, u32[]{:S(2)}) collective-permute-start(f32[4,128]{1,0:T(4,128)} %get-tuple-element.32), channel_id=1, source_target_pairs={{0,1},{1,0},{2,3},{3,2},{4,5},{5,4},{6,7},{7,6},{8,9},{9,8},{10,11... | collective-permute-start | bytes 6152 | tf_op jit(solution)/shard_map/ppermute | solution.py:362
  98.7 1.8 collective-permute-done.7
  101.1 2.9 %collective-permute-start.8 = (f32[4,128]{1,0:T(4,128)S(1)}, f32[4,128]{1,0:T(4,128)S(1)}, u32[]{:S(2)}, u32[]{:S(2)}) collective-permute-start(f32[4,128]{1,0:T(4,128)S(1)} %add.322), channel_id=1, source_target_pairs={{0,2},{1,3},{2,0},{3,1},{4,6},{5,7},{6,4},{7,5},{8,10},{9,11},{10,... | collective-permute-start | bytes 6152 | tf_op jit(solution)/shard_map/ppermute | solution.py:362
  104.0 2.2 %collective-permute-done.8 = f32[4,128]{1,0:T(4,128)S(1)} collective-permute-done((f32[4,128]{1,0:T(4,128)S(1)}, f32[4,128]{1,0:T(4,128)S(1)}, u32[]{:S(2)}, u32[]{:S(2)}) %collective-permute-start.8) | collective-permute-done | bytes 2080 | tf_op jit(solution)/shard_map/ppermute | solution.py:362
  106.2 3.6 %collective-permute-done.9 = f32[4,128]{1,0:T(4,128)S(1)} collective-permute-done((f32[4,128]{1,0:T(4,128)S(1)}, f32[4,128]{1,0:T(4,128)S(1)}, u32[]{:S(2)}, u32[]{:S(2)}) %collective-permute-start.9) | collective-permute-done | bytes 2080 | tf_op jit(solution)/shard_map/ppermute | solution.py:362
  110.0 4.3 %collective-permute-done.10 = f32[4,128]{1,0:T(4,128)S(1)} collective-permute-done((f32[4,128]{1,0:T(4,128)S(1)}, f32[4,128]{1,0:T(4,128)S(1)}, u32[]{:S(2)}, u32[]{:S(2)}) %collective-permute-start.10) | collective-permute-done | bytes 2080 | tf_op jit(solution)/shard_map/ppermute | solution.py:362
  114.3 3.2 %collective-permute-start.17 = (bf16[512,256]{1,0:T(8,128)(2,1)}, bf16[512,256]{1,0:T(8,128)(2,1)}, u32[]{:S(2)}, u32[]{:S(2)}) collective-permute-start(bf16[512,256]{1,0:T(8,128)(2,1)} %collective-permute-done.16.refs_5_), channel_id=1, source_target_pairs={{0,28},{1,29},{2,30},{3,31},{4,0},{5,1},{6,2},{7,3},{8,4},{9,5},{1... | collective-permute-start | bytes 786440 | tf_op jit(solution)/shard_map/ppermute | solution.py:47
  117.6 4.4 %collective-permute-start.11 = (f32[4,128]{1,0:T(4,128)S(1)}, f32[4,128]{1,0:T(4,128)}, u32[]{:S(2)}, u32[]{:S(2)}) collective-permute-start(f32[4,128]{1,0:T(4,128)S(1)} %add.325), channel_id=1, source_target_pairs={{0,16},{1,17},{2,18},{3,19},{4,20},{5,21},{6,22},{7,23},{8,24},{9,... | collective-permute-start | bytes 6152 | tf_op jit(solution)/shard_map/ppermute | solution.py:362
  123.8 2.2 %collective-permute-done.11 = f32[4,128]{1,0:T(4,128)} collective-permute-done((f32[4,128]{1,0:T(4,128)S(1)}, f32[4,128]{1,0:T(4,128)}, u32[]{:S(2)}, u32[]{:S(2)}) %collective-permute-start.11) | collective-permute-done | bytes 2080 | tf_op jit(solution)/shard_map/ppermute | solution.py:362
  125.9 2.0 %collective-permute-start.26 = (bf16[3,256,256]{2,1,0:T(8,128)(2,1)}, bf16[3,256,256]{2,1,0:T(8,128)(2,1)S(1)}, u32[]{:S(2)}, u32[]{:S(2)}) collective-permute-start(bf16[3,256,256]{2,1,0:T(8,128)(2,1)} %slice.46), channel_id=1, source_target_pairs={{0,192},{32,224},{64,0},{96,32},{128,64},{160,96},{192,128},{224,1... | collective-permute-start | bytes 1179656 | tf_op jit(solution)/shard_map/ppermute | solution.py:43
  129.3 1.6 slice.43
  130.9 2.0 collective-permute-start.18
  132.8 2.1 %collective-permute-done.25.refs_12_ = bf16[3,256,256]{2,1,0:T(8,128)(2,1)} collective-permute-done((bf16[3,256,256]{2,1,0:T(8,128)(2,1)}, bf16[3,256,256]{2,1,0:T(8,128)(2,1)}, u32[]{:S(2)}, u32[]{:S(2)}) %collective-permute-start.25) | collective-permute-done | bytes 393248 | tf_op jit(solution)/shard_map/ppermute | solution.py:43
  134.9 1.9 collective-permute-done.26.refs_13_.refs_3_
  138.1 1.6 slice.44
  139.6 2.8 %collective-permute-start.19 = (bf16[256,256]{1,0:T(8,128)(2,1)}, bf16[256,256]{1,0:T(8,128)(2,1)}, u32[]{:S(2)}, u32[]{:S(2)}) collective-permute-start(bf16[256,256]{1,0:T(8,128)(2,1)} %slice.44), channel_id=1, source_target_pairs={{0,28},{1,29},{2,30},{3,31},{4,0},{5,1},{6,2},{7,3},{8,4},{9,5},{1... | collective-permute-start | bytes 393224 | tf_op jit(solution)/shard_map/ppermute | solution.py:47
  144.0 2.2 %collective-permute-done.19.refs_8_ = bf16[256,256]{1,0:T(8,128)(2,1)} collective-permute-done((bf16[256,256]{1,0:T(8,128)(2,1)}, bf16[256,256]{1,0:T(8,128)(2,1)}, u32[]{:S(2)}, u32[]{:S(2)}) %collective-permute-start.19) | collective-permute-done | bytes 131104 | tf_op jit(solution)/shard_map/ppermute | solution.py:47
  150.0 10.3 %project.1 = (f32[512,256]{1,0:T(8,128)S(1)}, f32[512,256]{1,0:T(8,128)S(1)}, bf16[512,256]{1,0:T(8,128)(2,1)S(1)}, bf16[512,256]{1,0:T(8,128)(2,1)S(1)}, bf16[512,256]{1,0:T(8,128)(2,1)S(1)}) custom-call(s32[16]{0:T(128)S(1)} %stack.118.meta, f32[512,1]{1,0:T(8,128)S(1)} %copy-done, f32[8,256]{1,0:T(8,128)S(1)} %fusion.8.gain, ...), custom_call_target="tpu_custom_call" | custom-call | flops 2684354560 | bytes 10485760 | tf_op jit(solution)/shard_map/project/pallas_call | solution.py:214
  160.3 2.1 %collective-permute-start.37 = (bf16[128,256]{1,0:T(8,128)(2,1)S(1)}, bf16[128,256]{1,0:T(8,128)(2,1)S(1)}, u32[]{:S(2)}, u32[]{:S(2)}) collective-permute-start(bf16[128,256]{1,0:T(8,128)(2,1)S(1)} %get-tuple-element.48), channel_id=1, source_target_pairs={{0,3},{1,0},{2,1},{3,2},{4,7},{5,4},{6,5},{7,6},{8,11},{9,8},{10,9... | collective-permute-start | bytes 196616 | tf_op jit(solution)/shard_map/ppermute | solution.py:51
  163.4 2.5 %collective-permute-start.35 = (bf16[128,256]{1,0:T(8,128)(2,1)S(1)}, bf16[128,256]{1,0:T(8,128)(2,1)S(1)}, u32[]{:S(2)}, u32[]{:S(2)}) collective-permute-start(bf16[128,256]{1,0:T(8,128)(2,1)S(1)} %get-tuple-element.47), channel_id=1, source_target_pairs={{0,1},{1,2},{2,3},{3,0},{4,5},{5,6},{6,7},{7,4},{8,9},{9,10},{10,1... | collective-permute-start | bytes 196616 | tf_op jit(solution)/shard_map/ppermute | solution.py:51
  165.9 1.0 fusion.7
  167.6 1.0 collective-permute-start.33
  168.5 1.7 collective-permute-start.34
  170.5 2.1 %collective-permute-start.40 = (bf16[128,256]{1,0:T(8,128)(2,1)S(1)}, bf16[128,256]{1,0:T(8,128)(2,1)S(1)}, u32[]{:S(2)}, u32[]{:S(2)}) collective-permute-start(bf16[128,256]{1,0:T(8,128)(2,1)S(1)} %get-tuple-element.53), channel_id=1, source_target_pairs={{0,3},{1,0},{2,1},{3,2},{4,7},{5,4},{6,5},{7,6},{8,11},{9,8},{10,9... | collective-permute-start | bytes 196616 | tf_op jit(solution)/shard_map/ppermute | solution.py:51
  172.7 10.4 %collective-permute-done.40 = bf16[128,256]{1,0:T(8,128)(2,1)S(1)} collective-permute-done((bf16[128,256]{1,0:T(8,128)(2,1)S(1)}, bf16[128,256]{1,0:T(8,128)(2,1)S(1)}, u32[]{:S(2)}, u32[]{:S(2)}) %collective-permute-start.40) | collective-permute-done | bytes 65568 | tf_op jit(solution)/shard_map/ppermute | solution.py:51
  183.1 1.2 collective-permute-start.38
  184.4 3.0 %collective-permute-done.38 = bf16[128,256]{1,0:T(8,128)(2,1)S(1)} collective-permute-done((bf16[128,256]{1,0:T(8,128)(2,1)S(1)}, bf16[128,256]{1,0:T(8,128)(2,1)S(1)}, u32[]{:S(2)}, u32[]{:S(2)}) %collective-permute-start.38) | collective-permute-done | bytes 65568 | tf_op jit(solution)/shard_map/ppermute | solution.py:51
  187.4 7.9 %attend.1 = bf16[4,128,256]{2,1,0:T(8,128)(2,1)} custom-call(s32[8]{0:T(128)S(1)} %pad_add_fusion.meta, f32[512,256]{1,0:T(8,128)S(1)} %get-tuple-element.38.own, bf16[512,256]{1,0:T(8,128)(2,1)S(1)} %collective-permute-done.32.o1, bf16[512,256]{1,0:T(8,128)(2,1)S(1)} %collective-permute-done.33.o2, bf16[512,256]{1,0:T(8,128)(2,1)S(1)} %collective-permute-done.34.o3, ...), custom_call_target="tpu_custom_call" | custom-call | flops 1140850688 | bytes 4194304 | tf_op jit(solution)/shard_map/attend/pallas_call | solution.py:284
  (111 shorter events, 19.4 us)
Async XLA Ops:
  2.2 49.5 %copy-start.14 = (s32[64]{0:T(128)S(1)}, s32[64]{0:T(128)}, u32[]{:S(2)}) copy-start(s32[64]{0:T(128)} %param.18) | copy-start | bytes 772
  2.2 49.5 %copy-start.15 = (s32[64]{0:T(128)S(1)}, s32[64]{0:T(128)}, u32[]{:S(2)}) copy-start(s32[64]{0:T(128)} %param.19) | copy-start | bytes 772
  44.0 23.3 %collective-permute-start = (bf16[128,256]{1,0:T(8,128)(2,1)}, bf16[128,256]{1,0:T(8,128)(2,1)S(1)}, u32[]{:S(2)}, u32[]{:S(2)}) collective-permute-start(bf16[128,256]{1,0:T(8,128)(2,1)} %get-tuple-element.25), channel_id=1, source_target_pairs={{0,32},{32,0},{64,96},{96,64},{128,160},{160,128},{192,224},{224,1... | collective-permute-start | bytes 196616 | tf_op jit(solution)/shard_map/ppermute | solution.py:43
  44.1 25.3 %collective-permute-start.1 = (bf16[128,256]{1,0:T(8,128)(2,1)}, bf16[128,256]{1,0:T(8,128)(2,1)S(1)}, u32[]{:S(2)}, u32[]{:S(2)}) collective-permute-start(bf16[128,256]{1,0:T(8,128)(2,1)} %get-tuple-element.26), channel_id=1, source_target_pairs={{0,64},{32,96},{64,128},{96,160},{128,192},{160,224},{192,0},{224,... | collective-permute-start | bytes 196616 | tf_op jit(solution)/shard_map/ppermute | solution.py:43
  45.6 25.3 %collective-permute-start.2 = (bf16[128,256]{1,0:T(8,128)(2,1)}, bf16[128,256]{1,0:T(8,128)(2,1)S(1)}, u32[]{:S(2)}, u32[]{:S(2)}) collective-permute-start(bf16[128,256]{1,0:T(8,128)(2,1)} %get-tuple-element.27), channel_id=1, source_target_pairs={{0,96},{32,64},{64,160},{96,128},{128,224},{160,192},{192,32},{224... | collective-permute-start | bytes 196616 | tf_op jit(solution)/shard_map/ppermute | solution.py:43
  46.9 25.4 %collective-permute-start.3 = (bf16[128,256]{1,0:T(8,128)(2,1)}, bf16[128,256]{1,0:T(8,128)(2,1)S(1)}, u32[]{:S(2)}, u32[]{:S(2)}) collective-permute-start(bf16[128,256]{1,0:T(8,128)(2,1)} %get-tuple-element.28), channel_id=1, source_target_pairs={{0,128},{32,160},{64,192},{96,224},{128,0},{160,32},{192,64},{224,... | collective-permute-start | bytes 196616 | tf_op jit(solution)/shard_map/ppermute | solution.py:43
  48.6 5.7 %collective-permute-start.20 = (bf16[256,256]{1,0:T(8,128)(2,1)}, bf16[256,256]{1,0:T(8,128)(2,1)S(1)}, u32[]{:S(2)}, u32[]{:S(2)}) collective-permute-start(bf16[256,256]{1,0:T(8,128)(2,1)} %get-tuple-element.35), channel_id=1, source_target_pairs={{0,3},{1,0},{2,1},{3,2},{4,7},{5,4},{6,5},{7,6},{8,11},{9,8},{10,9... | collective-permute-start | bytes 393224 | tf_op jit(solution)/shard_map/ppermute | solution.py:51
  54.3 6.7 %collective-permute-start.21 = (bf16[256,256]{1,0:T(8,128)(2,1)}, bf16[256,256]{1,0:T(8,128)(2,1)S(1)}, u32[]{:S(2)}, u32[]{:S(2)}) collective-permute-start(bf16[256,256]{1,0:T(8,128)(2,1)} %get-tuple-element.36), channel_id=1, source_target_pairs={{0,2},{1,3},{2,0},{3,1},{4,6},{5,7},{6,4},{7,5},{8,10},{9,11},{10,... | collective-permute-start | bytes 393224 | tf_op jit(solution)/shard_map/ppermute | solution.py:51
  61.0 5.3 %collective-permute-start.22 = (bf16[256,256]{1,0:T(8,128)(2,1)}, bf16[256,256]{1,0:T(8,128)(2,1)S(1)}, u32[]{:S(2)}, u32[]{:S(2)}) collective-permute-start(bf16[256,256]{1,0:T(8,128)(2,1)} %get-tuple-element.37), channel_id=1, source_target_pairs={{0,1},{1,2},{2,3},{3,0},{4,5},{5,6},{6,7},{7,4},{8,9},{9,10},{10,1... | collective-permute-start | bytes 393224 | tf_op jit(solution)/shard_map/ppermute | solution.py:51
  66.3 8.5 %collective-permute-start.4 = (bf16[128,256]{1,0:T(8,128)(2,1)}, bf16[128,256]{1,0:T(8,128)(2,1)S(1)}, u32[]{:S(2)}, u32[]{:S(2)}) collective-permute-start(bf16[128,256]{1,0:T(8,128)(2,1)} %get-tuple-element.29), channel_id=1, source_target_pairs={{0,160},{32,128},{64,224},{96,192},{128,32},{160,0},{192,96},{224,... | collective-permute-start | bytes 196616 | tf_op jit(solution)/shard_map/ppermute | solution.py:43
  67.3 7.5 %copy-start.6 = (bf16[128,256]{1,0:T(8,128)(2,1)}, bf16[128,256]{1,0:T(8,128)(2,1)S(1)}, u32[]{:S(2)}) copy-start(bf16[128,256]{1,0:T(8,128)(2,1)S(1)} %collective-permute-done.refs_1_) | copy-start | bytes 196612
  67.3 7.5 %collective-permute-start.5 = (bf16[128,256]{1,0:T(8,128)(2,1)}, bf16[128,256]{1,0:T(8,128)(2,1)S(1)}, u32[]{:S(2)}, u32[]{:S(2)}) collective-permute-start(bf16[128,256]{1,0:T(8,128)(2,1)} %get-tuple-element.30), channel_id=1, source_target_pairs={{0,192},{32,224},{64,0},{96,32},{128,64},{160,96},{192,128},{224,1... | collective-permute-start | bytes 196616 | tf_op jit(solution)/shard_map/ppermute | solution.py:43
  69.4 5.4 %copy-start.7 = (bf16[128,256]{1,0:T(8,128)(2,1)}, bf16[128,256]{1,0:T(8,128)(2,1)S(1)}, u32[]{:S(2)}) copy-start(bf16[128,256]{1,0:T(8,128)(2,1)S(1)} %collective-permute-done.1.refs_2_) | copy-start | bytes 196612
  69.4 5.4 %collective-permute-start.6 = (bf16[128,256]{1,0:T(8,128)(2,1)}, bf16[128,256]{1,0:T(8,128)(2,1)S(1)}, u32[]{:S(2)}, u32[]{:S(2)}) collective-permute-start(bf16[128,256]{1,0:T(8,128)(2,1)} %get-tuple-element.31), channel_id=1, source_target_pairs={{0,224},{32,192},{64,32},{96,0},{128,96},{160,64},{192,160},{224,1... | collective-permute-start | bytes 196616 | tf_op jit(solution)/shard_map/ppermute | solution.py:43
  70.9 3.9 %copy-start.8 = (bf16[128,256]{1,0:T(8,128)(2,1)}, bf16[128,256]{1,0:T(8,128)(2,1)S(1)}, u32[]{:S(2)}) copy-start(bf16[128,256]{1,0:T(8,128)(2,1)S(1)} %collective-permute-done.2.refs_3_) | copy-start | bytes 196612
  70.9 46.6 %collective-permute-start.23 = (bf16[6,256,256]{2,1,0:T(8,128)(2,1)S(1)}, bf16[6,256,256]{2,1,0:T(8,128)(2,1)S(1)}, u32[]{:S(2)}, u32[]{:S(2)}) collective-permute-start(bf16[6,256,256]{2,1,0:T(8,128)(2,1)S(1)} %slice_dynamic-update-slice_fusion.refs_9_.refs_0_), channel_id=1, source_target_pairs={{0,64},{32,96},{64,128},{96,160},{128,192},{160,224},{192,0},{224,... | collective-permute-start | bytes 2359304 | tf_op jit(solution)/shard_map/ppermute | solution.py:43
  72.3 50.4 %collective-permute-start.24 = (bf16[6,256,256]{2,1,0:T(8,128)(2,1)S(1)}, bf16[6,256,256]{2,1,0:T(8,128)(2,1)S(1)}, u32[]{:S(2)}, u32[]{:S(2)}) collective-permute-start(bf16[6,256,256]{2,1,0:T(8,128)(2,1)S(1)} %slice_dynamic-update-slice_fusion.refs_9_.refs_0_), channel_id=1, source_target_pairs={{0,192},{32,224},{64,0},{96,32},{128,64},{160,96},{192,128},{224,1... | collective-permute-start | bytes 2359304 | tf_op jit(solution)/shard_map/ppermute | solution.py:43
  78.5 12.9 %collective-permute-start.12 = (bf16[512,256]{1,0:T(8,128)(2,1)}, bf16[512,256]{1,0:T(8,128)(2,1)S(1)}, u32[]{:S(2)}, u32[]{:S(2)}) collective-permute-start(bf16[512,256]{1,0:T(8,128)(2,1)} %get-tuple-element.33.refs_0_), channel_id=1, source_target_pairs={{0,4},{1,5},{2,6},{3,7},{4,8},{5,9},{6,10},{7,11},{8,12},{9,13},{1... | collective-permute-start | bytes 786440 | tf_op jit(solution)/shard_map/ppermute | solution.py:47
  80.2 11.9 %collective-permute-start.15 = (bf16[512,256]{1,0:T(8,128)(2,1)}, bf16[512,256]{1,0:T(8,128)(2,1)S(1)}, u32[]{:S(2)}, u32[]{:S(2)}) collective-permute-start(bf16[512,256]{1,0:T(8,128)(2,1)} %get-tuple-element.33.refs_0_), channel_id=1, source_target_pairs={{0,28},{1,29},{2,30},{3,31},{4,0},{5,1},{6,2},{7,3},{8,4},{9,5},{1... | collective-permute-start | bytes 786440 | tf_op jit(solution)/shard_map/ppermute | solution.py:47
  91.4 22.9 %collective-permute-start.13 = (bf16[512,256]{1,0:T(8,128)(2,1)S(1)}, bf16[512,256]{1,0:T(8,128)(2,1)}, u32[]{:S(2)}, u32[]{:S(2)}) collective-permute-start(bf16[512,256]{1,0:T(8,128)(2,1)S(1)} %collective-permute-done.12.refs_1_), channel_id=1, source_target_pairs={{0,4},{1,5},{2,6},{3,7},{4,8},{5,9},{6,10},{7,11},{8,12},{9,13},{1... | collective-permute-start | bytes 786440 | tf_op jit(solution)/shard_map/ppermute | solution.py:47
  92.1 22.2 %collective-permute-start.16 = (bf16[512,256]{1,0:T(8,128)(2,1)S(1)}, bf16[512,256]{1,0:T(8,128)(2,1)}, u32[]{:S(2)}, u32[]{:S(2)}) collective-permute-start(bf16[512,256]{1,0:T(8,128)(2,1)S(1)} %collective-permute-done.15.refs_4_), channel_id=1, source_target_pairs={{0,28},{1,29},{2,30},{3,31},{4,0},{5,1},{6,2},{7,3},{8,4},{9,5},{1... | collective-permute-start | bytes 786440 | tf_op jit(solution)/shard_map/ppermute | solution.py:47
  96.0 4.4 %collective-permute-start.7 = (f32[4,128]{1,0:T(4,128)}, f32[4,128]{1,0:T(4,128)S(1)}, u32[]{:S(2)}, u32[]{:S(2)}) collective-permute-start(f32[4,128]{1,0:T(4,128)} %get-tuple-element.32), channel_id=1, source_target_pairs={{0,1},{1,0},{2,3},{3,2},{4,5},{5,4},{6,7},{7,6},{8,9},{9,8},{10,11... | collective-permute-start | bytes 6152 | tf_op jit(solution)/shard_map/ppermute | solution.py:362
  101.1 5.1 %collective-permute-start.8 = (f32[4,128]{1,0:T(4,128)S(1)}, f32[4,128]{1,0:T(4,128)S(1)}, u32[]{:S(2)}, u32[]{:S(2)}) collective-permute-start(f32[4,128]{1,0:T(4,128)S(1)} %add.322), channel_id=1, source_target_pairs={{0,2},{1,3},{2,0},{3,1},{4,6},{5,7},{6,4},{7,5},{8,10},{9,11},{10,... | collective-permute-start | bytes 6152 | tf_op jit(solution)/shard_map/ppermute | solution.py:362
  106.2 3.6 %collective-permute-start.9 = (f32[4,128]{1,0:T(4,128)S(1)}, f32[4,128]{1,0:T(4,128)S(1)}, u32[]{:S(2)}, u32[]{:S(2)}) collective-permute-start(f32[4,128]{1,0:T(4,128)S(1)} %add.323), channel_id=1, source_target_pairs={{0,4},{1,5},{2,6},{3,7},{4,0},{5,1},{6,2},{7,3},{8,12},{9,13},{10,... | collective-permute-start | bytes 6152 | tf_op jit(solution)/shard_map/ppermute | solution.py:362
  109.8 4.5 %collective-permute-start.10 = (f32[4,128]{1,0:T(4,128)S(1)}, f32[4,128]{1,0:T(4,128)S(1)}, u32[]{:S(2)}, u32[]{:S(2)}) collective-permute-start(f32[4,128]{1,0:T(4,128)S(1)} %add.324), channel_id=1, source_target_pairs={{0,8},{1,9},{2,10},{3,11},{4,12},{5,13},{6,14},{7,15},{8,0},{9,1},... | collective-permute-start | bytes 6152 | tf_op jit(solution)/shard_map/ppermute | solution.py:362
  114.3 16.6 %collective-permute-start.27 = (bf16[6,256,256]{2,1,0:T(8,128)(2,1)S(1)}, bf16[6,256,256]{2,1,0:T(8,128)(2,1)S(1)}, u32[]{:S(2)}, u32[]{:S(2)}) collective-permute-start(bf16[6,256,256]{2,1,0:T(8,128)(2,1)S(1)} %slice_dynamic-update-slice_fusion.refs_9_.refs_0_), channel_id=1, source_target_pairs={{0,32},{32,0},{64,96},{96,64},{128,160},{160,128},{192,224},{224,1... | collective-permute-start | bytes 2359304 | tf_op jit(solution)/shard_map/ppermute | solution.py:43
  114.3 14.4 %collective-permute-start.14 = (bf16[512,256]{1,0:T(8,128)(2,1)}, bf16[512,256]{1,0:T(8,128)(2,1)}, u32[]{:S(2)}, u32[]{:S(2)}) collective-permute-start(bf16[512,256]{1,0:T(8,128)(2,1)} %collective-permute-done.13.refs_2_), channel_id=1, source_target_pairs={{0,4},{1,5},{2,6},{3,7},{4,8},{5,9},{6,10},{7,11},{8,12},{9,13},{1... | collective-permute-start | bytes 786440 | tf_op jit(solution)/shard_map/ppermute | solution.py:47
  114.3 14.5 %collective-permute-start.17 = (bf16[512,256]{1,0:T(8,128)(2,1)}, bf16[512,256]{1,0:T(8,128)(2,1)}, u32[]{:S(2)}, u32[]{:S(2)}) collective-permute-start(bf16[512,256]{1,0:T(8,128)(2,1)} %collective-permute-done.16.refs_5_), channel_id=1, source_target_pairs={{0,28},{1,29},{2,30},{3,31},{4,0},{5,1},{6,2},{7,3},{8,4},{9,5},{1... | collective-permute-start | bytes 786440 | tf_op jit(solution)/shard_map/ppermute | solution.py:47
  117.6 6.2 %copy-start.13 = (f32[4,128]{1,0:T(4,128)}, f32[4,128]{1,0:T(4,128)S(1)}, u32[]{:S(2)}) copy-start(f32[4,128]{1,0:T(4,128)S(1)} %add.325) | copy-start | bytes 6148
  117.6 8.4 %collective-permute-start.11 = (f32[4,128]{1,0:T(4,128)S(1)}, f32[4,128]{1,0:T(4,128)}, u32[]{:S(2)}, u32[]{:S(2)}) collective-permute-start(f32[4,128]{1,0:T(4,128)S(1)} %add.325), channel_id=1, source_target_pairs={{0,16},{1,17},{2,18},{3,19},{4,20},{5,21},{6,22},{7,23},{8,24},{9,... | collective-permute-start | bytes 6152 | tf_op jit(solution)/shard_map/ppermute | solution.py:362
  122.7 12.2 %collective-permute-start.25 = (bf16[3,256,256]{2,1,0:T(8,128)(2,1)}, bf16[3,256,256]{2,1,0:T(8,128)(2,1)}, u32[]{:S(2)}, u32[]{:S(2)}) collective-permute-start(bf16[3,256,256]{2,1,0:T(8,128)(2,1)} %slice.45), channel_id=1, source_target_pairs={{0,64},{32,96},{64,128},{96,160},{128,192},{160,224},{192,0},{224,... | collective-permute-start | bytes 1179656 | tf_op jit(solution)/shard_map/ppermute | solution.py:43
  125.9 10.9 %collective-permute-start.26 = (bf16[3,256,256]{2,1,0:T(8,128)(2,1)}, bf16[3,256,256]{2,1,0:T(8,128)(2,1)S(1)}, u32[]{:S(2)}, u32[]{:S(2)}) collective-permute-start(bf16[3,256,256]{2,1,0:T(8,128)(2,1)} %slice.46), channel_id=1, source_target_pairs={{0,192},{32,224},{64,0},{96,32},{128,64},{160,96},{192,128},{224,1... | collective-permute-start | bytes 1179656 | tf_op jit(solution)/shard_map/ppermute | solution.py:43
  128.7 17.5 %collective-permute-start.28 = (bf16[6,256,256]{2,1,0:T(8,128)(2,1)S(1)}, bf16[6,256,256]{2,1,0:T(8,128)(2,1)}, u32[]{:S(2)}, u32[]{:S(2)}) collective-permute-start(bf16[6,256,256]{2,1,0:T(8,128)(2,1)S(1)} %collective-permute-done.23.refs_10_.refs_1_), channel_id=1, source_target_pairs={{0,32},{32,0},{64,96},{96,64},{128,160},{160,128},{192,224},{224,1... | collective-permute-start | bytes 2359304 | tf_op jit(solution)/shard_map/ppermute | solution.py:43
  128.8 17.4 %collective-permute-start.29 = (bf16[6,256,256]{2,1,0:T(8,128)(2,1)S(1)}, bf16[6,256,256]{2,1,0:T(8,128)(2,1)}, u32[]{:S(2)}, u32[]{:S(2)}) collective-permute-start(bf16[6,256,256]{2,1,0:T(8,128)(2,1)S(1)} %collective-permute-done.24.refs_11_.refs_2_), channel_id=1, source_target_pairs={{0,32},{32,0},{64,96},{96,64},{128,160},{160,128},{192,224},{224,1... | collective-permute-start | bytes 2359304 | tf_op jit(solution)/shard_map/ppermute | solution.py:43
  130.9 8.8 %collective-permute-start.18 = (bf16[256,256]{1,0:T(8,128)(2,1)}, bf16[256,256]{1,0:T(8,128)(2,1)}, u32[]{:S(2)}, u32[]{:S(2)}) collective-permute-start(bf16[256,256]{1,0:T(8,128)(2,1)} %slice.43), channel_id=1, source_target_pairs={{0,4},{1,5},{2,6},{3,7},{4,8},{5,9},{6,10},{7,11},{8,12},{9,13},{1... | collective-permute-start | bytes 393224 | tf_op jit(solution)/shard_map/ppermute | solution.py:47
  134.9 11.2 %collective-permute-start.30 = (bf16[3,256,256]{2,1,0:T(8,128)(2,1)}, bf16[3,256,256]{2,1,0:T(8,128)(2,1)}, u32[]{:S(2)}, u32[]{:S(2)}) collective-permute-start(bf16[3,256,256]{2,1,0:T(8,128)(2,1)} %collective-permute-done.25.refs_12_), channel_id=1, source_target_pairs={{0,32},{32,0},{64,96},{96,64},{128,160},{160,128},{192,224},{224,1... | collective-permute-start | bytes 1179656 | tf_op jit(solution)/shard_map/ppermute | solution.py:43
  136.8 9.4 %collective-permute-start.31 = (bf16[3,256,256]{2,1,0:T(8,128)(2,1)S(1)}, bf16[3,256,256]{2,1,0:T(8,128)(2,1)}, u32[]{:S(2)}, u32[]{:S(2)}) collective-permute-start(bf16[3,256,256]{2,1,0:T(8,128)(2,1)S(1)} %collective-permute-done.26.refs_13_.refs_3_), channel_id=1, source_target_pairs={{0,32},{32,0},{64,96},{96,64},{128,160},{160,128},{192,224},{224,1... | collective-permute-start | bytes 1179656 | tf_op jit(solution)/shard_map/ppermute | solution.py:43
  139.6 6.5 %collective-permute-start.19 = (bf16[256,256]{1,0:T(8,128)(2,1)}, bf16[256,256]{1,0:T(8,128)(2,1)}, u32[]{:S(2)}, u32[]{:S(2)}) collective-permute-start(bf16[256,256]{1,0:T(8,128)(2,1)} %slice.44), channel_id=1, source_target_pairs={{0,28},{1,29},{2,30},{3,31},{4,0},{5,1},{6,2},{7,3},{8,4},{9,5},{1... | collective-permute-start | bytes 393224 | tf_op jit(solution)/shard_map/ppermute | solution.py:47
  160.3 24.0 %copy-start.16 = (s32[4]{0:T(128)S(1)}, s32[4]{0:T(128)}, u32[]{:S(2)}) copy-start(s32[4]{0:T(128)} %get-tuple-element.44) | copy-start | bytes 52
  160.3 8.2 %collective-permute-start.37 = (bf16[128,256]{1,0:T(8,128)(2,1)S(1)}, bf16[128,256]{1,0:T(8,128)(2,1)S(1)}, u32[]{:S(2)}, u32[]{:S(2)}) collective-permute-start(bf16[128,256]{1,0:T(8,128)(2,1)S(1)} %get-tuple-element.48), channel_id=1, source_target_pairs={{0,3},{1,0},{2,1},{3,2},{4,7},{5,4},{6,5},{7,6},{8,11},{9,8},{10,9... | collective-permute-start | bytes 196616 | tf_op jit(solution)/shard_map/ppermute | solution.py:51
  162.4 7.8 %collective-permute-start.36 = (bf16[128,256]{1,0:T(8,128)(2,1)S(1)}, bf16[128,256]{1,0:T(8,128)(2,1)S(1)}, u32[]{:S(2)}, u32[]{:S(2)}) collective-permute-start(bf16[128,256]{1,0:T(8,128)(2,1)S(1)} %get-tuple-element.49), channel_id=1, source_target_pairs={{0,2},{1,3},{2,0},{3,1},{4,6},{5,7},{6,4},{7,5},{8,10},{9,11},{10,... | collective-permute-start | bytes 196616 | tf_op jit(solution)/shard_map/ppermute | solution.py:51
  163.4 6.9 %collective-permute-start.35 = (bf16[128,256]{1,0:T(8,128)(2,1)S(1)}, bf16[128,256]{1,0:T(8,128)(2,1)S(1)}, u32[]{:S(2)}, u32[]{:S(2)}) collective-permute-start(bf16[128,256]{1,0:T(8,128)(2,1)S(1)} %get-tuple-element.47), channel_id=1, source_target_pairs={{0,1},{1,2},{2,3},{3,0},{4,5},{5,6},{6,7},{7,4},{8,9},{9,10},{10,1... | collective-permute-start | bytes 196616 | tf_op jit(solution)/shard_map/ppermute | solution.py:51
  166.9 20.5 %collective-permute-start.32 = (bf16[512,256]{1,0:T(8,128)(2,1)S(1)}, bf16[512,256]{1,0:T(8,128)(2,1)S(1)}, u32[]{:S(2)}, u32[]{:S(2)}) collective-permute-start(bf16[512,256]{1,0:T(8,128)(2,1)S(1)} %get-tuple-element.39), channel_id=1, source_target_pairs={{0,1},{1,2},{2,3},{3,0},{4,5},{5,6},{6,7},{7,4},{8,9},{9,10},{10,1... | collective-permute-start | bytes 786440 | tf_op jit(solution)/shard_map/ppermute | solution.py:51
  167.6 19.8 %collective-permute-start.33 = (bf16[512,256]{1,0:T(8,128)(2,1)S(1)}, bf16[512,256]{1,0:T(8,128)(2,1)S(1)}, u32[]{:S(2)}, u32[]{:S(2)}) collective-permute-start(bf16[512,256]{1,0:T(8,128)(2,1)S(1)} %get-tuple-element.40), channel_id=1, source_target_pairs={{0,2},{1,3},{2,0},{3,1},{4,6},{5,7},{6,4},{7,5},{8,10},{9,11},{10,... | collective-permute-start | bytes 786440 | tf_op jit(solution)/shard_map/ppermute | solution.py:51
  168.5 18.9 %collective-permute-start.34 = (bf16[512,256]{1,0:T(8,128)(2,1)S(1)}, bf16[512,256]{1,0:T(8,128)(2,1)S(1)}, u32[]{:S(2)}, u32[]{:S(2)}) collective-permute-start(bf16[512,256]{1,0:T(8,128)(2,1)S(1)} %get-tuple-element.41), channel_id=1, source_target_pairs={{0,3},{1,0},{2,1},{3,2},{4,7},{5,4},{6,5},{7,6},{8,11},{9,8},{10,9... | collective-permute-start | bytes 786440 | tf_op jit(solution)/shard_map/ppermute | solution.py:51
  170.5 12.5 %collective-permute-start.40 = (bf16[128,256]{1,0:T(8,128)(2,1)S(1)}, bf16[128,256]{1,0:T(8,128)(2,1)S(1)}, u32[]{:S(2)}, u32[]{:S(2)}) collective-permute-start(bf16[128,256]{1,0:T(8,128)(2,1)S(1)} %get-tuple-element.53), channel_id=1, source_target_pairs={{0,3},{1,0},{2,1},{3,2},{4,7},{5,4},{6,5},{7,6},{8,11},{9,8},{10,9... | collective-permute-start | bytes 196616 | tf_op jit(solution)/shard_map/ppermute | solution.py:51
  172.7 11.7 %collective-permute-start.39 = (bf16[128,256]{1,0:T(8,128)(2,1)S(1)}, bf16[128,256]{1,0:T(8,128)(2,1)S(1)}, u32[]{:S(2)}, u32[]{:S(2)}) collective-permute-start(bf16[128,256]{1,0:T(8,128)(2,1)S(1)} %get-tuple-element.53), channel_id=1, source_target_pairs={{0,2},{1,3},{2,0},{3,1},{4,6},{5,7},{6,4},{7,5},{8,10},{9,11},{10,... | collective-permute-start | bytes 196616 | tf_op jit(solution)/shard_map/ppermute | solution.py:51
  183.1 4.3 %collective-permute-start.38 = (bf16[128,256]{1,0:T(8,128)(2,1)S(1)}, bf16[128,256]{1,0:T(8,128)(2,1)S(1)}, u32[]{:S(2)}, u32[]{:S(2)}) collective-permute-start(bf16[128,256]{1,0:T(8,128)(2,1)S(1)} %get-tuple-element.53), channel_id=1, source_target_pairs={{0,1},{1,2},{2,3},{3,0},{4,5},{5,6},{6,7},{7,4},{8,9},{9,10},{10,1... | collective-permute-start | bytes 196616 | tf_op jit(solution)/shard_map/ppermute | solution.py:51
  (10 other events, 9.7 us)

commit v2 on v1

v2 whole, which is shorter than its diff:
```python
import functools

import jax
import jax.numpy as jnp
from jax import lax
from jax.experimental import pallas as pl
from jax.experimental.pallas import tpu as pltpu
from jax.sharding import PartitionSpec as P

HEAD_SIZE = 128
PROMPT_TOKENS = 2048
IN_DEV = 8
OUT_DEV = 4
ROWS = 128
XS, CORES, ZS, YS = 4, 2, 8, 4
TILE = 256
MODEL_WIDTH = 8192

EPSILON = 1e-05
ROPE_THETA = 500000.0
CONTEXT_BASE = 8192.0
STRETCH = 8.0
MASKED_SCORE = -1e30

def group_perm(dx, dc):
    return [
        (x * CORES + c, ((x + dx) % XS) * CORES + (c ^ dc)) for x in range(XS) for c in range(CORES)
    ]


def z_perm(d):
    return [(z * YS + y, ((z + d) % ZS) * YS + y) for z in range(ZS) for y in range(YS)]


def y_perm(d):
    return [(z * YS + y, z * YS + (y + d) % YS) for z in range(ZS) for y in range(YS)]


def send_group(v, dx, dc):
    return lax.ppermute(v, "group", group_perm(dx, dc))


def send_z(v, d):
    return lax.ppermute(v, "fsdp", z_perm(d))


def send_y(v, d):
    return lax.ppermute(v, "fsdp", y_perm(d))


def rope_tables(length, offset):
    half_dim = HEAD_SIZE // 2
    base_rate = ROPE_THETA ** (-(jnp.arange(half_dim, dtype=jnp.float32) * 2.0 / HEAD_SIZE))
    ratio = CONTEXT_BASE * base_rate / (2.0 * jnp.pi)
    smooth = jnp.clip((ratio - 1.0) / 3.0, 0.0, 1.0)
    inverse_rate = (1.0 - smooth) * base_rate / STRETCH + smooth * base_rate
    token_positions = jnp.arange(length, dtype=jnp.float32) + offset
    angles = token_positions[:, None] * inverse_rate[None, :]
    cosine, sine = jnp.cos(angles), jnp.sin(angles)
    return (
        jnp.concatenate([cosine, cosine], axis=1),
        jnp.concatenate([-sine, sine], axis=1),
    )


def swap_halves(v):
    half = HEAD_SIZE // 2
    return jnp.concatenate([v[:, half:], v[:, :half]], axis=1)


ANY = pl.BlockSpec(memory_space=pl.ANY)
VMEM = pl.BlockSpec(memory_space=pltpu.VMEM)
SMEM = pl.BlockSpec(memory_space=pltpu.SMEM)


def shaped(shape, dtype):
    return jax.ShapeDtypeStruct(shape, dtype)


def pack_kernel(place, keep, destination, hidden, wq, wk, wv, kc, vc, *rest):
    outs, parts, own, chosen, sems = rest[0:4], rest[4:7], rest[7], rest[8], rest[9]
    x, c, z, y = place[0], place[1], place[2], place[3]
    first = (x * CORES + c) * IN_DEV
    for i in range(8):
        chosen[i] = 0
    for b in range(IN_DEV):

        @pl.when(keep[first + b] == 1)
        def _():
            target = destination[first + b] // OUT_DEV
            dx = lax.rem(target // CORES + XS - x, XS)
            dc = lax.rem(target + c, CORES)
            chosen[dx * CORES + dc] = b

    cols = pl.ds(pl.multiple_of(z * HEAD_SIZE, HEAD_SIZE), HEAD_SIZE)
    rows = pl.ds(pl.multiple_of(y * TILE, TILE), TILE)
    copies = []
    for dx in range(XS):
        for dc in range(CORES):
            copies.append((hidden.at[chosen[dx * CORES + dc]], outs[dx].at[dc]))
    for r in range(1, 4):
        other = lax.rem(y + YS - r, YS)
        copies.append((wq.at[pl.ds(pl.multiple_of(other * TILE, TILE), TILE)], parts[r - 1]))
    copies.append((wq.at[rows], own.at[0]))
    copies.append((wk.at[rows, cols], own.at[1, :, pl.ds(0, HEAD_SIZE)]))
    copies.append((wv.at[rows, cols], own.at[1, :, pl.ds(HEAD_SIZE, HEAD_SIZE)]))
    copies.append((kc.at[:, cols], own.at[2, :, pl.ds(0, HEAD_SIZE)]))
    copies.append((vc.at[:, cols], own.at[2, :, pl.ds(HEAD_SIZE, HEAD_SIZE)]))
    started = [pltpu.make_async_copy(s, d, sems.at[i]) for i, (s, d) in enumerate(copies)]
    for copy in started:
        copy.start()
    for copy in started:
        copy.wait()


def pack(place, keep, destination, *arrays):
    bf16 = jnp.bfloat16
    return pl.pallas_call(
        pack_kernel,
        out_shape=[shaped((CORES, ROWS, TILE), bf16)] * 4
        + [shaped((TILE, TILE), bf16)] * 3
        + [shaped((3, TILE, TILE), bf16)],
        in_specs=[SMEM] * 3 + [ANY] * 6,
        out_specs=[VMEM] * 8,
        scratch_shapes=[pltpu.SMEM((8,), jnp.int32), pltpu.SemaphoreType.DMA((16,))],
        name="pack",
    )(place, keep, destination, *arrays)


def sort_kernel(source, *refs):
    pieces, out_ref = refs[:4], refs[4]
    for j in range(OUT_DEV):
        out_ref[pl.ds(j * ROWS, ROWS), :] = jnp.zeros((ROWS, TILE), jnp.bfloat16)
        for i in range(XS):

            @pl.when(source[j] == i)
            def _():
                out_ref[pl.ds(j * ROWS, ROWS), :] = pieces[i][1]


def sort_other(source, pieces):
    return pl.pallas_call(
        sort_kernel,
        out_shape=shaped((OUT_DEV * ROWS, TILE), jnp.bfloat16),
        in_specs=[SMEM] + [VMEM] * 4,
        out_specs=VMEM,
        name="sort",
    )(source, *pieces)


def unpack_kernel(source, *refs):
    pieces, swapped, x_ref, ss_ref = refs[:4], refs[4], refs[5], refs[6]
    ones = jnp.ones((8, TILE), jnp.float32)
    for j in range(OUT_DEV):
        rows = pl.ds(j * ROWS, ROWS)
        for i in range(XS):

            @pl.when(source[j] == i)
            def _():
                x_ref[rows, :] = pieces[i][0]

        @pl.when(source[j] == XS)
        def _():
            x_ref[rows, :] = swapped[rows, :]

        wide = x_ref[rows, :].astype(jnp.float32)
        sums = lax.dot_general(
            ones,
            wide * wide,
            (((1,), (1,)), ((), ())),
            precision=lax.Precision.HIGHEST,
            preferred_element_type=jnp.float32,
        )
        ss_ref[pl.ds(j, 1), :] = sums[0:1, :]


def unpack(source, pieces, swapped):
    return pl.pallas_call(
        unpack_kernel,
        out_shape=[
            shaped((OUT_DEV * ROWS, TILE), jnp.bfloat16),
            shaped((OUT_DEV, ROWS), jnp.float32),
        ],
        in_specs=[SMEM] + [VMEM] * 5,
        out_specs=[VMEM] * 2,
        name="unpack",
    )(source, *pieces, swapped)


SHARDS = 8
TOTAL = OUT_DEV * ROWS


def weight_block(weights, position, n):
    own, left, right, far_a, far_b = weights[5 * (position // 4) : 5 * (position // 4) + 5]
    if position % 4 < 3:
        return (own, left, right)[position % 4][n]
    return far_a[n] if n < 3 else far_b[n - 3]


def product(normed, rows, weights, n):
    total = None
    for p in range(SHARDS):
        term = jnp.dot(
            normed[rows, p * TILE : (p + 1) * TILE],
            weight_block(weights, p, n),
            preferred_element_type=jnp.float32,
        )
        total = term if total is None else total + term
    return total


def norm_kernel(meta, scale, gain, *refs):
    shards, weights = refs[:9], refs[9:19]
    normed, kv_ref = refs[19:21]

    def norm(src, rows, s):
        cols = pl.ds(pl.multiple_of(meta[8 + s] * TILE, TILE), TILE)
        normed[rows, cols] = (
            src[...].astype(jnp.float32) * scale[rows, :] * gain[pl.ds(meta[s], 1), :]
        ).astype(jnp.bfloat16)

    for s in range(7):
        norm(shards[s], pl.ds(0, TOTAL), s)
    norm(shards[7], pl.ds(0, TOTAL // 2), 7)
    norm(shards[8], pl.ds(TOTAL // 2, TOTAL // 2), 7)
    kv_ref[...] = product(normed, slice(0, TOTAL), weights, 4)


def norm_and_kv(meta, scale, gain, shards, weights):
    return pl.pallas_call(
        norm_kernel,
        out_shape=[
            shaped((TOTAL, SHARDS * TILE), jnp.bfloat16),
            shaped((TOTAL, TILE), jnp.float32),
        ],
        in_specs=[SMEM] + [VMEM] * 2 + [VMEM] * 9 + [VMEM] * 10,
        out_specs=[VMEM] * 2,
        cost_estimate=pl.CostEstimate(
            flops=2 * TOTAL * 2048 * 256, bytes_accessed=4 * 2**20, transcendentals=0
        ),
        name="norm_kv",
    )(meta, scale, gain, *shards, *weights)


def query_kernel(chunk, normed, *refs):
    weights = refs[:10]
    own_ref, others = refs[10], refs[11:14]
    rows = slice(chunk * TOTAL // 2, (chunk + 1) * TOTAL // 2)
    for n in (1, 2, 3):
        others[n - 1][...] = product(normed, rows, weights, n).astype(jnp.bfloat16)
    own_ref[...] = product(normed, rows, weights, 0)


def queries(chunk, normed, weights):
    half = TOTAL // 2
    return pl.pallas_call(
        functools.partial(query_kernel, chunk),
        out_shape=[shaped((half, TILE), jnp.float32)]
        + [shaped((half, TILE), jnp.bfloat16)] * 3,
        in_specs=[VMEM] * 11,
        out_specs=[VMEM] * 4,
        cost_estimate=pl.CostEstimate(
            flops=2 * half * 2048 * 1024, bytes_accessed=6 * 2**20, transcendentals=0
        ),
        name="queries",
    )(normed, *weights)


def attend_kernel(chunk, meta, own, o1, o2, o3, cosine, sine, fresh, *refs):
    caches, out_ref = refs[:8], refs[8]
    q = own[...] + o1[...].astype(jnp.float32) + o2[...].astype(jnp.float32)
    q = q + o3[...].astype(jnp.float32)
    turned = []
    for h in range(2):
        v = q[:, h * HEAD_SIZE : (h + 1) * HEAD_SIZE]
        turned.append((v * cosine[...] + swap_halves(v) * sine[...]).astype(jnp.bfloat16))
    wide_q = jnp.concatenate(turned, axis=0)
    valid = meta[2 * chunk + pl.program_id(0)]
    row = lax.broadcasted_iota(jnp.int32, (2 * ROWS, ROWS), 0) % ROWS
    column = lax.broadcasted_iota(jnp.int32, (2 * ROWS, ROWS), 1)
    allowed = (column <= row) & (column < valid)

    def score(keys):
        return lax.dot_general(
            wide_q, keys, (((1,), (1,)), ((), ())), preferred_element_type=jnp.float32
        ) * (HEAD_SIZE**-0.5)

    old = [score(cache[0, :, :HEAD_SIZE]) for cache in caches]
    new = jnp.where(allowed, score(fresh[0, :, :HEAD_SIZE]), MASKED_SCORE)
    top = jnp.maximum(
        jnp.max(functools.reduce(jnp.maximum, old), axis=1, keepdims=True),
        jnp.max(new, axis=1, keepdims=True),
    )
    old = [jnp.exp(v - top) for v in old]
    new = jnp.exp(new - top)
    total = jnp.sum(functools.reduce(jnp.add, old), axis=1, keepdims=True)
    total = total + jnp.sum(new, axis=1, keepdims=True)
    mixed = jnp.dot(
        new.astype(jnp.bfloat16), fresh[0, :, HEAD_SIZE:], preferred_element_type=jnp.float32
    )
    for v, cache in zip(old, caches):
        mixed = mixed + jnp.dot(
            v.astype(jnp.bfloat16), cache[0, :, HEAD_SIZE:], preferred_element_type=jnp.float32
        )
    mixed = jnp.where(row < valid, mixed / total, 0.0).astype(jnp.bfloat16)
    out_ref[0, :, :HEAD_SIZE] = mixed[:ROWS]
    out_ref[0, :, HEAD_SIZE:] = mixed[ROWS:]


def attend(chunk, meta, own, others, cosine, sine, fresh, caches, cache_blocks):
    by_slot = pl.BlockSpec((ROWS, TILE), lambda j, m: (j, 0))
    table = pl.BlockSpec((ROWS, HEAD_SIZE), lambda j, m: (0, 0))

    def cache_spec(block):
        return pl.BlockSpec((1, TILE, TILE), lambda j, m: (block, 0, 0))

    return pl.pallas_call(
        functools.partial(attend_kernel, chunk),
        out_shape=shaped((OUT_DEV // 2, ROWS, TILE), jnp.bfloat16),
        grid_spec=pltpu.PrefetchScalarGridSpec(
            num_scalar_prefetch=1,
            grid=(OUT_DEV // 2,),
            in_specs=[by_slot] * 4
            + [table] * 2
            + [pl.BlockSpec((1, ROWS, TILE), lambda j, m: (m[4 + 2 * chunk + j], 0, 0))]
            + [cache_spec(b) for b in cache_blocks],
            out_specs=pl.BlockSpec((1, ROWS, TILE), lambda j, m: (j, 0, 0)),
        ),
        cost_estimate=pl.CostEstimate(
            flops=4 * 512 * 2176 * 128, bytes_accessed=2 * 2**20, transcendentals=512 * 2176
        ),
        name="attend",
    )(meta, own, *others, cosine, sine, fresh, *caches)


def body(
    hidden,
    norm_gain,
    w_query,
    key_projection_weight,
    value_projection_weight,
    prompt_key_cache,
    prompt_value_cache,
    keep_flag,
    destination,
    row_counts,
):
    g = lax.axis_index("group")
    f = lax.axis_index("fsdp")
    x, c = g // CORES, g % CORES
    z, y = f // YS, f % YS
    tie = lax.optimization_barrier

    *pieces, part1, part2, part3, own_parts = pack(
        jnp.stack([x, c, z, y]).astype(jnp.int32),
        keep_flag,
        destination,
        hidden,
        w_query,
        key_projection_weight,
        value_projection_weight,
        prompt_key_cache,
        prompt_value_cache,
    )

    block_ids = jnp.arange(keep_flag.shape[0], dtype=jnp.int32)
    live = keep_flag == 1

    def slot_sources(core):
        slots = (x * CORES + core) * OUT_DEV + jnp.arange(OUT_DEV, dtype=jnp.int32)
        matched = live[None, :] & (destination[None, :] == slots[:, None])
        sources = jnp.sum(jnp.where(matched, block_ids[None, :], 0), axis=1)
        group = sources // IN_DEV
        distance = jnp.where(group % CORES == c, (x - group // CORES) % XS, XS)
        return distance.astype(jnp.int32), matched

    source_other, _ = slot_sources(1 - c)
    source_own, matched = slot_sources(c)
    lengths = jnp.sum(jnp.where(matched, row_counts[None, :], 0), axis=1)

    pieces = [pieces[0]] + [send_group(pieces[d], d, 0) for d in (1, 2, 3)]
    arrived = [send_y(part1, -1), send_y(part2, -2), send_y(part3, -3)]
    swapped = send_group(sort_other(source_other, pieces), 0, 1)
    rows, squares = unpack(source_own, pieces, swapped)

    own = jnp.concatenate([own_parts[:1], jnp.stack(arrived), own_parts[1:]], axis=0)

    def add_squares(value, bit):
        return value + lax.ppermute(value, "fsdp", [(i, i ^ bit) for i in range(ZS * YS)])

    left, right = send_group(own, 1, 0), send_group(own, -1, 0)
    fwd, bwd = [rows], [rows]

    def ring_step(squares, bit):
        a, b, squares = tie((fwd[-1], bwd[-1], squares))
        fwd.append(send_z(a, 1))
        bwd.append(send_z(b, -1))
        return add_squares(squares, bit)

    squares = ring_step(squares, 1)
    squares = ring_step(squares, 2)
    left, right, fwd[-1], bwd[-1] = tie((left, right, fwd[-1], bwd[-1]))
    far_a, far_b = send_group(left[:3], 1, 0), send_group(right[3:], -1, 0)
    squares = ring_step(squares, 4)
    a, b, squares = tie((fwd[3], bwd[3], squares))
    far = [send_z(a[: TOTAL // 2], 1), send_z(b[TOTAL // 2 :], -1)]
    squares = add_squares(squares, 8)
    squares = add_squares(squares, 16)
    scale = lax.rsqrt(squares / MODEL_WIDTH + EPSILON).reshape(TOTAL, 1)
    same_core = [own, left, right, far_a, far_b]
    other_core = [send_group(v, 0, 1) for v in same_core]
    weights = same_core + other_core

    shards = fwd[:4] + bwd[1:4] + far
    shard_ids = jnp.stack([(z + s) % ZS for s in (0, -1, -2, -3, 1, 2, 3, 4)])
    weight_ids = jnp.stack(
        [((x + dx) % XS) * CORES + cc for cc in (c, 1 - c) for dx in (0, -1, 1, 2)]
    )
    positions = jnp.sum(
        jnp.where(
            shard_ids[:, None] == weight_ids[None, :], jnp.arange(SHARDS, dtype=jnp.int32), 0
        ),
        axis=1,
    )
    gain = norm_gain.reshape(ZS, YS, TILE)
    gain = lax.dynamic_index_in_dim(gain, y, 1, keepdims=False).astype(jnp.float32)
    meta = jnp.concatenate([shard_ids, positions]).astype(jnp.int32)
    normed, kv_own = norm_and_kv(meta, scale, gain, shards, weights)

    kv_slots = kv_own.reshape(OUT_DEV, ROWS, TILE)
    kv_parts = [
        send_y(
            lax.dynamic_index_in_dim(kv_slots, (y + r) % YS, 0, keepdims=False).astype(
                jnp.bfloat16
            ),
            r,
        )
        for r in (1, 2, 3)
    ]
    kv = lax.dynamic_index_in_dim(kv_slots, y, 0, keepdims=False)
    for part in kv_parts:
        kv = kv + part.astype(jnp.float32)
    q_own0, *q_parts0 = queries(0, normed, weights)
    q_parts0 = [send_y(v, r) for r, v in zip((1, 2, 3), q_parts0)]
    q_own1, *q_parts1 = queries(1, normed, weights)
    q_parts1 = [send_y(v, r) for r, v in zip((1, 2, 3), q_parts1)]

    cosine, sine = rope_tables(ROWS, PROMPT_TOKENS)
    key = kv[:, :HEAD_SIZE]
    key = (key * cosine + swap_halves(key) * sine).astype(jnp.bfloat16)
    fresh_own = jnp.concatenate([key, kv[:, HEAD_SIZE:].astype(jnp.bfloat16)], axis=1)
    fresh = jnp.stack([fresh_own] + [send_y(fresh_own, r) for r in (1, 2, 3)])
    fresh_ids = (y - jnp.arange(OUT_DEV, dtype=jnp.int32)) % YS

    caches, cache_blocks = [], []
    for part in (same_core, other_core):
        caches += [part[0], part[1], part[2], part[4]]
        cache_blocks += [5, 5, 5, 2]
    meta = jnp.concatenate([lengths, fresh_ids]).astype(jnp.int32)
    tables = (cosine, sine, fresh, caches, cache_blocks)
    return jnp.concatenate(
        [
            attend(0, meta, q_own0, q_parts0, *tables),
            attend(1, meta, q_own1, q_parts1, *tables),
        ],
        axis=0,
    )


def solution(mesh):
    return jax.shard_map(
        body,
        mesh=mesh,
        in_specs=(
            P("group", None, "fsdp"),
            P(),
            P("group", "fsdp"),
            P("group", None),
            P("group", None),
            P("group", None),
            P("group", None),
            P(),
            P(),
            P(),
        ),
        out_specs=P("group", None, "fsdp"),
        check_vma=False,
    )
```

time: 197 us -> 140 us (0.71)
  waiting for transfers between devices: 49.7 us -> 18.6 us
  Pallas kernels: 62.9 us -> 36.2 us
  other arithmetic: 7.23 us -> 12.5 us
  starting transfers between devices: 60.8 us -> 58.7 us
    pallas_call x3 -> x7, Pallas kernels: 59.9 us -> 33 us  [the longest x2 11.2 us: attend(): pl.pallas_call(functools.partial(attend_kernel, chunk), out_shape=shaped(...]
    ppermute x12 -> x15, waiting for transfers between devices: 22.2 us -> 0.52 us  [send_y(): return lax.ppermute(v, 'fsdp', y_perm(d))]
    ppermute x16 -> x13, waiting for transfers between devices: 3.99 us -> 0.18 us  [send_group(): return lax.ppermute(v, 'group', group_perm(dx, dc))]
    ppermute x5, waiting for transfers between devices: 14.1 us -> 10.6 us  [add_squares(): lax.ppermute(value, 'fsdp', [(i, i ^ bit) for i in range(ZS * YS)])]
    ppermute x12 -> x15, starting transfers between devices: 19.5 us -> 22.9 us  [send_y(): return lax.ppermute(v, 'fsdp', y_perm(d))]
    ppermute x8, starting transfers between devices: 16.9 us -> 13.5 us  [send_z(): return lax.ppermute(v, 'fsdp', z_perm(d))]
    ppermute x16 -> x13, starting transfers between devices: 14.4 us -> 11.3 us  [send_group(): return lax.ppermute(v, 'group', group_perm(dx, dc))]
    unnamed x38 -> x56, local copies, waits for them, and re-layouts: 6.77 us -> 3.76 us
  transfers between devices with their start and end apart: 41 -> 41, of which waited for: 15 -> 11; matrix products, arithmetic and copies ran while one was open for 7% -> 14% of each run, Pallas kernels for 2% -> 15%
where the time goes in v2:
time: 140 us
  starting transfers between devices  58.7 us (42%)
  Pallas kernels  36.2 us (26%)
  waiting for transfers between devices  18.6 us (13%)
  local copies, waits for them, and re-layouts  13.4 us (10%)
  other arithmetic  12.5 us (9%)
    ppermute x15, starting transfers between devices, send_y(): return lax.ppermute(v, 'fsdp', y_perm(d))  22.9 us
    ppermute x8, starting transfers between devices, send_z(): return lax.ppermute(v, 'fsdp', z_perm(d))  13.5 us
    ppermute x13, starting transfers between devices, send_group(): return lax.ppermute(v, 'group', group_perm(dx, dc))  11.3 us
    pallas_call x2, Pallas kernels, attend(): pl.pallas_call(functools.partial(attend_kernel, chunk), out_shape=shaped(...  11.2 us
    ppermute x5, starting transfers between devices, add_squares(): lax.ppermute(value, 'fsdp', [(i, i ^ bit) for i in range(ZS * YS)])  11 us
    pallas_call x2, Pallas kernels, queries(): pl.pallas_call(functools.partial(query_kernel, chunk), out_shape=[shaped(...  10.8 us
    ppermute x5, waiting for transfers between devices, add_squares(): lax.ppermute(value, 'fsdp', [(i, i ^ bit) for i in range(ZS * YS)])  10.6 us
    ppermute x8, waiting for transfers between devices, send_z(): return lax.ppermute(v, 'fsdp', z_perm(d))  7.3 us
  transfers between devices with their start and end apart: 41, of which 11 were waited for; matrix products, arithmetic and copies ran while one was open for 14% of the time, Pallas kernels for 15%

profile of v2, /device:TPU:8, one launch (start us, length us, event | category | flops | bytes accessed | tf_op | source)
XLA Modules:
  0.0 139.7 jit_solution(2651776669059037683)
XLA Ops:
  0.6 3.5 %pack.1 = (bf16[2,128,256]{2,1,0:T(8,128)(2,1)}, bf16[2,128,256]{2,1,0:T(8,128)(2,1)}, bf16[2,128,256]{2,1,0:T(8,128)(2,1)}, bf16[2,128,256]{2,1,0:T(8,128)(2,1)...) custom-call(s32[4]{0:T(128)} %pad_add_fusion.1.place, ...), custom_call_target="tpu_custom_call" | custom-call | tf_op jit(solution)/shard_map/pack/pallas_call | solution.py:118
  4.2 2.3 %collective-permute-start = (bf16[256,256]{1,0:T(8,128)(2,1)}, bf16[256,256]{1,0:T(8,128)(2,1)S(1)}, u32[]{:S(2)}, u32[]{:S(2)}) collective-permute-start(bf16[256,256]{1,0:T(8,128)(2,1)} %get-tuple-element.42), channel_id=1, source_target_pairs={{0,3},{1,0},{2,1},{3,2},{4,7},{5,4},{6,5},{7,6},{8,11},{9,8},{10,9... | collective-permute-start | bytes 393224 | tf_op jit(solution)/shard_map/ppermute | solution.py:48
  7.4 1.4 collective-permute-start.5
  8.8 2.7 %collective-permute-start.6 = (bf16[2,128,256]{2,1,0:T(8,128)(2,1)}, bf16[2,128,256]{2,1,0:T(8,128)(2,1)S(1)}, u32[]{:S(2)}, u32[]{:S(2)}) collective-permute-start(bf16[2,128,256]{2,1,0:T(8,128)(2,1)} %get-tuple-element.47), channel_id=1, source_target_pairs={{0,128},{32,160},{64,192},{96,224},{128,0},{160,32},{192,64},{224,... | collective-permute-start | bytes 393224 | tf_op jit(solution)/shard_map/ppermute | solution.py:40
  11.5 1.4 %collective-permute-start.7 = (bf16[2,128,256]{2,1,0:T(8,128)(2,1)}, bf16[2,128,256]{2,1,0:T(8,128)(2,1)S(1)}, u32[]{:S(2)}, u32[]{:S(2)}) collective-permute-start(bf16[2,128,256]{2,1,0:T(8,128)(2,1)} %get-tuple-element.48), channel_id=1, source_target_pairs={{0,192},{32,224},{64,0},{96,32},{128,64},{160,96},{192,128},{224,1... | collective-permute-start | bytes 393224 | tf_op jit(solution)/shard_map/ppermute | solution.py:40
  15.2 1.9 %collective-permute-start.2 = (bf16[256,256]{1,0:T(8,128)(2,1)}, bf16[256,256]{1,0:T(8,128)(2,1)S(1)}, u32[]{:S(2)}, u32[]{:S(2)}) collective-permute-start(bf16[256,256]{1,0:T(8,128)(2,1)} %get-tuple-element.44), channel_id=1, source_target_pairs={{0,1},{1,2},{2,3},{3,0},{4,5},{5,6},{6,7},{7,4},{8,9},{9,10},{10,1... | collective-permute-start | bytes 393224 | tf_op jit(solution)/shard_map/ppermute | solution.py:48
  17.9 1.9 %sort.1 = bf16[512,256]{1,0:T(8,128)(2,1)} custom-call(s32[4]{0:T(128)} %compare_select_fusion.6.source, bf16[2,128,256]{2,1,0:T(8,128)(2,1)} %get-tuple-element.45.refs_0_, bf16[2,128,256]{2,1,0:T(8,128)(2,1)} %copy-done.6, bf16[2,128,256]{2,1,0:T(8,128)(2,1)} %copy-done.7, bf16[2,128,256]{2,1,0:T(8,128)(2,1)} %copy-done.8), custom_call_target="tpu_custom_call" | custom-call | tf_op jit(solution)/shard_map/sort/pallas_call | solution.py:142
  22.2 2.5 %collective-permute-start.4 = (bf16[6,256,256]{2,1,0:T(8,128)(2,1)S(1)}, bf16[6,256,256]{2,1,0:T(8,128)(2,1)S(1)}, u32[]{:S(2)}, u32[]{:S(2)}) collective-permute-start(bf16[6,256,256]{2,1,0:T(8,128)(2,1)S(1)} %slice_dynamic-update-slice_fusion.refs_9_.refs_0_), channel_id=1, source_target_pairs={{0,192},{32,224},{64,0},{96,32},{128,64},{160,96},{192,128},{224,1... | collective-permute-start | bytes 2359304 | tf_op jit(solution)/shard_map/ppermute | solution.py:40
  26.0 3.1 %unpack.1 = (bf16[512,256]{1,0:T(8,128)(2,1)}, f32[4,128]{1,0:T(4,128)}) custom-call(s32[4]{0:T(128)} %compare_select_fusion.7.source, bf16[2,128,256]{2,1,0:T(8,128)(2,1)} %get-tuple-element.45.refs_0_, bf16[2,128,256]{2,1,0:T(8,128)(2,1)} %copy-done.6, bf16[2,128,256]{2,1,0:T(8,128)(2,1)} %copy-done.7, bf16[2,128,256]{2,1,0:T(8,128)(2,1)} %copy-done.8, ...), custom_call_target="tpu_custom_call" | custom-call | tf_op jit(solution)/shard_map/unpack/pallas_call | solution.py:178
  29.2 1.9 %collective-permute-start.9 = (bf16[512,256]{1,0:T(8,128)(2,1)}, bf16[512,256]{1,0:T(8,128)(2,1)S(1)}, u32[]{:S(2)}, u32[]{:S(2)}) collective-permute-start(bf16[512,256]{1,0:T(8,128)(2,1)} %get-tuple-element.52.refs_0_), channel_id=1, source_target_pairs={{0,4},{1,5},{2,6},{3,7},{4,8},{5,9},{6,10},{7,11},{8,12},{9,13},{1... | collective-permute-start | bytes 786440 | tf_op jit(solution)/shard_map/ppermute | solution.py:44
  31.1 3.9 %collective-permute-start.10 = (bf16[512,256]{1,0:T(8,128)(2,1)}, bf16[512,256]{1,0:T(8,128)(2,1)S(1)}, u32[]{:S(2)}, u32[]{:S(2)}) collective-permute-start(bf16[512,256]{1,0:T(8,128)(2,1)} %get-tuple-element.52.refs_0_), channel_id=1, source_target_pairs={{0,28},{1,29},{2,30},{3,31},{4,0},{5,1},{6,2},{7,3},{8,4},{9,5},{1... | collective-permute-start | bytes 786440 | tf_op jit(solution)/shard_map/ppermute | solution.py:44
  35.0 2.3 %collective-permute-start.11 = (f32[4,128]{1,0:T(4,128)}, f32[4,128]{1,0:T(4,128)S(1)}, u32[]{:S(2)}, u32[]{:S(2)}) collective-permute-start(f32[4,128]{1,0:T(4,128)} %get-tuple-element.53), channel_id=1, source_target_pairs={{0,1},{1,0},{2,3},{3,2},{4,5},{5,4},{6,7},{7,6},{8,9},{9,8},{10,11... | collective-permute-start | bytes 6152 | tf_op jit(solution)/shard_map/ppermute | solution.py:390
  37.3 1.8 %collective-permute-done.11 = f32[4,128]{1,0:T(4,128)S(1)} collective-permute-done((f32[4,128]{1,0:T(4,128)}, f32[4,128]{1,0:T(4,128)S(1)}, u32[]{:S(2)}, u32[]{:S(2)}) %collective-permute-start.11) | collective-permute-done | bytes 2080 | tf_op jit(solution)/shard_map/ppermute | solution.py:390
  39.8 1.4 collective-permute-done.9.refs_1_
  41.2 3.2 %collective-permute-start.13 = (bf16[512,256]{1,0:T(8,128)(2,1)S(1)}, bf16[512,256]{1,0:T(8,128)(2,1)}, u32[]{:S(2)}, u32[]{:S(2)}) collective-permute-start(bf16[512,256]{1,0:T(8,128)(2,1)S(1)} %collective-permute-done.10.refs_4_), channel_id=1, source_target_pairs={{0,28},{1,29},{2,30},{3,31},{4,0},{5,1},{6,2},{7,3},{8,4},{9,5},{1... | collective-permute-start | bytes 786440 | tf_op jit(solution)/shard_map/ppermute | solution.py:44
  44.5 1.2 collective-permute-start.14
  45.6 3.9 %collective-permute-done.14 = f32[4,128]{1,0:T(4,128)S(1)} collective-permute-done((f32[4,128]{1,0:T(4,128)S(1)}, f32[4,128]{1,0:T(4,128)S(1)}, u32[]{:S(2)}, u32[]{:S(2)}) %collective-permute-start.14) | collective-permute-done | bytes 2080 | tf_op jit(solution)/shard_map/ppermute | solution.py:390
  49.7 1.7 %collective-permute-start.15 = (bf16[512,256]{1,0:T(8,128)(2,1)}, bf16[512,256]{1,0:T(8,128)(2,1)}, u32[]{:S(2)}, u32[]{:S(2)}) collective-permute-start(bf16[512,256]{1,0:T(8,128)(2,1)} %collective-permute-done.12.refs_2_), channel_id=1, source_target_pairs={{0,4},{1,5},{2,6},{3,7},{4,8},{5,9},{6,10},{7,11},{8,12},{9,13},{1... | collective-permute-start | bytes 786440 | tf_op jit(solution)/shard_map/ppermute | solution.py:44
  51.4 1.6 %collective-permute-start.16 = (bf16[512,256]{1,0:T(8,128)(2,1)}, bf16[512,256]{1,0:T(8,128)(2,1)}, u32[]{:S(2)}, u32[]{:S(2)}) collective-permute-start(bf16[512,256]{1,0:T(8,128)(2,1)} %collective-permute-done.13.refs_5_), channel_id=1, source_target_pairs={{0,28},{1,29},{2,30},{3,31},{4,0},{5,1},{6,2},{7,3},{8,4},{9,5},{1... | collective-permute-start | bytes 786440 | tf_op jit(solution)/shard_map/ppermute | solution.py:44
  53.4 1.0 fusion.7
  56.6 2.6 %collective-permute-done.17 = f32[4,128]{1,0:T(4,128)} collective-permute-done((f32[4,128]{1,0:T(4,128)S(1)}, f32[4,128]{1,0:T(4,128)}, u32[]{:S(2)}, u32[]{:S(2)}) %collective-permute-start.17) | collective-permute-done | bytes 2080 | tf_op jit(solution)/shard_map/ppermute | solution.py:390
  59.2 1.4 %collective-permute-start.23 = (bf16[3,256,256]{2,1,0:T(8,128)(2,1)}, bf16[3,256,256]{2,1,0:T(8,128)(2,1)S(1)}, u32[]{:S(2)}, u32[]{:S(2)}) collective-permute-start(bf16[3,256,256]{2,1,0:T(8,128)(2,1)} %slice.38), channel_id=1, source_target_pairs={{0,192},{32,224},{64,0},{96,32},{128,64},{160,96},{192,128},{224,1... | collective-permute-start | bytes 1179656 | tf_op jit(solution)/shard_map/ppermute | solution.py:40
  61.9 3.3 %collective-permute-start.18 = (f32[4,128]{1,0:T(4,128)S(1)}, f32[4,128]{1,0:T(4,128)S(1)}, u32[]{:S(2)}, u32[]{:S(2)}) collective-permute-start(f32[4,128]{1,0:T(4,128)S(1)} %add.303), channel_id=1, source_target_pairs={{0,8},{1,9},{2,10},{3,11},{4,12},{5,13},{6,14},{7,15},{8,0},{9,1},... | collective-permute-start | bytes 6152 | tf_op jit(solution)/shard_map/ppermute | solution.py:390
  66.8 1.3 fusion.8.gain
  68.1 3.8 %collective-permute-start.19 = (f32[4,128]{1,0:T(4,128)S(1)}, f32[4,128]{1,0:T(4,128)S(1)}, u32[]{:S(2)}, u32[]{:S(2)}) collective-permute-start(f32[4,128]{1,0:T(4,128)S(1)} %add.304), channel_id=1, source_target_pairs={{0,16},{1,17},{2,18},{3,19},{4,20},{5,21},{6,22},{7,23},{8,24},{9,... | collective-permute-start | bytes 6152 | tf_op jit(solution)/shard_map/ppermute | solution.py:390
  72.7 1.6 %slice.35 = bf16[256,256]{1,0:T(8,128)(2,1)} slice(bf16[512,256]{1,0:T(8,128)(2,1)} %collective-permute-done.15.refs_3_), slice={[0:256], [0:256]} | slice | bytes 262144 | tf_op jit(solution)/shard_map/slice | solution.py:407
  74.2 1.4 %collective-permute-done.19 = f32[4,128]{1,0:T(4,128)S(1)} collective-permute-done((f32[4,128]{1,0:T(4,128)S(1)}, f32[4,128]{1,0:T(4,128)S(1)}, u32[]{:S(2)}, u32[]{:S(2)}) %collective-permute-start.19) | collective-permute-done | bytes 2080 | tf_op jit(solution)/shard_map/ppermute | solution.py:390
  77.1 1.3 pad_add_fusion.meta
  78.4 1.6 %slice.36 = bf16[256,256]{1,0:T(8,128)(2,1)} slice(bf16[512,256]{1,0:T(8,128)(2,1)} %collective-permute-done.16.refs_6_), slice={[256:512], [0:256]} | slice | bytes 262144 | tf_op jit(solution)/shard_map/slice | solution.py:407
  79.9 2.2 %collective-permute-done.20.refs_7_ = bf16[256,256]{1,0:T(8,128)(2,1)} collective-permute-done((bf16[256,256]{1,0:T(8,128)(2,1)}, bf16[256,256]{1,0:T(8,128)(2,1)}, u32[]{:S(2)}, u32[]{:S(2)}) %collective-permute-start.20) | collective-permute-done | bytes 131104 | tf_op jit(solution)/shard_map/ppermute | solution.py:44
  83.7 3.7 %collective-permute-done.21.refs_8_ = bf16[256,256]{1,0:T(8,128)(2,1)} collective-permute-done((bf16[256,256]{1,0:T(8,128)(2,1)}, bf16[256,256]{1,0:T(8,128)(2,1)}, u32[]{:S(2)}, u32[]{:S(2)}) %collective-permute-start.21) | collective-permute-done | bytes 131104 | tf_op jit(solution)/shard_map/ppermute | solution.py:44
  87.5 5.6 %norm_kv.1 = (bf16[512,2048]{1,0:T(8,128)(2,1)}, f32[512,256]{1,0:T(8,128)}) custom-call(s32[16]{0:T(128)} %concatenate.26.meta, f32[512,1]{1,0:T(8,128)} %copy.14.scale, f32[8,256]{1,0:T(8,128)} %fusion.8.gain, bf16[512,256]{1,0:T(8,128)(2,1)} %get-tuple-element.52.refs_0_, bf16[512,256]{1,0:T(8,128)(2,1)} %copy-done.9, ...), custom_call_target="tpu_custom_call" | custom-call | flops 536870912 | bytes 4194304 | tf_op jit(solution)/shard_map/norm_kv/pallas_call | solution.py:231
  93.1 1.1 fusion.2
  94.2 1.1 collective-permute-start.34
  95.3 2.3 %collective-permute-start.33 = (bf16[128,256]{1,0:T(8,128)(2,1)S(1)}, bf16[128,256]{1,0:T(8,128)(2,1)S(1)}, u32[]{:S(2)}, u32[]{:S(2)}) collective-permute-start(bf16[128,256]{1,0:T(8,128)(2,1)S(1)} %get-tuple-element.84), channel_id=1, source_target_pairs={{0,2},{1,3},{2,0},{3,1},{4,6},{5,7},{6,4},{7,5},{8,10},{9,11},{10,... | collective-permute-start | bytes 196616 | tf_op jit(solution)/shard_map/ppermute | solution.py:48
  97.8 5.4 %queries.3 = (f32[256,256]{1,0:T(8,128)}, bf16[256,256]{1,0:T(8,128)(2,1)}, bf16[256,256]{1,0:T(8,128)(2,1)}, bf16[256,256]{1,0:T(8,128)(2,1)}) custom-call(bf16[512,2048]{1,0:T(8,128)(2,1)} %get-tuple-element.67.normed, bf16[6,256,256]{2,1,0:T(8,128)(2,1)} %copy-done.2, bf16[6,256,256]{2,1,0:T(8,128)(2,1)} %copy-done, bf16[6,256,256]{2,1,0:T(8,128)(2,1)} %copy-done.1, ...), custom_call_target="tpu_custom_call" | custom-call | flops 1073741824 | bytes 6291456 | tf_op jit(solution)/shard_map/queries/pallas_call | solution.py:257
  103.2 1.6 %collective-permute-start.38 = (bf16[256,256]{1,0:T(8,128)(2,1)}, bf16[256,256]{1,0:T(8,128)(2,1)S(1)}, u32[]{:S(2)}, u32[]{:S(2)}) collective-permute-start(bf16[256,256]{1,0:T(8,128)(2,1)} %get-tuple-element.74), channel_id=1, source_target_pairs={{0,1},{1,2},{2,3},{3,0},{4,5},{5,6},{6,7},{7,4},{8,9},{9,10},{10,1... | collective-permute-start | bytes 393224 | tf_op jit(solution)/shard_map/ppermute | solution.py:48
  104.8 2.3 %collective-permute-start.39 = (bf16[256,256]{1,0:T(8,128)(2,1)}, bf16[256,256]{1,0:T(8,128)(2,1)S(1)}, u32[]{:S(2)}, u32[]{:S(2)}) collective-permute-start(bf16[256,256]{1,0:T(8,128)(2,1)} %get-tuple-element.75), channel_id=1, source_target_pairs={{0,2},{1,3},{2,0},{3,1},{4,6},{5,7},{6,4},{7,5},{8,10},{9,11},{10,... | collective-permute-start | bytes 393224 | tf_op jit(solution)/shard_map/ppermute | solution.py:48
  107.1 1.3 collective-permute-start.40
  110.3 1.1 collective-permute-start.37
  111.4 1.1 collective-permute-start.36
  113.0 5.4 %queries.2 = (f32[256,256]{1,0:T(8,128)}, bf16[256,256]{1,0:T(8,128)(2,1)}, bf16[256,256]{1,0:T(8,128)(2,1)}, bf16[256,256]{1,0:T(8,128)(2,1)}) custom-call(bf16[512,2048]{1,0:T(8,128)(2,1)} %get-tuple-element.67.normed, bf16[6,256,256]{2,1,0:T(8,128)(2,1)} %copy-done.2, bf16[6,256,256]{2,1,0:T(8,128)(2,1)} %copy-done, bf16[6,256,256]{2,1,0:T(8,128)(2,1)} %copy-done.1, ...), custom_call_target="tpu_custom_call" | custom-call | flops 1073741824 | bytes 6291456 | tf_op jit(solution)/shard_map/queries/pallas_call | solution.py:257
  118.4 2.6 %collective-permute-start.29 = (bf16[256,256]{1,0:T(8,128)(2,1)}, bf16[256,256]{1,0:T(8,128)(2,1)S(1)}, u32[]{:S(2)}, u32[]{:S(2)}) collective-permute-start(bf16[256,256]{1,0:T(8,128)(2,1)} %get-tuple-element.69), channel_id=1, source_target_pairs={{0,1},{1,2},{2,3},{3,0},{4,5},{5,6},{6,7},{7,4},{8,9},{9,10},{10,1... | collective-permute-start | bytes 393224 | tf_op jit(solution)/shard_map/ppermute | solution.py:48
  121.0 1.1 collective-permute-start.30
  122.1 2.5 %collective-permute-start.31 = (bf16[256,256]{1,0:T(8,128)(2,1)}, bf16[256,256]{1,0:T(8,128)(2,1)S(1)}, u32[]{:S(2)}, u32[]{:S(2)}) collective-permute-start(bf16[256,256]{1,0:T(8,128)(2,1)} %get-tuple-element.71), channel_id=1, source_target_pairs={{0,3},{1,0},{2,1},{3,2},{4,7},{5,4},{6,5},{7,6},{8,11},{9,8},{10,9... | collective-permute-start | bytes 393224 | tf_op jit(solution)/shard_map/ppermute | solution.py:48
  126.1 5.5 %attend.3 = bf16[2,128,256]{2,1,0:T(8,128)(2,1)} custom-call(s32[8]{0:T(128)} %pad_add_fusion.meta, f32[256,256]{1,0:T(8,128)} %get-tuple-element.73.own, bf16[256,256]{1,0:T(8,128)(2,1)} %copy-done.15, bf16[256,256]{1,0:T(8,128)(2,1)} %copy-done.16, bf16[256,256]{1,0:T(8,128)(2,1)} %copy-done.17, f32[128,128]{1,0:T(8,128)} %get-tuple-element.89.cosine, ...), custom_call_target="tpu_custom_call" | custom-call | flops 570425344 | bytes 2097152 | tf_op jit(solution)/shard_map/attend/pallas_call | solution.py:318
  132.4 5.7 %attend.2 = bf16[2,128,256]{2,1,0:T(8,128)(2,1)} custom-call(s32[8]{0:T(128)} %pad_add_fusion.meta, f32[256,256]{1,0:T(8,128)} %get-tuple-element.68.own, bf16[256,256]{1,0:T(8,128)(2,1)} %copy-done.18, bf16[256,256]{1,0:T(8,128)(2,1)} %copy-done.19, bf16[256,256]{1,0:T(8,128)(2,1)} %copy-done.20, f32[128,128]{1,0:T(8,128)} %get-tuple-element.89.cosine, ...), custom_call_target="tpu_custom_call" | custom-call | flops 570425344 | bytes 2097152 | tf_op jit(solution)/shard_map/attend/pallas_call | solution.py:318
  138.1 1.6 %pad_maximum_fusion.1 = bf16[4,128,256]{2,1,0:T(8,128)(2,1)} fusion(bf16[2,128,256]{2,1,0:T(8,128)(2,1)S(1)} %copy-done.5, bf16[2,128,256]{2,1,0:T(8,128)(2,1)} %attend.2), kind=kLoop, calls=%fused_computation.1 | loop fusion | flops 131072 | bytes 524288 | tf_op jit(solution)/shard_map/concatenate | solution.py:462
  (135 shorter events, 23.1 us)
Async XLA Ops:
  0.6 13.2 %copy-start.25 = (s32[64]{0:T(128)S(1)}, s32[64]{0:T(128)}, u32[]{:S(2)}) copy-start(s32[64]{0:T(128)} %param.19) | copy-start | bytes 772
  4.2 50.2 %copy-start.21 = (bf16[8192]{0:T(1024)(128)(2,1)S(1)}, bf16[8192]{0:T(1024)(128)(2,1)}, u32[]{:S(2)}) copy-start(bf16[8192]{0:T(1024)(128)(2,1)} %param.11) | copy-start | bytes 49156
  4.2 15.7 %collective-permute-start = (bf16[256,256]{1,0:T(8,128)(2,1)}, bf16[256,256]{1,0:T(8,128)(2,1)S(1)}, u32[]{:S(2)}, u32[]{:S(2)}) collective-permute-start(bf16[256,256]{1,0:T(8,128)(2,1)} %get-tuple-element.42), channel_id=1, source_target_pairs={{0,3},{1,0},{2,1},{3,2},{4,7},{5,4},{6,5},{7,6},{8,11},{9,8},{10,9... | collective-permute-start | bytes 393224 | tf_op jit(solution)/shard_map/ppermute | solution.py:48
  6.4 13.5 %collective-permute-start.1 = (bf16[256,256]{1,0:T(8,128)(2,1)}, bf16[256,256]{1,0:T(8,128)(2,1)S(1)}, u32[]{:S(2)}, u32[]{:S(2)}) collective-permute-start(bf16[256,256]{1,0:T(8,128)(2,1)} %get-tuple-element.43), channel_id=1, source_target_pairs={{0,2},{1,3},{2,0},{3,1},{4,6},{5,7},{6,4},{7,5},{8,10},{9,11},{10,... | collective-permute-start | bytes 393224 | tf_op jit(solution)/shard_map/ppermute | solution.py:48
  7.4 7.9 %collective-permute-start.5 = (bf16[2,128,256]{2,1,0:T(8,128)(2,1)}, bf16[2,128,256]{2,1,0:T(8,128)(2,1)S(1)}, u32[]{:S(2)}, u32[]{:S(2)}) collective-permute-start(bf16[2,128,256]{2,1,0:T(8,128)(2,1)} %get-tuple-element.46), channel_id=1, source_target_pairs={{0,64},{32,96},{64,128},{96,160},{128,192},{160,224},{192,0},{224,... | collective-permute-start | bytes 393224 | tf_op jit(solution)/shard_map/ppermute | solution.py:40
  8.8 8.5 %collective-permute-start.6 = (bf16[2,128,256]{2,1,0:T(8,128)(2,1)}, bf16[2,128,256]{2,1,0:T(8,128)(2,1)S(1)}, u32[]{:S(2)}, u32[]{:S(2)}) collective-permute-start(bf16[2,128,256]{2,1,0:T(8,128)(2,1)} %get-tuple-element.47), channel_id=1, source_target_pairs={{0,128},{32,160},{64,192},{96,224},{128,0},{160,32},{192,64},{224,... | collective-permute-start | bytes 393224 | tf_op jit(solution)/shard_map/ppermute | solution.py:40
  11.5 5.8 %collective-permute-start.7 = (bf16[2,128,256]{2,1,0:T(8,128)(2,1)}, bf16[2,128,256]{2,1,0:T(8,128)(2,1)S(1)}, u32[]{:S(2)}, u32[]{:S(2)}) collective-permute-start(bf16[2,128,256]{2,1,0:T(8,128)(2,1)} %get-tuple-element.48), channel_id=1, source_target_pairs={{0,192},{32,224},{64,0},{96,32},{128,64},{160,96},{192,128},{224,1... | collective-permute-start | bytes 393224 | tf_op jit(solution)/shard_map/ppermute | solution.py:40
  15.2 5.2 %collective-permute-start.2 = (bf16[256,256]{1,0:T(8,128)(2,1)}, bf16[256,256]{1,0:T(8,128)(2,1)S(1)}, u32[]{:S(2)}, u32[]{:S(2)}) collective-permute-start(bf16[256,256]{1,0:T(8,128)(2,1)} %get-tuple-element.44), channel_id=1, source_target_pairs={{0,1},{1,2},{2,3},{3,0},{4,5},{5,6},{6,7},{7,4},{8,9},{9,10},{10,1... | collective-permute-start | bytes 393224 | tf_op jit(solution)/shard_map/ppermute | solution.py:48
  19.9 5.5 %collective-permute-start.8 = (bf16[512,256]{1,0:T(8,128)(2,1)}, bf16[512,256]{1,0:T(8,128)(2,1)S(1)}, u32[]{:S(2)}, u32[]{:S(2)}) collective-permute-start(bf16[512,256]{1,0:T(8,128)(2,1)} %sort.1), channel_id=1, source_target_pairs={{0,32},{32,0},{64,96},{96,64},{128,160},{160,128},{192,224},{224,1... | collective-permute-start | bytes 786440 | tf_op jit(solution)/shard_map/ppermute | solution.py:40
  21.4 66.0 %copy-start.2 = (bf16[6,256,256]{2,1,0:T(8,128)(2,1)}, bf16[6,256,256]{2,1,0:T(8,128)(2,1)S(1)}, u32[]{:S(2)}) copy-start(bf16[6,256,256]{2,1,0:T(8,128)(2,1)S(1)} %slice_dynamic-update-slice_fusion.refs_9_.refs_0_) | copy-start | bytes 2359300
  21.4 28.2 %collective-permute-start.3 = (bf16[6,256,256]{2,1,0:T(8,128)(2,1)S(1)}, bf16[6,256,256]{2,1,0:T(8,128)(2,1)S(1)}, u32[]{:S(2)}, u32[]{:S(2)}) collective-permute-start(bf16[6,256,256]{2,1,0:T(8,128)(2,1)S(1)} %slice_dynamic-update-slice_fusion.refs_9_.refs_0_), channel_id=1, source_target_pairs={{0,64},{32,96},{64,128},{96,160},{128,192},{160,224},{192,0},{224,... | collective-permute-start | bytes 2359304 | tf_op jit(solution)/shard_map/ppermute | solution.py:40
  22.2 27.4 %collective-permute-start.4 = (bf16[6,256,256]{2,1,0:T(8,128)(2,1)S(1)}, bf16[6,256,256]{2,1,0:T(8,128)(2,1)S(1)}, u32[]{:S(2)}, u32[]{:S(2)}) collective-permute-start(bf16[6,256,256]{2,1,0:T(8,128)(2,1)S(1)} %slice_dynamic-update-slice_fusion.refs_9_.refs_0_), channel_id=1, source_target_pairs={{0,192},{32,224},{64,0},{96,32},{128,64},{160,96},{192,128},{224,1... | collective-permute-start | bytes 2359304 | tf_op jit(solution)/shard_map/ppermute | solution.py:40
  29.2 12.0 %collective-permute-start.9 = (bf16[512,256]{1,0:T(8,128)(2,1)}, bf16[512,256]{1,0:T(8,128)(2,1)S(1)}, u32[]{:S(2)}, u32[]{:S(2)}) collective-permute-start(bf16[512,256]{1,0:T(8,128)(2,1)} %get-tuple-element.52.refs_0_), channel_id=1, source_target_pairs={{0,4},{1,5},{2,6},{3,7},{4,8},{5,9},{6,10},{7,11},{8,12},{9,13},{1... | collective-permute-start | bytes 786440 | tf_op jit(solution)/shard_map/ppermute | solution.py:44
  31.1 10.1 %collective-permute-start.10 = (bf16[512,256]{1,0:T(8,128)(2,1)}, bf16[512,256]{1,0:T(8,128)(2,1)S(1)}, u32[]{:S(2)}, u32[]{:S(2)}) collective-permute-start(bf16[512,256]{1,0:T(8,128)(2,1)} %get-tuple-element.52.refs_0_), channel_id=1, source_target_pairs={{0,28},{1,29},{2,30},{3,31},{4,0},{5,1},{6,2},{7,3},{8,4},{9,5},{1... | collective-permute-start | bytes 786440 | tf_op jit(solution)/shard_map/ppermute | solution.py:44
  35.0 4.0 %collective-permute-start.11 = (f32[4,128]{1,0:T(4,128)}, f32[4,128]{1,0:T(4,128)S(1)}, u32[]{:S(2)}, u32[]{:S(2)}) collective-permute-start(f32[4,128]{1,0:T(4,128)} %get-tuple-element.53), channel_id=1, source_target_pairs={{0,1},{1,0},{2,3},{3,2},{4,5},{5,4},{6,7},{7,6},{8,9},{9,8},{10,11... | collective-permute-start | bytes 6152 | tf_op jit(solution)/shard_map/ppermute | solution.py:390
  41.1 15.4 %copy-start.9 = (bf16[512,256]{1,0:T(8,128)(2,1)}, bf16[512,256]{1,0:T(8,128)(2,1)S(1)}, u32[]{:S(2)}) copy-start(bf16[512,256]{1,0:T(8,128)(2,1)S(1)} %collective-permute-done.9.refs_1_) | copy-start | bytes 786436
  41.2 8.5 %collective-permute-start.12 = (bf16[512,256]{1,0:T(8,128)(2,1)S(1)}, bf16[512,256]{1,0:T(8,128)(2,1)}, u32[]{:S(2)}, u32[]{:S(2)}) collective-permute-start(bf16[512,256]{1,0:T(8,128)(2,1)S(1)} %collective-permute-done.9.refs_1_), channel_id=1, source_target_pairs={{0,4},{1,5},{2,6},{3,7},{4,8},{5,9},{6,10},{7,11},{8,12},{9,13},{1... | collective-permute-start | bytes 786440 | tf_op jit(solution)/shard_map/ppermute | solution.py:44
  41.2 8.4 %collective-permute-start.13 = (bf16[512,256]{1,0:T(8,128)(2,1)S(1)}, bf16[512,256]{1,0:T(8,128)(2,1)}, u32[]{:S(2)}, u32[]{:S(2)}) collective-permute-start(bf16[512,256]{1,0:T(8,128)(2,1)S(1)} %collective-permute-done.10.refs_4_), channel_id=1, source_target_pairs={{0,28},{1,29},{2,30},{3,31},{4,0},{5,1},{6,2},{7,3},{8,4},{9,5},{1... | collective-permute-start | bytes 786440 | tf_op jit(solution)/shard_map/ppermute | solution.py:44
  44.5 5.1 %collective-permute-start.14 = (f32[4,128]{1,0:T(4,128)S(1)}, f32[4,128]{1,0:T(4,128)S(1)}, u32[]{:S(2)}, u32[]{:S(2)}) collective-permute-start(f32[4,128]{1,0:T(4,128)S(1)} %add.301), channel_id=1, source_target_pairs={{0,2},{1,3},{2,0},{3,1},{4,6},{5,7},{6,4},{7,5},{8,10},{9,11},{10,... | collective-permute-start | bytes 6152 | tf_op jit(solution)/shard_map/ppermute | solution.py:390
  49.6 18.5 %collective-permute-start.24 = (bf16[6,256,256]{2,1,0:T(8,128)(2,1)S(1)}, bf16[6,256,256]{2,1,0:T(8,128)(2,1)S(1)}, u32[]{:S(2)}, u32[]{:S(2)}) collective-permute-start(bf16[6,256,256]{2,1,0:T(8,128)(2,1)S(1)} %slice_dynamic-update-slice_fusion.refs_9_.refs_0_), channel_id=1, source_target_pairs={{0,32},{32,0},{64,96},{96,64},{128,160},{160,128},{192,224},{224,1... | collective-permute-start | bytes 2359304 | tf_op jit(solution)/shard_map/ppermute | solution.py:40
  49.6 37.8 %copy-start = (bf16[6,256,256]{2,1,0:T(8,128)(2,1)}, bf16[6,256,256]{2,1,0:T(8,128)(2,1)S(1)}, u32[]{:S(2)}) copy-start(bf16[6,256,256]{2,1,0:T(8,128)(2,1)S(1)} %collective-permute-done.3.refs_10_.refs_1_) | copy-start | bytes 2359300
  49.6 37.8 %copy-start.1 = (bf16[6,256,256]{2,1,0:T(8,128)(2,1)}, bf16[6,256,256]{2,1,0:T(8,128)(2,1)S(1)}, u32[]{:S(2)}) copy-start(bf16[6,256,256]{2,1,0:T(8,128)(2,1)S(1)} %collective-permute-done.4.refs_11_.refs_2_) | copy-start | bytes 2359300
  49.7 12.2 %collective-permute-start.15 = (bf16[512,256]{1,0:T(8,128)(2,1)}, bf16[512,256]{1,0:T(8,128)(2,1)}, u32[]{:S(2)}, u32[]{:S(2)}) collective-permute-start(bf16[512,256]{1,0:T(8,128)(2,1)} %collective-permute-done.12.refs_2_), channel_id=1, source_target_pairs={{0,4},{1,5},{2,6},{3,7},{4,8},{5,9},{6,10},{7,11},{8,12},{9,13},{1... | collective-permute-start | bytes 786440 | tf_op jit(solution)/shard_map/ppermute | solution.py:44
  51.4 10.5 %collective-permute-start.16 = (bf16[512,256]{1,0:T(8,128)(2,1)}, bf16[512,256]{1,0:T(8,128)(2,1)}, u32[]{:S(2)}, u32[]{:S(2)}) collective-permute-start(bf16[512,256]{1,0:T(8,128)(2,1)} %collective-permute-done.13.refs_5_), channel_id=1, source_target_pairs={{0,28},{1,29},{2,30},{3,31},{4,0},{5,1},{6,2},{7,3},{8,4},{9,5},{1... | collective-permute-start | bytes 786440 | tf_op jit(solution)/shard_map/ppermute | solution.py:44
  53.0 6.2 %collective-permute-start.17 = (f32[4,128]{1,0:T(4,128)S(1)}, f32[4,128]{1,0:T(4,128)}, u32[]{:S(2)}, u32[]{:S(2)}) collective-permute-start(f32[4,128]{1,0:T(4,128)S(1)} %add.302), channel_id=1, source_target_pairs={{0,4},{1,5},{2,6},{3,7},{4,0},{5,1},{6,2},{7,3},{8,12},{9,13},{10,... | collective-permute-start | bytes 6152 | tf_op jit(solution)/shard_map/ppermute | solution.py:390
  55.2 20.7 %collective-permute-start.22 = (bf16[3,256,256]{2,1,0:T(8,128)(2,1)}, bf16[3,256,256]{2,1,0:T(8,128)(2,1)}, u32[]{:S(2)}, u32[]{:S(2)}) collective-permute-start(bf16[3,256,256]{2,1,0:T(8,128)(2,1)} %slice.37), channel_id=1, source_target_pairs={{0,64},{32,96},{64,128},{96,160},{128,192},{160,224},{192,0},{224,... | collective-permute-start | bytes 1179656 | tf_op jit(solution)/shard_map/ppermute | solution.py:40
  59.2 16.7 %collective-permute-start.23 = (bf16[3,256,256]{2,1,0:T(8,128)(2,1)}, bf16[3,256,256]{2,1,0:T(8,128)(2,1)S(1)}, u32[]{:S(2)}, u32[]{:S(2)}) collective-permute-start(bf16[3,256,256]{2,1,0:T(8,128)(2,1)} %slice.38), channel_id=1, source_target_pairs={{0,192},{32,224},{64,0},{96,32},{128,64},{160,96},{192,128},{224,1... | collective-permute-start | bytes 1179656 | tf_op jit(solution)/shard_map/ppermute | solution.py:40
  61.9 4.9 %collective-permute-start.18 = (f32[4,128]{1,0:T(4,128)S(1)}, f32[4,128]{1,0:T(4,128)S(1)}, u32[]{:S(2)}, u32[]{:S(2)}) collective-permute-start(f32[4,128]{1,0:T(4,128)S(1)} %add.303), channel_id=1, source_target_pairs={{0,8},{1,9},{2,10},{3,11},{4,12},{5,13},{6,14},{7,15},{8,0},{9,1},... | collective-permute-start | bytes 6152 | tf_op jit(solution)/shard_map/ppermute | solution.py:390
  65.9 21.6 %collective-permute-start.25 = (bf16[6,256,256]{2,1,0:T(8,128)(2,1)S(1)}, bf16[6,256,256]{2,1,0:T(8,128)(2,1)}, u32[]{:S(2)}, u32[]{:S(2)}) collective-permute-start(bf16[6,256,256]{2,1,0:T(8,128)(2,1)S(1)} %collective-permute-done.3.refs_10_.refs_1_), channel_id=1, source_target_pairs={{0,32},{32,0},{64,96},{96,64},{128,160},{160,128},{192,224},{224,1... | collective-permute-start | bytes 2359304 | tf_op jit(solution)/shard_map/ppermute | solution.py:40
  66.8 20.7 %collective-permute-start.26 = (bf16[6,256,256]{2,1,0:T(8,128)(2,1)S(1)}, bf16[6,256,256]{2,1,0:T(8,128)(2,1)}, u32[]{:S(2)}, u32[]{:S(2)}) collective-permute-start(bf16[6,256,256]{2,1,0:T(8,128)(2,1)S(1)} %collective-permute-done.4.refs_11_.refs_2_), channel_id=1, source_target_pairs={{0,32},{32,0},{64,96},{96,64},{128,160},{160,128},{192,224},{224,1... | collective-permute-start | bytes 2359304 | tf_op jit(solution)/shard_map/ppermute | solution.py:40
  68.1 19.4 %copy-start.3 = (bf16[6,256,256]{2,1,0:T(8,128)(2,1)}, bf16[6,256,256]{2,1,0:T(8,128)(2,1)S(1)}, u32[]{:S(2)}) copy-start(bf16[6,256,256]{2,1,0:T(8,128)(2,1)S(1)} %collective-permute-done.24.refs_14_.refs_5_.refs_4_) | copy-start | bytes 2359300
  68.1 7.6 %collective-permute-start.19 = (f32[4,128]{1,0:T(4,128)S(1)}, f32[4,128]{1,0:T(4,128)S(1)}, u32[]{:S(2)}, u32[]{:S(2)}) collective-permute-start(f32[4,128]{1,0:T(4,128)S(1)} %add.304), channel_id=1, source_target_pairs={{0,16},{1,17},{2,18},{3,19},{4,20},{5,21},{6,22},{7,23},{8,24},{9,... | collective-permute-start | bytes 6152 | tf_op jit(solution)/shard_map/ppermute | solution.py:390
  75.6 6.5 %collective-permute-start.20 = (bf16[256,256]{1,0:T(8,128)(2,1)}, bf16[256,256]{1,0:T(8,128)(2,1)}, u32[]{:S(2)}, u32[]{:S(2)}) collective-permute-start(bf16[256,256]{1,0:T(8,128)(2,1)} %slice.35), channel_id=1, source_target_pairs={{0,4},{1,5},{2,6},{3,7},{4,8},{5,9},{6,10},{7,11},{8,12},{9,13},{1... | collective-permute-start | bytes 393224 | tf_op jit(solution)/shard_map/ppermute | solution.py:44
  75.9 11.5 %collective-permute-start.27 = (bf16[3,256,256]{2,1,0:T(8,128)(2,1)}, bf16[3,256,256]{2,1,0:T(8,128)(2,1)}, u32[]{:S(2)}, u32[]{:S(2)}) collective-permute-start(bf16[3,256,256]{2,1,0:T(8,128)(2,1)} %collective-permute-done.22.refs_12_.refs_3_), channel_id=1, source_target_pairs={{0,32},{32,0},{64,96},{96,64},{128,160},{160,128},{192,224},{224,1... | collective-permute-start | bytes 1179656 | tf_op jit(solution)/shard_map/ppermute | solution.py:40
  75.9 11.5 %collective-permute-start.28 = (bf16[3,256,256]{2,1,0:T(8,128)(2,1)S(1)}, bf16[3,256,256]{2,1,0:T(8,128)(2,1)}, u32[]{:S(2)}, u32[]{:S(2)}) collective-permute-start(bf16[3,256,256]{2,1,0:T(8,128)(2,1)S(1)} %collective-permute-done.23.refs_13_.refs_4_.refs_3_), channel_id=1, source_target_pairs={{0,32},{32,0},{64,96},{96,64},{128,160},{160,128},{192,224},{224,1... | collective-permute-start | bytes 1179656 | tf_op jit(solution)/shard_map/ppermute | solution.py:40
  82.1 5.3 %collective-permute-start.21 = (bf16[256,256]{1,0:T(8,128)(2,1)}, bf16[256,256]{1,0:T(8,128)(2,1)}, u32[]{:S(2)}, u32[]{:S(2)}) collective-permute-start(bf16[256,256]{1,0:T(8,128)(2,1)} %slice.36), channel_id=1, source_target_pairs={{0,28},{1,29},{2,30},{3,31},{4,0},{5,1},{6,2},{7,3},{8,4},{9,5},{1... | collective-permute-start | bytes 393224 | tf_op jit(solution)/shard_map/ppermute | solution.py:44
  94.2 12.9 %collective-permute-start.34 = (bf16[128,256]{1,0:T(8,128)(2,1)S(1)}, bf16[128,256]{1,0:T(8,128)(2,1)S(1)}, u32[]{:S(2)}, u32[]{:S(2)}) collective-permute-start(bf16[128,256]{1,0:T(8,128)(2,1)S(1)} %get-tuple-element.83), channel_id=1, source_target_pairs={{0,3},{1,0},{2,1},{3,2},{4,7},{5,4},{6,5},{7,6},{8,11},{9,8},{10,9... | collective-permute-start | bytes 196616 | tf_op jit(solution)/shard_map/ppermute | solution.py:48
  95.3 13.1 %collective-permute-start.33 = (bf16[128,256]{1,0:T(8,128)(2,1)S(1)}, bf16[128,256]{1,0:T(8,128)(2,1)S(1)}, u32[]{:S(2)}, u32[]{:S(2)}) collective-permute-start(bf16[128,256]{1,0:T(8,128)(2,1)S(1)} %get-tuple-element.84), channel_id=1, source_target_pairs={{0,2},{1,3},{2,0},{3,1},{4,6},{5,7},{6,4},{7,5},{8,10},{9,11},{10,... | collective-permute-start | bytes 196616 | tf_op jit(solution)/shard_map/ppermute | solution.py:48
  97.6 10.8 %collective-permute-start.32 = (bf16[128,256]{1,0:T(8,128)(2,1)S(1)}, bf16[128,256]{1,0:T(8,128)(2,1)S(1)}, u32[]{:S(2)}, u32[]{:S(2)}) collective-permute-start(bf16[128,256]{1,0:T(8,128)(2,1)S(1)} %get-tuple-element.82), channel_id=1, source_target_pairs={{0,1},{1,2},{2,3},{3,0},{4,5},{5,6},{6,7},{7,4},{8,9},{9,10},{10,1... | collective-permute-start | bytes 196616 | tf_op jit(solution)/shard_map/ppermute | solution.py:48
  103.2 9.3 %collective-permute-start.38 = (bf16[256,256]{1,0:T(8,128)(2,1)}, bf16[256,256]{1,0:T(8,128)(2,1)S(1)}, u32[]{:S(2)}, u32[]{:S(2)}) collective-permute-start(bf16[256,256]{1,0:T(8,128)(2,1)} %get-tuple-element.74), channel_id=1, source_target_pairs={{0,1},{1,2},{2,3},{3,0},{4,5},{5,6},{6,7},{7,4},{8,9},{9,10},{10,1... | collective-permute-start | bytes 393224 | tf_op jit(solution)/shard_map/ppermute | solution.py:48
  104.8 20.6 %collective-permute-start.39 = (bf16[256,256]{1,0:T(8,128)(2,1)}, bf16[256,256]{1,0:T(8,128)(2,1)S(1)}, u32[]{:S(2)}, u32[]{:S(2)}) collective-permute-start(bf16[256,256]{1,0:T(8,128)(2,1)} %get-tuple-element.75), channel_id=1, source_target_pairs={{0,2},{1,3},{2,0},{3,1},{4,6},{5,7},{6,4},{7,5},{8,10},{9,11},{10,... | collective-permute-start | bytes 393224 | tf_op jit(solution)/shard_map/ppermute | solution.py:48
  107.1 18.3 %collective-permute-start.40 = (bf16[256,256]{1,0:T(8,128)(2,1)}, bf16[256,256]{1,0:T(8,128)(2,1)S(1)}, u32[]{:S(2)}, u32[]{:S(2)}) collective-permute-start(bf16[256,256]{1,0:T(8,128)(2,1)} %get-tuple-element.76), channel_id=1, source_target_pairs={{0,3},{1,0},{2,1},{3,2},{4,7},{5,4},{6,5},{7,6},{8,11},{9,8},{10,9... | collective-permute-start | bytes 393224 | tf_op jit(solution)/shard_map/ppermute | solution.py:48
  110.3 8.1 %collective-permute-start.37 = (bf16[128,256]{1,0:T(8,128)(2,1)S(1)}, bf16[128,256]{1,0:T(8,128)(2,1)S(1)}, u32[]{:S(2)}, u32[]{:S(2)}) collective-permute-start(bf16[128,256]{1,0:T(8,128)(2,1)S(1)} %get-tuple-element.88), channel_id=1, source_target_pairs={{0,3},{1,0},{2,1},{3,2},{4,7},{5,4},{6,5},{7,6},{8,11},{9,8},{10,9... | collective-permute-start | bytes 196616 | tf_op jit(solution)/shard_map/ppermute | solution.py:48
  111.4 9.6 %collective-permute-start.36 = (bf16[128,256]{1,0:T(8,128)(2,1)S(1)}, bf16[128,256]{1,0:T(8,128)(2,1)S(1)}, u32[]{:S(2)}, u32[]{:S(2)}) collective-permute-start(bf16[128,256]{1,0:T(8,128)(2,1)S(1)} %get-tuple-element.88), channel_id=1, source_target_pairs={{0,2},{1,3},{2,0},{3,1},{4,6},{5,7},{6,4},{7,5},{8,10},{9,11},{10,... | collective-permute-start | bytes 196616 | tf_op jit(solution)/shard_map/ppermute | solution.py:48
  112.5 9.6 %collective-permute-start.35 = (bf16[128,256]{1,0:T(8,128)(2,1)S(1)}, bf16[128,256]{1,0:T(8,128)(2,1)S(1)}, u32[]{:S(2)}, u32[]{:S(2)}) collective-permute-start(bf16[128,256]{1,0:T(8,128)(2,1)S(1)} %get-tuple-element.88), channel_id=1, source_target_pairs={{0,1},{1,2},{2,3},{3,0},{4,5},{5,6},{6,7},{7,4},{8,9},{9,10},{10,1... | collective-permute-start | bytes 196616 | tf_op jit(solution)/shard_map/ppermute | solution.py:48
  118.4 13.3 %collective-permute-start.29 = (bf16[256,256]{1,0:T(8,128)(2,1)}, bf16[256,256]{1,0:T(8,128)(2,1)S(1)}, u32[]{:S(2)}, u32[]{:S(2)}) collective-permute-start(bf16[256,256]{1,0:T(8,128)(2,1)} %get-tuple-element.69), channel_id=1, source_target_pairs={{0,1},{1,2},{2,3},{3,0},{4,5},{5,6},{6,7},{7,4},{8,9},{9,10},{10,1... | collective-permute-start | bytes 393224 | tf_op jit(solution)/shard_map/ppermute | solution.py:48
  121.0 10.7 %collective-permute-start.30 = (bf16[256,256]{1,0:T(8,128)(2,1)}, bf16[256,256]{1,0:T(8,128)(2,1)S(1)}, u32[]{:S(2)}, u32[]{:S(2)}) collective-permute-start(bf16[256,256]{1,0:T(8,128)(2,1)} %get-tuple-element.70), channel_id=1, source_target_pairs={{0,2},{1,3},{2,0},{3,1},{4,6},{5,7},{6,4},{7,5},{8,10},{9,11},{10,... | collective-permute-start | bytes 393224 | tf_op jit(solution)/shard_map/ppermute | solution.py:48
  122.1 9.6 %collective-permute-start.31 = (bf16[256,256]{1,0:T(8,128)(2,1)}, bf16[256,256]{1,0:T(8,128)(2,1)S(1)}, u32[]{:S(2)}, u32[]{:S(2)}) collective-permute-start(bf16[256,256]{1,0:T(8,128)(2,1)} %get-tuple-element.71), channel_id=1, source_target_pairs={{0,3},{1,0},{2,1},{3,2},{4,7},{5,4},{6,5},{7,6},{8,11},{9,8},{10,9... | collective-permute-start | bytes 393224 | tf_op jit(solution)/shard_map/ppermute | solution.py:48
  (19 other events, 106.4 us)

commit v3 on v0

v3 whole, which is shorter than its diff:
```python
import functools

import jax
import jax.numpy as jnp
from jax import lax
from jax.experimental import pallas as pl
from jax.experimental.pallas import tpu as pltpu
from jax.sharding import PartitionSpec as P

HEAD_SIZE = 128
PROMPT_TOKENS = 2048
IN_DEV = 8
OUT_DEV = 4
ROWS = 128
XS, CORES, ZS, YS = 4, 2, 8, 4
TILE = 256
MODEL_WIDTH = 8192

EPSILON = 1e-05
ROPE_THETA = 500000.0
CONTEXT_BASE = 8192.0
STRETCH = 8.0
MASKED_SCORE = -1e30

def group_perm(dx, dc):
    return [
        (x * CORES + c, ((x + dx) % XS) * CORES + (c ^ dc)) for x in range(XS) for c in range(CORES)
    ]


def z_perm(d):
    return [(z * YS + y, ((z + d) % ZS) * YS + y) for z in range(ZS) for y in range(YS)]


def y_perm(d):
    return [(z * YS + y, z * YS + (y + d) % YS) for z in range(ZS) for y in range(YS)]


def send_group(v, dx, dc):
    return lax.ppermute(v, "group", group_perm(dx, dc))


def send_z(v, d):
    return lax.ppermute(v, "fsdp", z_perm(d))


def send_y(v, d):
    return lax.ppermute(v, "fsdp", y_perm(d))


def swap(v):
    return send_group(v, 0, 1)


def rope_tables(length, offset):
    half_dim = HEAD_SIZE // 2
    base_rate = ROPE_THETA ** (-(jnp.arange(half_dim, dtype=jnp.float32) * 2.0 / HEAD_SIZE))
    ratio = CONTEXT_BASE * base_rate / (2.0 * jnp.pi)
    smooth = jnp.clip((ratio - 1.0) / 3.0, 0.0, 1.0)
    inverse_rate = (1.0 - smooth) * base_rate / STRETCH + smooth * base_rate
    token_positions = jnp.arange(length, dtype=jnp.float32) + offset
    angles = token_positions[:, None] * inverse_rate[None, :]
    cosine, sine = jnp.cos(angles), jnp.sin(angles)
    return (
        jnp.concatenate([cosine, cosine], axis=1),
        jnp.concatenate([-sine, sine], axis=1),
    )


def swap_halves(v):
    half = HEAD_SIZE // 2
    return jnp.concatenate([v[:, half:], v[:, :half]], axis=1)


ANY = pl.BlockSpec(memory_space=pl.ANY)
VMEM = pl.BlockSpec(memory_space=pltpu.VMEM)
SMEM = pl.BlockSpec(memory_space=pltpu.SMEM)


def shaped(shape, dtype):
    return jax.ShapeDtypeStruct(shape, dtype)


def limit(mib):
    return pltpu.CompilerParams(vmem_limit_bytes=mib * 2**20)


def fetch_all(pairs, sems, first=0):
    copies = [
        pltpu.make_async_copy(s, d, sems.at[first + i]) for i, (s, d) in enumerate(pairs)
    ]
    for copy in copies:
        copy.start()
    return copies


def await_all(copies):
    for copy in copies:
        copy.wait()


def pack_kernel(place, keep, destination, hidden, wq, wk, wv, kc, vc, *rest):
    outs, parts, own, chosen, sems = rest[0:4], rest[4:7], rest[7], rest[8], rest[9]
    x, c, z, y = place[0], place[1], place[2], place[3]
    first = (x * CORES + c) * IN_DEV
    cols = pl.ds(pl.multiple_of(z * HEAD_SIZE, HEAD_SIZE), HEAD_SIZE)
    rows = pl.ds(pl.multiple_of(y * TILE, TILE), TILE)
    pairs = []
    for r in range(1, 4):
        other = lax.rem(y + YS - r, YS)
        pairs.append((wq.at[pl.ds(pl.multiple_of(other * TILE, TILE), TILE)], parts[r - 1]))
    pairs.append((wq.at[rows], own.at[0]))
    pairs.append((wk.at[rows, cols], own.at[1, :, pl.ds(0, HEAD_SIZE)]))
    pairs.append((wv.at[rows, cols], own.at[1, :, pl.ds(HEAD_SIZE, HEAD_SIZE)]))
    pairs.append((kc.at[:, cols], own.at[2, :, pl.ds(0, HEAD_SIZE)]))
    pairs.append((vc.at[:, cols], own.at[2, :, pl.ds(HEAD_SIZE, HEAD_SIZE)]))
    copies = fetch_all(pairs, sems)

    for i in range(8):
        chosen[i] = 0
    for b in range(IN_DEV):

        @pl.when(keep[first + b] == 1)
        def _():
            target = lax.div(destination[first + b], OUT_DEV)
            dx = lax.rem(lax.div(target, CORES) + XS - x, XS)
            dc = lax.rem(target + c, CORES)
            chosen[dx * CORES + dc] = b

    pairs = [(hidden.at[chosen[i]], outs[i // CORES].at[i % CORES]) for i in range(8)]
    await_all(copies + fetch_all(pairs, sems, 8))


def pack(place, keep, destination, *arrays):
    bf16 = jnp.bfloat16
    return pl.pallas_call(
        pack_kernel,
        out_shape=[shaped((CORES, ROWS, TILE), bf16)] * 4
        + [shaped((TILE, TILE), bf16)] * 3
        + [shaped((3, TILE, TILE), bf16)],
        in_specs=[SMEM] * 3 + [ANY] * 6,
        out_specs=[VMEM] * 8,
        scratch_shapes=[pltpu.SMEM((8,), jnp.int32), pltpu.SemaphoreType.DMA((16,))],
        compiler_params=limit(56),
        name="pack",
    )(place, keep, destination, *arrays)


def plan_kernel(place, keep, destination, counts, out):
    x, c = place[0], place[1]

    def step(b, _):
        target = destination[b]
        group = lax.div(target, OUT_DEV)

        @pl.when((keep[b] == 1) & (lax.div(group, CORES) == x))
        def _():
            slot = lax.rem(target, OUT_DEV)
            source = lax.div(b, IN_DEV)
            other = lax.rem(group + c, CORES)
            dx = lax.rem(x + XS - lax.div(source, CORES), XS)
            out[other * OUT_DEV + slot] = jnp.where(lax.rem(source, CORES) == c, dx, XS)

            @pl.when(other == 0)
            def _():
                out[2 * OUT_DEV + slot] = counts[b]

        return 0

    lax.fori_loop(0, keep.shape[0], step, 0)


def plan(place, keep, destination, counts):
    return pl.pallas_call(
        plan_kernel,
        out_shape=shaped((3 * OUT_DEV,), jnp.int32),
        in_specs=[SMEM] * 4,
        out_specs=SMEM,
        compiler_params=limit(1),
        name="plan",
    )(place, keep, destination, counts)


SHARDS = 8
TOTAL = OUT_DEV * ROWS


def sort_kernel(source, *refs):
    pieces, own_ref, other_ref = refs[:4], refs[4], refs[5]
    for side, out_ref in ((0, own_ref), (1, other_ref)):
        for j in range(OUT_DEV):
            for i in range(XS):

                @pl.when(source[side * OUT_DEV + j] == i)
                def _():
                    out_ref[pl.ds(j * ROWS, ROWS), :] = pieces[i][side]


def sort_pieces(source, pieces):
    return pl.pallas_call(
        sort_kernel,
        out_shape=[shaped((TOTAL, TILE), jnp.bfloat16)] * 2,
        in_specs=[SMEM] + [VMEM] * 4,
        out_specs=[VMEM] * 2,
        compiler_params=limit(2),
        name="sort",
    )(source, *pieces)


def unpack_kernel(source, held, swapped, out_ref):
    for j in range(OUT_DEV):
        rows = pl.ds(j * ROWS, ROWS)
        there = source[j] == XS

        @pl.when(there)
        def _():
            out_ref[rows, :] = swapped[rows, :]

        @pl.when(jnp.logical_not(there))
        def _():
            out_ref[rows, :] = held[rows, :]


def unpack(source, held, swapped):
    return pl.pallas_call(
        unpack_kernel,
        out_shape=shaped((TOTAL, TILE), jnp.bfloat16),
        in_specs=[SMEM] + [VMEM] * 2,
        out_specs=VMEM,
        compiler_params=limit(2),
        name="unpack",
    )(source, held, swapped)


def squares_kernel(*refs):
    shards, out_ref = refs[:8], refs[8]
    total = None
    for shard in shards:
        wide = shard[...].astype(jnp.float32)
        total = wide * wide if total is None else total + wide * wide
    out_ref[...] = lax.dot_general(
        jnp.ones((8, TILE), jnp.float32),
        total,
        (((1,), (1,)), ((), ())),
        precision=lax.Precision.HIGHEST,
        preferred_element_type=jnp.float32,
    )


def sum_squares(shards):
    return pl.pallas_call(
        squares_kernel,
        out_shape=shaped((8, TOTAL), jnp.float32),
        in_specs=[VMEM] * 8,
        out_specs=VMEM,
        compiler_params=limit(2),
        name="squares",
    )(*shards)


SHARD_Z = (0, -1, -2, -3, 1, 2, 3, 4)


def product(normed, tiles, n):
    total = None
    for p in range(SHARDS):
        term = jnp.dot(
            normed[:, p * TILE : (p + 1) * TILE], tiles[p, n], preferred_element_type=jnp.float32
        )
        total = term if total is None else total + term
    return total


def project_kernel(place, s0, s1, s2, s3, gain, *refs):
    shards, weights = refs[:8], refs[8:18]
    own_ref, kv_ref, parts, cache_ref = refs[18], refs[19], refs[20:23], refs[23]
    held, tiles, normed, kv, own, sent, sems = refs[24:]
    x, c, z, y = place[0], place[1], place[2], place[3]
    copies = fetch_all([(shard, held.at[i]) for i, shard in enumerate(shards)], sems)
    pairs = []
    for half in range(2):
        base = 4 * half
        own_w, left, right, far_a, far_b = weights[5 * half : 5 * half + 5]
        for i, w in enumerate((own_w, left, right)):
            pairs.append((w, tiles.at[base + i]))
        pairs.append((far_a, tiles.at[base + 3, pl.ds(0, 3)]))
        pairs.append((far_b, tiles.at[base + 3, pl.ds(3, 3)]))
    fetched = fetch_all(pairs, sems, 8)
    sums = s0[...] + s1[...] + s2[...] + s3[...]
    scale = jnp.transpose(lax.rsqrt(sums / MODEL_WIDTH + EPSILON))[:, :1]
    for i, dz in enumerate(SHARD_Z):
        k = lax.rem(z + ZS + dz, ZS)
        ahead = lax.rem(lax.div(k, CORES) + XS - x, XS)
        order = jnp.where(ahead == 3, 1, jnp.where(ahead == 0, 0, ahead + 1))
        position = order + 4 * lax.rem(k + c, CORES)
        cols = pl.ds(pl.multiple_of(position * TILE, TILE), TILE)
        copies[i].wait()
        normed[:, cols] = (
            held[i].astype(jnp.float32) * scale * gain[pl.ds(k * YS + y, 1), :]
        ).astype(jnp.bfloat16)
    await_all(fetched)
    kv[...] = product(normed, tiles, 4)

    def slot(j):
        return kv.at[pl.ds(pl.multiple_of(j * ROWS, ROWS), ROWS)]

    outgoing = fetch_all([(slot(y), kv_ref)], sems, 18)
    outgoing += fetch_all(
        [(tiles.at[p, 5], cache_ref.at[pl.ds(p * TILE, TILE)]) for p in range(SHARDS)], sems, 23
    )
    for r in (1, 2, 3):
        sent[r - 1, pl.ds(TOTAL, ROWS), :] = slot(lax.rem(y + r, YS))[...].astype(jnp.bfloat16)
    for r in (2, 1, 3):
        sent[r - 1, pl.ds(0, TOTAL), :] = product(normed, tiles, r).astype(jnp.bfloat16)
        outgoing += fetch_all([(sent.at[r - 1], parts[r - 1])], sems, 18 + r)
    own[...] = product(normed, tiles, 0)
    outgoing += fetch_all([(own, own_ref)], sems, 22)
    await_all(outgoing)


def project(place, sums, gain, shards, weights):
    f32, bf16 = jnp.float32, jnp.bfloat16
    return pl.pallas_call(
        project_kernel,
        out_shape=[shaped((TOTAL, TILE), f32), shaped((ROWS, TILE), f32)]
        + [shaped((TOTAL + ROWS, TILE), bf16)] * 3
        + [shaped((PROMPT_TOKENS, TILE), bf16)],
        in_specs=[SMEM] + [VMEM] * 5 + [ANY] * 18,
        out_specs=[ANY] * 6,
        scratch_shapes=[
            pltpu.VMEM((SHARDS, TOTAL, TILE), bf16),
            pltpu.VMEM((SHARDS, 6, TILE, TILE), bf16),
            pltpu.VMEM((TOTAL, SHARDS * TILE), bf16),
            pltpu.VMEM((TOTAL, TILE), f32),
            pltpu.VMEM((TOTAL, TILE), f32),
            pltpu.VMEM((3, TOTAL + ROWS, TILE), bf16),
            pltpu.SemaphoreType.DMA((31,)),
        ],
        compiler_params=limit(56),
        cost_estimate=pl.CostEstimate(
            flops=2 * TOTAL * 2048 * 1280, bytes_accessed=10 * 2**20, transcendentals=0
        ),
        name="project",
    )(place, *sums, gain, *shards, *weights)


def rotate(v, cosine, sine):
    return v * cosine + swap_halves(v) * sine


def fresh_kernel(own_ref, p1, p2, p3, cosine, sine, out, held, own, sems):
    copies = fetch_all(
        [(p.at[pl.ds(TOTAL, ROWS)], held.at[i]) for i, p in enumerate((p1, p2, p3))], sems
    )
    await_all(fetch_all([(own_ref, own)], sems, 3))
    v = own[...]
    for i, copy in enumerate(copies):
        copy.wait()
        v = v + held[i].astype(jnp.float32)
    out[:, :HEAD_SIZE] = rotate(v[:, :HEAD_SIZE], cosine[...], sine[...]).astype(jnp.bfloat16)
    out[:, HEAD_SIZE:] = v[:, HEAD_SIZE:].astype(jnp.bfloat16)


def fresh_keys(own, parts, cosine, sine):
    return pl.pallas_call(
        fresh_kernel,
        out_shape=shaped((ROWS, TILE), jnp.bfloat16),
        in_specs=[ANY] * 4 + [VMEM] * 2,
        out_specs=VMEM,
        scratch_shapes=[
            pltpu.VMEM((3, ROWS, TILE), jnp.bfloat16),
            pltpu.VMEM((ROWS, TILE), jnp.float32),
            pltpu.SemaphoreType.DMA((4,)),
        ],
        compiler_params=limit(4),
        name="fresh",
    )(own, *parts, cosine, sine)


FACTOR = HEAD_SIZE**-0.5 * 1.4426950408889634


def prompt_kernel(own_ref, p1, p2, p3, cosine, sine, *refs):
    cache_ref, q_ref, mixed_ref, top_ref, total_ref = refs[:5]
    held, caches, own, sems = refs[5:]
    parts = fetch_all(
        [(p.at[pl.ds(0, TOTAL)], held.at[i]) for i, p in enumerate((p1, p2, p3))], sems
    )
    kept = fetch_all([(cache_ref, caches), (own_ref, own)], sems, 3)
    await_all(parts + kept)

    def step(j, _):
        rows = pl.ds(pl.multiple_of(j * ROWS, ROWS), ROWS)
        q = own[rows, :]
        for i in range(3):
            q = q + held[i, rows, :].astype(jnp.float32)
        halves = (q[:, :HEAD_SIZE], q[:, HEAD_SIZE:])
        wide_q = jnp.concatenate(
            [rotate(v, cosine[...], sine[...]).astype(jnp.bfloat16) for v in halves], axis=0
        )
        q_ref[j] = wide_q
        scores = [
            lax.dot_general(
                wide_q,
                caches[i * TILE : (i + 1) * TILE, :HEAD_SIZE],
                (((1,), (1,)), ((), ())),
                preferred_element_type=jnp.float32,
            )
            for i in range(8)
        ]
        top = jnp.max(functools.reduce(jnp.maximum, scores), axis=1, keepdims=True)
        scores = [jnp.exp2((v - top) * FACTOR) for v in scores]
        total = jnp.sum(functools.reduce(jnp.add, scores), axis=1, keepdims=True)
        mixed = None
        for i, v in enumerate(scores):
            term = jnp.dot(
                v.astype(jnp.bfloat16),
                caches[i * TILE : (i + 1) * TILE, HEAD_SIZE:],
                preferred_element_type=jnp.float32,
            )
            mixed = term if mixed is None else mixed + term
        mixed_ref[j] = mixed
        top_ref[j] = jnp.broadcast_to(top, (2 * ROWS, HEAD_SIZE))
        total_ref[j] = jnp.broadcast_to(total, (2 * ROWS, HEAD_SIZE))
        return 0

    lax.fori_loop(0, OUT_DEV, step, 0)


def attend_prompt(own, others, cosine, sine, cache):
    per_slot = (OUT_DEV, 2 * ROWS, HEAD_SIZE)
    return pl.pallas_call(
        prompt_kernel,
        out_shape=[shaped(per_slot, jnp.bfloat16)] + [shaped(per_slot, jnp.float32)] * 3,
        in_specs=[ANY] * 4 + [VMEM] * 2 + [ANY],
        out_specs=[VMEM] * 4,
        scratch_shapes=[
            pltpu.VMEM((3, TOTAL, TILE), jnp.bfloat16),
            pltpu.VMEM((PROMPT_TOKENS, TILE), jnp.bfloat16),
            pltpu.VMEM((TOTAL, TILE), jnp.float32),
            pltpu.SemaphoreType.DMA((5,)),
        ],
        compiler_params=limit(24),
        cost_estimate=pl.CostEstimate(
            flops=4 * 1024 * 2048 * 128, bytes_accessed=2 * 2**20, transcendentals=1024 * 2048
        ),
        name="prompt",
    )(own, *others, cosine, sine, cache)


def finish_kernel(place, slots, q, mixed_ref, top_ref, total_ref, f0, f1, f2, f3, out_ref, fresh):
    y = place[3]
    for r, part in enumerate((f0, f1, f2, f3)):
        fresh[lax.rem(y + YS - r, YS)] = part[...]
    row = lax.broadcasted_iota(jnp.int32, (2 * ROWS, ROWS), 0) % ROWS
    column = lax.broadcasted_iota(jnp.int32, (2 * ROWS, ROWS), 1)
    for j in range(OUT_DEV):
        valid = slots[2 * OUT_DEV + j]
        scores = lax.dot_general(
            q[j],
            fresh[j, :, :HEAD_SIZE],
            (((1,), (1,)), ((), ())),
            preferred_element_type=jnp.float32,
        )
        scores = jnp.where((column <= row) & (column < valid), scores, MASKED_SCORE)
        top = jnp.maximum(top_ref[j], jnp.max(scores, axis=1, keepdims=True))
        scores = jnp.exp2((scores - top) * FACTOR)
        rescale = jnp.exp2((top_ref[j] - top) * FACTOR)
        total = total_ref[j] * rescale + jnp.sum(scores, axis=1, keepdims=True)
        mixed = mixed_ref[j] * rescale + jnp.dot(
            scores.astype(jnp.bfloat16),
            fresh[j, :, HEAD_SIZE:],
            preferred_element_type=jnp.float32,
        )
        mixed = jnp.where(row < valid, mixed / total, 0.0).astype(jnp.bfloat16)
        out_ref[j, :, :HEAD_SIZE] = mixed[:ROWS]
        out_ref[j, :, HEAD_SIZE:] = mixed[ROWS:]


def finish(place, slots, prompt, fresh):
    return pl.pallas_call(
        finish_kernel,
        out_shape=shaped((OUT_DEV, ROWS, TILE), jnp.bfloat16),
        in_specs=[SMEM] * 2 + [VMEM] * 8,
        out_specs=VMEM,
        scratch_shapes=[pltpu.VMEM((OUT_DEV, ROWS, TILE), jnp.bfloat16)],
        compiler_params=limit(8),
        name="finish",
    )(place, slots, *prompt, *fresh)


def body(
    hidden,
    norm_gain,
    w_query,
    key_projection_weight,
    value_projection_weight,
    prompt_key_cache,
    prompt_value_cache,
    keep_flag,
    destination,
    row_counts,
):
    g = lax.axis_index("group")
    f = lax.axis_index("fsdp")
    place = jnp.stack([g // CORES, g % CORES, f // YS, f % YS]).astype(jnp.int32)
    tie = lax.optimization_barrier

    *pieces, part1, part2, part3, own_parts = pack(
        place,
        keep_flag,
        destination,
        hidden,
        w_query,
        key_projection_weight,
        value_projection_weight,
        prompt_key_cache,
        prompt_value_cache,
    )
    slots = plan(place, keep_flag, destination, row_counts)

    for d in (1, 3, 2):
        pieces[d] = send_group(pieces[d], d, 0)
    arrived = [send_y(part1, -1), send_y(part2, -2), send_y(part3, -3)]
    pieces, arrived = tie((pieces, arrived))
    inward, outward = sort_pieces(slots, pieces)
    swapped, arrived = tie((swap(outward), arrived))
    rows = unpack(slots, inward, swapped)

    own = jnp.concatenate([own_parts[:1], jnp.stack(arrived), own_parts[1:]], axis=0)
    f1, b1 = send_z(rows, 1), send_z(rows, -1)
    left, right = send_group(own, 1, 0), send_group(own, -1, 0)
    own_swapped = swap(own)
    f1, b1, own_swapped = tie((f1, b1, own_swapped))
    f2, b2 = send_z(f1, 1), send_z(b1, -1)
    f2, b2, left, right = tie((f2, b2, left, right))
    f3, b3 = send_z(f2, 1), send_z(b2, -1)
    far_a, far_b = send_group(left[:3], 1, 0), send_group(right[3:], -1, 0)
    left_swapped = swap(left)
    f3, b3, left_swapped, right = tie((f3, b3, left_swapped, right))
    far, right_swapped = send_z(f3, 1), swap(right)
    far, right_swapped, far_a, far_b = tie((far, right_swapped, far_a, far_b))
    shards = [rows, f1, f2, f3, b1, b2, b3, far]
    sums = sum_squares(shards)
    sums = [sums] + [send_y(sums, r) for r in (1, 2, 3)]
    same_core = [own, left, right, far_a, far_b]
    other_core = [own_swapped, left_swapped, right_swapped, swap(far_a), swap(far_b)]
    weights = same_core + other_core
    gain = norm_gain.astype(jnp.float32).reshape(ZS * YS, TILE)
    q_own, kv_own, *parts, cache = project(place, sums, gain, shards, weights)

    parts = [send_y(v, r) for r, v in zip((1, 2, 3), parts)]
    cosine, sine = rope_tables(ROWS, PROMPT_TOKENS)
    fresh = fresh_keys(kv_own, parts, cosine, sine)
    fresh = [fresh] + [send_y(fresh, r) for r in (1, 2, 3)]
    prompt = attend_prompt(q_own, parts, cosine, sine, cache)
    return finish(place, slots, prompt, fresh)


def solution(mesh):
    return jax.shard_map(
        body,
        mesh=mesh,
        in_specs=(
            P("group", None, "fsdp"),
            P(),
            P("group", "fsdp"),
            P("group", None),
            P("group", None),
            P("group", None),
            P("group", None),
            P(),
            P(),
            P(),
        ),
        out_specs=P("group", None, "fsdp"),
        check_vma=False,
    )
```

time: 295 us -> 125 us (0.42)
  waiting for transfers between devices: 169 us -> 43.6 us
  starting transfers between devices: 3.61 us -> 47.1 us
  matrix products: 42.1 us -> 0 us
  blocking collectives: 28.7 us -> 0 us
  Pallas kernels: 0 us -> 23.8 us
  other arithmetic: 15.5 us -> 1.04 us
  between operations: 13.4 us -> 0.46 us
  local copies, waits for them, and re-layouts: 21 us -> 8.15 us
    all_gather x4 -> x0, waiting for transfers between devices: 157 us -> none  [the longest x1 145 us: attend(): gathered = lax.all_gather(blocks, 'fsdp', axis=2, tiled=True)]
    ppermute x0 -> x32, starting transfers between devices: none -> 47.1 us  [the longest x12 19.3 us: send_y(): return lax.ppermute(v, 'fsdp', y_perm(d))]
    ppermute x0 -> x32, waiting for transfers between devices: none -> 43.6 us  [the longest x12 16.9 us: send_y(): return lax.ppermute(v, 'fsdp', y_perm(d))]
    dot_general x8 -> x0, matrix products: 42.1 us -> none  [the longest x1 14 us: attend(): jnp.dot(normalized_input, pieces[0], preferred_element_type=jnp.float32)]
    all_gather x2 -> x0, blocking collectives: 28.7 us -> none  [the longest x1 15.3 us: attend(): lax.all_gather(prompt_values, 'group', axis=0, tiled=True)]
    pallas_call x0 -> x9, Pallas kernels: none -> 23.8 us  [the longest x1 8.34 us: project(): pl.pallas_call(project_kernel, out_shape=[shaped((TOTAL, TILE), f32), sha...]
    reduce_sum x4 -> x0, other arithmetic: 11.2 us -> none  [the longest x1 7.42 us: attend(): jnp.mean(rows_wide * rows_wide, axis=1, keepdims=True) + EPSILON]
    all_to_all x1 -> x0, waiting for transfers between devices: 10.2 us -> none  [body(): lax.all_to_all(packed, 'group', split_axis=0, concat_axis=0, tiled=True)]
  transfers between devices with their start and end apart: 5 -> 32, of which waited for: 5 -> 14; matrix products, arithmetic and copies ran while one was open for 21% -> 2% of each run, Pallas kernels for 0% -> 7%
where the time goes in v3:
time: 125 us; the launch traced here: 124 us
  starting transfers between devices  47.1 us (38%)
  waiting for transfers between devices  43.6 us (35%)
  Pallas kernels  23.8 us (19%)
  local copies, waits for them, and re-layouts  8.15 us (7%)
    ppermute x12, starting transfers between devices, send_y(): return lax.ppermute(v, 'fsdp', y_perm(d))  19.3 us
    ppermute x12, waiting for transfers between devices, send_y(): return lax.ppermute(v, 'fsdp', y_perm(d))  16.9 us
    ppermute x7, waiting for transfers between devices, send_z(): return lax.ppermute(v, 'fsdp', z_perm(d))  16.8 us
    ppermute x7, starting transfers between devices, send_z(): return lax.ppermute(v, 'fsdp', z_perm(d))  14.5 us
    ppermute x13, starting transfers between devices, send_group(): return lax.ppermute(v, 'group', group_perm(dx, dc))  13.3 us
    ppermute x13, waiting for transfers between devices, send_group(): return lax.ppermute(v, 'group', group_perm(dx, dc))  9.92 us
    pallas_call x1, Pallas kernels, project(): pl.pallas_call(project_kernel, out_shape=[shaped((TOTAL, TILE), f32), sha...  8.34 us
    unnamed x62, local copies, waits for them, and re-layouts  6.5 us
  transfers between devices with their start and end apart: 32, of which 14 were waited for; matrix products, arithmetic and copies ran while one was open for 2% of the time, Pallas kernels for 7%

profile of v3, /device:TPU:8, one launch (start us, length us, event | category | flops | bytes accessed | tf_op | source)
XLA Modules:
  0.0 124.1 jit_solution(6953302923874541531)
XLA Ops:
  0.0 0.6 pad_add_fusion.place
  0.6 3.4 %pack.1 = (bf16[2,128,256]{2,1,0:T(8,128)(2,1)}, bf16[2,128,256]{2,1,0:T(8,128)(2,1)}, bf16[2,128,256]{2,1,0:T(8,128)(2,1)}, bf16[2,128,256]{2,1,0:T(8,128)(2,1)...) custom-call(s32[4]{0:T(128)} %pad_add_fusion.place, ...), custom_call_target="tpu_custom_call" | custom-call | tf_op jit(solution)/shard_map/pack/pallas_call | solution.py:136
  4.0 1.6 %collective-permute-start = (bf16[2,128,256]{2,1,0:T(8,128)(2,1)}, bf16[2,128,256]{2,1,0:T(8,128)(2,1)S(1)}, u32[]{:S(2)}, u32[]{:S(2)}) collective-permute-start(bf16[2,128,256]{2,1,0:T(8,128)(2,1)} %get-tuple-element.52), channel_id=1, source_target_pairs={{0,64},{32,96},{64,128},{96,160},{128,192},{160,224},{192,0},{224,... | collective-permute-start | bytes 393224 | tf_op jit(solution)/shard_map/ppermute | solution.py:40
  5.6 2.7 %collective-permute-start.1 = (bf16[2,128,256]{2,1,0:T(8,128)(2,1)}, bf16[2,128,256]{2,1,0:T(8,128)(2,1)S(1)}, u32[]{:S(2)}, u32[]{:S(2)}) collective-permute-start(bf16[2,128,256]{2,1,0:T(8,128)(2,1)} %get-tuple-element.53), channel_id=1, source_target_pairs={{0,128},{32,160},{64,192},{96,224},{128,0},{160,32},{192,64},{224,... | collective-permute-start | bytes 393224 | tf_op jit(solution)/shard_map/ppermute | solution.py:40
  8.3 1.4 %collective-permute-start.2 = (bf16[2,128,256]{2,1,0:T(8,128)(2,1)}, bf16[2,128,256]{2,1,0:T(8,128)(2,1)S(1)}, u32[]{:S(2)}, u32[]{:S(2)}) collective-permute-start(bf16[2,128,256]{2,1,0:T(8,128)(2,1)} %get-tuple-element.54), channel_id=1, source_target_pairs={{0,192},{32,224},{64,0},{96,32},{128,64},{160,96},{192,128},{224,1... | collective-permute-start | bytes 393224 | tf_op jit(solution)/shard_map/ppermute | solution.py:40
  10.2 2.6 %collective-permute-start.4 = (bf16[256,256]{1,0:T(8,128)(2,1)}, bf16[256,256]{1,0:T(8,128)(2,1)S(1)}, u32[]{:S(2)}, u32[]{:S(2)}) collective-permute-start(bf16[256,256]{1,0:T(8,128)(2,1)} %get-tuple-element.56), channel_id=1, source_target_pairs={{0,2},{1,3},{2,0},{3,1},{4,6},{5,7},{6,4},{7,5},{8,10},{9,11},{10,... | collective-permute-start | bytes 393224 | tf_op jit(solution)/shard_map/ppermute | solution.py:48
  12.8 1.9 %collective-permute-start.5 = (bf16[256,256]{1,0:T(8,128)(2,1)}, bf16[256,256]{1,0:T(8,128)(2,1)S(1)}, u32[]{:S(2)}, u32[]{:S(2)}) collective-permute-start(bf16[256,256]{1,0:T(8,128)(2,1)} %get-tuple-element.57), channel_id=1, source_target_pairs={{0,1},{1,2},{2,3},{3,0},{4,5},{5,6},{6,7},{7,4},{8,9},{9,10},{10,1... | collective-permute-start | bytes 393224 | tf_op jit(solution)/shard_map/ppermute | solution.py:48
  14.7 2.7 %plan.1.source.slots = s32[12]{0:T(128)S(1)} custom-call(s32[4]{0:T(128)S(1)} %copy-done.11, s32[64]{0:T(128)S(1)} %copy-done.13, s32[64]{0:T(128)S(1)} %copy-done.14, s32[64]{0:T(128)S(1)} %copy-done.15), custom_call_target="tpu_custom_call" | custom-call | tf_op jit(solution)/shard_map/plan/pallas_call | solution.py:174
  17.4 0.7 collective-permute-done.4
  18.2 0.8 collective-permute-done.5
  18.9 0.9 copy-done.9
  19.9 0.8 sort.1
  20.8 0.9 slice_dynamic-update-slice_fusion.1
  22.3 1.0 slice_dynamic-update-slice_fusion.refs_8_
  24.1 2.6 %collective-permute-start.13 = (bf16[6,256,256]{2,1,0:T(8,128)(2,1)S(1)}, bf16[6,256,256]{2,1,0:T(8,128)(2,1)S(1)}, u32[]{:S(2)}, u32[]{:S(2)}) collective-permute-start(bf16[6,256,256]{2,1,0:T(8,128)(2,1)S(1)} %slice_dynamic-update-slice_fusion.refs_8_), channel_id=1, source_target_pairs={{0,192},{32,224},{64,0},{96,32},{128,64},{160,96},{192,128},{224,1... | collective-permute-start | bytes 2359304 | tf_op jit(solution)/shard_map/ppermute | solution.py:40
  27.4 2.0 %collective-permute-start.7 = (bf16[512,256]{1,0:T(8,128)(2,1)S(1)}, bf16[512,256]{1,0:T(8,128)(2,1)S(1)}, u32[]{:S(2)}, u32[]{:S(2)}) collective-permute-start(bf16[512,256]{1,0:T(8,128)(2,1)S(1)} %unpack.1.refs_0_), channel_id=1, source_target_pairs={{0,4},{1,5},{2,6},{3,7},{4,8},{5,9},{6,10},{7,11},{8,12},{9,13},{1... | collective-permute-start | bytes 786440 | tf_op jit(solution)/shard_map/ppermute | solution.py:44
  29.4 4.0 %collective-permute-start.8 = (bf16[512,256]{1,0:T(8,128)(2,1)S(1)}, bf16[512,256]{1,0:T(8,128)(2,1)S(1)}, u32[]{:S(2)}, u32[]{:S(2)}) collective-permute-start(bf16[512,256]{1,0:T(8,128)(2,1)S(1)} %unpack.1.refs_0_), channel_id=1, source_target_pairs={{0,28},{1,29},{2,30},{3,31},{4,0},{5,1},{6,2},{7,3},{8,4},{9,5},{1... | collective-permute-start | bytes 786440 | tf_op jit(solution)/shard_map/ppermute | solution.py:44
  33.4 6.2 %collective-permute-done.7.refs_1_ = bf16[512,256]{1,0:T(8,128)(2,1)S(1)} collective-permute-done((bf16[512,256]{1,0:T(8,128)(2,1)S(1)}, bf16[512,256]{1,0:T(8,128)(2,1)S(1)}, u32[]{:S(2)}, u32[]{:S(2)}) %collective-permute-start.7) | collective-permute-done | bytes 262176 | tf_op jit(solution)/shard_map/ppermute | solution.py:44
  39.7 3.2 %collective-permute-start.11 = (bf16[512,256]{1,0:T(8,128)(2,1)S(1)}, bf16[512,256]{1,0:T(8,128)(2,1)S(1)}, u32[]{:S(2)}, u32[]{:S(2)}) collective-permute-start(bf16[512,256]{1,0:T(8,128)(2,1)S(1)} %collective-permute-done.8.refs_4_), channel_id=1, source_target_pairs={{0,28},{1,29},{2,30},{3,31},{4,0},{5,1},{6,2},{7,3},{8,4},{9,5},{1... | collective-permute-start | bytes 786440 | tf_op jit(solution)/shard_map/ppermute | solution.py:44
  42.9 1.6 %collective-permute-done.12.refs_9_ = bf16[6,256,256]{2,1,0:T(8,128)(2,1)S(1)} collective-permute-done((bf16[6,256,256]{2,1,0:T(8,128)(2,1)S(1)}, bf16[6,256,256]{2,1,0:T(8,128)(2,1)S(1)}, u32[]{:S(2)}, u32[]{:S(2)}) %collective-permute-start.12) | collective-permute-done | bytes 786464 | tf_op jit(solution)/shard_map/ppermute | solution.py:40
  44.6 3.8 %collective-permute-done.10.refs_2_ = bf16[512,256]{1,0:T(8,128)(2,1)S(1)} collective-permute-done((bf16[512,256]{1,0:T(8,128)(2,1)S(1)}, bf16[512,256]{1,0:T(8,128)(2,1)S(1)}, u32[]{:S(2)}, u32[]{:S(2)}) %collective-permute-start.10) | collective-permute-done | bytes 262176 | tf_op jit(solution)/shard_map/ppermute | solution.py:44
  48.5 1.8 %collective-permute-start.14 = (bf16[512,256]{1,0:T(8,128)(2,1)S(1)}, bf16[512,256]{1,0:T(8,128)(2,1)S(1)}, u32[]{:S(2)}, u32[]{:S(2)}) collective-permute-start(bf16[512,256]{1,0:T(8,128)(2,1)S(1)} %collective-permute-done.10.refs_2_), channel_id=1, source_target_pairs={{0,4},{1,5},{2,6},{3,7},{4,8},{5,9},{6,10},{7,11},{8,12},{9,13},{1... | collective-permute-start | bytes 786440 | tf_op jit(solution)/shard_map/ppermute | solution.py:44
  50.3 1.5 %collective-permute-start.15 = (bf16[512,256]{1,0:T(8,128)(2,1)S(1)}, bf16[512,256]{1,0:T(8,128)(2,1)S(1)}, u32[]{:S(2)}, u32[]{:S(2)}) collective-permute-start(bf16[512,256]{1,0:T(8,128)(2,1)S(1)} %collective-permute-done.11.refs_5_), channel_id=1, source_target_pairs={{0,28},{1,29},{2,30},{3,31},{4,0},{5,1},{6,2},{7,3},{8,4},{9,5},{1... | collective-permute-start | bytes 786440 | tf_op jit(solution)/shard_map/ppermute | solution.py:44
  51.8 6.6 %collective-permute-done.14.refs_3_ = bf16[512,256]{1,0:T(8,128)(2,1)S(1)} collective-permute-done((bf16[512,256]{1,0:T(8,128)(2,1)S(1)}, bf16[512,256]{1,0:T(8,128)(2,1)S(1)}, u32[]{:S(2)}, u32[]{:S(2)}) %collective-permute-start.14) | collective-permute-done | bytes 262176 | tf_op jit(solution)/shard_map/ppermute | solution.py:44
  58.7 0.9 copy-done.23
  59.7 3.2 %collective-permute-start.20 = (bf16[3,256,256]{2,1,0:T(8,128)(2,1)S(1)}, bf16[3,256,256]{2,1,0:T(8,128)(2,1)}, u32[]{:S(2)}, u32[]{:S(2)}) collective-permute-start(bf16[3,256,256]{2,1,0:T(8,128)(2,1)S(1)} %slice.15), channel_id=1, source_target_pairs={{0,192},{32,224},{64,0},{96,32},{128,64},{160,96},{192,128},{224,1... | collective-permute-start | bytes 1179656 | tf_op jit(solution)/shard_map/ppermute | solution.py:40
  63.0 1.8 %collective-permute-start.17 = (bf16[512,256]{1,0:T(8,128)(2,1)S(1)}, bf16[512,256]{1,0:T(8,128)(2,1)S(1)}, u32[]{:S(2)}, u32[]{:S(2)}) collective-permute-start(bf16[512,256]{1,0:T(8,128)(2,1)S(1)} %collective-permute-done.14.refs_3_), channel_id=1, source_target_pairs={{0,4},{1,5},{2,6},{3,7},{4,8},{5,9},{6,10},{7,11},{8,12},{9,13},{1... | collective-permute-start | bytes 786440 | tf_op jit(solution)/shard_map/ppermute | solution.py:44
  64.8 7.7 %collective-permute-done.19.refs_11_ = bf16[3,256,256]{2,1,0:T(8,128)(2,1)S(1)} collective-permute-done((bf16[3,256,256]{2,1,0:T(8,128)(2,1)S(1)}, bf16[3,256,256]{2,1,0:T(8,128)(2,1)S(1)}, u32[]{:S(2)}, u32[]{:S(2)}) %collective-permute-start.19) | collective-permute-done | bytes 393248 | tf_op jit(solution)/shard_map/ppermute | solution.py:40
  73.1 0.8 squares.1.s0
  74.0 1.5 %collective-permute-start.21 = (f32[8,512]{1,0:T(8,128)S(1)}, f32[8,512]{1,0:T(8,128)S(1)}, u32[]{:S(2)}, u32[]{:S(2)}) collective-permute-start(f32[8,512]{1,0:T(8,128)S(1)} %squares.1.s0), channel_id=1, source_target_pairs={{0,1},{1,2},{2,3},{3,0},{4,5},{5,6},{6,7},{7,4},{8,9},{9,10},{10,1... | collective-permute-start | bytes 49160 | tf_op jit(solution)/shard_map/ppermute | solution.py:48
  75.5 3.5 %collective-permute-start.22 = (f32[8,512]{1,0:T(8,128)S(1)}, f32[8,512]{1,0:T(8,128)S(1)}, u32[]{:S(2)}, u32[]{:S(2)}) collective-permute-start(f32[8,512]{1,0:T(8,128)S(1)} %squares.1.s0), channel_id=1, source_target_pairs={{0,2},{1,3},{2,0},{3,1},{4,6},{5,7},{6,4},{7,5},{8,10},{9,11},{10,... | collective-permute-start | bytes 49160 | tf_op jit(solution)/shard_map/ppermute | solution.py:48
  79.0 0.6 reshape.27.gain
  79.6 1.1 collective-permute-done.22.s2
  80.7 2.0 %collective-permute-done.23.s3 = f32[8,512]{1,0:T(8,128)S(1)} collective-permute-done((f32[8,512]{1,0:T(8,128)S(1)}, f32[8,512]{1,0:T(8,128)S(1)}, u32[]{:S(2)}, u32[]{:S(2)}) %collective-permute-start.23) | collective-permute-done | bytes 16416 | tf_op jit(solution)/shard_map/ppermute | solution.py:48
  83.3 8.3 %project.1 = (f32[512,256]{1,0:T(8,128)}, f32[128,256]{1,0:T(8,128)}, bf16[640,256]{1,0:T(8,128)(2,1)}, bf16[640,256]{1,0:T(8,128)(2,1)}, bf16[640,256]{1,0:T(8,128)(2,1)}, /*index=5*/bf16[2048,256]{1,0:T(8,128)(2,1)}) custom-call(s32[4]{0:T(128)} %pad_add_fusion.place, f32[8,512]{1,0:T(8,128)} %copy-done.10, f32[8,512]{1,0:T(8,128)} %copy-done.26, ...), custom_call_target="tpu_custom_call" | custom-call | flops 2684354560 | bytes 10485760 | tf_op jit(solution)/shard_map/project/pallas_call | solution.py:323
  91.7 2.2 %collective-permute-start.27 = (bf16[640,256]{1,0:T(8,128)(2,1)}, bf16[640,256]{1,0:T(8,128)(2,1)S(1)}, u32[]{:S(2)}, u32[]{:S(2)}) collective-permute-start(bf16[640,256]{1,0:T(8,128)(2,1)} %get-tuple-element.89), channel_id=1, source_target_pairs={{0,2},{1,3},{2,0},{3,1},{4,6},{5,7},{6,4},{7,5},{8,10},{9,11},{10,... | collective-permute-start | bytes 983048 | tf_op jit(solution)/shard_map/ppermute | solution.py:48
  94.0 1.9 %collective-permute-start.28 = (bf16[640,256]{1,0:T(8,128)(2,1)}, bf16[640,256]{1,0:T(8,128)(2,1)S(1)}, u32[]{:S(2)}, u32[]{:S(2)}) collective-permute-start(bf16[640,256]{1,0:T(8,128)(2,1)} %get-tuple-element.90), channel_id=1, source_target_pairs={{0,3},{1,0},{2,1},{3,2},{4,7},{5,4},{6,5},{7,6},{8,11},{9,8},{10,9... | collective-permute-start | bytes 983048 | tf_op jit(solution)/shard_map/ppermute | solution.py:48
  96.3 6.3 %collective-permute-done.26.p1 = bf16[640,256]{1,0:T(8,128)(2,1)S(1)} collective-permute-done((bf16[640,256]{1,0:T(8,128)(2,1)}, bf16[640,256]{1,0:T(8,128)(2,1)S(1)}, u32[]{:S(2)}, u32[]{:S(2)}) %collective-permute-start.26) | collective-permute-done | bytes 327712 | tf_op jit(solution)/shard_map/ppermute | solution.py:48
  102.6 1.6 %collective-permute-done.27.p2 = bf16[640,256]{1,0:T(8,128)(2,1)S(1)} collective-permute-done((bf16[640,256]{1,0:T(8,128)(2,1)}, bf16[640,256]{1,0:T(8,128)(2,1)S(1)}, u32[]{:S(2)}, u32[]{:S(2)}) %collective-permute-start.27) | collective-permute-done | bytes 327712 | tf_op jit(solution)/shard_map/ppermute | solution.py:48
  104.2 4.4 %collective-permute-done.28.p3 = bf16[640,256]{1,0:T(8,128)(2,1)S(1)} collective-permute-done((bf16[640,256]{1,0:T(8,128)(2,1)}, bf16[640,256]{1,0:T(8,128)(2,1)S(1)}, u32[]{:S(2)}, u32[]{:S(2)}) %collective-permute-start.28) | collective-permute-done | bytes 327712 | tf_op jit(solution)/shard_map/ppermute | solution.py:48
  108.6 0.9 copy-done.8
  110.0 0.7 collective-permute-start.29
  110.7 2.4 %collective-permute-start.30 = (bf16[128,256]{1,0:T(8,128)(2,1)S(1)}, bf16[128,256]{1,0:T(8,128)(2,1)S(1)}, u32[]{:S(2)}, u32[]{:S(2)}) collective-permute-start(bf16[128,256]{1,0:T(8,128)(2,1)S(1)} %fresh.1.f0), channel_id=1, source_target_pairs={{0,2},{1,3},{2,0},{3,1},{4,6},{5,7},{6,4},{7,5},{8,10},{9,11},{10,... | collective-permute-start | bytes 196616 | tf_op jit(solution)/shard_map/ppermute | solution.py:48
  113.1 2.0 %collective-permute-start.31 = (bf16[128,256]{1,0:T(8,128)(2,1)S(1)}, bf16[128,256]{1,0:T(8,128)(2,1)S(1)}, u32[]{:S(2)}, u32[]{:S(2)}) collective-permute-start(bf16[128,256]{1,0:T(8,128)(2,1)S(1)} %fresh.1.f0), channel_id=1, source_target_pairs={{0,3},{1,0},{2,1},{3,2},{4,7},{5,4},{6,5},{7,6},{8,11},{9,8},{10,9... | collective-permute-start | bytes 196616 | tf_op jit(solution)/shard_map/ppermute | solution.py:48
  115.2 1.2 copy-done.16
  116.4 1.0 copy-done.17
  117.4 4.7 %prompt.1 = (bf16[4,256,128]{2,1,0:T(8,128)(2,1)S(1)}, f32[4,256,128]{2,1,0:T(8,128)S(1)}, f32[4,256,128]{2,1,0:T(8,128)S(1)}, f32[4,256,128]{2,1,0:T(8,128)S(1)}) custom-call(f32[512,256]{1,0:T(8,128)S(1)} %copy-done.17, bf16[640,256]{1,0:T(8,128)(2,1)S(1)} %collective-permute-done.26.p1, bf16[640,256]{1,0:T(8,128)(2,1)S(1)} %collective-permute-done.27.p2, ...), custom_call_target="tpu_custom_call" | custom-call | flops 1073741824 | bytes 2097152 | tf_op jit(solution)/shard_map/prompt/pallas_call | solution.py:432
  122.1 2.0 %finish.1 = bf16[4,128,256]{2,1,0:T(8,128)(2,1)} custom-call(s32[4]{0:T(128)S(1)} %copy-done.12, s32[12]{0:T(128)S(1)} %plan.1.source.slots, bf16[4,256,128]{2,1,0:T(8,128)(2,1)S(1)} %get-tuple-element.92.q, f32[4,256,128]{2,1,0:T(8,128)S(1)} %get-tuple-element.93.mixed_ref, f32[4,256,128]{2,1,0:T(8,128)S(1)} %get-tuple-element.94.top_ref, ...), custom_call_target="tpu_custom_call" | custom-call | tf_op jit(solution)/shard_map/finish/pallas_call | solution.py:481
  (96 shorter events, 5.4 us)
Async XLA Ops:
  0.6 14.1 %copy-start.11 = (s32[4]{0:T(128)S(1)}, s32[4]{0:T(128)}, u32[]{:S(2)}) copy-start(s32[4]{0:T(128)} %pad_add_fusion.place) | copy-start | bytes 52
  0.6 14.1 %copy-start.13 = (s32[64]{0:T(128)S(1)}, s32[64]{0:T(128)}, u32[]{:S(2)}) copy-start(s32[64]{0:T(128)} %keep.3) | copy-start | bytes 772
  0.6 14.1 %copy-start.14 = (s32[64]{0:T(128)S(1)}, s32[64]{0:T(128)}, u32[]{:S(2)}) copy-start(s32[64]{0:T(128)} %destination.3) | copy-start | bytes 772
  0.6 14.1 %copy-start.15 = (s32[64]{0:T(128)S(1)}, s32[64]{0:T(128)}, u32[]{:S(2)}) copy-start(s32[64]{0:T(128)} %counts.1) | copy-start | bytes 772
  4.0 8.8 %collective-permute-start = (bf16[2,128,256]{2,1,0:T(8,128)(2,1)}, bf16[2,128,256]{2,1,0:T(8,128)(2,1)S(1)}, u32[]{:S(2)}, u32[]{:S(2)}) collective-permute-start(bf16[2,128,256]{2,1,0:T(8,128)(2,1)} %get-tuple-element.52), channel_id=1, source_target_pairs={{0,64},{32,96},{64,128},{96,160},{128,192},{160,224},{192,0},{224,... | collective-permute-start | bytes 393224 | tf_op jit(solution)/shard_map/ppermute | solution.py:40
  5.6 11.8 %collective-permute-start.1 = (bf16[2,128,256]{2,1,0:T(8,128)(2,1)}, bf16[2,128,256]{2,1,0:T(8,128)(2,1)S(1)}, u32[]{:S(2)}, u32[]{:S(2)}) collective-permute-start(bf16[2,128,256]{2,1,0:T(8,128)(2,1)} %get-tuple-element.53), channel_id=1, source_target_pairs={{0,128},{32,160},{64,192},{96,224},{128,0},{160,32},{192,64},{224,... | collective-permute-start | bytes 393224 | tf_op jit(solution)/shard_map/ppermute | solution.py:40
  8.3 9.1 %collective-permute-start.2 = (bf16[2,128,256]{2,1,0:T(8,128)(2,1)}, bf16[2,128,256]{2,1,0:T(8,128)(2,1)S(1)}, u32[]{:S(2)}, u32[]{:S(2)}) collective-permute-start(bf16[2,128,256]{2,1,0:T(8,128)(2,1)} %get-tuple-element.54), channel_id=1, source_target_pairs={{0,192},{32,224},{64,0},{96,32},{128,64},{160,96},{192,128},{224,1... | collective-permute-start | bytes 393224 | tf_op jit(solution)/shard_map/ppermute | solution.py:40
  9.7 7.7 %collective-permute-start.3 = (bf16[256,256]{1,0:T(8,128)(2,1)}, bf16[256,256]{1,0:T(8,128)(2,1)S(1)}, u32[]{:S(2)}, u32[]{:S(2)}) collective-permute-start(bf16[256,256]{1,0:T(8,128)(2,1)} %get-tuple-element.55), channel_id=1, source_target_pairs={{0,3},{1,0},{2,1},{3,2},{4,7},{5,4},{6,5},{7,6},{8,11},{9,8},{10,9... | collective-permute-start | bytes 393224 | tf_op jit(solution)/shard_map/ppermute | solution.py:48
  10.2 8.0 %collective-permute-start.4 = (bf16[256,256]{1,0:T(8,128)(2,1)}, bf16[256,256]{1,0:T(8,128)(2,1)S(1)}, u32[]{:S(2)}, u32[]{:S(2)}) collective-permute-start(bf16[256,256]{1,0:T(8,128)(2,1)} %get-tuple-element.56), channel_id=1, source_target_pairs={{0,2},{1,3},{2,0},{3,1},{4,6},{5,7},{6,4},{7,5},{8,10},{9,11},{10,... | collective-permute-start | bytes 393224 | tf_op jit(solution)/shard_map/ppermute | solution.py:48
  12.8 6.2 %collective-permute-start.5 = (bf16[256,256]{1,0:T(8,128)(2,1)}, bf16[256,256]{1,0:T(8,128)(2,1)S(1)}, u32[]{:S(2)}, u32[]{:S(2)}) collective-permute-start(bf16[256,256]{1,0:T(8,128)(2,1)} %get-tuple-element.57), channel_id=1, source_target_pairs={{0,1},{1,2},{2,3},{3,0},{4,5},{5,6},{6,7},{7,4},{8,9},{9,10},{10,1... | collective-permute-start | bytes 393224 | tf_op jit(solution)/shard_map/ppermute | solution.py:48
  20.7 1.6 %collective-permute-start.6 = (bf16[512,256]{1,0:T(8,128)(2,1)S(1)}, bf16[512,256]{1,0:T(8,128)(2,1)S(1)}, u32[]{:S(2)}, u32[]{:S(2)}) collective-permute-start(bf16[512,256]{1,0:T(8,128)(2,1)S(1)} %get-tuple-element.63), channel_id=1, source_target_pairs={{0,32},{32,0},{64,96},{96,64},{128,160},{160,128},{192,224},{224,1... | collective-permute-start | bytes 786440 | tf_op jit(solution)/shard_map/ppermute | solution.py:40
  23.3 25.1 %copy-start.20 = (bf16[6,256,256]{2,1,0:T(8,128)(2,1)}, bf16[6,256,256]{2,1,0:T(8,128)(2,1)S(1)}, u32[]{:S(2)}) copy-start(bf16[6,256,256]{2,1,0:T(8,128)(2,1)S(1)} %slice_dynamic-update-slice_fusion.refs_8_) | copy-start | bytes 2359300
  23.3 16.3 %collective-permute-start.9 = (bf16[6,256,256]{2,1,0:T(8,128)(2,1)S(1)}, bf16[6,256,256]{2,1,0:T(8,128)(2,1)S(1)}, u32[]{:S(2)}, u32[]{:S(2)}) collective-permute-start(bf16[6,256,256]{2,1,0:T(8,128)(2,1)S(1)} %slice_dynamic-update-slice_fusion.refs_8_), channel_id=1, source_target_pairs={{0,32},{32,0},{64,96},{96,64},{128,160},{160,128},{192,224},{224,1... | collective-permute-start | bytes 2359304 | tf_op jit(solution)/shard_map/ppermute | solution.py:40
  23.5 21.0 %collective-permute-start.12 = (bf16[6,256,256]{2,1,0:T(8,128)(2,1)S(1)}, bf16[6,256,256]{2,1,0:T(8,128)(2,1)S(1)}, u32[]{:S(2)}, u32[]{:S(2)}) collective-permute-start(bf16[6,256,256]{2,1,0:T(8,128)(2,1)S(1)} %slice_dynamic-update-slice_fusion.refs_8_), channel_id=1, source_target_pairs={{0,64},{32,96},{64,128},{96,160},{128,192},{160,224},{192,0},{224,... | collective-permute-start | bytes 2359304 | tf_op jit(solution)/shard_map/ppermute | solution.py:40
  24.1 20.4 %collective-permute-start.13 = (bf16[6,256,256]{2,1,0:T(8,128)(2,1)S(1)}, bf16[6,256,256]{2,1,0:T(8,128)(2,1)S(1)}, u32[]{:S(2)}, u32[]{:S(2)}) collective-permute-start(bf16[6,256,256]{2,1,0:T(8,128)(2,1)S(1)} %slice_dynamic-update-slice_fusion.refs_8_), channel_id=1, source_target_pairs={{0,192},{32,224},{64,0},{96,32},{128,64},{160,96},{192,128},{224,1... | collective-permute-start | bytes 2359304 | tf_op jit(solution)/shard_map/ppermute | solution.py:40
  26.8 52.2 %copy-start.21 = (bf16[8192]{0:T(1024)(128)(2,1)S(1)}, bf16[8192]{0:T(1024)(128)(2,1)}, u32[]{:S(2)}) copy-start(bf16[8192]{0:T(1024)(128)(2,1)} %param.11) | copy-start | bytes 49156
  27.4 55.3 %copy-start = (bf16[512,256]{1,0:T(8,128)(2,1)}, bf16[512,256]{1,0:T(8,128)(2,1)S(1)}, u32[]{:S(2)}) copy-start(bf16[512,256]{1,0:T(8,128)(2,1)S(1)} %unpack.1.refs_0_) | copy-start | bytes 786436
  27.4 12.2 %collective-permute-start.7 = (bf16[512,256]{1,0:T(8,128)(2,1)S(1)}, bf16[512,256]{1,0:T(8,128)(2,1)S(1)}, u32[]{:S(2)}, u32[]{:S(2)}) collective-permute-start(bf16[512,256]{1,0:T(8,128)(2,1)S(1)} %unpack.1.refs_0_), channel_id=1, source_target_pairs={{0,4},{1,5},{2,6},{3,7},{4,8},{5,9},{6,10},{7,11},{8,12},{9,13},{1... | collective-permute-start | bytes 786440 | tf_op jit(solution)/shard_map/ppermute | solution.py:44
  29.4 10.2 %collective-permute-start.8 = (bf16[512,256]{1,0:T(8,128)(2,1)S(1)}, bf16[512,256]{1,0:T(8,128)(2,1)S(1)}, u32[]{:S(2)}, u32[]{:S(2)}) collective-permute-start(bf16[512,256]{1,0:T(8,128)(2,1)S(1)} %unpack.1.refs_0_), channel_id=1, source_target_pairs={{0,28},{1,29},{2,30},{3,31},{4,0},{5,1},{6,2},{7,3},{8,4},{9,5},{1... | collective-permute-start | bytes 786440 | tf_op jit(solution)/shard_map/ppermute | solution.py:44
  39.6 43.1 %copy-start.1 = (bf16[512,256]{1,0:T(8,128)(2,1)}, bf16[512,256]{1,0:T(8,128)(2,1)S(1)}, u32[]{:S(2)}) copy-start(bf16[512,256]{1,0:T(8,128)(2,1)S(1)} %collective-permute-done.7.refs_1_) | copy-start | bytes 786436
  39.6 43.1 %copy-start.2 = (bf16[512,256]{1,0:T(8,128)(2,1)}, bf16[512,256]{1,0:T(8,128)(2,1)S(1)}, u32[]{:S(2)}) copy-start(bf16[512,256]{1,0:T(8,128)(2,1)S(1)} %collective-permute-done.8.refs_4_) | copy-start | bytes 786436
  39.6 19.0 %copy-start.22 = (bf16[6,256,256]{2,1,0:T(8,128)(2,1)}, bf16[6,256,256]{2,1,0:T(8,128)(2,1)S(1)}, u32[]{:S(2)}) copy-start(bf16[6,256,256]{2,1,0:T(8,128)(2,1)S(1)} %collective-permute-done.9.refs_13_) | copy-start | bytes 2359300
  39.6 8.7 %collective-permute-start.10 = (bf16[512,256]{1,0:T(8,128)(2,1)S(1)}, bf16[512,256]{1,0:T(8,128)(2,1)S(1)}, u32[]{:S(2)}, u32[]{:S(2)}) collective-permute-start(bf16[512,256]{1,0:T(8,128)(2,1)S(1)} %collective-permute-done.7.refs_1_), channel_id=1, source_target_pairs={{0,4},{1,5},{2,6},{3,7},{4,8},{5,9},{6,10},{7,11},{8,12},{9,13},{1... | collective-permute-start | bytes 786440 | tf_op jit(solution)/shard_map/ppermute | solution.py:44
  39.7 8.7 %collective-permute-start.11 = (bf16[512,256]{1,0:T(8,128)(2,1)S(1)}, bf16[512,256]{1,0:T(8,128)(2,1)S(1)}, u32[]{:S(2)}, u32[]{:S(2)}) collective-permute-start(bf16[512,256]{1,0:T(8,128)(2,1)S(1)} %collective-permute-done.8.refs_4_), channel_id=1, source_target_pairs={{0,28},{1,29},{2,30},{3,31},{4,0},{5,1},{6,2},{7,3},{8,4},{9,5},{1... | collective-permute-start | bytes 786440 | tf_op jit(solution)/shard_map/ppermute | solution.py:44
  44.6 38.2 %copy-start.18 = (bf16[6,256,256]{2,1,0:T(8,128)(2,1)}, bf16[6,256,256]{2,1,0:T(8,128)(2,1)S(1)}, u32[]{:S(2)}) copy-start(bf16[6,256,256]{2,1,0:T(8,128)(2,1)S(1)} %collective-permute-done.12.refs_9_) | copy-start | bytes 2359300
  44.6 30.9 %copy-start.19 = (bf16[6,256,256]{2,1,0:T(8,128)(2,1)}, bf16[6,256,256]{2,1,0:T(8,128)(2,1)S(1)}, u32[]{:S(2)}) copy-start(bf16[6,256,256]{2,1,0:T(8,128)(2,1)S(1)} %collective-permute-done.13.refs_10_) | copy-start | bytes 2359300
  48.4 34.4 %copy-start.3 = (bf16[512,256]{1,0:T(8,128)(2,1)}, bf16[512,256]{1,0:T(8,128)(2,1)S(1)}, u32[]{:S(2)}) copy-start(bf16[512,256]{1,0:T(8,128)(2,1)S(1)} %collective-permute-done.10.refs_2_) | copy-start | bytes 786436
  48.4 34.4 %copy-start.4 = (bf16[512,256]{1,0:T(8,128)(2,1)}, bf16[512,256]{1,0:T(8,128)(2,1)S(1)}, u32[]{:S(2)}) copy-start(bf16[512,256]{1,0:T(8,128)(2,1)S(1)} %collective-permute-done.11.refs_5_) | copy-start | bytes 786436
  48.4 10.3 %collective-permute-start.16 = (bf16[6,256,256]{2,1,0:T(8,128)(2,1)S(1)}, bf16[6,256,256]{2,1,0:T(8,128)(2,1)S(1)}, u32[]{:S(2)}, u32[]{:S(2)}) collective-permute-start(bf16[6,256,256]{2,1,0:T(8,128)(2,1)S(1)} %collective-permute-done.12.refs_9_), channel_id=1, source_target_pairs={{0,32},{32,0},{64,96},{96,64},{128,160},{160,128},{192,224},{224,1... | collective-permute-start | bytes 2359304 | tf_op jit(solution)/shard_map/ppermute | solution.py:40
  48.5 9.9 %collective-permute-start.14 = (bf16[512,256]{1,0:T(8,128)(2,1)S(1)}, bf16[512,256]{1,0:T(8,128)(2,1)S(1)}, u32[]{:S(2)}, u32[]{:S(2)}) collective-permute-start(bf16[512,256]{1,0:T(8,128)(2,1)S(1)} %collective-permute-done.10.refs_2_), channel_id=1, source_target_pairs={{0,4},{1,5},{2,6},{3,7},{4,8},{5,9},{6,10},{7,11},{8,12},{9,13},{1... | collective-permute-start | bytes 786440 | tf_op jit(solution)/shard_map/ppermute | solution.py:44
  50.3 8.4 %collective-permute-start.15 = (bf16[512,256]{1,0:T(8,128)(2,1)S(1)}, bf16[512,256]{1,0:T(8,128)(2,1)S(1)}, u32[]{:S(2)}, u32[]{:S(2)}) collective-permute-start(bf16[512,256]{1,0:T(8,128)(2,1)S(1)} %collective-permute-done.11.refs_5_), channel_id=1, source_target_pairs={{0,28},{1,29},{2,30},{3,31},{4,0},{5,1},{6,2},{7,3},{8,4},{9,5},{1... | collective-permute-start | bytes 786440 | tf_op jit(solution)/shard_map/ppermute | solution.py:44
  58.4 24.4 %copy-start.5 = (bf16[512,256]{1,0:T(8,128)(2,1)}, bf16[512,256]{1,0:T(8,128)(2,1)S(1)}, u32[]{:S(2)}) copy-start(bf16[512,256]{1,0:T(8,128)(2,1)S(1)} %collective-permute-done.14.refs_3_) | copy-start | bytes 786436
  58.6 24.2 %copy-start.6 = (bf16[512,256]{1,0:T(8,128)(2,1)}, bf16[512,256]{1,0:T(8,128)(2,1)S(1)}, u32[]{:S(2)}) copy-start(bf16[512,256]{1,0:T(8,128)(2,1)S(1)} %collective-permute-done.15.refs_6_) | copy-start | bytes 786436
  59.6 12.9 %collective-permute-start.18 = (bf16[6,256,256]{2,1,0:T(8,128)(2,1)S(1)}, bf16[6,256,256]{2,1,0:T(8,128)(2,1)S(1)}, u32[]{:S(2)}, u32[]{:S(2)}) collective-permute-start(bf16[6,256,256]{2,1,0:T(8,128)(2,1)S(1)} %collective-permute-done.13.refs_10_), channel_id=1, source_target_pairs={{0,32},{32,0},{64,96},{96,64},{128,160},{160,128},{192,224},{224,1... | collective-permute-start | bytes 2359304 | tf_op jit(solution)/shard_map/ppermute | solution.py:40
  59.7 12.8 %collective-permute-start.19 = (bf16[3,256,256]{2,1,0:T(8,128)(2,1)S(1)}, bf16[3,256,256]{2,1,0:T(8,128)(2,1)S(1)}, u32[]{:S(2)}, u32[]{:S(2)}) collective-permute-start(bf16[3,256,256]{2,1,0:T(8,128)(2,1)S(1)} %slice.14), channel_id=1, source_target_pairs={{0,64},{32,96},{64,128},{96,160},{128,192},{160,224},{192,0},{224,... | collective-permute-start | bytes 1179656 | tf_op jit(solution)/shard_map/ppermute | solution.py:40
  59.7 12.7 %collective-permute-start.20 = (bf16[3,256,256]{2,1,0:T(8,128)(2,1)S(1)}, bf16[3,256,256]{2,1,0:T(8,128)(2,1)}, u32[]{:S(2)}, u32[]{:S(2)}) collective-permute-start(bf16[3,256,256]{2,1,0:T(8,128)(2,1)S(1)} %slice.15), channel_id=1, source_target_pairs={{0,192},{32,224},{64,0},{96,32},{128,64},{160,96},{192,128},{224,1... | collective-permute-start | bytes 1179656 | tf_op jit(solution)/shard_map/ppermute | solution.py:40
  63.0 9.5 %collective-permute-start.17 = (bf16[512,256]{1,0:T(8,128)(2,1)S(1)}, bf16[512,256]{1,0:T(8,128)(2,1)S(1)}, u32[]{:S(2)}, u32[]{:S(2)}) collective-permute-start(bf16[512,256]{1,0:T(8,128)(2,1)S(1)} %collective-permute-done.14.refs_3_), channel_id=1, source_target_pairs={{0,4},{1,5},{2,6},{3,7},{4,8},{5,9},{6,10},{7,11},{8,12},{9,13},{1... | collective-permute-start | bytes 786440 | tf_op jit(solution)/shard_map/ppermute | solution.py:44
  72.5 10.2 %collective-permute-start.24 = (bf16[3,256,256]{2,1,0:T(8,128)(2,1)S(1)}, bf16[3,256,256]{2,1,0:T(8,128)(2,1)}, u32[]{:S(2)}, u32[]{:S(2)}) collective-permute-start(bf16[3,256,256]{2,1,0:T(8,128)(2,1)S(1)} %collective-permute-done.19.refs_11_), channel_id=1, source_target_pairs={{0,32},{32,0},{64,96},{96,64},{128,160},{160,128},{192,224},{224,1... | collective-permute-start | bytes 1179656 | tf_op jit(solution)/shard_map/ppermute | solution.py:40
  72.6 10.1 %collective-permute-start.25 = (bf16[3,256,256]{2,1,0:T(8,128)(2,1)}, bf16[3,256,256]{2,1,0:T(8,128)(2,1)}, u32[]{:S(2)}, u32[]{:S(2)}) collective-permute-start(bf16[3,256,256]{2,1,0:T(8,128)(2,1)} %collective-permute-done.20.refs_12_), channel_id=1, source_target_pairs={{0,32},{32,0},{64,96},{96,64},{128,160},{160,128},{192,224},{224,1... | collective-permute-start | bytes 1179656 | tf_op jit(solution)/shard_map/ppermute | solution.py:40
  74.0 5.7 %collective-permute-start.21 = (f32[8,512]{1,0:T(8,128)S(1)}, f32[8,512]{1,0:T(8,128)S(1)}, u32[]{:S(2)}, u32[]{:S(2)}) collective-permute-start(f32[8,512]{1,0:T(8,128)S(1)} %squares.1.s0), channel_id=1, source_target_pairs={{0,1},{1,2},{2,3},{3,0},{4,5},{5,6},{6,7},{7,4},{8,9},{9,10},{10,1... | collective-permute-start | bytes 49160 | tf_op jit(solution)/shard_map/ppermute | solution.py:48
  75.5 5.2 %collective-permute-start.22 = (f32[8,512]{1,0:T(8,128)S(1)}, f32[8,512]{1,0:T(8,128)S(1)}, u32[]{:S(2)}, u32[]{:S(2)}) collective-permute-start(f32[8,512]{1,0:T(8,128)S(1)} %squares.1.s0), channel_id=1, source_target_pairs={{0,2},{1,3},{2,0},{3,1},{4,6},{5,7},{6,4},{7,5},{8,10},{9,11},{10,... | collective-permute-start | bytes 49160 | tf_op jit(solution)/shard_map/ppermute | solution.py:48
  79.0 3.7 %collective-permute-start.23 = (f32[8,512]{1,0:T(8,128)S(1)}, f32[8,512]{1,0:T(8,128)S(1)}, u32[]{:S(2)}, u32[]{:S(2)}) collective-permute-start(f32[8,512]{1,0:T(8,128)S(1)} %squares.1.s0), channel_id=1, source_target_pairs={{0,3},{1,0},{2,1},{3,2},{4,7},{5,4},{6,5},{7,6},{8,11},{9,8},{10,9... | collective-permute-start | bytes 49160 | tf_op jit(solution)/shard_map/ppermute | solution.py:48
  91.6 10.9 %collective-permute-start.26 = (bf16[640,256]{1,0:T(8,128)(2,1)}, bf16[640,256]{1,0:T(8,128)(2,1)S(1)}, u32[]{:S(2)}, u32[]{:S(2)}) collective-permute-start(bf16[640,256]{1,0:T(8,128)(2,1)} %get-tuple-element.88), channel_id=1, source_target_pairs={{0,1},{1,2},{2,3},{3,0},{4,5},{5,6},{6,7},{7,4},{8,9},{9,10},{10,1... | collective-permute-start | bytes 983048 | tf_op jit(solution)/shard_map/ppermute | solution.py:48
  91.7 12.4 %collective-permute-start.27 = (bf16[640,256]{1,0:T(8,128)(2,1)}, bf16[640,256]{1,0:T(8,128)(2,1)S(1)}, u32[]{:S(2)}, u32[]{:S(2)}) collective-permute-start(bf16[640,256]{1,0:T(8,128)(2,1)} %get-tuple-element.89), channel_id=1, source_target_pairs={{0,2},{1,3},{2,0},{3,1},{4,6},{5,7},{6,4},{7,5},{8,10},{9,11},{10,... | collective-permute-start | bytes 983048 | tf_op jit(solution)/shard_map/ppermute | solution.py:48
  94.0 14.6 %collective-permute-start.28 = (bf16[640,256]{1,0:T(8,128)(2,1)}, bf16[640,256]{1,0:T(8,128)(2,1)S(1)}, u32[]{:S(2)}, u32[]{:S(2)}) collective-permute-start(bf16[640,256]{1,0:T(8,128)(2,1)} %get-tuple-element.90), channel_id=1, source_target_pairs={{0,3},{1,0},{2,1},{3,2},{4,7},{5,4},{6,5},{7,6},{8,11},{9,8},{10,9... | collective-permute-start | bytes 983048 | tf_op jit(solution)/shard_map/ppermute | solution.py:48
  110.0 12.1 %collective-permute-start.29 = (bf16[128,256]{1,0:T(8,128)(2,1)S(1)}, bf16[128,256]{1,0:T(8,128)(2,1)S(1)}, u32[]{:S(2)}, u32[]{:S(2)}) collective-permute-start(bf16[128,256]{1,0:T(8,128)(2,1)S(1)} %fresh.1.f0), channel_id=1, source_target_pairs={{0,1},{1,2},{2,3},{3,0},{4,5},{5,6},{6,7},{7,4},{8,9},{9,10},{10,1... | collective-permute-start | bytes 196616 | tf_op jit(solution)/shard_map/ppermute | solution.py:48
  110.7 11.4 %collective-permute-start.30 = (bf16[128,256]{1,0:T(8,128)(2,1)S(1)}, bf16[128,256]{1,0:T(8,128)(2,1)S(1)}, u32[]{:S(2)}, u32[]{:S(2)}) collective-permute-start(bf16[128,256]{1,0:T(8,128)(2,1)S(1)} %fresh.1.f0), channel_id=1, source_target_pairs={{0,2},{1,3},{2,0},{3,1},{4,6},{5,7},{6,4},{7,5},{8,10},{9,11},{10,... | collective-permute-start | bytes 196616 | tf_op jit(solution)/shard_map/ppermute | solution.py:48
  113.1 9.0 %collective-permute-start.31 = (bf16[128,256]{1,0:T(8,128)(2,1)S(1)}, bf16[128,256]{1,0:T(8,128)(2,1)S(1)}, u32[]{:S(2)}, u32[]{:S(2)}) collective-permute-start(bf16[128,256]{1,0:T(8,128)(2,1)S(1)} %fresh.1.f0), channel_id=1, source_target_pairs={{0,3},{1,0},{2,1},{3,2},{4,7},{5,4},{6,5},{7,6},{8,11},{9,8},{10,9... | collective-permute-start | bytes 196616 | tf_op jit(solution)/shard_map/ppermute | solution.py:48
  (13 other events, 59.1 us)

commit v4 on v3

--- a/solution.py
+++ b/solution.py
@@ -22,34 +22,31 @@
 STRETCH = 8.0
 MASKED_SCORE = -1e30
 
-def group_perm(dx, dc):
-    return [
-        (x * CORES + c, ((x + dx) % XS) * CORES + (c ^ dc)) for x in range(XS) for c in range(CORES)
-    ]
-
-
-def z_perm(d):
-    return [(z * YS + y, ((z + d) % ZS) * YS + y) for z in range(ZS) for y in range(YS)]
-
-
-def y_perm(d):
-    return [(z * YS + y, z * YS + (y + d) % YS) for z in range(ZS) for y in range(YS)]
-
-
-def send_group(v, dx, dc):
-    return lax.ppermute(v, "group", group_perm(dx, dc))
-
-
-def send_z(v, d):
-    return lax.ppermute(v, "fsdp", z_perm(d))
-
-
-def send_y(v, d):
-    return lax.ppermute(v, "fsdp", y_perm(d))
+def other_of(a, r, size):
+    return (a + (r if a % 2 == 0 else -r)) % size
+
+
+def send_x(v, r):
+    perm = [(x * CORES + c, other_of(x, r, XS) * CORES + c) for x in range(XS) for c in range(CORES)]
+    return lax.ppermute(v, "group", perm)
 
 
 def swap(v):
-    return send_group(v, 0, 1)
+    return lax.ppermute(v, "group", [(g, g ^ 1) for g in range(XS * CORES)])
+
+
+def send_z(v, r):
+    perm = [(z * YS + y, other_of(z, r, ZS) * YS + y) for z in range(ZS) for y in range(YS)]
+    return lax.ppermute(v, "fsdp", perm)
+
+
+def send_y(v, r):
+    perm = [(z * YS + y, z * YS + (y + r) % YS) for z in range(ZS) for y in range(YS)]
+    return lax.ppermute(v, "fsdp", perm)
+
+
+def relation(a, b):
+    return lax.rem(4 + (1 - 2 * lax.rem(a, 2)) * (b - a), 4)
 
 
 def rope_tables(length, offset):
@@ -123,7 +120,7 @@
         @pl.when(keep[first + b] == 1)
         def _():
             target = lax.div(destination[first + b], OUT_DEV)
-            dx = lax.rem(lax.div(target, CORES) + XS - x, XS)
+            dx = relation(x, lax.div(target, CORES))
             dc = lax.rem(target + c, CORES)
             chosen[dx * CORES + dc] = b
 
@@ -146,8 +143,9 @@
     )(place, keep, destination, *arrays)
 
 
-def plan_kernel(place, keep, destination, counts, out):
+def plan_kernel(place, keep, destination, counts, piece, out, held):
     x, c = place[0], place[1]
+    held[...] = piece[...]
 
     def step(b, _):
         target = destination[b]
@@ -158,7 +156,7 @@
             slot = lax.rem(target, OUT_DEV)
             source = lax.div(b, IN_DEV)
             other = lax.rem(group + c, CORES)
-            dx = lax.rem(x + XS - lax.div(source, CORES), XS)
+            dx = relation(x, lax.div(source, CORES))
             out[other * OUT_DEV + slot] = jnp.where(lax.rem(source, CORES) == c, dx, XS)
 
             @pl.when(other == 0)
@@ -170,19 +168,20 @@
     lax.fori_loop(0, keep.shape[0], step, 0)
 
 
-def plan(place, keep, destination, counts):
+def plan(place, keep, destination, counts, piece):
     return pl.pallas_call(
         plan_kernel,
-        out_shape=shaped((3 * OUT_DEV,), jnp.int32),
-        in_specs=[SMEM] * 4,
-        out_specs=SMEM,
+        out_shape=[shaped((3 * OUT_DEV,), jnp.int32), shaped(piece.shape, piece.dtype)],
+        in_specs=[SMEM] * 4 + [VMEM],
+        out_specs=[SMEM, VMEM],
         compiler_params=limit(1),
         name="plan",
-    )(place, keep, destination, counts)
+    )(place, keep, destination, counts, piece)
 
 
 SHARDS = 8
 TOTAL = OUT_DEV * ROWS
+EXTRA = 16
 
 
 def sort_kernel(source, *refs):
@@ -207,58 +206,66 @@
     )(source, *pieces)
 
 
-def unpack_kernel(source, held, swapped, out_ref):
+def unpack_kernel(source, held, swapped, x_ref, sums_ref):
     for j in range(OUT_DEV):
         rows = pl.ds(j * ROWS, ROWS)
         there = source[j] == XS
 
         @pl.when(there)
         def _():
-            out_ref[rows, :] = swapped[rows, :]
+            x_ref[rows, :] = swapped[rows, :]
 
         @pl.when(jnp.logical_not(there))
         def _():
-            out_ref[rows, :] = held[rows, :]
-
-
-def unpack(source, held, swapped):
-    return pl.pallas_call(
-        unpack_kernel,
-        out_shape=shaped((TOTAL, TILE), jnp.bfloat16),
-        in_specs=[SMEM] + [VMEM] * 2,
-        out_specs=VMEM,
-        compiler_params=limit(2),
-        name="unpack",
-    )(source, held, swapped)
-
-
-def squares_kernel(*refs):
-    shards, out_ref = refs[:8], refs[8]
-    total = None
-    for shard in shards:
-        wide = shard[...].astype(jnp.float32)
-        total = wide * wide if total is None else total + wide * wide
-    out_ref[...] = lax.dot_general(
+            x_ref[rows, :] = held[rows, :]
+
+    wide = x_ref[...].astype(jnp.float32)
+    sums_ref[...] = lax.dot_general(
         jnp.ones((8, TILE), jnp.float32),
-        total,
+        wide * wide,
         (((1,), (1,)), ((), ())),
         precision=lax.Precision.HIGHEST,
         preferred_element_type=jnp.float32,
     )
 
 
-def sum_squares(shards):
-    return pl.pallas_call(
-        squares_kernel,
-        out_shape=shaped((8, TOTAL), jnp.float32),
-        in_specs=[VMEM] * 8,
+def unpack(source, held, swapped):
+    return pl.pallas_call(
+        unpack_kernel,
+        out_shape=[shaped((TOTAL, TILE), jnp.bfloat16), shaped((8, TOTAL), jnp.float32)],
+        in_specs=[SMEM] + [VMEM] * 2,
+        out_specs=[VMEM] * 2,
+        compiler_params=limit(2),
+        name="unpack",
+    )(source, held, swapped)
+
+
+def label_kernel(x, s0, s1, s2, s3, out):
+    out[pl.ds(0, TOTAL), :] = x[...]
+    value = s0[0:1, :] + s1[0:1, :] + s2[0:1, :] + s3[0:1, :]
+    row = lax.broadcasted_iota(jnp.int32, (EXTRA, TILE), 0)
+    table = jnp.zeros((EXTRA, TILE), jnp.float32)
+    for term in range(3):
+        rounded = value.astype(jnp.bfloat16).astype(jnp.float32)
+        value = value - rounded
+        for half in range(2):
+            line = rounded[:, half * TILE : (half + 1) * TILE]
+            table = jnp.where(row == 2 * term + half, line, table)
+    out[pl.ds(TOTAL, EXTRA), :] = table.astype(jnp.bfloat16)
+
+
+def label(x, sums):
+    return pl.pallas_call(
+        label_kernel,
+        out_shape=shaped((TOTAL + EXTRA, TILE), jnp.bfloat16),
+        in_specs=[VMEM] * 5,
         out_specs=VMEM,
-        compiler_params=limit(2),
-        name="squares",
-    )(*shards)
-
-
-SHARD_Z = (0, -1, -2, -3, 1, 2, 3, 4)
+        compiler_params=limit(4),
+        name="label",
+    )(x, *sums)
+
+
+SHARD_Z = (0, 1, 2, 3, -1, -2, -3, 4)
 
 
 def product(normed, tiles, n):
@@ -271,10 +278,10 @@
     return total
 
 
-def project_kernel(place, s0, s1, s2, s3, gain, *refs):
+def project_kernel(place, gain, *refs):
     shards, weights = refs[:8], refs[8:18]
-    own_ref, kv_ref, parts, cache_ref = refs[18], refs[19], refs[20:23], refs[23]
-    held, tiles, normed, kv, own, sent, sems = refs[24:]
+    own_ref, parts, cache_ref = refs[18], refs[19:22], refs[22]
+    held, tiles, normed, kv, own, sent, sems = refs[23:]
     x, c, z, y = place[0], place[1], place[2], place[3]
     copies = fetch_all([(shard, held.at[i]) for i, shard in enumerate(shards)], sems)
     pairs = []
@@ -286,17 +293,21 @@
         pairs.append((far_a, tiles.at[base + 3, pl.ds(0, 3)]))
         pairs.append((far_b, tiles.at[base + 3, pl.ds(3, 3)]))
     fetched = fetch_all(pairs, sems, 8)
-    sums = s0[...] + s1[...] + s2[...] + s3[...]
-    scale = jnp.transpose(lax.rsqrt(sums / MODEL_WIDTH + EPSILON))[:, :1]
+    await_all(copies)
+    sums = functools.reduce(
+        jnp.add, [held[i, TOTAL:, :].astype(jnp.float32) for i in range(SHARDS)]
+    )
+    scale = lax.rsqrt((sums[0:2] + sums[2:4] + sums[4:6]) / MODEL_WIDTH + EPSILON)
+    scale = jnp.transpose(jnp.concatenate([scale] * 4, axis=0))
+    scale = jnp.concatenate([scale[:, 0:1], scale[:, 1:2]], axis=0)
     for i, dz in enumerate(SHARD_Z):
-        k = lax.rem(z + ZS + dz, ZS)
-        ahead = lax.rem(lax.div(k, CORES) + XS - x, XS)
-        order = jnp.where(ahead == 3, 1, jnp.where(ahead == 0, 0, ahead + 1))
+        k = lax.rem(z + ZS + (1 - 2 * lax.rem(z, 2)) * dz, ZS)
+        related = relation(x, lax.div(k, CORES))
+        order = jnp.where(related >= 2, 5 - related, related)
         position = order + 4 * lax.rem(k + c, CORES)
         cols = pl.ds(pl.multiple_of(position * TILE, TILE), TILE)
-        copies[i].wait()
         normed[:, cols] = (
-            held[i].astype(jnp.float32) * scale * gain[pl.ds(k * YS + y, 1), :]
+            held[i, :TOTAL, :].astype(jnp.float32) * scale * gain[pl.ds(k * YS + y, 1), :]
         ).astype(jnp.bfloat16)
     await_all(fetched)
     kv[...] = product(normed, tiles, 4)
@@ -304,7 +315,7 @@
     def slot(j):
         return kv.at[pl.ds(pl.multiple_of(j * ROWS, ROWS), ROWS)]
 
-    outgoing = fetch_all([(slot(y), kv_ref)], sems, 18)
+    outgoing = fetch_all([(slot(y), own_ref.at[pl.ds(TOTAL, ROWS)])], sems, 18)
     outgoing += fetch_all(
         [(tiles.at[p, 5], cache_ref.at[pl.ds(p * TILE, TILE)]) for p in range(SHARDS)], sems, 23
     )
@@ -314,21 +325,21 @@
         sent[r - 1, pl.ds(0, TOTAL), :] = product(normed, tiles, r).astype(jnp.bfloat16)
         outgoing += fetch_all([(sent.at[r - 1], parts[r - 1])], sems, 18 + r)
     own[...] = product(normed, tiles, 0)
-    outgoing += fetch_all([(own, own_ref)], sems, 22)
+    outgoing += fetch_all([(own, own_ref.at[pl.ds(0, TOTAL)])], sems, 22)
     await_all(outgoing)
 
 
-def project(place, sums, gain, shards, weights):
+def project(place, gain, shards, weights):
     f32, bf16 = jnp.float32, jnp.bfloat16
     return pl.pallas_call(
         project_kernel,
-        out_shape=[shaped((TOTAL, TILE), f32), shaped((ROWS, TILE), f32)]
+        out_shape=[shaped((TOTAL + ROWS, TILE), f32)]
         + [shaped((TOTAL + ROWS, TILE), bf16)] * 3
         + [shaped((PROMPT_TOKENS, TILE), bf16)],
-        in_specs=[SMEM] + [VMEM] * 5 + [ANY] * 18,
-        out_specs=[ANY] * 6,
+        in_specs=[SMEM, VMEM] + [ANY] * 18,
+        out_specs=[ANY] * 5,
         scratch_shapes=[
-            pltpu.VMEM((SHARDS, TOTAL, TILE), bf16),
+            pltpu.VMEM((SHARDS, TOTAL + EXTRA, TILE), bf16),
             pltpu.VMEM((SHARDS, 6, TILE, TILE), bf16),
             pltpu.VMEM((TOTAL, SHARDS * TILE), bf16),
             pltpu.VMEM((TOTAL, TILE), f32),
@@ -341,37 +352,30 @@
             flops=2 * TOTAL * 2048 * 1280, bytes_accessed=10 * 2**20, transcendentals=0
         ),
         name="project",
-    )(place, *sums, gain, *shards, *weights)
+    )(place, gain, *shards, *weights)
 
 
 def rotate(v, cosine, sine):
     return v * cosine + swap_halves(v) * sine
 
 
-def fresh_kernel(own_ref, p1, p2, p3, cosine, sine, out, held, own, sems):
-    copies = fetch_all(
-        [(p.at[pl.ds(TOTAL, ROWS)], held.at[i]) for i, p in enumerate((p1, p2, p3))], sems
-    )
-    await_all(fetch_all([(own_ref, own)], sems, 3))
+def fresh_kernel(own, p1, p2, p3, cosine, sine, out):
     v = own[...]
-    for i, copy in enumerate(copies):
-        copy.wait()
-        v = v + held[i].astype(jnp.float32)
+    for part in (p1, p2, p3):
+        v = v + part[...].astype(jnp.float32)
     out[:, :HEAD_SIZE] = rotate(v[:, :HEAD_SIZE], cosine[...], sine[...]).astype(jnp.bfloat16)
     out[:, HEAD_SIZE:] = v[:, HEAD_SIZE:].astype(jnp.bfloat16)
 
 
 def fresh_keys(own, parts, cosine, sine):
+    last = pl.BlockSpec((ROWS, TILE), lambda i: (OUT_DEV, 0))
+    table = pl.BlockSpec((ROWS, HEAD_SIZE), lambda i: (0, 0))
     return pl.pallas_call(
         fresh_kernel,
         out_shape=shaped((ROWS, TILE), jnp.bfloat16),
-        in_specs=[ANY] * 4 + [VMEM] * 2,
-        out_specs=VMEM,
-        scratch_shapes=[
-            pltpu.VMEM((3, ROWS, TILE), jnp.bfloat16),
-            pltpu.VMEM((ROWS, TILE), jnp.float32),
-            pltpu.SemaphoreType.DMA((4,)),
-        ],
+        grid=(1,),
+        in_specs=[last] * 4 + [table] * 2,
+        out_specs=pl.BlockSpec((ROWS, TILE), lambda i: (0, 0)),
         compiler_params=limit(4),
         name="fresh",
     )(own, *parts, cosine, sine)
@@ -380,20 +384,28 @@
 FACTOR = HEAD_SIZE**-0.5 * 1.4426950408889634
 
 
-def prompt_kernel(own_ref, p1, p2, p3, cosine, sine, *refs):
-    cache_ref, q_ref, mixed_ref, top_ref, total_ref = refs[:5]
-    held, caches, own, sems = refs[5:]
-    parts = fetch_all(
-        [(p.at[pl.ds(0, TOTAL)], held.at[i]) for i, p in enumerate((p1, p2, p3))], sems
-    )
-    kept = fetch_all([(cache_ref, caches), (own_ref, own)], sems, 3)
-    await_all(parts + kept)
-
+def stage_kernel(own_ref, cache_ref, own, cache, sems):
+    await_all(fetch_all([(own_ref, own), (cache_ref, cache)], sems))
+
+
+def stage(own, cache):
+    return pl.pallas_call(
+        stage_kernel,
+        out_shape=[shaped(own.shape, own.dtype), shaped(cache.shape, cache.dtype)],
+        in_specs=[ANY] * 2,
+        out_specs=[VMEM] * 2,
+        scratch_shapes=[pltpu.SemaphoreType.DMA((2,))],
+        compiler_params=limit(2),
+        name="stage",
+    )(own, cache)
+
+
+def prompt_kernel(own, p1, p2, p3, cosine, sine, caches, q_ref, mixed_ref, top_ref, total_ref):
     def step(j, _):
         rows = pl.ds(pl.multiple_of(j * ROWS, ROWS), ROWS)
         q = own[rows, :]
-        for i in range(3):
-            q = q + held[i, rows, :].astype(jnp.float32)
+        for part in (p1, p2, p3):
+            q = q + part[rows, :].astype(jnp.float32)
         halves = (q[:, :HEAD_SIZE], q[:, HEAD_SIZE:])
         wide_q = jnp.concatenate(
             [rotate(v, cosine[...], sine[...]).astype(jnp.bfloat16) for v in halves], axis=0
@@ -432,15 +444,9 @@
     return pl.pallas_call(
         prompt_kernel,
         out_shape=[shaped(per_slot, jnp.bfloat16)] + [shaped(per_slot, jnp.float32)] * 3,
-        in_specs=[ANY] * 4 + [VMEM] * 2 + [ANY],
+        in_specs=[VMEM] * 7,
         out_specs=[VMEM] * 4,
-        scratch_shapes=[
-            pltpu.VMEM((3, TOTAL, TILE), jnp.bfloat16),
-            pltpu.VMEM((PROMPT_TOKENS, TILE), jnp.bfloat16),
-            pltpu.VMEM((TOTAL, TILE), jnp.float32),
-            pltpu.SemaphoreType.DMA((5,)),
-        ],
-        compiler_params=limit(24),
+        compiler_params=limit(16),
         cost_estimate=pl.CostEstimate(
             flops=4 * 1024 * 2048 * 128, bytes_accessed=2 * 2**20, transcendentals=1024 * 2048
         ),
@@ -517,41 +523,41 @@
         prompt_key_cache,
         prompt_value_cache,
     )
-    slots = plan(place, keep_flag, destination, row_counts)
-
-    for d in (1, 3, 2):
-        pieces[d] = send_group(pieces[d], d, 0)
+    slots, pieces[0] = plan(place, keep_flag, destination, row_counts, pieces[0])
+
+    for r in (1, 3, 2):
+        pieces[r] = send_x(pieces[r], r)
     arrived = [send_y(part1, -1), send_y(part2, -2), send_y(part3, -3)]
     pieces, arrived = tie((pieces, arrived))
     inward, outward = sort_pieces(slots, pieces)
-    swapped, arrived = tie((swap(outward), arrived))
-    rows = unpack(slots, inward, swapped)
-
+    rows, sums = unpack(slots, inward, swap(outward))
+    sums = [sums] + [send_y(sums, r) for r in (1, 2, 3)]
+
+    rows = label(rows, sums)
+    rows, arrived = tie((rows, arrived))
+    a1, b1 = send_z(rows, 1), send_z(rows, -1)
     own = jnp.concatenate([own_parts[:1], jnp.stack(arrived), own_parts[1:]], axis=0)
-    f1, b1 = send_z(rows, 1), send_z(rows, -1)
-    left, right = send_group(own, 1, 0), send_group(own, -1, 0)
+    near, next_ = send_x(own, 1), send_x(own, -1)
     own_swapped = swap(own)
-    f1, b1, own_swapped = tie((f1, b1, own_swapped))
-    f2, b2 = send_z(f1, 1), send_z(b1, -1)
-    f2, b2, left, right = tie((f2, b2, left, right))
-    f3, b3 = send_z(f2, 1), send_z(b2, -1)
-    far_a, far_b = send_group(left[:3], 1, 0), send_group(right[3:], -1, 0)
-    left_swapped = swap(left)
-    f3, b3, left_swapped, right = tie((f3, b3, left_swapped, right))
-    far, right_swapped = send_z(f3, 1), swap(right)
-    far, right_swapped, far_a, far_b = tie((far, right_swapped, far_a, far_b))
-    shards = [rows, f1, f2, f3, b1, b2, b3, far]
-    sums = sum_squares(shards)
-    sums = [sums] + [send_y(sums, r) for r in (1, 2, 3)]
-    same_core = [own, left, right, far_a, far_b]
-    other_core = [own_swapped, left_swapped, right_swapped, swap(far_a), swap(far_b)]
-    weights = same_core + other_core
+    a1, b1, own_swapped = tie((a1, b1, own_swapped))
+    a2, b2 = send_z(b1, 1), send_z(a1, -1)
+    a2, b2, near, next_ = tie((a2, b2, near, next_))
+    a3, b3 = send_z(b2, 1), send_z(a2, -1)
+    far_a, far_b = send_x(next_[:3], 1), send_x(near[3:], -1)
+    near_swapped = swap(near)
+    a3, b3, far_a, far_b, near_swapped, next_ = tie((a3, b3, far_a, far_b, near_swapped, next_))
+    far, next_swapped = send_z(b3, 1), swap(next_)
+    far_a_swapped, far_b_swapped = swap(far_a), swap(far_b)
+    shards = [rows, a1, a2, a3, b1, b2, b3, far]
+    weights = [own, near, next_, far_a, far_b]
+    weights += [own_swapped, near_swapped, next_swapped, far_a_swapped, far_b_swapped]
     gain = norm_gain.astype(jnp.float32).reshape(ZS * YS, TILE)
-    q_own, kv_own, *parts, cache = project(place, sums, gain, shards, weights)
+    q_own, *parts, cache = project(place, gain, shards, weights)
 
     parts = [send_y(v, r) for r, v in zip((1, 2, 3), parts)]
+    q_own, cache = stage(q_own, cache)
     cosine, sine = rope_tables(ROWS, PROMPT_TOKENS)
-    fresh = fresh_keys(kv_own, parts, cosine, sine)
+    fresh = fresh_keys(q_own, parts, cosine, sine)
     fresh = [fresh] + [send_y(fresh, r) for r in (1, 2, 3)]
     prompt = attend_prompt(q_own, parts, cosine, sine, cache)
     return finish(place, slots, prompt, fresh)

time: 125 us -> 119 us (0.952)
  starting transfers between devices: 47.1 us -> 44.2 us
  local copies, waits for them, and re-layouts: 8.15 us -> 5.83 us
    ppermute x32, starting transfers between devices: 47.1 us -> 44.2 us  [the longest x12 18.7 us: send_y(): return lax.ppermute(v, 'fsdp', perm)]
    unnamed x62 -> x46, local copies, waits for them, and re-layouts: 6.5 us -> 5.13 us
    pallas_call x4 -> x5, Pallas kernels: 12.5 us -> 12.6 us  [the longest x1 8.3 us: project(): pl.pallas_call(project_kernel, out_shape=[shaped((TOTAL + ROWS, TILE), f3...]
  transfers between devices with their start and end apart: 32 -> 32, of which waited for: 14 -> 18; matrix products, arithmetic and copies ran while one was open for 2% -> 2% of each run, Pallas kernels for 7% -> 6%
where the time goes in v4:
time: 119 us; the launch traced here: 118 us
  starting transfers between devices  44.2 us (37%)
  waiting for transfers between devices  43.4 us (36%)
  Pallas kernels  23.3 us (20%)
  local copies, waits for them, and re-layouts  5.83 us (5%)
    ppermute x7, waiting for transfers between devices, send_z(): return lax.ppermute(v, 'fsdp', perm)  24.8 us
    ppermute x12, starting transfers between devices, send_y(): return lax.ppermute(v, 'fsdp', perm)  18.7 us
    ppermute x7, starting transfers between devices, send_z(): return lax.ppermute(v, 'fsdp', perm)  14.4 us
    ppermute x12, waiting for transfers between devices, send_y(): return lax.ppermute(v, 'fsdp', perm)  14.2 us
    ppermute x7, starting transfers between devices, send_x(): return lax.ppermute(v, 'group', perm)  10.2 us
    pallas_call x1, Pallas kernels, project(): pl.pallas_call(project_kernel, out_shape=[shaped((TOTAL + ROWS, TILE), f3...  8.3 us
    unnamed x46, local copies, waits for them, and re-layouts  5.13 us
    pallas_call x1, Pallas kernels, attend_prompt(): pl.pallas_call(prompt_kernel, out_shape=[shaped(per_slot, jnp.bfloat16)]...  4.47 us
  transfers between devices with their start and end apart: 32, of which 18 were waited for; matrix products, arithmetic and copies ran while one was open for 2% of the time, Pallas kernels for 6%

profile of v4, /device:TPU:8, one launch (start us, length us, event | category | flops | bytes accessed | tf_op | source)
XLA Modules:
  0.0 118.1 jit_solution(14014155139630477170)
XLA Ops:
  0.0 0.7 pad_add_fusion.place
  0.7 3.4 %pack.1 = (bf16[2,128,256]{2,1,0:T(8,128)(2,1)}, bf16[2,128,256]{2,1,0:T(8,128)(2,1)}, bf16[2,128,256]{2,1,0:T(8,128)(2,1)}, bf16[2,128,256]{2,1,0:T(8,128)(2,1)...) custom-call(s32[4]{0:T(128)} %pad_add_fusion.place, ...), custom_call_target="tpu_custom_call" | custom-call | tf_op jit(solution)/shard_map/pack/pallas_call | solution.py:133
  4.0 1.6 %collective-permute-start = (bf16[2,128,256]{2,1,0:T(8,128)(2,1)}, bf16[2,128,256]{2,1,0:T(8,128)(2,1)S(1)}, u32[]{:S(2)}, u32[]{:S(2)}) collective-permute-start(bf16[2,128,256]{2,1,0:T(8,128)(2,1)} %get-tuple-element.57), channel_id=1, source_target_pairs={{0,64},{32,96},{64,0},{96,32},{128,192},{160,224},{192,128},{224,1... | collective-permute-start | bytes 393224 | tf_op jit(solution)/shard_map/ppermute | solution.py:31
  5.6 2.7 %collective-permute-start.1 = (bf16[2,128,256]{2,1,0:T(8,128)(2,1)}, bf16[2,128,256]{2,1,0:T(8,128)(2,1)S(1)}, u32[]{:S(2)}, u32[]{:S(2)}) collective-permute-start(bf16[2,128,256]{2,1,0:T(8,128)(2,1)} %get-tuple-element.58), channel_id=1, source_target_pairs={{0,128},{32,160},{64,192},{96,224},{128,0},{160,32},{192,64},{224,... | collective-permute-start | bytes 393224 | tf_op jit(solution)/shard_map/ppermute | solution.py:31
  8.8 2.2 %collective-permute-start.3 = (bf16[256,256]{1,0:T(8,128)(2,1)}, bf16[256,256]{1,0:T(8,128)(2,1)S(1)}, u32[]{:S(2)}, u32[]{:S(2)}) collective-permute-start(bf16[256,256]{1,0:T(8,128)(2,1)} %get-tuple-element.60), channel_id=1, source_target_pairs={{0,3},{1,0},{2,1},{3,2},{4,7},{5,4},{6,5},{7,6},{8,11},{9,8},{10,9... | collective-permute-start | bytes 393224 | tf_op jit(solution)/shard_map/ppermute | solution.py:45
  11.0 0.9 collective-permute-start.4
  11.9 1.9 %collective-permute-start.5 = (bf16[256,256]{1,0:T(8,128)(2,1)}, bf16[256,256]{1,0:T(8,128)(2,1)S(1)}, u32[]{:S(2)}, u32[]{:S(2)}) collective-permute-start(bf16[256,256]{1,0:T(8,128)(2,1)} %get-tuple-element.62), channel_id=1, source_target_pairs={{0,1},{1,2},{2,3},{3,0},{4,5},{5,6},{6,7},{7,4},{8,9},{9,10},{10,1... | collective-permute-start | bytes 393224 | tf_op jit(solution)/shard_map/ppermute | solution.py:45
  13.8 0.9 copy-done.3
  14.7 2.8 %plan.1 = (s32[12]{0:T(128)S(1)}, bf16[2,128,256]{2,1,0:T(8,128)(2,1)S(1)}) custom-call(s32[4]{0:T(128)S(1)} %copy-done.4, s32[64]{0:T(128)S(1)} %copy-done.6, s32[64]{0:T(128)S(1)} %copy-done.7, s32[64]{0:T(128)S(1)} %copy-done.8, bf16[2,128,256]{2,1,0:T(8,128)(2,1)S(1)} %copy-done.3), custom_call_target="tpu_custom_call" | custom-call | tf_op jit(solution)/shard_map/plan/pallas_call | solution.py:172
  18.0 0.8 sort.1
  18.9 1.5 %collective-permute-done.6.swapped = bf16[512,256]{1,0:T(8,128)(2,1)S(1)} collective-permute-done((bf16[512,256]{1,0:T(8,128)(2,1)S(1)}, bf16[512,256]{1,0:T(8,128)(2,1)S(1)}, u32[]{:S(2)}, u32[]{:S(2)}) %collective-permute-start.6) | collective-permute-done | bytes 262176 | tf_op jit(solution)/shard_map/ppermute | solution.py:35
  20.5 1.1 unpack.1
  21.6 1.5 %collective-permute-start.7 = (f32[8,512]{1,0:T(8,128)S(1)}, f32[8,512]{1,0:T(8,128)S(1)}, u32[]{:S(2)}, u32[]{:S(2)}) collective-permute-start(f32[8,512]{1,0:T(8,128)S(1)} %get-tuple-element.70.s0), channel_id=1, source_target_pairs={{0,1},{1,2},{2,3},{3,0},{4,5},{5,6},{6,7},{7,4},{8,9},{9,10},{10,1... | collective-permute-start | bytes 49160 | tf_op jit(solution)/shard_map/ppermute | solution.py:45
  23.0 3.5 %collective-permute-start.8 = (f32[8,512]{1,0:T(8,128)S(1)}, f32[8,512]{1,0:T(8,128)S(1)}, u32[]{:S(2)}, u32[]{:S(2)}) collective-permute-start(f32[8,512]{1,0:T(8,128)S(1)} %get-tuple-element.70.s0), channel_id=1, source_target_pairs={{0,2},{1,3},{2,0},{3,1},{4,6},{5,7},{6,4},{7,5},{8,10},{9,11},{10,... | collective-permute-start | bytes 49160 | tf_op jit(solution)/shard_map/ppermute | solution.py:45
  26.6 0.9 slice_dynamic-update-slice_fusion.1
  27.5 0.8 collective-permute-done.8.s2
  28.3 2.0 %collective-permute-done.9.s3 = f32[8,512]{1,0:T(8,128)S(1)} collective-permute-done((f32[8,512]{1,0:T(8,128)S(1)}, f32[8,512]{1,0:T(8,128)S(1)}, u32[]{:S(2)}, u32[]{:S(2)}) %collective-permute-start.9) | collective-permute-done | bytes 16416 | tf_op jit(solution)/shard_map/ppermute | solution.py:45
  30.9 2.6 %collective-permute-start.16 = (bf16[6,256,256]{2,1,0:T(8,128)(2,1)S(1)}, bf16[6,256,256]{2,1,0:T(8,128)(2,1)S(1)}, u32[]{:S(2)}, u32[]{:S(2)}) collective-permute-start(bf16[6,256,256]{2,1,0:T(8,128)(2,1)S(1)} %slice_dynamic-update-slice_fusion.refs_8_), channel_id=1, source_target_pairs={{0,192},{32,224},{64,128},{96,160},{128,64},{160,96},{192,0},{224,... | collective-permute-start | bytes 2359304 | tf_op jit(solution)/shard_map/ppermute | solution.py:31
  33.5 1.9 %collective-permute-start.10 = (bf16[528,256]{1,0:T(8,128)(2,1)S(1)}, bf16[528,256]{1,0:T(8,128)(2,1)S(1)}, u32[]{:S(2)}, u32[]{:S(2)}) collective-permute-start(bf16[528,256]{1,0:T(8,128)(2,1)S(1)} %label.1.refs_0_), channel_id=1, source_target_pairs={{0,4},{1,5},{2,6},{3,7},{4,0},{5,1},{6,2},{7,3},{8,12},{9,13},{10,... | collective-permute-start | bytes 811016 | tf_op jit(solution)/shard_map/ppermute | solution.py:40
  35.4 4.9 %collective-permute-start.11 = (bf16[528,256]{1,0:T(8,128)(2,1)S(1)}, bf16[528,256]{1,0:T(8,128)(2,1)S(1)}, u32[]{:S(2)}, u32[]{:S(2)}) collective-permute-start(bf16[528,256]{1,0:T(8,128)(2,1)S(1)} %label.1.refs_0_), channel_id=1, source_target_pairs={{0,28},{1,29},{2,30},{3,31},{4,8},{5,9},{6,10},{7,11},{8,4},{9,5},... | collective-permute-start | bytes 811016 | tf_op jit(solution)/shard_map/ppermute | solution.py:40
  40.4 1.7 %collective-permute-done.10.refs_1_ = bf16[528,256]{1,0:T(8,128)(2,1)S(1)} collective-permute-done((bf16[528,256]{1,0:T(8,128)(2,1)S(1)}, bf16[528,256]{1,0:T(8,128)(2,1)S(1)}, u32[]{:S(2)}, u32[]{:S(2)}) %collective-permute-start.10) | collective-permute-done | bytes 270368 | tf_op jit(solution)/shard_map/ppermute | solution.py:40
  42.1 4.7 %collective-permute-done.11.refs_4_ = bf16[528,256]{1,0:T(8,128)(2,1)S(1)} collective-permute-done((bf16[528,256]{1,0:T(8,128)(2,1)S(1)}, bf16[528,256]{1,0:T(8,128)(2,1)S(1)}, u32[]{:S(2)}, u32[]{:S(2)}) %collective-permute-start.11) | collective-permute-done | bytes 270368 | tf_op jit(solution)/shard_map/ppermute | solution.py:40
  46.9 3.0 %collective-permute-start.14 = (bf16[528,256]{1,0:T(8,128)(2,1)S(1)}, bf16[528,256]{1,0:T(8,128)(2,1)S(1)}, u32[]{:S(2)}, u32[]{:S(2)}) collective-permute-start(bf16[528,256]{1,0:T(8,128)(2,1)S(1)} %collective-permute-done.10.refs_1_), channel_id=1, source_target_pairs={{0,28},{1,29},{2,30},{3,31},{4,8},{5,9},{6,10},{7,11},{8,4},{9,5},... | collective-permute-start | bytes 811016 | tf_op jit(solution)/shard_map/ppermute | solution.py:40
  50.5 1.2 %collective-permute-done.16.refs_10_ = bf16[6,256,256]{2,1,0:T(8,128)(2,1)S(1)} collective-permute-done((bf16[6,256,256]{2,1,0:T(8,128)(2,1)S(1)}, bf16[6,256,256]{2,1,0:T(8,128)(2,1)S(1)}, u32[]{:S(2)}, u32[]{:S(2)}) %collective-permute-start.16) | collective-permute-done | bytes 786464 | tf_op jit(solution)/shard_map/ppermute | solution.py:31
  51.7 2.7 %collective-permute-done.13.refs_2_ = bf16[528,256]{1,0:T(8,128)(2,1)S(1)} collective-permute-done((bf16[528,256]{1,0:T(8,128)(2,1)S(1)}, bf16[528,256]{1,0:T(8,128)(2,1)S(1)}, u32[]{:S(2)}, u32[]{:S(2)}) %collective-permute-start.13) | collective-permute-done | bytes 270368 | tf_op jit(solution)/shard_map/ppermute | solution.py:40
  54.4 1.3 %collective-permute-done.14.refs_5_ = bf16[528,256]{1,0:T(8,128)(2,1)S(1)} collective-permute-done((bf16[528,256]{1,0:T(8,128)(2,1)S(1)}, bf16[528,256]{1,0:T(8,128)(2,1)S(1)}, u32[]{:S(2)}, u32[]{:S(2)}) %collective-permute-start.14) | collective-permute-done | bytes 270368 | tf_op jit(solution)/shard_map/ppermute | solution.py:40
  55.9 1.2 %collective-permute-start.19 = (bf16[3,256,256]{2,1,0:T(8,128)(2,1)S(1)}, bf16[3,256,256]{2,1,0:T(8,128)(2,1)}, u32[]{:S(2)}, u32[]{:S(2)}) collective-permute-start(bf16[3,256,256]{2,1,0:T(8,128)(2,1)S(1)} %slice.14), channel_id=1, source_target_pairs={{0,64},{32,96},{64,0},{96,32},{128,192},{160,224},{192,128},{224,1... | collective-permute-start | bytes 1179656 | tf_op jit(solution)/shard_map/ppermute | solution.py:31
  57.2 1.2 %collective-permute-start.20 = (bf16[3,256,256]{2,1,0:T(8,128)(2,1)S(1)}, bf16[3,256,256]{2,1,0:T(8,128)(2,1)}, u32[]{:S(2)}, u32[]{:S(2)}) collective-permute-start(bf16[3,256,256]{2,1,0:T(8,128)(2,1)S(1)} %slice.15), channel_id=1, source_target_pairs={{0,192},{32,224},{64,128},{96,160},{128,64},{160,96},{192,0},{224,... | collective-permute-start | bytes 1179656 | tf_op jit(solution)/shard_map/ppermute | solution.py:31
  58.8 3.6 %collective-permute-start.18 = (bf16[528,256]{1,0:T(8,128)(2,1)S(1)}, bf16[528,256]{1,0:T(8,128)(2,1)}, u32[]{:S(2)}, u32[]{:S(2)}) collective-permute-start(bf16[528,256]{1,0:T(8,128)(2,1)S(1)} %collective-permute-done.13.refs_2_), channel_id=1, source_target_pairs={{0,28},{1,29},{2,30},{3,31},{4,8},{5,9},{6,10},{7,11},{8,4},{9,5},... | collective-permute-start | bytes 811016 | tf_op jit(solution)/shard_map/ppermute | solution.py:40
  62.4 4.3 %collective-permute-done.17.refs_3_ = bf16[528,256]{1,0:T(8,128)(2,1)S(1)} collective-permute-done((bf16[528,256]{1,0:T(8,128)(2,1)S(1)}, bf16[528,256]{1,0:T(8,128)(2,1)S(1)}, u32[]{:S(2)}, u32[]{:S(2)}) %collective-permute-start.17) | collective-permute-done | bytes 270368 | tf_op jit(solution)/shard_map/ppermute | solution.py:40
  66.7 2.1 %collective-permute-done.18.refs_6_ = bf16[528,256]{1,0:T(8,128)(2,1)} collective-permute-done((bf16[528,256]{1,0:T(8,128)(2,1)S(1)}, bf16[528,256]{1,0:T(8,128)(2,1)}, u32[]{:S(2)}, u32[]{:S(2)}) %collective-permute-start.18) | collective-permute-done | bytes 270368 | tf_op jit(solution)/shard_map/ppermute | solution.py:40
  68.8 0.9 collective-permute-done.20.refs_12_
  69.7 0.9 copy-done.15
  71.7 0.6 reshape.27.gain
  72.3 8.0 %collective-permute-done.22.refs_7_ = bf16[528,256]{1,0:T(8,128)(2,1)} collective-permute-done((bf16[528,256]{1,0:T(8,128)(2,1)}, bf16[528,256]{1,0:T(8,128)(2,1)}, u32[]{:S(2)}, u32[]{:S(2)}) %collective-permute-start.22) | collective-permute-done | bytes 270368 | tf_op jit(solution)/shard_map/ppermute | solution.py:40
  80.4 8.3 %project.1 = (f32[640,256]{1,0:T(8,128)}, bf16[640,256]{1,0:T(8,128)(2,1)}, bf16[640,256]{1,0:T(8,128)(2,1)}, bf16[640,256]{1,0:T(8,128)(2,1)}, bf16[2048,256]{1,0:T(8,128)(2,1)}) custom-call(s32[4]{0:T(128)} %pad_add_fusion.place, f32[32,256]{1,0:T(8,128)} %reshape.27.gain, bf16[528,256]{1,0:T(8,128)(2,1)} %copy-done.2, bf16[528,256]{1,0:T(8,128)(2,1)} %copy-done.16, ...), custom_call_target="tpu_custom_call" | custom-call | flops 2684354560 | bytes 10485760 | tf_op jit(solution)/shard_map/project/pallas_call | solution.py:334
  88.8 2.2 %collective-permute-start.27 = (bf16[640,256]{1,0:T(8,128)(2,1)}, bf16[640,256]{1,0:T(8,128)(2,1)S(1)}, u32[]{:S(2)}, u32[]{:S(2)}) collective-permute-start(bf16[640,256]{1,0:T(8,128)(2,1)} %get-tuple-element.96), channel_id=1, source_target_pairs={{0,2},{1,3},{2,0},{3,1},{4,6},{5,7},{6,4},{7,5},{8,10},{9,11},{10,... | collective-permute-start | bytes 983048 | tf_op jit(solution)/shard_map/ppermute | solution.py:45
  91.1 1.9 %collective-permute-start.28 = (bf16[640,256]{1,0:T(8,128)(2,1)}, bf16[640,256]{1,0:T(8,128)(2,1)S(1)}, u32[]{:S(2)}, u32[]{:S(2)}) collective-permute-start(bf16[640,256]{1,0:T(8,128)(2,1)} %get-tuple-element.97), channel_id=1, source_target_pairs={{0,3},{1,0},{2,1},{3,2},{4,7},{5,4},{6,5},{7,6},{8,11},{9,8},{10,9... | collective-permute-start | bytes 983048 | tf_op jit(solution)/shard_map/ppermute | solution.py:45
  93.4 1.2 %copy-done = bf16[2048,256]{1,0:T(8,128)(2,1)S(1)} copy-done((bf16[2048,256]{1,0:T(8,128)(2,1)S(1)}, bf16[2048,256]{1,0:T(8,128)(2,1)}, u32[]{:S(2)}) %copy-start) | copy-done | bytes 1048600
  94.6 1.1 copy-done.1
  96.0 3.7 %collective-permute-done.26.p1 = bf16[640,256]{1,0:T(8,128)(2,1)S(1)} collective-permute-done((bf16[640,256]{1,0:T(8,128)(2,1)}, bf16[640,256]{1,0:T(8,128)(2,1)S(1)}, u32[]{:S(2)}, u32[]{:S(2)}) %collective-permute-start.26) | collective-permute-done | bytes 327712 | tf_op jit(solution)/shard_map/ppermute | solution.py:45
  99.7 1.6 %collective-permute-done.27.p2 = bf16[640,256]{1,0:T(8,128)(2,1)S(1)} collective-permute-done((bf16[640,256]{1,0:T(8,128)(2,1)}, bf16[640,256]{1,0:T(8,128)(2,1)S(1)}, u32[]{:S(2)}, u32[]{:S(2)}) %collective-permute-start.27) | collective-permute-done | bytes 327712 | tf_op jit(solution)/shard_map/ppermute | solution.py:45
  101.3 5.6 %collective-permute-done.28.p3 = bf16[640,256]{1,0:T(8,128)(2,1)S(1)} collective-permute-done((bf16[640,256]{1,0:T(8,128)(2,1)}, bf16[640,256]{1,0:T(8,128)(2,1)S(1)}, u32[]{:S(2)}, u32[]{:S(2)}) %collective-permute-start.28) | collective-permute-done | bytes 327712 | tf_op jit(solution)/shard_map/ppermute | solution.py:45
  107.0 0.7 collective-permute-start.29
  107.7 2.0 %collective-permute-start.30 = (bf16[128,256]{1,0:T(8,128)(2,1)S(1)}, bf16[128,256]{1,0:T(8,128)(2,1)S(1)}, u32[]{:S(2)}, u32[]{:S(2)}) collective-permute-start(bf16[128,256]{1,0:T(8,128)(2,1)S(1)} %fresh.1.f0), channel_id=1, source_target_pairs={{0,2},{1,3},{2,0},{3,1},{4,6},{5,7},{6,4},{7,5},{8,10},{9,11},{10,... | collective-permute-start | bytes 196616 | tf_op jit(solution)/shard_map/ppermute | solution.py:45
  109.7 1.9 %collective-permute-start.31 = (bf16[128,256]{1,0:T(8,128)(2,1)S(1)}, bf16[128,256]{1,0:T(8,128)(2,1)S(1)}, u32[]{:S(2)}, u32[]{:S(2)}) collective-permute-start(bf16[128,256]{1,0:T(8,128)(2,1)S(1)} %fresh.1.f0), channel_id=1, source_target_pairs={{0,3},{1,0},{2,1},{3,2},{4,7},{5,4},{6,5},{7,6},{8,11},{9,8},{10,9... | collective-permute-start | bytes 196616 | tf_op jit(solution)/shard_map/ppermute | solution.py:45
  111.6 4.5 %prompt.1 = (bf16[4,256,128]{2,1,0:T(8,128)(2,1)S(1)}, f32[4,256,128]{2,1,0:T(8,128)S(1)}, f32[4,256,128]{2,1,0:T(8,128)S(1)}, f32[4,256,128]{2,1,0:T(8,128)S(1)}) custom-call(f32[640,256]{1,0:T(8,128)S(1)} %get-tuple-element.94.own, bf16[640,256]{1,0:T(8,128)(2,1)S(1)} %collective-permute-done.26.p1, bf16[640,256]{1,0:T(8,128)(2,1)S(1)} %collective-permute-done.27.p2, ...), custom_call_target="tpu_custom_call" | custom-call | flops 1073741824 | bytes 2097152 | tf_op jit(solution)/shard_map/prompt/pallas_call | solution.py:444
  116.1 2.0 %finish.1 = bf16[4,128,256]{2,1,0:T(8,128)(2,1)} custom-call(s32[4]{0:T(128)S(1)} %copy-done.5, s32[12]{0:T(128)S(1)} %get-tuple-element.55.source.slots, bf16[4,256,128]{2,1,0:T(8,128)(2,1)S(1)} %get-tuple-element.99.q, f32[4,256,128]{2,1,0:T(8,128)S(1)} %get-tuple-element.100.mixed_ref, f32[4,256,128]{2,1,0:T(8,128)S(1)} %get-tuple-element.101.top_ref, ...), custom_call_target="tpu_custom_call" | custom-call | tf_op jit(solution)/shard_map/finish/pallas_call | solution.py:487
  (81 shorter events, 5.0 us)
Async XLA Ops:
  0.7 13.1 %copy-start.4 = (s32[4]{0:T(128)S(1)}, s32[4]{0:T(128)}, u32[]{:S(2)}) copy-start(s32[4]{0:T(128)} %pad_add_fusion.place) | copy-start | bytes 52
  0.7 13.1 %copy-start.6 = (s32[64]{0:T(128)S(1)}, s32[64]{0:T(128)}, u32[]{:S(2)}) copy-start(s32[64]{0:T(128)} %keep.3) | copy-start | bytes 772
  0.7 13.1 %copy-start.7 = (s32[64]{0:T(128)S(1)}, s32[64]{0:T(128)}, u32[]{:S(2)}) copy-start(s32[64]{0:T(128)} %destination.3) | copy-start | bytes 772
  0.7 13.1 %copy-start.8 = (s32[64]{0:T(128)S(1)}, s32[64]{0:T(128)}, u32[]{:S(2)}) copy-start(s32[64]{0:T(128)} %counts.1) | copy-start | bytes 772
  4.0 7.8 %collective-permute-start = (bf16[2,128,256]{2,1,0:T(8,128)(2,1)}, bf16[2,128,256]{2,1,0:T(8,128)(2,1)S(1)}, u32[]{:S(2)}, u32[]{:S(2)}) collective-permute-start(bf16[2,128,256]{2,1,0:T(8,128)(2,1)} %get-tuple-element.57), channel_id=1, source_target_pairs={{0,64},{32,96},{64,0},{96,32},{128,192},{160,224},{192,128},{224,1... | collective-permute-start | bytes 393224 | tf_op jit(solution)/shard_map/ppermute | solution.py:31
  5.6 11.9 %collective-permute-start.1 = (bf16[2,128,256]{2,1,0:T(8,128)(2,1)}, bf16[2,128,256]{2,1,0:T(8,128)(2,1)S(1)}, u32[]{:S(2)}, u32[]{:S(2)}) collective-permute-start(bf16[2,128,256]{2,1,0:T(8,128)(2,1)} %get-tuple-element.58), channel_id=1, source_target_pairs={{0,128},{32,160},{64,192},{96,224},{128,0},{160,32},{192,64},{224,... | collective-permute-start | bytes 393224 | tf_op jit(solution)/shard_map/ppermute | solution.py:31
  8.3 9.2 %collective-permute-start.2 = (bf16[2,128,256]{2,1,0:T(8,128)(2,1)}, bf16[2,128,256]{2,1,0:T(8,128)(2,1)S(1)}, u32[]{:S(2)}, u32[]{:S(2)}) collective-permute-start(bf16[2,128,256]{2,1,0:T(8,128)(2,1)} %get-tuple-element.59), channel_id=1, source_target_pairs={{0,192},{32,224},{64,128},{96,160},{128,64},{160,96},{192,0},{224,... | collective-permute-start | bytes 393224 | tf_op jit(solution)/shard_map/ppermute | solution.py:31
  8.8 8.7 %collective-permute-start.3 = (bf16[256,256]{1,0:T(8,128)(2,1)}, bf16[256,256]{1,0:T(8,128)(2,1)S(1)}, u32[]{:S(2)}, u32[]{:S(2)}) collective-permute-start(bf16[256,256]{1,0:T(8,128)(2,1)} %get-tuple-element.60), channel_id=1, source_target_pairs={{0,3},{1,0},{2,1},{3,2},{4,7},{5,4},{6,5},{7,6},{8,11},{9,8},{10,9... | collective-permute-start | bytes 393224 | tf_op jit(solution)/shard_map/ppermute | solution.py:45
  11.0 6.7 %collective-permute-start.4 = (bf16[256,256]{1,0:T(8,128)(2,1)}, bf16[256,256]{1,0:T(8,128)(2,1)S(1)}, u32[]{:S(2)}, u32[]{:S(2)}) collective-permute-start(bf16[256,256]{1,0:T(8,128)(2,1)} %get-tuple-element.61), channel_id=1, source_target_pairs={{0,2},{1,3},{2,0},{3,1},{4,6},{5,7},{6,4},{7,5},{8,10},{9,11},{10,... | collective-permute-start | bytes 393224 | tf_op jit(solution)/shard_map/ppermute | solution.py:45
  11.9 6.2 %collective-permute-start.5 = (bf16[256,256]{1,0:T(8,128)(2,1)}, bf16[256,256]{1,0:T(8,128)(2,1)S(1)}, u32[]{:S(2)}, u32[]{:S(2)}) collective-permute-start(bf16[256,256]{1,0:T(8,128)(2,1)} %get-tuple-element.62), channel_id=1, source_target_pairs={{0,1},{1,2},{2,3},{3,0},{4,5},{5,6},{6,7},{7,4},{8,9},{9,10},{10,1... | collective-permute-start | bytes 393224 | tf_op jit(solution)/shard_map/ppermute | solution.py:45
  14.7 15.7 %copy-start.9 = (bf16[3,256,256]{2,1,0:T(8,128)(2,1)S(1)}, bf16[3,256,256]{2,1,0:T(8,128)(2,1)}, u32[]{:S(2)}) copy-start(bf16[3,256,256]{2,1,0:T(8,128)(2,1)} %get-tuple-element.75) | copy-start | bytes 1179652
  18.8 1.6 %collective-permute-start.6 = (bf16[512,256]{1,0:T(8,128)(2,1)S(1)}, bf16[512,256]{1,0:T(8,128)(2,1)S(1)}, u32[]{:S(2)}, u32[]{:S(2)}) collective-permute-start(bf16[512,256]{1,0:T(8,128)(2,1)S(1)} %get-tuple-element.68), channel_id=1, source_target_pairs={{0,32},{32,0},{64,96},{96,64},{128,160},{160,128},{192,224},{224,1... | collective-permute-start | bytes 786440 | tf_op jit(solution)/shard_map/ppermute | solution.py:35
  20.5 51.2 %copy-start.13 = (bf16[8192]{0:T(1024)(128)(2,1)S(1)}, bf16[8192]{0:T(1024)(128)(2,1)}, u32[]{:S(2)}) copy-start(bf16[8192]{0:T(1024)(128)(2,1)} %param.11) | copy-start | bytes 49156
  21.6 5.9 %collective-permute-start.7 = (f32[8,512]{1,0:T(8,128)S(1)}, f32[8,512]{1,0:T(8,128)S(1)}, u32[]{:S(2)}, u32[]{:S(2)}) collective-permute-start(f32[8,512]{1,0:T(8,128)S(1)} %get-tuple-element.70.s0), channel_id=1, source_target_pairs={{0,1},{1,2},{2,3},{3,0},{4,5},{5,6},{6,7},{7,4},{8,9},{9,10},{10,1... | collective-permute-start | bytes 49160 | tf_op jit(solution)/shard_map/ppermute | solution.py:45
  23.0 5.2 %collective-permute-start.8 = (f32[8,512]{1,0:T(8,128)S(1)}, f32[8,512]{1,0:T(8,128)S(1)}, u32[]{:S(2)}, u32[]{:S(2)}) collective-permute-start(f32[8,512]{1,0:T(8,128)S(1)} %get-tuple-element.70.s0), channel_id=1, source_target_pairs={{0,2},{1,3},{2,0},{3,1},{4,6},{5,7},{6,4},{7,5},{8,10},{9,11},{10,... | collective-permute-start | bytes 49160 | tf_op jit(solution)/shard_map/ppermute | solution.py:45
  26.6 3.7 %collective-permute-start.9 = (f32[8,512]{1,0:T(8,128)S(1)}, f32[8,512]{1,0:T(8,128)S(1)}, u32[]{:S(2)}, u32[]{:S(2)}) collective-permute-start(f32[8,512]{1,0:T(8,128)S(1)} %get-tuple-element.70.s0), channel_id=1, source_target_pairs={{0,3},{1,0},{2,1},{3,2},{4,7},{5,4},{6,5},{7,6},{8,11},{9,8},{10,9... | collective-permute-start | bytes 49160 | tf_op jit(solution)/shard_map/ppermute | solution.py:45
  30.3 50.0 %copy-start.2 = (bf16[528,256]{1,0:T(8,128)(2,1)}, bf16[528,256]{1,0:T(8,128)(2,1)S(1)}, u32[]{:S(2)}) copy-start(bf16[528,256]{1,0:T(8,128)(2,1)S(1)} %label.1.refs_0_) | copy-start | bytes 811012
  30.4 49.9 %copy-start.12 = (bf16[6,256,256]{2,1,0:T(8,128)(2,1)}, bf16[6,256,256]{2,1,0:T(8,128)(2,1)S(1)}, u32[]{:S(2)}) copy-start(bf16[6,256,256]{2,1,0:T(8,128)(2,1)S(1)} %slice_dynamic-update-slice_fusion.refs_8_) | copy-start | bytes 2359300
  30.5 16.3 %collective-permute-start.12 = (bf16[6,256,256]{2,1,0:T(8,128)(2,1)S(1)}, bf16[6,256,256]{2,1,0:T(8,128)(2,1)S(1)}, u32[]{:S(2)}, u32[]{:S(2)}) collective-permute-start(bf16[6,256,256]{2,1,0:T(8,128)(2,1)S(1)} %slice_dynamic-update-slice_fusion.refs_8_), channel_id=1, source_target_pairs={{0,32},{32,0},{64,96},{96,64},{128,160},{160,128},{192,224},{224,1... | collective-permute-start | bytes 2359304 | tf_op jit(solution)/shard_map/ppermute | solution.py:35
  30.6 20.0 %collective-permute-start.15 = (bf16[6,256,256]{2,1,0:T(8,128)(2,1)S(1)}, bf16[6,256,256]{2,1,0:T(8,128)(2,1)S(1)}, u32[]{:S(2)}, u32[]{:S(2)}) collective-permute-start(bf16[6,256,256]{2,1,0:T(8,128)(2,1)S(1)} %slice_dynamic-update-slice_fusion.refs_8_), channel_id=1, source_target_pairs={{0,64},{32,96},{64,0},{96,32},{128,192},{160,224},{192,128},{224,1... | collective-permute-start | bytes 2359304 | tf_op jit(solution)/shard_map/ppermute | solution.py:31
  30.9 20.8 %collective-permute-start.16 = (bf16[6,256,256]{2,1,0:T(8,128)(2,1)S(1)}, bf16[6,256,256]{2,1,0:T(8,128)(2,1)S(1)}, u32[]{:S(2)}, u32[]{:S(2)}) collective-permute-start(bf16[6,256,256]{2,1,0:T(8,128)(2,1)S(1)} %slice_dynamic-update-slice_fusion.refs_8_), channel_id=1, source_target_pairs={{0,192},{32,224},{64,128},{96,160},{128,64},{160,96},{192,0},{224,... | collective-permute-start | bytes 2359304 | tf_op jit(solution)/shard_map/ppermute | solution.py:31
  33.5 8.6 %collective-permute-start.10 = (bf16[528,256]{1,0:T(8,128)(2,1)S(1)}, bf16[528,256]{1,0:T(8,128)(2,1)S(1)}, u32[]{:S(2)}, u32[]{:S(2)}) collective-permute-start(bf16[528,256]{1,0:T(8,128)(2,1)S(1)} %label.1.refs_0_), channel_id=1, source_target_pairs={{0,4},{1,5},{2,6},{3,7},{4,0},{5,1},{6,2},{7,3},{8,12},{9,13},{10,... | collective-permute-start | bytes 811016 | tf_op jit(solution)/shard_map/ppermute | solution.py:40
  35.4 11.3 %collective-permute-start.11 = (bf16[528,256]{1,0:T(8,128)(2,1)S(1)}, bf16[528,256]{1,0:T(8,128)(2,1)S(1)}, u32[]{:S(2)}, u32[]{:S(2)}) collective-permute-start(bf16[528,256]{1,0:T(8,128)(2,1)S(1)} %label.1.refs_0_), channel_id=1, source_target_pairs={{0,28},{1,29},{2,30},{3,31},{4,8},{5,9},{6,10},{7,11},{8,4},{9,5},... | collective-permute-start | bytes 811016 | tf_op jit(solution)/shard_map/ppermute | solution.py:40
  42.1 13.6 %copy-start.16 = (bf16[528,256]{1,0:T(8,128)(2,1)}, bf16[528,256]{1,0:T(8,128)(2,1)S(1)}, u32[]{:S(2)}) copy-start(bf16[528,256]{1,0:T(8,128)(2,1)S(1)} %collective-permute-done.10.refs_1_) | copy-start | bytes 811012
  46.8 9.0 %copy-start.17 = (bf16[528,256]{1,0:T(8,128)(2,1)}, bf16[528,256]{1,0:T(8,128)(2,1)S(1)}, u32[]{:S(2)}) copy-start(bf16[528,256]{1,0:T(8,128)(2,1)S(1)} %collective-permute-done.11.refs_4_) | copy-start | bytes 811012
  46.8 33.6 %copy-start.14 = (bf16[6,256,256]{2,1,0:T(8,128)(2,1)}, bf16[6,256,256]{2,1,0:T(8,128)(2,1)S(1)}, u32[]{:S(2)}) copy-start(bf16[6,256,256]{2,1,0:T(8,128)(2,1)S(1)} %collective-permute-done.12.refs_13_) | copy-start | bytes 2359300
  46.8 7.7 %collective-permute-start.13 = (bf16[528,256]{1,0:T(8,128)(2,1)S(1)}, bf16[528,256]{1,0:T(8,128)(2,1)S(1)}, u32[]{:S(2)}, u32[]{:S(2)}) collective-permute-start(bf16[528,256]{1,0:T(8,128)(2,1)S(1)} %collective-permute-done.11.refs_4_), channel_id=1, source_target_pairs={{0,4},{1,5},{2,6},{3,7},{4,0},{5,1},{6,2},{7,3},{8,12},{9,13},{10,... | collective-permute-start | bytes 811016 | tf_op jit(solution)/shard_map/ppermute | solution.py:40
  46.9 8.9 %collective-permute-start.14 = (bf16[528,256]{1,0:T(8,128)(2,1)S(1)}, bf16[528,256]{1,0:T(8,128)(2,1)S(1)}, u32[]{:S(2)}, u32[]{:S(2)}) collective-permute-start(bf16[528,256]{1,0:T(8,128)(2,1)S(1)} %collective-permute-done.10.refs_1_), channel_id=1, source_target_pairs={{0,28},{1,29},{2,30},{3,31},{4,8},{5,9},{6,10},{7,11},{8,4},{9,5},... | collective-permute-start | bytes 811016 | tf_op jit(solution)/shard_map/ppermute | solution.py:40
  50.5 29.9 %copy-start.10 = (bf16[6,256,256]{2,1,0:T(8,128)(2,1)}, bf16[6,256,256]{2,1,0:T(8,128)(2,1)S(1)}, u32[]{:S(2)}) copy-start(bf16[6,256,256]{2,1,0:T(8,128)(2,1)S(1)} %collective-permute-done.15.refs_9_) | copy-start | bytes 2359300
  51.7 28.7 %copy-start.11 = (bf16[6,256,256]{2,1,0:T(8,128)(2,1)}, bf16[6,256,256]{2,1,0:T(8,128)(2,1)S(1)}, u32[]{:S(2)}) copy-start(bf16[6,256,256]{2,1,0:T(8,128)(2,1)S(1)} %collective-permute-done.16.refs_10_) | copy-start | bytes 2359300
  54.4 16.2 %copy-start.18 = (bf16[528,256]{1,0:T(8,128)(2,1)}, bf16[528,256]{1,0:T(8,128)(2,1)S(1)}, u32[]{:S(2)}) copy-start(bf16[528,256]{1,0:T(8,128)(2,1)S(1)} %collective-permute-done.13.refs_2_) | copy-start | bytes 811012
  55.7 15.4 %copy-start.19 = (bf16[528,256]{1,0:T(8,128)(2,1)}, bf16[528,256]{1,0:T(8,128)(2,1)S(1)}, u32[]{:S(2)}) copy-start(bf16[528,256]{1,0:T(8,128)(2,1)S(1)} %collective-permute-done.14.refs_5_) | copy-start | bytes 811012
  55.7 14.0 %collective-permute-start.21 = (bf16[6,256,256]{2,1,0:T(8,128)(2,1)S(1)}, bf16[6,256,256]{2,1,0:T(8,128)(2,1)S(1)}, u32[]{:S(2)}, u32[]{:S(2)}) collective-permute-start(bf16[6,256,256]{2,1,0:T(8,128)(2,1)S(1)} %collective-permute-done.15.refs_9_), channel_id=1, source_target_pairs={{0,32},{32,0},{64,96},{96,64},{128,160},{160,128},{192,224},{224,1... | collective-permute-start | bytes 2359304 | tf_op jit(solution)/shard_map/ppermute | solution.py:35
  55.9 12.9 %collective-permute-start.19 = (bf16[3,256,256]{2,1,0:T(8,128)(2,1)S(1)}, bf16[3,256,256]{2,1,0:T(8,128)(2,1)}, u32[]{:S(2)}, u32[]{:S(2)}) collective-permute-start(bf16[3,256,256]{2,1,0:T(8,128)(2,1)S(1)} %slice.14), channel_id=1, source_target_pairs={{0,64},{32,96},{64,0},{96,32},{128,192},{160,224},{192,128},{224,1... | collective-permute-start | bytes 1179656 | tf_op jit(solution)/shard_map/ppermute | solution.py:31
  57.2 12.5 %collective-permute-start.20 = (bf16[3,256,256]{2,1,0:T(8,128)(2,1)S(1)}, bf16[3,256,256]{2,1,0:T(8,128)(2,1)}, u32[]{:S(2)}, u32[]{:S(2)}) collective-permute-start(bf16[3,256,256]{2,1,0:T(8,128)(2,1)S(1)} %slice.15), channel_id=1, source_target_pairs={{0,192},{32,224},{64,128},{96,160},{128,64},{160,96},{192,0},{224,... | collective-permute-start | bytes 1179656 | tf_op jit(solution)/shard_map/ppermute | solution.py:31
  58.4 8.3 %collective-permute-start.17 = (bf16[528,256]{1,0:T(8,128)(2,1)S(1)}, bf16[528,256]{1,0:T(8,128)(2,1)S(1)}, u32[]{:S(2)}, u32[]{:S(2)}) collective-permute-start(bf16[528,256]{1,0:T(8,128)(2,1)S(1)} %collective-permute-done.14.refs_5_), channel_id=1, source_target_pairs={{0,4},{1,5},{2,6},{3,7},{4,0},{5,1},{6,2},{7,3},{8,12},{9,13},{10,... | collective-permute-start | bytes 811016 | tf_op jit(solution)/shard_map/ppermute | solution.py:40
  58.8 10.0 %collective-permute-start.18 = (bf16[528,256]{1,0:T(8,128)(2,1)S(1)}, bf16[528,256]{1,0:T(8,128)(2,1)}, u32[]{:S(2)}, u32[]{:S(2)}) collective-permute-start(bf16[528,256]{1,0:T(8,128)(2,1)S(1)} %collective-permute-done.13.refs_2_), channel_id=1, source_target_pairs={{0,28},{1,29},{2,30},{3,31},{4,8},{5,9},{6,10},{7,11},{8,4},{9,5},... | collective-permute-start | bytes 811016 | tf_op jit(solution)/shard_map/ppermute | solution.py:40
  70.6 9.8 %collective-permute-start.23 = (bf16[6,256,256]{2,1,0:T(8,128)(2,1)S(1)}, bf16[6,256,256]{2,1,0:T(8,128)(2,1)}, u32[]{:S(2)}, u32[]{:S(2)}) collective-permute-start(bf16[6,256,256]{2,1,0:T(8,128)(2,1)S(1)} %collective-permute-done.16.refs_10_), channel_id=1, source_target_pairs={{0,32},{32,0},{64,96},{96,64},{128,160},{160,128},{192,224},{224,1... | collective-permute-start | bytes 2359304 | tf_op jit(solution)/shard_map/ppermute | solution.py:35
  70.6 9.7 %collective-permute-start.24 = (bf16[3,256,256]{2,1,0:T(8,128)(2,1)}, bf16[3,256,256]{2,1,0:T(8,128)(2,1)}, u32[]{:S(2)}, u32[]{:S(2)}) collective-permute-start(bf16[3,256,256]{2,1,0:T(8,128)(2,1)} %collective-permute-done.19.refs_11_), channel_id=1, source_target_pairs={{0,32},{32,0},{64,96},{96,64},{128,160},{160,128},{192,224},{224,1... | collective-permute-start | bytes 1179656 | tf_op jit(solution)/shard_map/ppermute | solution.py:35
  71.1 9.2 %collective-permute-start.25 = (bf16[3,256,256]{2,1,0:T(8,128)(2,1)}, bf16[3,256,256]{2,1,0:T(8,128)(2,1)}, u32[]{:S(2)}, u32[]{:S(2)}) collective-permute-start(bf16[3,256,256]{2,1,0:T(8,128)(2,1)} %collective-permute-done.20.refs_12_), channel_id=1, source_target_pairs={{0,32},{32,0},{64,96},{96,64},{128,160},{160,128},{192,224},{224,1... | collective-permute-start | bytes 1179656 | tf_op jit(solution)/shard_map/ppermute | solution.py:35
  71.2 9.1 %collective-permute-start.22 = (bf16[528,256]{1,0:T(8,128)(2,1)}, bf16[528,256]{1,0:T(8,128)(2,1)}, u32[]{:S(2)}, u32[]{:S(2)}) collective-permute-start(bf16[528,256]{1,0:T(8,128)(2,1)} %collective-permute-done.18.refs_6_), channel_id=1, source_target_pairs={{0,4},{1,5},{2,6},{3,7},{4,0},{5,1},{6,2},{7,3},{8,12},{9,13},{10,... | collective-permute-start | bytes 811016 | tf_op jit(solution)/shard_map/ppermute | solution.py:40
  88.7 10.9 %collective-permute-start.26 = (bf16[640,256]{1,0:T(8,128)(2,1)}, bf16[640,256]{1,0:T(8,128)(2,1)S(1)}, u32[]{:S(2)}, u32[]{:S(2)}) collective-permute-start(bf16[640,256]{1,0:T(8,128)(2,1)} %get-tuple-element.95), channel_id=1, source_target_pairs={{0,1},{1,2},{2,3},{3,0},{4,5},{5,6},{6,7},{7,4},{8,9},{9,10},{10,1... | collective-permute-start | bytes 983048 | tf_op jit(solution)/shard_map/ppermute | solution.py:45
  88.8 12.5 %collective-permute-start.27 = (bf16[640,256]{1,0:T(8,128)(2,1)}, bf16[640,256]{1,0:T(8,128)(2,1)S(1)}, u32[]{:S(2)}, u32[]{:S(2)}) collective-permute-start(bf16[640,256]{1,0:T(8,128)(2,1)} %get-tuple-element.96), channel_id=1, source_target_pairs={{0,2},{1,3},{2,0},{3,1},{4,6},{5,7},{6,4},{7,5},{8,10},{9,11},{10,... | collective-permute-start | bytes 983048 | tf_op jit(solution)/shard_map/ppermute | solution.py:45
  91.1 15.8 %collective-permute-start.28 = (bf16[640,256]{1,0:T(8,128)(2,1)}, bf16[640,256]{1,0:T(8,128)(2,1)S(1)}, u32[]{:S(2)}, u32[]{:S(2)}) collective-permute-start(bf16[640,256]{1,0:T(8,128)(2,1)} %get-tuple-element.97), channel_id=1, source_target_pairs={{0,3},{1,0},{2,1},{3,2},{4,7},{5,4},{6,5},{7,6},{8,11},{9,8},{10,9... | collective-permute-start | bytes 983048 | tf_op jit(solution)/shard_map/ppermute | solution.py:45
  107.0 9.1 %copy-start.5 = (s32[4]{0:T(128)S(1)}, s32[4]{0:T(128)}, u32[]{:S(2)}) copy-start(s32[4]{0:T(128)} %pad_add_fusion.place) | copy-start | bytes 52
  107.0 9.1 %collective-permute-start.29 = (bf16[128,256]{1,0:T(8,128)(2,1)S(1)}, bf16[128,256]{1,0:T(8,128)(2,1)S(1)}, u32[]{:S(2)}, u32[]{:S(2)}) collective-permute-start(bf16[128,256]{1,0:T(8,128)(2,1)S(1)} %fresh.1.f0), channel_id=1, source_target_pairs={{0,1},{1,2},{2,3},{3,0},{4,5},{5,6},{6,7},{7,4},{8,9},{9,10},{10,1... | collective-permute-start | bytes 196616 | tf_op jit(solution)/shard_map/ppermute | solution.py:45
  107.7 8.4 %collective-permute-start.30 = (bf16[128,256]{1,0:T(8,128)(2,1)S(1)}, bf16[128,256]{1,0:T(8,128)(2,1)S(1)}, u32[]{:S(2)}, u32[]{:S(2)}) collective-permute-start(bf16[128,256]{1,0:T(8,128)(2,1)S(1)} %fresh.1.f0), channel_id=1, source_target_pairs={{0,2},{1,3},{2,0},{3,1},{4,6},{5,7},{6,4},{7,5},{8,10},{9,11},{10,... | collective-permute-start | bytes 196616 | tf_op jit(solution)/shard_map/ppermute | solution.py:45
  109.7 6.4 %collective-permute-start.31 = (bf16[128,256]{1,0:T(8,128)(2,1)S(1)}, bf16[128,256]{1,0:T(8,128)(2,1)S(1)}, u32[]{:S(2)}, u32[]{:S(2)}) collective-permute-start(bf16[128,256]{1,0:T(8,128)(2,1)S(1)} %fresh.1.f0), channel_id=1, source_target_pairs={{0,3},{1,0},{2,1},{3,2},{4,7},{5,4},{6,5},{7,6},{8,11},{9,8},{10,9... | collective-permute-start | bytes 196616 | tf_op jit(solution)/shard_map/ppermute | solution.py:45
  (5 other events, 8.7 us)

commit v5 on v4

--- a/solution.py
+++ b/solution.py
@@ -96,10 +96,11 @@
         copy.wait()
 
 
-def pack_kernel(place, keep, destination, hidden, wq, wk, wv, kc, vc, *rest):
+def pack_kernel(keep, destination, hidden, wq, wk, wv, kc, vc, *rest):
     outs, parts, own, chosen, sems = rest[0:4], rest[4:7], rest[7], rest[8], rest[9]
-    x, c, z, y = place[0], place[1], place[2], place[3]
-    first = (x * CORES + c) * IN_DEV
+    g, f = lax.axis_index("group"), lax.axis_index("fsdp")
+    x, c, z, y = lax.div(g, CORES), lax.rem(g, CORES), lax.div(f, YS), lax.rem(f, YS)
+    first = g * IN_DEV
     cols = pl.ds(pl.multiple_of(z * HEAD_SIZE, HEAD_SIZE), HEAD_SIZE)
     rows = pl.ds(pl.multiple_of(y * TILE, TILE), TILE)
     pairs = []
@@ -128,19 +129,19 @@
     await_all(copies + fetch_all(pairs, sems, 8))
 
 
-def pack(place, keep, destination, *arrays):
+def pack(keep, destination, *arrays):
     bf16 = jnp.bfloat16
     return pl.pallas_call(
         pack_kernel,
         out_shape=[shaped((CORES, ROWS, TILE), bf16)] * 4
         + [shaped((TILE, TILE), bf16)] * 3
         + [shaped((3, TILE, TILE), bf16)],
-        in_specs=[SMEM] * 3 + [ANY] * 6,
+        in_specs=[SMEM] * 2 + [ANY] * 6,
         out_specs=[VMEM] * 8,
         scratch_shapes=[pltpu.SMEM((8,), jnp.int32), pltpu.SemaphoreType.DMA((16,))],
         compiler_params=limit(56),
         name="pack",
-    )(place, keep, destination, *arrays)
+    )(keep, destination, *arrays)
 
 
 def plan_kernel(place, keep, destination, counts, piece, out, held):
@@ -513,7 +514,6 @@
     tie = lax.optimization_barrier
 
     *pieces, part1, part2, part3, own_parts = pack(
-        place,
         keep_flag,
         destination,
         hidden,
@@ -523,10 +523,11 @@
         prompt_key_cache,
         prompt_value_cache,
     )
-    slots, pieces[0] = plan(place, keep_flag, destination, row_counts, pieces[0])
 
     for r in (1, 3, 2):
         pieces[r] = send_x(pieces[r], r)
+    pieces[0], pieces[1] = tie((pieces[0], pieces[1]))
+    slots, pieces[0] = plan(place, keep_flag, destination, row_counts, pieces[0])
     arrived = [send_y(part1, -1), send_y(part2, -2), send_y(part3, -3)]
     pieces, arrived = tie((pieces, arrived))
     inward, outward = sort_pieces(slots, pieces)
@@ -534,19 +535,17 @@
     sums = [sums] + [send_y(sums, r) for r in (1, 2, 3)]
 
     rows = label(rows, sums)
-    rows, arrived = tie((rows, arrived))
-    a1, b1 = send_z(rows, 1), send_z(rows, -1)
     own = jnp.concatenate([own_parts[:1], jnp.stack(arrived), own_parts[1:]], axis=0)
     near, next_ = send_x(own, 1), send_x(own, -1)
-    own_swapped = swap(own)
+    rows, own = tie((rows, own))
+    a1, b1, own_swapped = send_z(rows, 1), send_z(rows, -1), swap(own)
     a1, b1, own_swapped = tie((a1, b1, own_swapped))
     a2, b2 = send_z(b1, 1), send_z(a1, -1)
     a2, b2, near, next_ = tie((a2, b2, near, next_))
     a3, b3 = send_z(b2, 1), send_z(a2, -1)
     far_a, far_b = send_x(next_[:3], 1), send_x(near[3:], -1)
-    near_swapped = swap(near)
-    a3, b3, far_a, far_b, near_swapped, next_ = tie((a3, b3, far_a, far_b, near_swapped, next_))
-    far, next_swapped = send_z(b3, 1), swap(next_)
+    a3, b3, far_a, far_b, near, next_ = tie((a3, b3, far_a, far_b, near, next_))
+    far, near_swapped, next_swapped = send_z(b3, 1), swap(near), swap(next_)
     far_a_swapped, far_b_swapped = swap(far_a), swap(far_b)
     shards = [rows, a1, a2, a3, b1, b2, b3, far]
     weights = [own, near, next_, far_a, far_b]

time: 119 us -> 115 us (0.966)
  waiting for transfers between devices: 43.4 us -> 41.3 us
    unnamed x46 -> x44, local copies, waits for them, and re-layouts: 5.13 us -> 4.22 us
  transfers between devices with their start and end apart: 32 -> 32, of which waited for: 18 -> 15; matrix products, arithmetic and copies ran while one was open for 2% -> 2% of each run, Pallas kernels for 6% -> 7%
where the time goes in v5:
time: 115 us; the launch traced here: 114 us
  starting transfers between devices  43.7 us (38%)
  waiting for transfers between devices  41.3 us (36%)
  Pallas kernels  23.3 us (20%)
  local copies, waits for them, and re-layouts  4.91 us (4%)
    ppermute x7, waiting for transfers between devices, send_z(): return lax.ppermute(v, 'fsdp', perm)  23.8 us
    ppermute x12, starting transfers between devices, send_y(): return lax.ppermute(v, 'fsdp', perm)  18.1 us
    ppermute x12, waiting for transfers between devices, send_y(): return lax.ppermute(v, 'fsdp', perm)  14.3 us
    ppermute x7, starting transfers between devices, send_z(): return lax.ppermute(v, 'fsdp', perm)  14 us
    ppermute x7, starting transfers between devices, send_x(): return lax.ppermute(v, 'group', perm)  10.3 us
    pallas_call x1, Pallas kernels, project(): pl.pallas_call(project_kernel, out_shape=[shaped((TOTAL + ROWS, TILE), f3...  8.31 us
    pallas_call x1, Pallas kernels, attend_prompt(): pl.pallas_call(prompt_kernel, out_shape=[shaped(per_slot, jnp.bfloat16)]...  4.47 us
    unnamed x44, local copies, waits for them, and re-layouts  4.22 us
  transfers between devices with their start and end apart: 32, of which 15 were waited for; matrix products, arithmetic and copies ran while one was open for 2% of the time, Pallas kernels for 7%

profile of v5, /device:TPU:8, one launch (start us, length us, event | category | flops | bytes accessed | tf_op | source)
XLA Modules:
  0.0 114.2 jit_solution(2614440176781426526)
XLA Ops:
  0.0 3.4 %pack.1 = (bf16[2,128,256]{2,1,0:T(8,128)(2,1)}, bf16[2,128,256]{2,1,0:T(8,128)(2,1)}, bf16[2,128,256]{2,1,0:T(8,128)(2,1)}, bf16[2,128,256]{2,1,0:T(8,128)(2,1)...) custom-call(s32[64]{0:T(128)} %keep.3, ...), custom_call_target="tpu_custom_call" | custom-call | tf_op jit(solution)/shard_map/pack/pallas_call | solution.py:134
  3.4 1.6 %collective-permute-start = (bf16[2,128,256]{2,1,0:T(8,128)(2,1)}, bf16[2,128,256]{2,1,0:T(8,128)(2,1)S(1)}, u32[]{:S(2)}, u32[]{:S(2)}) collective-permute-start(bf16[2,128,256]{2,1,0:T(8,128)(2,1)} %get-tuple-element.55), channel_id=1, source_target_pairs={{0,64},{32,96},{64,0},{96,32},{128,192},{160,224},{192,128},{224,1... | collective-permute-start | bytes 393224 | tf_op jit(solution)/shard_map/ppermute | solution.py:31
  5.0 2.7 %collective-permute-start.1 = (bf16[2,128,256]{2,1,0:T(8,128)(2,1)}, bf16[2,128,256]{2,1,0:T(8,128)(2,1)S(1)}, u32[]{:S(2)}, u32[]{:S(2)}) collective-permute-start(bf16[2,128,256]{2,1,0:T(8,128)(2,1)} %get-tuple-element.60), channel_id=1, source_target_pairs={{0,128},{32,160},{64,192},{96,224},{128,0},{160,32},{192,64},{224,... | collective-permute-start | bytes 393224 | tf_op jit(solution)/shard_map/ppermute | solution.py:31
  7.7 0.5 collective-permute-start.2
  8.2 2.2 %collective-permute-start.3 = (bf16[256,256]{1,0:T(8,128)(2,1)}, bf16[256,256]{1,0:T(8,128)(2,1)S(1)}, u32[]{:S(2)}, u32[]{:S(2)}) collective-permute-start(bf16[256,256]{1,0:T(8,128)(2,1)} %get-tuple-element.62), channel_id=1, source_target_pairs={{0,3},{1,0},{2,1},{3,2},{4,7},{5,4},{6,5},{7,6},{8,11},{9,8},{10,9... | collective-permute-start | bytes 393224 | tf_op jit(solution)/shard_map/ppermute | solution.py:45
  10.4 0.9 collective-permute-start.4
  11.2 1.9 %collective-permute-start.5 = (bf16[256,256]{1,0:T(8,128)(2,1)}, bf16[256,256]{1,0:T(8,128)(2,1)S(1)}, u32[]{:S(2)}, u32[]{:S(2)}) collective-permute-start(bf16[256,256]{1,0:T(8,128)(2,1)} %get-tuple-element.64), channel_id=1, source_target_pairs={{0,1},{1,2},{2,3},{3,0},{4,5},{5,6},{6,7},{7,4},{8,9},{9,10},{10,1... | collective-permute-start | bytes 393224 | tf_op jit(solution)/shard_map/ppermute | solution.py:45
  13.1 0.9 slice_dynamic-update-slice_fusion.1
  14.2 0.9 copy-done.3
  15.1 2.8 %plan.1 = (s32[12]{0:T(128)S(1)}, bf16[2,128,256]{2,1,0:T(8,128)(2,1)S(1)}) custom-call(s32[4]{0:T(128)S(1)} %pad_add_fusion.place, s32[64]{0:T(128)S(1)} %copy-done.6, s32[64]{0:T(128)S(1)} %copy-done.7, s32[64]{0:T(128)S(1)} %copy-done.8, bf16[2,128,256]{2,1,0:T(8,128)(2,1)S(1)} %copy-done.3), custom_call_target="tpu_custom_call" | custom-call | tf_op jit(solution)/shard_map/plan/pallas_call | solution.py:173
  17.9 0.8 sort.1
  18.9 1.5 %collective-permute-done.6.swapped = bf16[512,256]{1,0:T(8,128)(2,1)S(1)} collective-permute-done((bf16[512,256]{1,0:T(8,128)(2,1)S(1)}, bf16[512,256]{1,0:T(8,128)(2,1)S(1)}, u32[]{:S(2)}, u32[]{:S(2)}) %collective-permute-start.6) | collective-permute-done | bytes 262176 | tf_op jit(solution)/shard_map/ppermute | solution.py:35
  20.4 1.1 unpack.1
  21.5 1.4 %collective-permute-start.7 = (f32[8,512]{1,0:T(8,128)S(1)}, f32[8,512]{1,0:T(8,128)S(1)}, u32[]{:S(2)}, u32[]{:S(2)}) collective-permute-start(f32[8,512]{1,0:T(8,128)S(1)} %get-tuple-element.72.s0), channel_id=1, source_target_pairs={{0,1},{1,2},{2,3},{3,0},{4,5},{5,6},{6,7},{7,4},{8,9},{9,10},{10,1... | collective-permute-start | bytes 49160 | tf_op jit(solution)/shard_map/ppermute | solution.py:45
  22.9 3.1 %collective-permute-start.8 = (f32[8,512]{1,0:T(8,128)S(1)}, f32[8,512]{1,0:T(8,128)S(1)}, u32[]{:S(2)}, u32[]{:S(2)}) collective-permute-start(f32[8,512]{1,0:T(8,128)S(1)} %get-tuple-element.72.s0), channel_id=1, source_target_pairs={{0,2},{1,3},{2,0},{3,1},{4,6},{5,7},{6,4},{7,5},{8,10},{9,11},{10,... | collective-permute-start | bytes 49160 | tf_op jit(solution)/shard_map/ppermute | solution.py:45
  26.0 2.1 %collective-permute-done.8.s2 = f32[8,512]{1,0:T(8,128)S(1)} collective-permute-done((f32[8,512]{1,0:T(8,128)S(1)}, f32[8,512]{1,0:T(8,128)S(1)}, u32[]{:S(2)}, u32[]{:S(2)}) %collective-permute-start.8) | collective-permute-done | bytes 16416 | tf_op jit(solution)/shard_map/ppermute | solution.py:45
  28.1 1.6 %collective-permute-done.9.s3 = f32[8,512]{1,0:T(8,128)S(1)} collective-permute-done((f32[8,512]{1,0:T(8,128)S(1)}, f32[8,512]{1,0:T(8,128)S(1)}, u32[]{:S(2)}, u32[]{:S(2)}) %collective-permute-start.9) | collective-permute-done | bytes 16416 | tf_op jit(solution)/shard_map/ppermute | solution.py:45
  30.2 2.6 %collective-permute-start.16 = (bf16[6,256,256]{2,1,0:T(8,128)(2,1)S(1)}, bf16[6,256,256]{2,1,0:T(8,128)(2,1)S(1)}, u32[]{:S(2)}, u32[]{:S(2)}) collective-permute-start(bf16[6,256,256]{2,1,0:T(8,128)(2,1)S(1)} %slice_dynamic-update-slice_fusion.refs_8_), channel_id=1, source_target_pairs={{0,192},{32,224},{64,128},{96,160},{128,64},{160,96},{192,0},{224,... | collective-permute-start | bytes 2359304 | tf_op jit(solution)/shard_map/ppermute | solution.py:31
  32.8 1.9 %collective-permute-start.10 = (bf16[528,256]{1,0:T(8,128)(2,1)S(1)}, bf16[528,256]{1,0:T(8,128)(2,1)S(1)}, u32[]{:S(2)}, u32[]{:S(2)}) collective-permute-start(bf16[528,256]{1,0:T(8,128)(2,1)S(1)} %label.1.refs_0_), channel_id=1, source_target_pairs={{0,4},{1,5},{2,6},{3,7},{4,0},{5,1},{6,2},{7,3},{8,12},{9,13},{10,... | collective-permute-start | bytes 811016 | tf_op jit(solution)/shard_map/ppermute | solution.py:40
  34.7 4.9 %collective-permute-start.11 = (bf16[528,256]{1,0:T(8,128)(2,1)S(1)}, bf16[528,256]{1,0:T(8,128)(2,1)S(1)}, u32[]{:S(2)}, u32[]{:S(2)}) collective-permute-start(bf16[528,256]{1,0:T(8,128)(2,1)S(1)} %label.1.refs_0_), channel_id=1, source_target_pairs={{0,28},{1,29},{2,30},{3,31},{4,8},{5,9},{6,10},{7,11},{8,4},{9,5},... | collective-permute-start | bytes 811016 | tf_op jit(solution)/shard_map/ppermute | solution.py:40
  39.6 1.7 %collective-permute-done.10.refs_1_ = bf16[528,256]{1,0:T(8,128)(2,1)S(1)} collective-permute-done((bf16[528,256]{1,0:T(8,128)(2,1)S(1)}, bf16[528,256]{1,0:T(8,128)(2,1)S(1)}, u32[]{:S(2)}, u32[]{:S(2)}) %collective-permute-start.10) | collective-permute-done | bytes 270368 | tf_op jit(solution)/shard_map/ppermute | solution.py:40
  41.4 4.7 %collective-permute-done.11.refs_4_ = bf16[528,256]{1,0:T(8,128)(2,1)S(1)} collective-permute-done((bf16[528,256]{1,0:T(8,128)(2,1)S(1)}, bf16[528,256]{1,0:T(8,128)(2,1)S(1)}, u32[]{:S(2)}, u32[]{:S(2)}) %collective-permute-start.11) | collective-permute-done | bytes 270368 | tf_op jit(solution)/shard_map/ppermute | solution.py:40
  46.1 3.0 %collective-permute-start.14 = (bf16[528,256]{1,0:T(8,128)(2,1)S(1)}, bf16[528,256]{1,0:T(8,128)(2,1)S(1)}, u32[]{:S(2)}, u32[]{:S(2)}) collective-permute-start(bf16[528,256]{1,0:T(8,128)(2,1)S(1)} %collective-permute-done.10.refs_1_), channel_id=1, source_target_pairs={{0,28},{1,29},{2,30},{3,31},{4,8},{5,9},{6,10},{7,11},{8,4},{9,5},... | collective-permute-start | bytes 811016 | tf_op jit(solution)/shard_map/ppermute | solution.py:40
  49.2 0.6 collective-permute-done.15.refs_9_
  49.8 1.2 %collective-permute-done.16.refs_10_ = bf16[6,256,256]{2,1,0:T(8,128)(2,1)S(1)} collective-permute-done((bf16[6,256,256]{2,1,0:T(8,128)(2,1)S(1)}, bf16[6,256,256]{2,1,0:T(8,128)(2,1)S(1)}, u32[]{:S(2)}, u32[]{:S(2)}) %collective-permute-start.16) | collective-permute-done | bytes 786464 | tf_op jit(solution)/shard_map/ppermute | solution.py:31
  51.0 2.7 %collective-permute-done.13.refs_2_ = bf16[528,256]{1,0:T(8,128)(2,1)S(1)} collective-permute-done((bf16[528,256]{1,0:T(8,128)(2,1)S(1)}, bf16[528,256]{1,0:T(8,128)(2,1)S(1)}, u32[]{:S(2)}, u32[]{:S(2)}) %collective-permute-start.13) | collective-permute-done | bytes 270368 | tf_op jit(solution)/shard_map/ppermute | solution.py:40
  53.7 1.3 %collective-permute-done.14.refs_5_ = bf16[528,256]{1,0:T(8,128)(2,1)S(1)} collective-permute-done((bf16[528,256]{1,0:T(8,128)(2,1)S(1)}, bf16[528,256]{1,0:T(8,128)(2,1)S(1)}, u32[]{:S(2)}, u32[]{:S(2)}) %collective-permute-start.14) | collective-permute-done | bytes 270368 | tf_op jit(solution)/shard_map/ppermute | solution.py:40
  55.0 1.1 collective-permute-start.19
  56.1 1.5 %collective-permute-start.20 = (bf16[3,256,256]{2,1,0:T(8,128)(2,1)S(1)}, bf16[3,256,256]{2,1,0:T(8,128)(2,1)}, u32[]{:S(2)}, u32[]{:S(2)}) collective-permute-start(bf16[3,256,256]{2,1,0:T(8,128)(2,1)S(1)} %slice.15), channel_id=1, source_target_pairs={{0,192},{32,224},{64,128},{96,160},{128,64},{160,96},{192,0},{224,... | collective-permute-start | bytes 1179656 | tf_op jit(solution)/shard_map/ppermute | solution.py:31
  58.0 3.6 %collective-permute-start.18 = (bf16[528,256]{1,0:T(8,128)(2,1)S(1)}, bf16[528,256]{1,0:T(8,128)(2,1)}, u32[]{:S(2)}, u32[]{:S(2)}) collective-permute-start(bf16[528,256]{1,0:T(8,128)(2,1)S(1)} %collective-permute-done.13.refs_2_), channel_id=1, source_target_pairs={{0,28},{1,29},{2,30},{3,31},{4,8},{5,9},{6,10},{7,11},{8,4},{9,5},... | collective-permute-start | bytes 811016 | tf_op jit(solution)/shard_map/ppermute | solution.py:40
  61.6 2.4 %collective-permute-done.17.refs_3_ = bf16[528,256]{1,0:T(8,128)(2,1)S(1)} collective-permute-done((bf16[528,256]{1,0:T(8,128)(2,1)S(1)}, bf16[528,256]{1,0:T(8,128)(2,1)S(1)}, u32[]{:S(2)}, u32[]{:S(2)}) %collective-permute-start.17) | collective-permute-done | bytes 270368 | tf_op jit(solution)/shard_map/ppermute | solution.py:40
  64.1 2.8 %collective-permute-done.18.refs_6_ = bf16[528,256]{1,0:T(8,128)(2,1)} collective-permute-done((bf16[528,256]{1,0:T(8,128)(2,1)S(1)}, bf16[528,256]{1,0:T(8,128)(2,1)}, u32[]{:S(2)}, u32[]{:S(2)}) %collective-permute-start.18) | collective-permute-done | bytes 270368 | tf_op jit(solution)/shard_map/ppermute | solution.py:40
  67.0 0.5 collective-permute-start.23
  68.0 0.6 reshape.27.gain
  68.6 8.2 %collective-permute-done.21.refs_7_ = bf16[528,256]{1,0:T(8,128)(2,1)} collective-permute-done((bf16[528,256]{1,0:T(8,128)(2,1)}, bf16[528,256]{1,0:T(8,128)(2,1)}, u32[]{:S(2)}, u32[]{:S(2)}) %collective-permute-start.21) | collective-permute-done | bytes 270368 | tf_op jit(solution)/shard_map/ppermute | solution.py:40
  76.9 8.3 %project.1 = (f32[640,256]{1,0:T(8,128)}, bf16[640,256]{1,0:T(8,128)(2,1)}, bf16[640,256]{1,0:T(8,128)(2,1)}, bf16[640,256]{1,0:T(8,128)(2,1)}, bf16[2048,256]{1,0:T(8,128)(2,1)}) custom-call(s32[4]{0:T(128)} %copy-done.4, f32[32,256]{1,0:T(8,128)} %reshape.27.gain, bf16[528,256]{1,0:T(8,128)(2,1)} %copy-done.2, bf16[528,256]{1,0:T(8,128)(2,1)} %copy-done.15, ...), custom_call_target="tpu_custom_call" | custom-call | flops 2684354560 | bytes 10485760 | tf_op jit(solution)/shard_map/project/pallas_call | solution.py:335
  85.3 2.2 %collective-permute-start.27 = (bf16[640,256]{1,0:T(8,128)(2,1)}, bf16[640,256]{1,0:T(8,128)(2,1)S(1)}, u32[]{:S(2)}, u32[]{:S(2)}) collective-permute-start(bf16[640,256]{1,0:T(8,128)(2,1)} %get-tuple-element.96), channel_id=1, source_target_pairs={{0,2},{1,3},{2,0},{3,1},{4,6},{5,7},{6,4},{7,5},{8,10},{9,11},{10,... | collective-permute-start | bytes 983048 | tf_op jit(solution)/shard_map/ppermute | solution.py:45
  87.5 1.9 %collective-permute-start.28 = (bf16[640,256]{1,0:T(8,128)(2,1)}, bf16[640,256]{1,0:T(8,128)(2,1)S(1)}, u32[]{:S(2)}, u32[]{:S(2)}) collective-permute-start(bf16[640,256]{1,0:T(8,128)(2,1)} %get-tuple-element.97), channel_id=1, source_target_pairs={{0,3},{1,0},{2,1},{3,2},{4,7},{5,4},{6,5},{7,6},{8,11},{9,8},{10,9... | collective-permute-start | bytes 983048 | tf_op jit(solution)/shard_map/ppermute | solution.py:45
  89.8 1.2 %copy-done = bf16[2048,256]{1,0:T(8,128)(2,1)S(1)} copy-done((bf16[2048,256]{1,0:T(8,128)(2,1)S(1)}, bf16[2048,256]{1,0:T(8,128)(2,1)}, u32[]{:S(2)}) %copy-start) | copy-done | bytes 1048600
  91.1 1.1 copy-done.1
  92.4 3.7 %collective-permute-done.26.p1 = bf16[640,256]{1,0:T(8,128)(2,1)S(1)} collective-permute-done((bf16[640,256]{1,0:T(8,128)(2,1)}, bf16[640,256]{1,0:T(8,128)(2,1)S(1)}, u32[]{:S(2)}, u32[]{:S(2)}) %collective-permute-start.26) | collective-permute-done | bytes 327712 | tf_op jit(solution)/shard_map/ppermute | solution.py:45
  96.1 1.6 %collective-permute-done.27.p2 = bf16[640,256]{1,0:T(8,128)(2,1)S(1)} collective-permute-done((bf16[640,256]{1,0:T(8,128)(2,1)}, bf16[640,256]{1,0:T(8,128)(2,1)S(1)}, u32[]{:S(2)}, u32[]{:S(2)}) %collective-permute-start.27) | collective-permute-done | bytes 327712 | tf_op jit(solution)/shard_map/ppermute | solution.py:45
  97.8 5.2 %collective-permute-done.28.p3 = bf16[640,256]{1,0:T(8,128)(2,1)S(1)} collective-permute-done((bf16[640,256]{1,0:T(8,128)(2,1)}, bf16[640,256]{1,0:T(8,128)(2,1)S(1)}, u32[]{:S(2)}, u32[]{:S(2)}) %collective-permute-start.28) | collective-permute-done | bytes 327712 | tf_op jit(solution)/shard_map/ppermute | solution.py:45
  103.1 0.7 collective-permute-start.29
  103.8 2.0 %collective-permute-start.30 = (bf16[128,256]{1,0:T(8,128)(2,1)S(1)}, bf16[128,256]{1,0:T(8,128)(2,1)S(1)}, u32[]{:S(2)}, u32[]{:S(2)}) collective-permute-start(bf16[128,256]{1,0:T(8,128)(2,1)S(1)} %fresh.1.f0), channel_id=1, source_target_pairs={{0,2},{1,3},{2,0},{3,1},{4,6},{5,7},{6,4},{7,5},{8,10},{9,11},{10,... | collective-permute-start | bytes 196616 | tf_op jit(solution)/shard_map/ppermute | solution.py:45
  105.8 1.9 %collective-permute-start.31 = (bf16[128,256]{1,0:T(8,128)(2,1)S(1)}, bf16[128,256]{1,0:T(8,128)(2,1)S(1)}, u32[]{:S(2)}, u32[]{:S(2)}) collective-permute-start(bf16[128,256]{1,0:T(8,128)(2,1)S(1)} %fresh.1.f0), channel_id=1, source_target_pairs={{0,3},{1,0},{2,1},{3,2},{4,7},{5,4},{6,5},{7,6},{8,11},{9,8},{10,9... | collective-permute-start | bytes 196616 | tf_op jit(solution)/shard_map/ppermute | solution.py:45
  107.7 4.5 %prompt.1 = (bf16[4,256,128]{2,1,0:T(8,128)(2,1)S(1)}, f32[4,256,128]{2,1,0:T(8,128)S(1)}, f32[4,256,128]{2,1,0:T(8,128)S(1)}, f32[4,256,128]{2,1,0:T(8,128)S(1)}) custom-call(f32[640,256]{1,0:T(8,128)S(1)} %get-tuple-element.94.own, bf16[640,256]{1,0:T(8,128)(2,1)S(1)} %collective-permute-done.26.p1, bf16[640,256]{1,0:T(8,128)(2,1)S(1)} %collective-permute-done.27.p2, ...), custom_call_target="tpu_custom_call" | custom-call | flops 1073741824 | bytes 2097152 | tf_op jit(solution)/shard_map/prompt/pallas_call | solution.py:445
  112.2 2.0 %finish.1 = bf16[4,128,256]{2,1,0:T(8,128)(2,1)} custom-call(s32[4]{0:T(128)S(1)} %copy-done.5, s32[12]{0:T(128)S(1)} %get-tuple-element.57.source.slots, bf16[4,256,128]{2,1,0:T(8,128)(2,1)S(1)} %get-tuple-element.99.q, f32[4,256,128]{2,1,0:T(8,128)S(1)} %get-tuple-element.100.mixed_ref, f32[4,256,128]{2,1,0:T(8,128)S(1)} %get-tuple-element.101.top_ref, ...), custom_call_target="tpu_custom_call" | custom-call | tf_op jit(solution)/shard_map/finish/pallas_call | solution.py:488
  (79 shorter events, 2.9 us)
Async XLA Ops:
  0.0 14.1 %copy-start.6 = (s32[64]{0:T(128)S(1)}, s32[64]{0:T(128)}, u32[]{:S(2)}) copy-start(s32[64]{0:T(128)} %keep.3) | copy-start | bytes 772
  0.0 14.1 %copy-start.7 = (s32[64]{0:T(128)S(1)}, s32[64]{0:T(128)}, u32[]{:S(2)}) copy-start(s32[64]{0:T(128)} %destination.3) | copy-start | bytes 772
  0.0 14.2 %copy-start.8 = (s32[64]{0:T(128)S(1)}, s32[64]{0:T(128)}, u32[]{:S(2)}) copy-start(s32[64]{0:T(128)} %counts.1) | copy-start | bytes 772
  3.4 7.8 %collective-permute-start = (bf16[2,128,256]{2,1,0:T(8,128)(2,1)}, bf16[2,128,256]{2,1,0:T(8,128)(2,1)S(1)}, u32[]{:S(2)}, u32[]{:S(2)}) collective-permute-start(bf16[2,128,256]{2,1,0:T(8,128)(2,1)} %get-tuple-element.55), channel_id=1, source_target_pairs={{0,64},{32,96},{64,0},{96,32},{128,192},{160,224},{192,128},{224,1... | collective-permute-start | bytes 393224 | tf_op jit(solution)/shard_map/ppermute | solution.py:31
  5.0 12.9 %collective-permute-start.1 = (bf16[2,128,256]{2,1,0:T(8,128)(2,1)}, bf16[2,128,256]{2,1,0:T(8,128)(2,1)S(1)}, u32[]{:S(2)}, u32[]{:S(2)}) collective-permute-start(bf16[2,128,256]{2,1,0:T(8,128)(2,1)} %get-tuple-element.60), channel_id=1, source_target_pairs={{0,128},{32,160},{64,192},{96,224},{128,0},{160,32},{192,64},{224,... | collective-permute-start | bytes 393224 | tf_op jit(solution)/shard_map/ppermute | solution.py:31
  7.7 10.2 %collective-permute-start.2 = (bf16[2,128,256]{2,1,0:T(8,128)(2,1)}, bf16[2,128,256]{2,1,0:T(8,128)(2,1)S(1)}, u32[]{:S(2)}, u32[]{:S(2)}) collective-permute-start(bf16[2,128,256]{2,1,0:T(8,128)(2,1)} %get-tuple-element.61), channel_id=1, source_target_pairs={{0,192},{32,224},{64,128},{96,160},{128,64},{160,96},{192,0},{224,... | collective-permute-start | bytes 393224 | tf_op jit(solution)/shard_map/ppermute | solution.py:31
  8.2 9.7 %collective-permute-start.3 = (bf16[256,256]{1,0:T(8,128)(2,1)}, bf16[256,256]{1,0:T(8,128)(2,1)S(1)}, u32[]{:S(2)}, u32[]{:S(2)}) collective-permute-start(bf16[256,256]{1,0:T(8,128)(2,1)} %get-tuple-element.62), channel_id=1, source_target_pairs={{0,3},{1,0},{2,1},{3,2},{4,7},{5,4},{6,5},{7,6},{8,11},{9,8},{10,9... | collective-permute-start | bytes 393224 | tf_op jit(solution)/shard_map/ppermute | solution.py:45
  10.4 7.6 %collective-permute-start.4 = (bf16[256,256]{1,0:T(8,128)(2,1)}, bf16[256,256]{1,0:T(8,128)(2,1)S(1)}, u32[]{:S(2)}, u32[]{:S(2)}) collective-permute-start(bf16[256,256]{1,0:T(8,128)(2,1)} %get-tuple-element.63), channel_id=1, source_target_pairs={{0,2},{1,3},{2,0},{3,1},{4,6},{5,7},{6,4},{7,5},{8,10},{9,11},{10,... | collective-permute-start | bytes 393224 | tf_op jit(solution)/shard_map/ppermute | solution.py:45
  11.2 6.7 %collective-permute-start.5 = (bf16[256,256]{1,0:T(8,128)(2,1)}, bf16[256,256]{1,0:T(8,128)(2,1)S(1)}, u32[]{:S(2)}, u32[]{:S(2)}) collective-permute-start(bf16[256,256]{1,0:T(8,128)(2,1)} %get-tuple-element.64), channel_id=1, source_target_pairs={{0,1},{1,2},{2,3},{3,0},{4,5},{5,6},{6,7},{7,4},{8,9},{9,10},{10,1... | collective-permute-start | bytes 393224 | tf_op jit(solution)/shard_map/ppermute | solution.py:45
  14.1 42.0 %copy-start.4 = (s32[4]{0:T(128)}, s32[4]{0:T(128)S(1)}, u32[]{:S(2)}) copy-start(s32[4]{0:T(128)S(1)} %pad_add_fusion.place) | copy-start | bytes 52
  15.1 10.9 %copy-start.9 = (bf16[3,256,256]{2,1,0:T(8,128)(2,1)S(1)}, bf16[3,256,256]{2,1,0:T(8,128)(2,1)}, u32[]{:S(2)}) copy-start(bf16[3,256,256]{2,1,0:T(8,128)(2,1)} %get-tuple-element.73) | copy-start | bytes 1179652
  18.7 49.2 %copy-start.13 = (bf16[8192]{0:T(1024)(128)(2,1)S(1)}, bf16[8192]{0:T(1024)(128)(2,1)}, u32[]{:S(2)}) copy-start(bf16[8192]{0:T(1024)(128)(2,1)} %param.11) | copy-start | bytes 49156
  18.8 1.6 %collective-permute-start.6 = (bf16[512,256]{1,0:T(8,128)(2,1)S(1)}, bf16[512,256]{1,0:T(8,128)(2,1)S(1)}, u32[]{:S(2)}, u32[]{:S(2)}) collective-permute-start(bf16[512,256]{1,0:T(8,128)(2,1)S(1)} %get-tuple-element.70), channel_id=1, source_target_pairs={{0,32},{32,0},{64,96},{96,64},{128,160},{160,128},{192,224},{224,1... | collective-permute-start | bytes 786440 | tf_op jit(solution)/shard_map/ppermute | solution.py:35
  21.5 4.5 %collective-permute-start.7 = (f32[8,512]{1,0:T(8,128)S(1)}, f32[8,512]{1,0:T(8,128)S(1)}, u32[]{:S(2)}, u32[]{:S(2)}) collective-permute-start(f32[8,512]{1,0:T(8,128)S(1)} %get-tuple-element.72.s0), channel_id=1, source_target_pairs={{0,1},{1,2},{2,3},{3,0},{4,5},{5,6},{6,7},{7,4},{8,9},{9,10},{10,1... | collective-permute-start | bytes 49160 | tf_op jit(solution)/shard_map/ppermute | solution.py:45
  22.9 5.2 %collective-permute-start.8 = (f32[8,512]{1,0:T(8,128)S(1)}, f32[8,512]{1,0:T(8,128)S(1)}, u32[]{:S(2)}, u32[]{:S(2)}) collective-permute-start(f32[8,512]{1,0:T(8,128)S(1)} %get-tuple-element.72.s0), channel_id=1, source_target_pairs={{0,2},{1,3},{2,0},{3,1},{4,6},{5,7},{6,4},{7,5},{8,10},{9,11},{10,... | collective-permute-start | bytes 49160 | tf_op jit(solution)/shard_map/ppermute | solution.py:45
  25.9 3.7 %collective-permute-start.9 = (f32[8,512]{1,0:T(8,128)S(1)}, f32[8,512]{1,0:T(8,128)S(1)}, u32[]{:S(2)}, u32[]{:S(2)}) collective-permute-start(f32[8,512]{1,0:T(8,128)S(1)} %get-tuple-element.72.s0), channel_id=1, source_target_pairs={{0,3},{1,0},{2,1},{3,2},{4,7},{5,4},{6,5},{7,6},{8,11},{9,8},{10,9... | collective-permute-start | bytes 49160 | tf_op jit(solution)/shard_map/ppermute | solution.py:45
  25.9 50.9 %copy-start.12 = (bf16[6,256,256]{2,1,0:T(8,128)(2,1)}, bf16[6,256,256]{2,1,0:T(8,128)(2,1)S(1)}, u32[]{:S(2)}) copy-start(bf16[6,256,256]{2,1,0:T(8,128)(2,1)S(1)} %slice_dynamic-update-slice_fusion.refs_8_) | copy-start | bytes 2359300
  29.7 47.1 %copy-start.2 = (bf16[528,256]{1,0:T(8,128)(2,1)}, bf16[528,256]{1,0:T(8,128)(2,1)S(1)}, u32[]{:S(2)}) copy-start(bf16[528,256]{1,0:T(8,128)(2,1)S(1)} %label.1.refs_0_) | copy-start | bytes 811012
  29.7 16.3 %collective-permute-start.12 = (bf16[6,256,256]{2,1,0:T(8,128)(2,1)S(1)}, bf16[6,256,256]{2,1,0:T(8,128)(2,1)S(1)}, u32[]{:S(2)}, u32[]{:S(2)}) collective-permute-start(bf16[6,256,256]{2,1,0:T(8,128)(2,1)S(1)} %slice_dynamic-update-slice_fusion.refs_8_), channel_id=1, source_target_pairs={{0,32},{32,0},{64,96},{96,64},{128,160},{160,128},{192,224},{224,1... | collective-permute-start | bytes 2359304 | tf_op jit(solution)/shard_map/ppermute | solution.py:35
  29.8 20.0 %collective-permute-start.15 = (bf16[6,256,256]{2,1,0:T(8,128)(2,1)S(1)}, bf16[6,256,256]{2,1,0:T(8,128)(2,1)S(1)}, u32[]{:S(2)}, u32[]{:S(2)}) collective-permute-start(bf16[6,256,256]{2,1,0:T(8,128)(2,1)S(1)} %slice_dynamic-update-slice_fusion.refs_8_), channel_id=1, source_target_pairs={{0,64},{32,96},{64,0},{96,32},{128,192},{160,224},{192,128},{224,1... | collective-permute-start | bytes 2359304 | tf_op jit(solution)/shard_map/ppermute | solution.py:31
  30.2 20.8 %collective-permute-start.16 = (bf16[6,256,256]{2,1,0:T(8,128)(2,1)S(1)}, bf16[6,256,256]{2,1,0:T(8,128)(2,1)S(1)}, u32[]{:S(2)}, u32[]{:S(2)}) collective-permute-start(bf16[6,256,256]{2,1,0:T(8,128)(2,1)S(1)} %slice_dynamic-update-slice_fusion.refs_8_), channel_id=1, source_target_pairs={{0,192},{32,224},{64,128},{96,160},{128,64},{160,96},{192,0},{224,... | collective-permute-start | bytes 2359304 | tf_op jit(solution)/shard_map/ppermute | solution.py:31
  32.8 8.6 %collective-permute-start.10 = (bf16[528,256]{1,0:T(8,128)(2,1)S(1)}, bf16[528,256]{1,0:T(8,128)(2,1)S(1)}, u32[]{:S(2)}, u32[]{:S(2)}) collective-permute-start(bf16[528,256]{1,0:T(8,128)(2,1)S(1)} %label.1.refs_0_), channel_id=1, source_target_pairs={{0,4},{1,5},{2,6},{3,7},{4,0},{5,1},{6,2},{7,3},{8,12},{9,13},{10,... | collective-permute-start | bytes 811016 | tf_op jit(solution)/shard_map/ppermute | solution.py:40
  34.7 11.3 %collective-permute-start.11 = (bf16[528,256]{1,0:T(8,128)(2,1)S(1)}, bf16[528,256]{1,0:T(8,128)(2,1)S(1)}, u32[]{:S(2)}, u32[]{:S(2)}) collective-permute-start(bf16[528,256]{1,0:T(8,128)(2,1)S(1)} %label.1.refs_0_), channel_id=1, source_target_pairs={{0,28},{1,29},{2,30},{3,31},{4,8},{5,9},{6,10},{7,11},{8,4},{9,5},... | collective-permute-start | bytes 811016 | tf_op jit(solution)/shard_map/ppermute | solution.py:40
  41.4 12.3 %copy-start.15 = (bf16[528,256]{1,0:T(8,128)(2,1)}, bf16[528,256]{1,0:T(8,128)(2,1)S(1)}, u32[]{:S(2)}) copy-start(bf16[528,256]{1,0:T(8,128)(2,1)S(1)} %collective-permute-done.10.refs_1_) | copy-start | bytes 811012
  46.0 7.7 %copy-start.16 = (bf16[528,256]{1,0:T(8,128)(2,1)}, bf16[528,256]{1,0:T(8,128)(2,1)S(1)}, u32[]{:S(2)}) copy-start(bf16[528,256]{1,0:T(8,128)(2,1)S(1)} %collective-permute-done.11.refs_4_) | copy-start | bytes 811012
  46.0 30.8 %copy-start.14 = (bf16[6,256,256]{2,1,0:T(8,128)(2,1)}, bf16[6,256,256]{2,1,0:T(8,128)(2,1)S(1)}, u32[]{:S(2)}) copy-start(bf16[6,256,256]{2,1,0:T(8,128)(2,1)S(1)} %collective-permute-done.12.refs_13_) | copy-start | bytes 2359300
  46.0 7.7 %collective-permute-start.13 = (bf16[528,256]{1,0:T(8,128)(2,1)S(1)}, bf16[528,256]{1,0:T(8,128)(2,1)S(1)}, u32[]{:S(2)}, u32[]{:S(2)}) collective-permute-start(bf16[528,256]{1,0:T(8,128)(2,1)S(1)} %collective-permute-done.11.refs_4_), channel_id=1, source_target_pairs={{0,4},{1,5},{2,6},{3,7},{4,0},{5,1},{6,2},{7,3},{8,12},{9,13},{10,... | collective-permute-start | bytes 811016 | tf_op jit(solution)/shard_map/ppermute | solution.py:40
  46.1 8.9 %collective-permute-start.14 = (bf16[528,256]{1,0:T(8,128)(2,1)S(1)}, bf16[528,256]{1,0:T(8,128)(2,1)S(1)}, u32[]{:S(2)}, u32[]{:S(2)}) collective-permute-start(bf16[528,256]{1,0:T(8,128)(2,1)S(1)} %collective-permute-done.10.refs_1_), channel_id=1, source_target_pairs={{0,28},{1,29},{2,30},{3,31},{4,8},{5,9},{6,10},{7,11},{8,4},{9,5},... | collective-permute-start | bytes 811016 | tf_op jit(solution)/shard_map/ppermute | solution.py:40
  49.8 27.1 %copy-start.10 = (bf16[6,256,256]{2,1,0:T(8,128)(2,1)}, bf16[6,256,256]{2,1,0:T(8,128)(2,1)S(1)}, u32[]{:S(2)}) copy-start(bf16[6,256,256]{2,1,0:T(8,128)(2,1)S(1)} %collective-permute-done.15.refs_9_) | copy-start | bytes 2359300
  51.0 25.9 %copy-start.11 = (bf16[6,256,256]{2,1,0:T(8,128)(2,1)}, bf16[6,256,256]{2,1,0:T(8,128)(2,1)S(1)}, u32[]{:S(2)}) copy-start(bf16[6,256,256]{2,1,0:T(8,128)(2,1)S(1)} %collective-permute-done.16.refs_10_) | copy-start | bytes 2359300
  53.7 13.2 %copy-start.17 = (bf16[528,256]{1,0:T(8,128)(2,1)}, bf16[528,256]{1,0:T(8,128)(2,1)S(1)}, u32[]{:S(2)}) copy-start(bf16[528,256]{1,0:T(8,128)(2,1)S(1)} %collective-permute-done.13.refs_2_) | copy-start | bytes 811012
  55.0 12.0 %copy-start.18 = (bf16[528,256]{1,0:T(8,128)(2,1)}, bf16[528,256]{1,0:T(8,128)(2,1)S(1)}, u32[]{:S(2)}) copy-start(bf16[528,256]{1,0:T(8,128)(2,1)S(1)} %collective-permute-done.14.refs_5_) | copy-start | bytes 811012
  55.0 11.8 %collective-permute-start.19 = (bf16[3,256,256]{2,1,0:T(8,128)(2,1)S(1)}, bf16[3,256,256]{2,1,0:T(8,128)(2,1)}, u32[]{:S(2)}, u32[]{:S(2)}) collective-permute-start(bf16[3,256,256]{2,1,0:T(8,128)(2,1)S(1)} %slice.14), channel_id=1, source_target_pairs={{0,64},{32,96},{64,0},{96,32},{128,192},{160,224},{192,128},{224,1... | collective-permute-start | bytes 1179656 | tf_op jit(solution)/shard_map/ppermute | solution.py:31
  56.1 10.7 %collective-permute-start.20 = (bf16[3,256,256]{2,1,0:T(8,128)(2,1)S(1)}, bf16[3,256,256]{2,1,0:T(8,128)(2,1)}, u32[]{:S(2)}, u32[]{:S(2)}) collective-permute-start(bf16[3,256,256]{2,1,0:T(8,128)(2,1)S(1)} %slice.15), channel_id=1, source_target_pairs={{0,192},{32,224},{64,128},{96,160},{128,64},{160,96},{192,0},{224,... | collective-permute-start | bytes 1179656 | tf_op jit(solution)/shard_map/ppermute | solution.py:31
  57.6 6.5 %collective-permute-start.17 = (bf16[528,256]{1,0:T(8,128)(2,1)S(1)}, bf16[528,256]{1,0:T(8,128)(2,1)S(1)}, u32[]{:S(2)}, u32[]{:S(2)}) collective-permute-start(bf16[528,256]{1,0:T(8,128)(2,1)S(1)} %collective-permute-done.14.refs_5_), channel_id=1, source_target_pairs={{0,4},{1,5},{2,6},{3,7},{4,0},{5,1},{6,2},{7,3},{8,12},{9,13},{10,... | collective-permute-start | bytes 811016 | tf_op jit(solution)/shard_map/ppermute | solution.py:40
  58.0 8.8 %collective-permute-start.18 = (bf16[528,256]{1,0:T(8,128)(2,1)S(1)}, bf16[528,256]{1,0:T(8,128)(2,1)}, u32[]{:S(2)}, u32[]{:S(2)}) collective-permute-start(bf16[528,256]{1,0:T(8,128)(2,1)S(1)} %collective-permute-done.13.refs_2_), channel_id=1, source_target_pairs={{0,28},{1,29},{2,30},{3,31},{4,8},{5,9},{6,10},{7,11},{8,4},{9,5},... | collective-permute-start | bytes 811016 | tf_op jit(solution)/shard_map/ppermute | solution.py:40
  66.9 9.9 %collective-permute-start.22 = (bf16[6,256,256]{2,1,0:T(8,128)(2,1)S(1)}, bf16[6,256,256]{2,1,0:T(8,128)(2,1)}, u32[]{:S(2)}, u32[]{:S(2)}) collective-permute-start(bf16[6,256,256]{2,1,0:T(8,128)(2,1)S(1)} %collective-permute-done.15.refs_9_), channel_id=1, source_target_pairs={{0,32},{32,0},{64,96},{96,64},{128,160},{160,128},{192,224},{224,1... | collective-permute-start | bytes 2359304 | tf_op jit(solution)/shard_map/ppermute | solution.py:35
  67.0 9.8 %collective-permute-start.23 = (bf16[6,256,256]{2,1,0:T(8,128)(2,1)S(1)}, bf16[6,256,256]{2,1,0:T(8,128)(2,1)}, u32[]{:S(2)}, u32[]{:S(2)}) collective-permute-start(bf16[6,256,256]{2,1,0:T(8,128)(2,1)S(1)} %collective-permute-done.16.refs_10_), channel_id=1, source_target_pairs={{0,32},{32,0},{64,96},{96,64},{128,160},{160,128},{192,224},{224,1... | collective-permute-start | bytes 2359304 | tf_op jit(solution)/shard_map/ppermute | solution.py:35
  67.5 9.3 %collective-permute-start.24 = (bf16[3,256,256]{2,1,0:T(8,128)(2,1)}, bf16[3,256,256]{2,1,0:T(8,128)(2,1)}, u32[]{:S(2)}, u32[]{:S(2)}) collective-permute-start(bf16[3,256,256]{2,1,0:T(8,128)(2,1)} %collective-permute-done.19.refs_11_), channel_id=1, source_target_pairs={{0,32},{32,0},{64,96},{96,64},{128,160},{160,128},{192,224},{224,1... | collective-permute-start | bytes 1179656 | tf_op jit(solution)/shard_map/ppermute | solution.py:35
  67.6 9.2 %collective-permute-start.25 = (bf16[3,256,256]{2,1,0:T(8,128)(2,1)}, bf16[3,256,256]{2,1,0:T(8,128)(2,1)}, u32[]{:S(2)}, u32[]{:S(2)}) collective-permute-start(bf16[3,256,256]{2,1,0:T(8,128)(2,1)} %collective-permute-done.20.refs_12_), channel_id=1, source_target_pairs={{0,32},{32,0},{64,96},{96,64},{128,160},{160,128},{192,224},{224,1... | collective-permute-start | bytes 1179656 | tf_op jit(solution)/shard_map/ppermute | solution.py:35
  68.0 8.8 %collective-permute-start.21 = (bf16[528,256]{1,0:T(8,128)(2,1)}, bf16[528,256]{1,0:T(8,128)(2,1)}, u32[]{:S(2)}, u32[]{:S(2)}) collective-permute-start(bf16[528,256]{1,0:T(8,128)(2,1)} %collective-permute-done.18.refs_6_), channel_id=1, source_target_pairs={{0,4},{1,5},{2,6},{3,7},{4,0},{5,1},{6,2},{7,3},{8,12},{9,13},{10,... | collective-permute-start | bytes 811016 | tf_op jit(solution)/shard_map/ppermute | solution.py:40
  85.2 10.9 %collective-permute-start.26 = (bf16[640,256]{1,0:T(8,128)(2,1)}, bf16[640,256]{1,0:T(8,128)(2,1)S(1)}, u32[]{:S(2)}, u32[]{:S(2)}) collective-permute-start(bf16[640,256]{1,0:T(8,128)(2,1)} %get-tuple-element.95), channel_id=1, source_target_pairs={{0,1},{1,2},{2,3},{3,0},{4,5},{5,6},{6,7},{7,4},{8,9},{9,10},{10,1... | collective-permute-start | bytes 983048 | tf_op jit(solution)/shard_map/ppermute | solution.py:45
  85.3 12.5 %collective-permute-start.27 = (bf16[640,256]{1,0:T(8,128)(2,1)}, bf16[640,256]{1,0:T(8,128)(2,1)S(1)}, u32[]{:S(2)}, u32[]{:S(2)}) collective-permute-start(bf16[640,256]{1,0:T(8,128)(2,1)} %get-tuple-element.96), channel_id=1, source_target_pairs={{0,2},{1,3},{2,0},{3,1},{4,6},{5,7},{6,4},{7,5},{8,10},{9,11},{10,... | collective-permute-start | bytes 983048 | tf_op jit(solution)/shard_map/ppermute | solution.py:45
  87.5 15.5 %collective-permute-start.28 = (bf16[640,256]{1,0:T(8,128)(2,1)}, bf16[640,256]{1,0:T(8,128)(2,1)S(1)}, u32[]{:S(2)}, u32[]{:S(2)}) collective-permute-start(bf16[640,256]{1,0:T(8,128)(2,1)} %get-tuple-element.97), channel_id=1, source_target_pairs={{0,3},{1,0},{2,1},{3,2},{4,7},{5,4},{6,5},{7,6},{8,11},{9,8},{10,9... | collective-permute-start | bytes 983048 | tf_op jit(solution)/shard_map/ppermute | solution.py:45
  103.1 9.1 %copy-start.5 = (s32[4]{0:T(128)S(1)}, s32[4]{0:T(128)}, u32[]{:S(2)}) copy-start(s32[4]{0:T(128)} %copy-done.4) | copy-start | bytes 52
  103.1 9.1 %collective-permute-start.29 = (bf16[128,256]{1,0:T(8,128)(2,1)S(1)}, bf16[128,256]{1,0:T(8,128)(2,1)S(1)}, u32[]{:S(2)}, u32[]{:S(2)}) collective-permute-start(bf16[128,256]{1,0:T(8,128)(2,1)S(1)} %fresh.1.f0), channel_id=1, source_target_pairs={{0,1},{1,2},{2,3},{3,0},{4,5},{5,6},{6,7},{7,4},{8,9},{9,10},{10,1... | collective-permute-start | bytes 196616 | tf_op jit(solution)/shard_map/ppermute | solution.py:45
  103.8 8.4 %collective-permute-start.30 = (bf16[128,256]{1,0:T(8,128)(2,1)S(1)}, bf16[128,256]{1,0:T(8,128)(2,1)S(1)}, u32[]{:S(2)}, u32[]{:S(2)}) collective-permute-start(bf16[128,256]{1,0:T(8,128)(2,1)S(1)} %fresh.1.f0), channel_id=1, source_target_pairs={{0,2},{1,3},{2,0},{3,1},{4,6},{5,7},{6,4},{7,5},{8,10},{9,11},{10,... | collective-permute-start | bytes 196616 | tf_op jit(solution)/shard_map/ppermute | solution.py:45
  105.8 6.4 %collective-permute-start.31 = (bf16[128,256]{1,0:T(8,128)(2,1)S(1)}, bf16[128,256]{1,0:T(8,128)(2,1)S(1)}, u32[]{:S(2)}, u32[]{:S(2)}) collective-permute-start(bf16[128,256]{1,0:T(8,128)(2,1)S(1)} %fresh.1.f0), channel_id=1, source_target_pairs={{0,3},{1,0},{2,1},{3,2},{4,7},{5,4},{6,5},{7,6},{8,11},{9,8},{10,9... | collective-permute-start | bytes 196616 | tf_op jit(solution)/shard_map/ppermute | solution.py:45
  (4 other events, 6.6 us)

commit v6 on v5

--- a/solution.py
+++ b/solution.py
@@ -147,32 +147,26 @@
 def plan_kernel(place, keep, destination, counts, piece, out, held):
     x, c = place[0], place[1]
     held[...] = piece[...]
-
-    def step(b, _):
-        target = destination[b]
-        group = lax.div(target, OUT_DEV)
-
-        @pl.when((keep[b] == 1) & (lax.div(group, CORES) == x))
-        def _():
-            slot = lax.rem(target, OUT_DEV)
-            source = lax.div(b, IN_DEV)
-            other = lax.rem(group + c, CORES)
-            dx = relation(x, lax.div(source, CORES))
-            out[other * OUT_DEV + slot] = jnp.where(lax.rem(source, CORES) == c, dx, XS)
-
-            @pl.when(other == 0)
-            def _():
-                out[2 * OUT_DEV + slot] = counts[b]
-
-        return 0
-
-    lax.fori_loop(0, keep.shape[0], step, 0)
+    for chip in range(XS):
+        dx = relation(x, chip)
+        for core in range(CORES):
+            found = jnp.where(c == core, dx, XS)
+            for i in range(IN_DEV):
+                b = (chip * CORES + core) * IN_DEV + i
+                target = destination[b]
+                slot = target & (OUT_DEV - 1)
+                group = target >> 2
+                other = (group ^ c) & 1
+                here = (keep[b] == 1) & ((group >> 1) == x)
+                out[jnp.where(here, other * OUT_DEV + slot, 3 * OUT_DEV)] = found
+                mine = here & (other == 0)
+                out[jnp.where(mine, 2 * OUT_DEV + slot, 3 * OUT_DEV + 1)] = counts[b]
 
 
 def plan(place, keep, destination, counts, piece):
     return pl.pallas_call(
         plan_kernel,
-        out_shape=[shaped((3 * OUT_DEV,), jnp.int32), shaped(piece.shape, piece.dtype)],
+        out_shape=[shaped((4 * OUT_DEV,), jnp.int32), shaped(piece.shape, piece.dtype)],
         in_specs=[SMEM] * 4 + [VMEM],
         out_specs=[SMEM, VMEM],
         compiler_params=limit(1),
@@ -269,9 +263,22 @@
 SHARD_Z = (0, 1, 2, 3, -1, -2, -3, 4)
 
 
-def product(normed, tiles, n):
+def block_copies(weights, tiles, start, count, sems, first):
+    pairs = []
+    for position in range(SHARDS):
+        base, begin = 5 * (position // 4), start
+        source = weights[base + position % 4] if position % 4 < 3 else weights[base + 3]
+        if position % 4 == 3 and start >= 3:
+            source, begin = weights[base + 4], start - 3
+        pairs.append((source.at[pl.ds(begin, count)], tiles.at[position]))
+    return fetch_all(pairs, sems, first)
+
+
+def product(normed, tiles, n, copies=None):
     total = None
     for p in range(SHARDS):
+        if copies is not None:
+            copies[p].wait()
         term = jnp.dot(
             normed[:, p * TILE : (p + 1) * TILE], tiles[p, n], preferred_element_type=jnp.float32
         )
@@ -279,21 +286,13 @@
     return total
 
 
-def project_kernel(place, gain, *refs):
+def first_kernel(place, gain, *refs):
     shards, weights = refs[:8], refs[8:18]
-    own_ref, parts, cache_ref = refs[18], refs[19:22], refs[22]
-    held, tiles, normed, kv, own, sent, sems = refs[23:]
+    normed_ref, part_ref, kv_ref, kv_parts = refs[18:22]
+    held, tiles, normed, kv, sent, small, sems = refs[22:]
     x, c, z, y = place[0], place[1], place[2], place[3]
     copies = fetch_all([(shard, held.at[i]) for i, shard in enumerate(shards)], sems)
-    pairs = []
-    for half in range(2):
-        base = 4 * half
-        own_w, left, right, far_a, far_b = weights[5 * half : 5 * half + 5]
-        for i, w in enumerate((own_w, left, right)):
-            pairs.append((w, tiles.at[base + i]))
-        pairs.append((far_a, tiles.at[base + 3, pl.ds(0, 3)]))
-        pairs.append((far_b, tiles.at[base + 3, pl.ds(3, 3)]))
-    fetched = fetch_all(pairs, sems, 8)
+    fetched = block_copies(weights, tiles, 3, 2, sems, 8)
     await_all(copies)
     sums = functools.reduce(
         jnp.add, [held[i, TOTAL:, :].astype(jnp.float32) for i in range(SHARDS)]
@@ -310,59 +309,149 @@
         normed[:, cols] = (
             held[i, :TOTAL, :].astype(jnp.float32) * scale * gain[pl.ds(k * YS + y, 1), :]
         ).astype(jnp.bfloat16)
-    await_all(fetched)
-    kv[...] = product(normed, tiles, 4)
+    outgoing = fetch_all([(normed, normed_ref)], sems, 16)
+    kv[...] = product(normed, tiles, 1, fetched)
 
     def slot(j):
         return kv.at[pl.ds(pl.multiple_of(j * ROWS, ROWS), ROWS)]
 
-    outgoing = fetch_all([(slot(y), own_ref.at[pl.ds(TOTAL, ROWS)])], sems, 18)
-    outgoing += fetch_all(
-        [(tiles.at[p, 5], cache_ref.at[pl.ds(p * TILE, TILE)]) for p in range(SHARDS)], sems, 23
-    )
-    for r in (1, 2, 3):
-        sent[r - 1, pl.ds(TOTAL, ROWS), :] = slot(lax.rem(y + r, YS))[...].astype(jnp.bfloat16)
-    for r in (2, 1, 3):
-        sent[r - 1, pl.ds(0, TOTAL), :] = product(normed, tiles, r).astype(jnp.bfloat16)
-        outgoing += fetch_all([(sent.at[r - 1], parts[r - 1])], sems, 18 + r)
-    own[...] = product(normed, tiles, 0)
-    outgoing += fetch_all([(own, own_ref.at[pl.ds(0, TOTAL)])], sems, 22)
+    sent[pl.ds(TOTAL, ROWS), :] = slot(lax.rem(y + 2, YS))[...].astype(jnp.bfloat16)
+    for i, r in enumerate((1, 3)):
+        small[i] = slot(lax.rem(y + r, YS))[...].astype(jnp.bfloat16)
+    outgoing += fetch_all([(slot(y), kv_ref), (small, kv_parts)], sems, 17)
+    sent[pl.ds(0, TOTAL), :] = product(normed, tiles, 0).astype(jnp.bfloat16)
+    outgoing += fetch_all([(sent, part_ref)], sems, 19)
     await_all(outgoing)
 
 
-def project(place, gain, shards, weights):
+def project_first(place, gain, shards, weights):
     f32, bf16 = jnp.float32, jnp.bfloat16
     return pl.pallas_call(
-        project_kernel,
-        out_shape=[shaped((TOTAL + ROWS, TILE), f32)]
-        + [shaped((TOTAL + ROWS, TILE), bf16)] * 3
-        + [shaped((PROMPT_TOKENS, TILE), bf16)],
+        first_kernel,
+        out_shape=[
+            shaped((TOTAL, SHARDS * TILE), bf16),
+            shaped((TOTAL + ROWS, TILE), bf16),
+            shaped((ROWS, TILE), f32),
+            shaped((2, ROWS, TILE), bf16),
+        ],
         in_specs=[SMEM, VMEM] + [ANY] * 18,
-        out_specs=[ANY] * 5,
+        out_specs=[ANY] * 4,
         scratch_shapes=[
             pltpu.VMEM((SHARDS, TOTAL + EXTRA, TILE), bf16),
-            pltpu.VMEM((SHARDS, 6, TILE, TILE), bf16),
+            pltpu.VMEM((SHARDS, 2, TILE, TILE), bf16),
             pltpu.VMEM((TOTAL, SHARDS * TILE), bf16),
             pltpu.VMEM((TOTAL, TILE), f32),
-            pltpu.VMEM((TOTAL, TILE), f32),
-            pltpu.VMEM((3, TOTAL + ROWS, TILE), bf16),
-            pltpu.SemaphoreType.DMA((31,)),
+            pltpu.VMEM((TOTAL + ROWS, TILE), bf16),
+            pltpu.VMEM((2, ROWS, TILE), bf16),
+            pltpu.SemaphoreType.DMA((20,)),
         ],
         compiler_params=limit(56),
         cost_estimate=pl.CostEstimate(
-            flops=2 * TOTAL * 2048 * 1280, bytes_accessed=10 * 2**20, transcendentals=0
+            flops=2 * TOTAL * 2048 * 512, bytes_accessed=6 * 2**20, transcendentals=0
         ),
-        name="project",
+        name="project_first",
     )(place, gain, *shards, *weights)
+
+
+def second_kernel(normed_ref, kv_parts, *refs):
+    weights, parts = refs[:10], refs[10:12]
+    tiles, normed, sent, sems = refs[12:]
+    rows = fetch_all([(normed_ref, normed)], sems)
+    fetched = block_copies(weights, tiles, 1, 2, sems, 1)
+    last = pl.ds(TOTAL, ROWS)
+    small = fetch_all([(kv_parts.at[i], sent.at[i, last]) for i in range(2)], sems, 9)
+    await_all(rows)
+    outgoing = []
+    for i in range(2):
+        found = product(normed, tiles, i, fetched if i == 0 else None)
+        sent[i, pl.ds(0, TOTAL), :] = found.astype(jnp.bfloat16)
+        small[i].wait()
+        outgoing += fetch_all([(sent.at[i], parts[i])], sems, 11 + i)
+    await_all(outgoing)
+
+
+def project_second(normed, kv_parts, weights):
+    bf16 = jnp.bfloat16
+    return pl.pallas_call(
+        second_kernel,
+        out_shape=[shaped((TOTAL + ROWS, TILE), bf16)] * 2,
+        in_specs=[ANY] * 12,
+        out_specs=[ANY] * 2,
+        scratch_shapes=[
+            pltpu.VMEM((SHARDS, 2, TILE, TILE), bf16),
+            pltpu.VMEM((TOTAL, SHARDS * TILE), bf16),
+            pltpu.VMEM((2, TOTAL + ROWS, TILE), bf16),
+            pltpu.SemaphoreType.DMA((13,)),
+        ],
+        compiler_params=limit(56),
+        cost_estimate=pl.CostEstimate(
+            flops=2 * TOTAL * 2048 * 512, bytes_accessed=6 * 2**20, transcendentals=0
+        ),
+        name="project_second",
+    )(normed, kv_parts, *weights)
+
+
+def third_kernel(normed_ref, kv_ref, _, *refs):
+    weights, own_ref = refs[:10], refs[10]
+    tiles, normed, own, sems = refs[11:]
+    rows = fetch_all([(normed_ref, normed)], sems)
+    fetched = block_copies(weights, tiles, 0, 1, sems, 1)
+    small = fetch_all([(kv_ref, own.at[pl.ds(TOTAL, ROWS)])], sems, 9)
+    await_all(rows)
+    own[pl.ds(0, TOTAL), :] = product(normed, tiles, 0, fetched)
+    await_all(small)
+    await_all(fetch_all([(own, own_ref)], sems, 10))
+
+
+def project_third(normed, kv_own, after, weights):
+    return pl.pallas_call(
+        third_kernel,
+        out_shape=shaped((TOTAL + ROWS, TILE), jnp.float32),
+        in_specs=[ANY] * 13,
+        out_specs=ANY,
+        scratch_shapes=[
+            pltpu.VMEM((SHARDS, 1, TILE, TILE), jnp.bfloat16),
+            pltpu.VMEM((TOTAL, SHARDS * TILE), jnp.bfloat16),
+            pltpu.VMEM((TOTAL + ROWS, TILE), jnp.float32),
+            pltpu.SemaphoreType.DMA((11,)),
+        ],
+        compiler_params=limit(56),
+        name="project_third",
+    )(normed, kv_own, after, *weights)
+
+
+def gather_kernel(*refs):
+    weights, cache_ref, caches, sems = refs[:10], refs[10], refs[11], refs[12]
+    outgoing = []
+    for p, copy in enumerate(block_copies(weights, caches, 5, 1, sems, 0)):
+        copy.wait()
+        here = cache_ref.at[pl.ds(p * TILE, TILE)]
+        outgoing += fetch_all([(caches.at[p, 0], here)], sems, SHARDS + p)
+    await_all(outgoing)
+
+
+def gather_cache(weights):
+    return pl.pallas_call(
+        gather_kernel,
+        out_shape=shaped((PROMPT_TOKENS, TILE), jnp.bfloat16),
+        in_specs=[ANY] * 10,
+        out_specs=ANY,
+        scratch_shapes=[
+            pltpu.VMEM((SHARDS, 1, TILE, TILE), jnp.bfloat16),
+            pltpu.SemaphoreType.DMA((2 * SHARDS,)),
+        ],
+        compiler_params=limit(56),
+        name="gather",
+    )(*weights)
 
 
 def rotate(v, cosine, sine):
     return v * cosine + swap_halves(v) * sine
 
 
-def fresh_kernel(own, p1, p2, p3, cosine, sine, out):
+def fresh_kernel(own, p1, p3, cosine, sine, out):
     v = own[...]
-    for part in (p1, p2, p3):
+    for part in (p1, p3):
         v = v + part[...].astype(jnp.float32)
     out[:, :HEAD_SIZE] = rotate(v[:, :HEAD_SIZE], cosine[...], sine[...]).astype(jnp.bfloat16)
     out[:, HEAD_SIZE:] = v[:, HEAD_SIZE:].astype(jnp.bfloat16)
@@ -375,7 +464,7 @@
         fresh_kernel,
         out_shape=shaped((ROWS, TILE), jnp.bfloat16),
         grid=(1,),
-        in_specs=[last] * 4 + [table] * 2,
+        in_specs=[last] * 3 + [table] * 2,
         out_specs=pl.BlockSpec((ROWS, TILE), lambda i: (0, 0)),
         compiler_params=limit(4),
         name="fresh",
@@ -385,27 +474,30 @@
 FACTOR = HEAD_SIZE**-0.5 * 1.4426950408889634
 
 
-def stage_kernel(own_ref, cache_ref, own, cache, sems):
-    await_all(fetch_all([(own_ref, own), (cache_ref, cache)], sems))
-
-
-def stage(own, cache):
+def stage_kernel(own_ref, cache_ref, part, own, cache, sems):
+    copies = fetch_all([(own_ref, own), (cache_ref, cache)], sems)
+    copies[0].wait()
+    own[...] += part[...].astype(jnp.float32)
+    copies[1].wait()
+
+
+def stage(own, cache, part):
     return pl.pallas_call(
         stage_kernel,
         out_shape=[shaped(own.shape, own.dtype), shaped(cache.shape, cache.dtype)],
-        in_specs=[ANY] * 2,
+        in_specs=[ANY] * 2 + [VMEM],
         out_specs=[VMEM] * 2,
         scratch_shapes=[pltpu.SemaphoreType.DMA((2,))],
         compiler_params=limit(2),
         name="stage",
-    )(own, cache)
-
-
-def prompt_kernel(own, p1, p2, p3, cosine, sine, caches, q_ref, mixed_ref, top_ref, total_ref):
+    )(own, cache, part)
+
+
+def prompt_kernel(own, p1, p3, cosine, sine, caches, q_ref, mixed_ref, top_ref, total_ref):
     def step(j, _):
         rows = pl.ds(pl.multiple_of(j * ROWS, ROWS), ROWS)
         q = own[rows, :]
-        for part in (p1, p2, p3):
+        for part in (p1, p3):
             q = q + part[rows, :].astype(jnp.float32)
         halves = (q[:, :HEAD_SIZE], q[:, HEAD_SIZE:])
         wide_q = jnp.concatenate(
@@ -445,7 +537,7 @@
     return pl.pallas_call(
         prompt_kernel,
         out_shape=[shaped(per_slot, jnp.bfloat16)] + [shaped(per_slot, jnp.float32)] * 3,
-        in_specs=[VMEM] * 7,
+        in_specs=[VMEM] * 6,
         out_specs=[VMEM] * 4,
         compiler_params=limit(16),
         cost_estimate=pl.CostEstimate(
@@ -529,13 +621,15 @@
     pieces[0], pieces[1] = tie((pieces[0], pieces[1]))
     slots, pieces[0] = plan(place, keep_flag, destination, row_counts, pieces[0])
     arrived = [send_y(part1, -1), send_y(part2, -2), send_y(part3, -3)]
-    pieces, arrived = tie((pieces, arrived))
+    pieces, arrived[0] = tie((pieces, arrived[0]))
     inward, outward = sort_pieces(slots, pieces)
     rows, sums = unpack(slots, inward, swap(outward))
     sums = [sums] + [send_y(sums, r) for r in (1, 2, 3)]
 
+    sums, arrived = tie((sums, arrived))
     rows = label(rows, sums)
-    own = jnp.concatenate([own_parts[:1], jnp.stack(arrived), own_parts[1:]], axis=0)
+    arrived = jnp.stack([arrived[0], arrived[2], arrived[1]])
+    own = jnp.concatenate([own_parts[:1], arrived, own_parts[1:]], axis=0)
     near, next_ = send_x(own, 1), send_x(own, -1)
     rows, own = tie((rows, own))
     a1, b1, own_swapped = send_z(rows, 1), send_z(rows, -1), swap(own)
@@ -551,10 +645,15 @@
     weights = [own, near, next_, far_a, far_b]
     weights += [own_swapped, near_swapped, next_swapped, far_a_swapped, far_b_swapped]
     gain = norm_gain.astype(jnp.float32).reshape(ZS * YS, TILE)
-    q_own, *parts, cache = project(place, gain, shards, weights)
-
-    parts = [send_y(v, r) for r, v in zip((1, 2, 3), parts)]
-    q_own, cache = stage(q_own, cache)
+    cache = gather_cache(weights)
+    gain, cache = tie((gain, cache))
+    normed, part2, kv_own, kv_parts = project_first(place, gain, shards, weights)
+    part2 = send_y(part2, 2)
+    part1, part3 = project_second(normed, kv_parts, weights)
+
+    parts = [send_y(part1, 1), send_y(part3, 3)]
+    q_own = project_third(normed, kv_own, part1, weights)
+    q_own, cache = stage(q_own, cache, part2)
     cosine, sine = rope_tables(ROWS, PROMPT_TOKENS)
     fresh = fresh_keys(q_own, parts, cosine, sine)
     fresh = [fresh] + [send_y(fresh, r) for r in (1, 2, 3)]

time: 115 us -> 111 us (0.965)
  waiting for transfers between devices: 41.3 us -> 29.3 us
  Pallas kernels: 23.3 us -> 31.9 us
  local copies, waits for them, and re-layouts: 4.91 us -> 3.69 us
  starting transfers between devices: 43.7 us -> 44.9 us
    ppermute x12, waiting for transfers between devices: 14.3 us -> 2.85 us  [send_y(): return lax.ppermute(v, 'fsdp', perm)]
    pallas_call x2 -> x5, Pallas kernels: 11.1 us -> 19.7 us  [the longest x1 6.58 us: project_first(): pl.pallas_call(first_kernel, out_shape=[shaped((TOTAL, SHARDS * TILE), bf...]
    ppermute x7, waiting for transfers between devices: 23.8 us -> 16.9 us  [send_z(): return lax.ppermute(v, 'fsdp', perm)]
    ppermute x7, waiting for transfers between devices: 1.83 us -> 6.46 us  [send_x(): return lax.ppermute(v, 'group', perm)]
    ppermute x12, starting transfers between devices: 18.1 us -> 20.7 us  [send_y(): return lax.ppermute(v, 'fsdp', perm)]
    ppermute x6, waiting for transfers between devices: 1.48 us -> 3.07 us  [swap(): return lax.ppermute(v, 'group', [(g, g ^ 1) for g in range(XS * CORES)])]
    unnamed x44, local copies, waits for them, and re-layouts: 4.22 us -> 2.99 us
  transfers between devices with their start and end apart: 32 -> 32, of which waited for: 15 -> 18; matrix products, arithmetic and copies ran while one was open for 2% -> 2% of each run, Pallas kernels for 7% -> 17%
where the time goes in v6:
time: 111 us
  starting transfers between devices  44.9 us (40%)
  Pallas kernels  31.9 us (29%)
  waiting for transfers between devices  29.3 us (26%)
  local copies, waits for them, and re-layouts  3.69 us (3%)
    ppermute x12, starting transfers between devices, send_y(): return lax.ppermute(v, 'fsdp', perm)  20.7 us
    ppermute x7, waiting for transfers between devices, send_z(): return lax.ppermute(v, 'fsdp', perm)  16.9 us
    ppermute x7, starting transfers between devices, send_z(): return lax.ppermute(v, 'fsdp', perm)  13.3 us
    ppermute x7, starting transfers between devices, send_x(): return lax.ppermute(v, 'group', perm)  9.56 us
    pallas_call x1, Pallas kernels, project_first(): pl.pallas_call(first_kernel, out_shape=[shaped((TOTAL, SHARDS * TILE), bf...  6.58 us
    ppermute x7, waiting for transfers between devices, send_x(): return lax.ppermute(v, 'group', perm)  6.46 us
    pallas_call x1, Pallas kernels, project_second(): pl.pallas_call(second_kernel, out_shape=[shaped((TOTAL + ROWS, TILE), bf1...  5.18 us
    pallas_call x1, Pallas kernels, attend_prompt(): pl.pallas_call(prompt_kernel, out_shape=[shaped(per_slot, jnp.bfloat16)]...  4.51 us
  transfers between devices with their start and end apart: 32, of which 18 were waited for; matrix products, arithmetic and copies ran while one was open for 2% of the time, Pallas kernels for 17%

profile of v6, /device:TPU:8, one launch (start us, length us, event | category | flops | bytes accessed | tf_op | source)
XLA Modules:
  0.0 110.7 jit_solution(7873586863291913719)
XLA Ops:
  0.0 3.4 %pack.1 = (bf16[2,128,256]{2,1,0:T(8,128)(2,1)}, bf16[2,128,256]{2,1,0:T(8,128)(2,1)}, bf16[2,128,256]{2,1,0:T(8,128)(2,1)}, bf16[2,128,256]{2,1,0:T(8,128)(2,1)...) custom-call(s32[64]{0:T(128)} %keep.3, ...), custom_call_target="tpu_custom_call" | custom-call | tf_op jit(solution)/shard_map/pack/pallas_call | solution.py:134
  3.4 1.6 %collective-permute-start = (bf16[2,128,256]{2,1,0:T(8,128)(2,1)}, bf16[2,128,256]{2,1,0:T(8,128)(2,1)S(1)}, u32[]{:S(2)}, u32[]{:S(2)}) collective-permute-start(bf16[2,128,256]{2,1,0:T(8,128)(2,1)} %get-tuple-element.63), channel_id=1, source_target_pairs={{0,64},{32,96},{64,0},{96,32},{128,192},{160,224},{192,128},{224,1... | collective-permute-start | bytes 393224 | tf_op jit(solution)/shard_map/ppermute | solution.py:31
  5.0 2.8 %collective-permute-start.1 = (bf16[2,128,256]{2,1,0:T(8,128)(2,1)}, bf16[2,128,256]{2,1,0:T(8,128)(2,1)S(1)}, u32[]{:S(2)}, u32[]{:S(2)}) collective-permute-start(bf16[2,128,256]{2,1,0:T(8,128)(2,1)} %get-tuple-element.68), channel_id=1, source_target_pairs={{0,128},{32,160},{64,192},{96,224},{128,0},{160,32},{192,64},{224,... | collective-permute-start | bytes 393224 | tf_op jit(solution)/shard_map/ppermute | solution.py:31
  8.2 2.2 %collective-permute-start.3 = (bf16[256,256]{1,0:T(8,128)(2,1)}, bf16[256,256]{1,0:T(8,128)(2,1)S(1)}, u32[]{:S(2)}, u32[]{:S(2)}) collective-permute-start(bf16[256,256]{1,0:T(8,128)(2,1)} %get-tuple-element.70), channel_id=1, source_target_pairs={{0,3},{1,0},{2,1},{3,2},{4,7},{5,4},{6,5},{7,6},{8,11},{9,8},{10,9... | collective-permute-start | bytes 393224 | tf_op jit(solution)/shard_map/ppermute | solution.py:45
  10.5 0.9 copy-done.3
  11.4 1.6 %plan.1 = (s32[16]{0:T(128)S(1)}, bf16[2,128,256]{2,1,0:T(8,128)(2,1)S(1)}) custom-call(s32[4]{0:T(128)S(1)} %pad_add_fusion.place, s32[64]{0:T(128)S(1)} %copy-done.6, s32[64]{0:T(128)S(1)} %copy-done.7, s32[64]{0:T(128)S(1)} %copy-done.8, bf16[2,128,256]{2,1,0:T(8,128)(2,1)S(1)} %copy-done.3), custom_call_target="tpu_custom_call" | custom-call | tf_op jit(solution)/shard_map/plan/pallas_call | solution.py:167
  12.9 1.1 collective-permute-done.1.refs_2_
  14.0 2.0 %collective-permute-done.2.refs_3_ = bf16[2,128,256]{2,1,0:T(8,128)(2,1)S(1)} collective-permute-done((bf16[2,128,256]{2,1,0:T(8,128)(2,1)}, bf16[2,128,256]{2,1,0:T(8,128)(2,1)S(1)}, u32[]{:S(2)}, u32[]{:S(2)}) %collective-permute-start.2) | collective-permute-done | bytes 131104 | tf_op jit(solution)/shard_map/ppermute | solution.py:31
  16.1 0.8 sort.1
  17.0 2.4 %collective-permute-start.8 = (bf16[256,256]{1,0:T(8,128)(2,1)}, bf16[256,256]{1,0:T(8,128)(2,1)S(1)}, u32[]{:S(2)}, u32[]{:S(2)}) collective-permute-start(bf16[256,256]{1,0:T(8,128)(2,1)} %get-tuple-element.80), channel_id=1, source_target_pairs={{0,2},{1,3},{2,0},{3,1},{4,6},{5,7},{6,4},{7,5},{8,10},{9,11},{10,... | collective-permute-start | bytes 393224 | tf_op jit(solution)/shard_map/ppermute | solution.py:45
  19.4 1.1 %unpack.1 = (bf16[512,256]{1,0:T(8,128)(2,1)S(1)}, f32[8,512]{1,0:T(8,128)S(1)}) custom-call(s32[16]{0:T(128)S(1)} %get-tuple-element.65.source.slots, bf16[512,256]{1,0:T(8,128)(2,1)S(1)} %get-tuple-element.75.held, bf16[512,256]{1,0:T(8,128)(2,1)S(1)} %collective-permute-done.4.swapped), custom_call_target="tpu_custom_call" | custom-call | tf_op jit(solution)/shard_map/unpack/pallas_call | solution.py:228
  20.5 1.8 %collective-permute-start.5 = (f32[8,512]{1,0:T(8,128)S(1)}, f32[8,512]{1,0:T(8,128)S(1)}, u32[]{:S(2)}, u32[]{:S(2)}) collective-permute-start(f32[8,512]{1,0:T(8,128)S(1)} %get-tuple-element.82.s0), channel_id=1, source_target_pairs={{0,1},{1,2},{2,3},{3,0},{4,5},{5,6},{6,7},{7,4},{8,9},{9,10},{10,1... | collective-permute-start | bytes 49160 | tf_op jit(solution)/shard_map/ppermute | solution.py:45
  22.3 2.3 %collective-permute-start.6 = (f32[8,512]{1,0:T(8,128)S(1)}, f32[8,512]{1,0:T(8,128)S(1)}, u32[]{:S(2)}, u32[]{:S(2)}) collective-permute-start(f32[8,512]{1,0:T(8,128)S(1)} %get-tuple-element.82.s0), channel_id=1, source_target_pairs={{0,2},{1,3},{2,0},{3,1},{4,6},{5,7},{6,4},{7,5},{8,10},{9,11},{10,... | collective-permute-start | bytes 49160 | tf_op jit(solution)/shard_map/ppermute | solution.py:45
  24.6 1.9 %collective-permute-start.7 = (f32[8,512]{1,0:T(8,128)S(1)}, f32[8,512]{1,0:T(8,128)S(1)}, u32[]{:S(2)}, u32[]{:S(2)}) collective-permute-start(f32[8,512]{1,0:T(8,128)S(1)} %get-tuple-element.82.s0), channel_id=1, source_target_pairs={{0,3},{1,0},{2,1},{3,2},{4,7},{5,4},{6,5},{7,6},{8,11},{9,8},{10,9... | collective-permute-start | bytes 49160 | tf_op jit(solution)/shard_map/ppermute | solution.py:45
  26.5 0.9 slice_dynamic-update-slice_fusion.1
  28.7 1.4 %collective-permute-start.16 = (bf16[6,256,256]{2,1,0:T(8,128)(2,1)S(1)}, bf16[6,256,256]{2,1,0:T(8,128)(2,1)S(1)}, u32[]{:S(2)}, u32[]{:S(2)}) collective-permute-start(bf16[6,256,256]{2,1,0:T(8,128)(2,1)S(1)} %slice_dynamic-update-slice_fusion.refs_0_.refs_8_), channel_id=1, source_target_pairs={{0,192},{32,224},{64,128},{96,160},{128,64},{160,96},{192,0},{224,... | collective-permute-start | bytes 2359304 | tf_op jit(solution)/shard_map/ppermute | solution.py:31
  30.1 1.9 %collective-permute-start.10 = (bf16[528,256]{1,0:T(8,128)(2,1)S(1)}, bf16[528,256]{1,0:T(8,128)(2,1)S(1)}, u32[]{:S(2)}, u32[]{:S(2)}) collective-permute-start(bf16[528,256]{1,0:T(8,128)(2,1)S(1)} %label.1.refs_0_), channel_id=1, source_target_pairs={{0,4},{1,5},{2,6},{3,7},{4,0},{5,1},{6,2},{7,3},{8,12},{9,13},{10,... | collective-permute-start | bytes 811016 | tf_op jit(solution)/shard_map/ppermute | solution.py:40
  32.0 4.9 %collective-permute-start.11 = (bf16[528,256]{1,0:T(8,128)(2,1)S(1)}, bf16[528,256]{1,0:T(8,128)(2,1)S(1)}, u32[]{:S(2)}, u32[]{:S(2)}) collective-permute-start(bf16[528,256]{1,0:T(8,128)(2,1)S(1)} %label.1.refs_0_), channel_id=1, source_target_pairs={{0,28},{1,29},{2,30},{3,31},{4,8},{5,9},{6,10},{7,11},{8,4},{9,5},... | collective-permute-start | bytes 811016 | tf_op jit(solution)/shard_map/ppermute | solution.py:40
  36.9 1.8 %collective-permute-done.10.refs_1_ = bf16[528,256]{1,0:T(8,128)(2,1)S(1)} collective-permute-done((bf16[528,256]{1,0:T(8,128)(2,1)S(1)}, bf16[528,256]{1,0:T(8,128)(2,1)S(1)}, u32[]{:S(2)}, u32[]{:S(2)}) %collective-permute-start.10) | collective-permute-done | bytes 270368 | tf_op jit(solution)/shard_map/ppermute | solution.py:40
  38.7 4.6 %collective-permute-done.11.refs_4_ = bf16[528,256]{1,0:T(8,128)(2,1)S(1)} collective-permute-done((bf16[528,256]{1,0:T(8,128)(2,1)S(1)}, bf16[528,256]{1,0:T(8,128)(2,1)S(1)}, u32[]{:S(2)}, u32[]{:S(2)}) %collective-permute-start.11) | collective-permute-done | bytes 270368 | tf_op jit(solution)/shard_map/ppermute | solution.py:40
  43.4 3.0 %collective-permute-start.14 = (bf16[528,256]{1,0:T(8,128)(2,1)S(1)}, bf16[528,256]{1,0:T(8,128)(2,1)S(1)}, u32[]{:S(2)}, u32[]{:S(2)}) collective-permute-start(bf16[528,256]{1,0:T(8,128)(2,1)S(1)} %collective-permute-done.10.refs_1_), channel_id=1, source_target_pairs={{0,28},{1,29},{2,30},{3,31},{4,8},{5,9},{6,10},{7,11},{8,4},{9,5},... | collective-permute-start | bytes 811016 | tf_op jit(solution)/shard_map/ppermute | solution.py:40
  46.4 2.1 %collective-permute-done.15.refs_1_.refs_9_ = bf16[6,256,256]{2,1,0:T(8,128)(2,1)S(1)} collective-permute-done((bf16[6,256,256]{2,1,0:T(8,128)(2,1)S(1)}, bf16[6,256,256]{2,1,0:T(8,128)(2,1)S(1)}, u32[]{:S(2)}, u32[]{:S(2)}) %collective-permute-start.15) | collective-permute-done | bytes 786464 | tf_op jit(solution)/shard_map/ppermute | solution.py:31
  48.6 1.2 %collective-permute-done.16.refs_2_.refs_10_ = bf16[6,256,256]{2,1,0:T(8,128)(2,1)S(1)} collective-permute-done((bf16[6,256,256]{2,1,0:T(8,128)(2,1)S(1)}, bf16[6,256,256]{2,1,0:T(8,128)(2,1)S(1)}, u32[]{:S(2)}, u32[]{:S(2)}) %collective-permute-start.16) | collective-permute-done | bytes 786464 | tf_op jit(solution)/shard_map/ppermute | solution.py:31
  49.8 1.2 %collective-permute-done.13.refs_2_ = bf16[528,256]{1,0:T(8,128)(2,1)S(1)} collective-permute-done((bf16[528,256]{1,0:T(8,128)(2,1)S(1)}, bf16[528,256]{1,0:T(8,128)(2,1)S(1)}, u32[]{:S(2)}, u32[]{:S(2)}) %collective-permute-start.13) | collective-permute-done | bytes 270368 | tf_op jit(solution)/shard_map/ppermute | solution.py:40
  51.0 1.3 %collective-permute-done.14.refs_5_ = bf16[528,256]{1,0:T(8,128)(2,1)S(1)} collective-permute-done((bf16[528,256]{1,0:T(8,128)(2,1)S(1)}, bf16[528,256]{1,0:T(8,128)(2,1)S(1)}, u32[]{:S(2)}, u32[]{:S(2)}) %collective-permute-start.14) | collective-permute-done | bytes 270368 | tf_op jit(solution)/shard_map/ppermute | solution.py:40
  52.3 1.2 %collective-permute-start.19 = (bf16[3,256,256]{2,1,0:T(8,128)(2,1)S(1)}, bf16[3,256,256]{2,1,0:T(8,128)(2,1)}, u32[]{:S(2)}, u32[]{:S(2)}) collective-permute-start(bf16[3,256,256]{2,1,0:T(8,128)(2,1)S(1)} %slice.14), channel_id=1, source_target_pairs={{0,64},{32,96},{64,0},{96,32},{128,192},{160,224},{192,128},{224,1... | collective-permute-start | bytes 1179656 | tf_op jit(solution)/shard_map/ppermute | solution.py:31
  53.6 2.1 %collective-permute-start.20 = (bf16[3,256,256]{2,1,0:T(8,128)(2,1)S(1)}, bf16[3,256,256]{2,1,0:T(8,128)(2,1)}, u32[]{:S(2)}, u32[]{:S(2)}) collective-permute-start(bf16[3,256,256]{2,1,0:T(8,128)(2,1)S(1)} %slice.15), channel_id=1, source_target_pairs={{0,192},{32,224},{64,128},{96,160},{128,64},{160,96},{192,0},{224,... | collective-permute-start | bytes 1179656 | tf_op jit(solution)/shard_map/ppermute | solution.py:31
  56.1 2.8 %collective-permute-start.18 = (bf16[528,256]{1,0:T(8,128)(2,1)S(1)}, bf16[528,256]{1,0:T(8,128)(2,1)}, u32[]{:S(2)}, u32[]{:S(2)}) collective-permute-start(bf16[528,256]{1,0:T(8,128)(2,1)S(1)} %collective-permute-done.13.refs_2_), channel_id=1, source_target_pairs={{0,28},{1,29},{2,30},{3,31},{4,8},{5,9},{6,10},{7,11},{8,4},{9,5},... | collective-permute-start | bytes 811016 | tf_op jit(solution)/shard_map/ppermute | solution.py:40
  58.9 3.2 %collective-permute-done.17.refs_3_ = bf16[528,256]{1,0:T(8,128)(2,1)S(1)} collective-permute-done((bf16[528,256]{1,0:T(8,128)(2,1)S(1)}, bf16[528,256]{1,0:T(8,128)(2,1)S(1)}, u32[]{:S(2)}, u32[]{:S(2)}) %collective-permute-start.17) | collective-permute-done | bytes 270368 | tf_op jit(solution)/shard_map/ppermute | solution.py:40
  62.1 2.0 %collective-permute-done.18.refs_6_ = bf16[528,256]{1,0:T(8,128)(2,1)} collective-permute-done((bf16[528,256]{1,0:T(8,128)(2,1)S(1)}, bf16[528,256]{1,0:T(8,128)(2,1)}, u32[]{:S(2)}, u32[]{:S(2)}) %collective-permute-start.18) | collective-permute-done | bytes 270368 | tf_op jit(solution)/shard_map/ppermute | solution.py:40
  65.4 0.6 reshape.28.gain
  66.0 1.9 %collective-permute-done.23.refs_8_.refs_16_ = bf16[3,256,256]{2,1,0:T(8,128)(2,1)} collective-permute-done((bf16[3,256,256]{2,1,0:T(8,128)(2,1)}, bf16[3,256,256]{2,1,0:T(8,128)(2,1)}, u32[]{:S(2)}, u32[]{:S(2)}) %collective-permute-start.23) | collective-permute-done | bytes 393248 | tf_op jit(solution)/shard_map/ppermute | solution.py:35
  68.0 1.1 %collective-permute-done.24.refs_9_.refs_17_ = bf16[3,256,256]{2,1,0:T(8,128)(2,1)} collective-permute-done((bf16[3,256,256]{2,1,0:T(8,128)(2,1)}, bf16[3,256,256]{2,1,0:T(8,128)(2,1)}, u32[]{:S(2)}, u32[]{:S(2)}) %collective-permute-start.24) | collective-permute-done | bytes 393248 | tf_op jit(solution)/shard_map/ppermute | solution.py:35
  69.1 2.1 %gather.1.cache_ref = bf16[2048,256]{1,0:T(8,128)(2,1)} custom-call(bf16[6,256,256]{2,1,0:T(8,128)(2,1)} %copy-done.11, bf16[6,256,256]{2,1,0:T(8,128)(2,1)} %copy-done.9, bf16[6,256,256]{2,1,0:T(8,128)(2,1)} %copy-done.10, bf16[3,256,256]{2,1,0:T(8,128)(2,1)} %collective-permute-done.19.refs_3_.refs_11_, ...), custom_call_target="tpu_custom_call" | custom-call | tf_op jit(solution)/shard_map/gather/pallas_call | solution.py:434
  71.3 2.8 %collective-permute-done.25.refs_7_ = bf16[528,256]{1,0:T(8,128)(2,1)} collective-permute-done((bf16[528,256]{1,0:T(8,128)(2,1)}, bf16[528,256]{1,0:T(8,128)(2,1)}, u32[]{:S(2)}, u32[]{:S(2)}) %collective-permute-start.25) | collective-permute-done | bytes 270368 | tf_op jit(solution)/shard_map/ppermute | solution.py:40
  74.1 6.6 %project_first.1 = (bf16[512,2048]{1,0:T(8,128)(2,1)}, bf16[640,256]{1,0:T(8,128)(2,1)}, f32[128,256]{1,0:T(8,128)}, bf16[2,128,256]{2,1,0:T(8,128)(2,1)}) custom-call(s32[4]{0:T(128)} %copy-done.4, f32[32,256]{1,0:T(8,128)} %reshape.28.gain, bf16[528,256]{1,0:T(8,128)(2,1)} %copy-done.2, bf16[528,256]{1,0:T(8,128)(2,1)} %copy-done.14, ...), custom_call_target="tpu_custom_call" | custom-call | flops 1073741824 | bytes 6291456 | tf_op jit(solution)/shard_map/project_first/pallas_call | solution.py:329
  80.7 2.4 %collective-permute-start.26 = (bf16[640,256]{1,0:T(8,128)(2,1)}, bf16[640,256]{1,0:T(8,128)(2,1)S(1)}, u32[]{:S(2)}, u32[]{:S(2)}) collective-permute-start(bf16[640,256]{1,0:T(8,128)(2,1)} %get-tuple-element.111), channel_id=1, source_target_pairs={{0,2},{1,3},{2,0},{3,1},{4,6},{5,7},{6,4},{7,5},{8,10},{9,11},{10,... | collective-permute-start | bytes 983048 | tf_op jit(solution)/shard_map/ppermute | solution.py:45
  83.0 5.2 %project_second.1 = (bf16[640,256]{1,0:T(8,128)(2,1)}, bf16[640,256]{1,0:T(8,128)(2,1)}) custom-call(bf16[512,2048]{1,0:T(8,128)(2,1)} %get-tuple-element.106.normed_ref, bf16[2,128,256]{2,1,0:T(8,128)(2,1)} %get-tuple-element.108.kv_parts, bf16[6,256,256]{2,1,0:T(8,128)(2,1)} %copy-done.11, bf16[6,256,256]{2,1,0:T(8,128)(2,1)} %copy-done.9, ...), custom_call_target="tpu_custom_call" | custom-call | flops 1073741824 | bytes 6291456 | tf_op jit(solution)/shard_map/project_second/pallas_call | solution.py:375
  88.2 1.0 collective-permute-start.27
  89.2 1.1 collective-permute-start.28
  90.7 4.2 %project_third.1.own_ref = f32[640,256]{1,0:T(8,128)} custom-call(bf16[512,2048]{1,0:T(8,128)(2,1)} %get-tuple-element.106.normed_ref, f32[128,256]{1,0:T(8,128)} %get-tuple-element.107.kv_ref, bf16[640,256]{1,0:T(8,128)(2,1)} %get-tuple-element.109._, bf16[6,256,256]{2,1,0:T(8,128)(2,1)} %copy-done.11, bf16[6,256,256]{2,1,0:T(8,128)(2,1)} %copy-done.9, ...), custom_call_target="tpu_custom_call" | custom-call | tf_op jit(solution)/shard_map/project_third/pallas_call | solution.py:407
  95.0 1.1 copy-done.1
  96.4 1.7 %collective-permute-done.27.p1 = bf16[640,256]{1,0:T(8,128)(2,1)S(1)} collective-permute-done((bf16[640,256]{1,0:T(8,128)(2,1)}, bf16[640,256]{1,0:T(8,128)(2,1)S(1)}, u32[]{:S(2)}, u32[]{:S(2)}) %collective-permute-start.27) | collective-permute-done | bytes 327712 | tf_op jit(solution)/shard_map/ppermute | solution.py:45
  98.5 1.5 %collective-permute-start.29 = (bf16[128,256]{1,0:T(8,128)(2,1)S(1)}, bf16[128,256]{1,0:T(8,128)(2,1)S(1)}, u32[]{:S(2)}, u32[]{:S(2)}) collective-permute-start(bf16[128,256]{1,0:T(8,128)(2,1)S(1)} %fresh.1.f0), channel_id=1, source_target_pairs={{0,1},{1,2},{2,3},{3,0},{4,5},{5,6},{6,7},{7,4},{8,9},{9,10},{10,1... | collective-permute-start | bytes 196616 | tf_op jit(solution)/shard_map/ppermute | solution.py:45
  100.0 2.8 %collective-permute-start.30 = (bf16[128,256]{1,0:T(8,128)(2,1)S(1)}, bf16[128,256]{1,0:T(8,128)(2,1)S(1)}, u32[]{:S(2)}, u32[]{:S(2)}) collective-permute-start(bf16[128,256]{1,0:T(8,128)(2,1)S(1)} %fresh.1.f0), channel_id=1, source_target_pairs={{0,2},{1,3},{2,0},{3,1},{4,6},{5,7},{6,4},{7,5},{8,10},{9,11},{10,... | collective-permute-start | bytes 196616 | tf_op jit(solution)/shard_map/ppermute | solution.py:45
  102.7 1.4 %collective-permute-start.31 = (bf16[128,256]{1,0:T(8,128)(2,1)S(1)}, bf16[128,256]{1,0:T(8,128)(2,1)S(1)}, u32[]{:S(2)}, u32[]{:S(2)}) collective-permute-start(bf16[128,256]{1,0:T(8,128)(2,1)S(1)} %fresh.1.f0), channel_id=1, source_target_pairs={{0,3},{1,0},{2,1},{3,2},{4,7},{5,4},{6,5},{7,6},{8,11},{9,8},{10,9... | collective-permute-start | bytes 196616 | tf_op jit(solution)/shard_map/ppermute | solution.py:45
  104.2 4.5 %prompt.1 = (bf16[4,256,128]{2,1,0:T(8,128)(2,1)S(1)}, f32[4,256,128]{2,1,0:T(8,128)S(1)}, f32[4,256,128]{2,1,0:T(8,128)S(1)}, f32[4,256,128]{2,1,0:T(8,128)S(1)}) custom-call(f32[640,256]{1,0:T(8,128)S(1)} %get-tuple-element.112.own, bf16[640,256]{1,0:T(8,128)(2,1)S(1)} %collective-permute-done.27.p1, bf16[640,256]{1,0:T(8,128)(2,1)S(1)} %collective-permute-done.28.p3, ...), custom_call_target="tpu_custom_call" | custom-call | flops 1073741824 | bytes 2097152 | tf_op jit(solution)/shard_map/prompt/pallas_call | solution.py:537
  108.7 2.0 %finish.1 = bf16[4,128,256]{2,1,0:T(8,128)(2,1)} custom-call(s32[4]{0:T(128)S(1)} %copy-done.5, s32[16]{0:T(128)S(1)} %get-tuple-element.65.source.slots, bf16[4,256,128]{2,1,0:T(8,128)(2,1)S(1)} %get-tuple-element.115.q, f32[4,256,128]{2,1,0:T(8,128)S(1)} %get-tuple-element.116.mixed_ref, f32[4,256,128]{2,1,0:T(8,128)S(1)} %get-tuple-element.117.top_ref, ...), custom_call_target="tpu_custom_call" | custom-call | tf_op jit(solution)/shard_map/finish/pallas_call | solution.py:580
  (82 shorter events, 4.8 us)
Async XLA Ops:
  0.0 10.4 %copy-start.6 = (s32[64]{0:T(128)S(1)}, s32[64]{0:T(128)}, u32[]{:S(2)}) copy-start(s32[64]{0:T(128)} %keep.3) | copy-start | bytes 772
  0.0 10.4 %copy-start.7 = (s32[64]{0:T(128)S(1)}, s32[64]{0:T(128)}, u32[]{:S(2)}) copy-start(s32[64]{0:T(128)} %destination.3) | copy-start | bytes 772
  0.0 10.5 %copy-start.8 = (s32[64]{0:T(128)S(1)}, s32[64]{0:T(128)}, u32[]{:S(2)}) copy-start(s32[64]{0:T(128)} %counts.1) | copy-start | bytes 772
  3.4 7.0 %collective-permute-start = (bf16[2,128,256]{2,1,0:T(8,128)(2,1)}, bf16[2,128,256]{2,1,0:T(8,128)(2,1)S(1)}, u32[]{:S(2)}, u32[]{:S(2)}) collective-permute-start(bf16[2,128,256]{2,1,0:T(8,128)(2,1)} %get-tuple-element.63), channel_id=1, source_target_pairs={{0,64},{32,96},{64,0},{96,32},{128,192},{160,224},{192,128},{224,1... | collective-permute-start | bytes 393224 | tf_op jit(solution)/shard_map/ppermute | solution.py:31
  5.0 9.1 %collective-permute-start.1 = (bf16[2,128,256]{2,1,0:T(8,128)(2,1)}, bf16[2,128,256]{2,1,0:T(8,128)(2,1)S(1)}, u32[]{:S(2)}, u32[]{:S(2)}) collective-permute-start(bf16[2,128,256]{2,1,0:T(8,128)(2,1)} %get-tuple-element.68), channel_id=1, source_target_pairs={{0,128},{32,160},{64,192},{96,224},{128,0},{160,32},{192,64},{224,... | collective-permute-start | bytes 393224 | tf_op jit(solution)/shard_map/ppermute | solution.py:31
  7.8 8.3 %collective-permute-start.2 = (bf16[2,128,256]{2,1,0:T(8,128)(2,1)}, bf16[2,128,256]{2,1,0:T(8,128)(2,1)S(1)}, u32[]{:S(2)}, u32[]{:S(2)}) collective-permute-start(bf16[2,128,256]{2,1,0:T(8,128)(2,1)} %get-tuple-element.69), channel_id=1, source_target_pairs={{0,192},{32,224},{64,128},{96,160},{128,64},{160,96},{192,0},{224,... | collective-permute-start | bytes 393224 | tf_op jit(solution)/shard_map/ppermute | solution.py:31
  8.2 7.9 %collective-permute-start.3 = (bf16[256,256]{1,0:T(8,128)(2,1)}, bf16[256,256]{1,0:T(8,128)(2,1)S(1)}, u32[]{:S(2)}, u32[]{:S(2)}) collective-permute-start(bf16[256,256]{1,0:T(8,128)(2,1)} %get-tuple-element.70), channel_id=1, source_target_pairs={{0,3},{1,0},{2,1},{3,2},{4,7},{5,4},{6,5},{7,6},{8,11},{9,8},{10,9... | collective-permute-start | bytes 393224 | tf_op jit(solution)/shard_map/ppermute | solution.py:45
  10.4 43.1 %copy-start.4 = (s32[4]{0:T(128)}, s32[4]{0:T(128)S(1)}, u32[]{:S(2)}) copy-start(s32[4]{0:T(128)S(1)} %pad_add_fusion.place) | copy-start | bytes 52
  11.4 17.0 %copy-start.13 = (bf16[3,256,256]{2,1,0:T(8,128)(2,1)S(1)}, bf16[3,256,256]{2,1,0:T(8,128)(2,1)}, u32[]{:S(2)}) copy-start(bf16[3,256,256]{2,1,0:T(8,128)(2,1)} %get-tuple-element.86) | copy-start | bytes 1179652
  16.9 2.5 %collective-permute-start.4 = (bf16[512,256]{1,0:T(8,128)(2,1)S(1)}, bf16[512,256]{1,0:T(8,128)(2,1)S(1)}, u32[]{:S(2)}, u32[]{:S(2)}) collective-permute-start(bf16[512,256]{1,0:T(8,128)(2,1)S(1)} %get-tuple-element.76), channel_id=1, source_target_pairs={{0,32},{32,0},{64,96},{96,64},{128,160},{160,128},{192,224},{224,1... | collective-permute-start | bytes 786440 | tf_op jit(solution)/shard_map/ppermute | solution.py:35
  17.0 10.5 %collective-permute-start.8 = (bf16[256,256]{1,0:T(8,128)(2,1)}, bf16[256,256]{1,0:T(8,128)(2,1)S(1)}, u32[]{:S(2)}, u32[]{:S(2)}) collective-permute-start(bf16[256,256]{1,0:T(8,128)(2,1)} %get-tuple-element.80), channel_id=1, source_target_pairs={{0,2},{1,3},{2,0},{3,1},{4,6},{5,7},{6,4},{7,5},{8,10},{9,11},{10,... | collective-permute-start | bytes 393224 | tf_op jit(solution)/shard_map/ppermute | solution.py:45
  19.4 8.5 %collective-permute-start.9 = (bf16[256,256]{1,0:T(8,128)(2,1)}, bf16[256,256]{1,0:T(8,128)(2,1)S(1)}, u32[]{:S(2)}, u32[]{:S(2)}) collective-permute-start(bf16[256,256]{1,0:T(8,128)(2,1)} %get-tuple-element.81), channel_id=1, source_target_pairs={{0,1},{1,2},{2,3},{3,0},{4,5},{5,6},{6,7},{7,4},{8,9},{9,10},{10,1... | collective-permute-start | bytes 393224 | tf_op jit(solution)/shard_map/ppermute | solution.py:45
  19.4 46.0 %copy-start.19 = (bf16[8192]{0:T(1024)(128)(2,1)S(1)}, bf16[8192]{0:T(1024)(128)(2,1)}, u32[]{:S(2)}) copy-start(bf16[8192]{0:T(1024)(128)(2,1)} %param.11) | copy-start | bytes 49156
  20.5 7.6 %collective-permute-start.5 = (f32[8,512]{1,0:T(8,128)S(1)}, f32[8,512]{1,0:T(8,128)S(1)}, u32[]{:S(2)}, u32[]{:S(2)}) collective-permute-start(f32[8,512]{1,0:T(8,128)S(1)} %get-tuple-element.82.s0), channel_id=1, source_target_pairs={{0,1},{1,2},{2,3},{3,0},{4,5},{5,6},{6,7},{7,4},{8,9},{9,10},{10,1... | collective-permute-start | bytes 49160 | tf_op jit(solution)/shard_map/ppermute | solution.py:45
  22.3 5.8 %collective-permute-start.6 = (f32[8,512]{1,0:T(8,128)S(1)}, f32[8,512]{1,0:T(8,128)S(1)}, u32[]{:S(2)}, u32[]{:S(2)}) collective-permute-start(f32[8,512]{1,0:T(8,128)S(1)} %get-tuple-element.82.s0), channel_id=1, source_target_pairs={{0,2},{1,3},{2,0},{3,1},{4,6},{5,7},{6,4},{7,5},{8,10},{9,11},{10,... | collective-permute-start | bytes 49160 | tf_op jit(solution)/shard_map/ppermute | solution.py:45
  24.6 3.7 %collective-permute-start.7 = (f32[8,512]{1,0:T(8,128)S(1)}, f32[8,512]{1,0:T(8,128)S(1)}, u32[]{:S(2)}, u32[]{:S(2)}) collective-permute-start(f32[8,512]{1,0:T(8,128)S(1)} %get-tuple-element.82.s0), channel_id=1, source_target_pairs={{0,3},{1,0},{2,1},{3,2},{4,7},{5,4},{6,5},{7,6},{8,11},{9,8},{10,9... | collective-permute-start | bytes 49160 | tf_op jit(solution)/shard_map/ppermute | solution.py:45
  28.4 40.7 %copy-start.11 = (bf16[6,256,256]{2,1,0:T(8,128)(2,1)}, bf16[6,256,256]{2,1,0:T(8,128)(2,1)S(1)}, u32[]{:S(2)}) copy-start(bf16[6,256,256]{2,1,0:T(8,128)(2,1)S(1)} %slice_dynamic-update-slice_fusion.refs_0_.refs_8_) | copy-start | bytes 2359300
  28.5 42.8 %copy-start.2 = (bf16[528,256]{1,0:T(8,128)(2,1)}, bf16[528,256]{1,0:T(8,128)(2,1)S(1)}, u32[]{:S(2)}) copy-start(bf16[528,256]{1,0:T(8,128)(2,1)S(1)} %label.1.refs_0_) | copy-start | bytes 811012
  28.5 14.8 %collective-permute-start.12 = (bf16[6,256,256]{2,1,0:T(8,128)(2,1)S(1)}, bf16[6,256,256]{2,1,0:T(8,128)(2,1)S(1)}, u32[]{:S(2)}, u32[]{:S(2)}) collective-permute-start(bf16[6,256,256]{2,1,0:T(8,128)(2,1)S(1)} %slice_dynamic-update-slice_fusion.refs_0_.refs_8_), channel_id=1, source_target_pairs={{0,32},{32,0},{64,96},{96,64},{128,160},{160,128},{192,224},{224,1... | collective-permute-start | bytes 2359304 | tf_op jit(solution)/shard_map/ppermute | solution.py:35
  28.6 20.0 %collective-permute-start.15 = (bf16[6,256,256]{2,1,0:T(8,128)(2,1)S(1)}, bf16[6,256,256]{2,1,0:T(8,128)(2,1)S(1)}, u32[]{:S(2)}, u32[]{:S(2)}) collective-permute-start(bf16[6,256,256]{2,1,0:T(8,128)(2,1)S(1)} %slice_dynamic-update-slice_fusion.refs_0_.refs_8_), channel_id=1, source_target_pairs={{0,64},{32,96},{64,0},{96,32},{128,192},{160,224},{192,128},{224,1... | collective-permute-start | bytes 2359304 | tf_op jit(solution)/shard_map/ppermute | solution.py:31
  28.7 21.1 %collective-permute-start.16 = (bf16[6,256,256]{2,1,0:T(8,128)(2,1)S(1)}, bf16[6,256,256]{2,1,0:T(8,128)(2,1)S(1)}, u32[]{:S(2)}, u32[]{:S(2)}) collective-permute-start(bf16[6,256,256]{2,1,0:T(8,128)(2,1)S(1)} %slice_dynamic-update-slice_fusion.refs_0_.refs_8_), channel_id=1, source_target_pairs={{0,192},{32,224},{64,128},{96,160},{128,64},{160,96},{192,0},{224,... | collective-permute-start | bytes 2359304 | tf_op jit(solution)/shard_map/ppermute | solution.py:31
  30.1 8.6 %collective-permute-start.10 = (bf16[528,256]{1,0:T(8,128)(2,1)S(1)}, bf16[528,256]{1,0:T(8,128)(2,1)S(1)}, u32[]{:S(2)}, u32[]{:S(2)}) collective-permute-start(bf16[528,256]{1,0:T(8,128)(2,1)S(1)} %label.1.refs_0_), channel_id=1, source_target_pairs={{0,4},{1,5},{2,6},{3,7},{4,0},{5,1},{6,2},{7,3},{8,12},{9,13},{10,... | collective-permute-start | bytes 811016 | tf_op jit(solution)/shard_map/ppermute | solution.py:40
  32.0 11.3 %collective-permute-start.11 = (bf16[528,256]{1,0:T(8,128)(2,1)S(1)}, bf16[528,256]{1,0:T(8,128)(2,1)S(1)}, u32[]{:S(2)}, u32[]{:S(2)}) collective-permute-start(bf16[528,256]{1,0:T(8,128)(2,1)S(1)} %label.1.refs_0_), channel_id=1, source_target_pairs={{0,28},{1,29},{2,30},{3,31},{4,8},{5,9},{6,10},{7,11},{8,4},{9,5},... | collective-permute-start | bytes 811016 | tf_op jit(solution)/shard_map/ppermute | solution.py:40
  38.7 12.3 %copy-start.14 = (bf16[528,256]{1,0:T(8,128)(2,1)}, bf16[528,256]{1,0:T(8,128)(2,1)S(1)}, u32[]{:S(2)}) copy-start(bf16[528,256]{1,0:T(8,128)(2,1)S(1)} %collective-permute-done.10.refs_1_) | copy-start | bytes 811012
  43.3 7.7 %copy-start.15 = (bf16[528,256]{1,0:T(8,128)(2,1)}, bf16[528,256]{1,0:T(8,128)(2,1)S(1)}, u32[]{:S(2)}) copy-start(bf16[528,256]{1,0:T(8,128)(2,1)S(1)} %collective-permute-done.11.refs_4_) | copy-start | bytes 811012
  43.3 25.8 %copy-start.12 = (bf16[6,256,256]{2,1,0:T(8,128)(2,1)}, bf16[6,256,256]{2,1,0:T(8,128)(2,1)S(1)}, u32[]{:S(2)}) copy-start(bf16[6,256,256]{2,1,0:T(8,128)(2,1)S(1)} %collective-permute-done.12.refs_5_.refs_13_) | copy-start | bytes 2359300
  43.3 7.7 %collective-permute-start.13 = (bf16[528,256]{1,0:T(8,128)(2,1)S(1)}, bf16[528,256]{1,0:T(8,128)(2,1)S(1)}, u32[]{:S(2)}, u32[]{:S(2)}) collective-permute-start(bf16[528,256]{1,0:T(8,128)(2,1)S(1)} %collective-permute-done.11.refs_4_), channel_id=1, source_target_pairs={{0,4},{1,5},{2,6},{3,7},{4,0},{5,1},{6,2},{7,3},{8,12},{9,13},{10,... | collective-permute-start | bytes 811016 | tf_op jit(solution)/shard_map/ppermute | solution.py:40
  43.4 8.9 %collective-permute-start.14 = (bf16[528,256]{1,0:T(8,128)(2,1)S(1)}, bf16[528,256]{1,0:T(8,128)(2,1)S(1)}, u32[]{:S(2)}, u32[]{:S(2)}) collective-permute-start(bf16[528,256]{1,0:T(8,128)(2,1)S(1)} %collective-permute-done.10.refs_1_), channel_id=1, source_target_pairs={{0,28},{1,29},{2,30},{3,31},{4,8},{5,9},{6,10},{7,11},{8,4},{9,5},... | collective-permute-start | bytes 811016 | tf_op jit(solution)/shard_map/ppermute | solution.py:40
  48.6 20.6 %copy-start.9 = (bf16[6,256,256]{2,1,0:T(8,128)(2,1)}, bf16[6,256,256]{2,1,0:T(8,128)(2,1)S(1)}, u32[]{:S(2)}) copy-start(bf16[6,256,256]{2,1,0:T(8,128)(2,1)S(1)} %collective-permute-done.15.refs_1_.refs_9_) | copy-start | bytes 2359300
  49.8 19.4 %copy-start.10 = (bf16[6,256,256]{2,1,0:T(8,128)(2,1)}, bf16[6,256,256]{2,1,0:T(8,128)(2,1)S(1)}, u32[]{:S(2)}) copy-start(bf16[6,256,256]{2,1,0:T(8,128)(2,1)S(1)} %collective-permute-done.16.refs_2_.refs_10_) | copy-start | bytes 2359300
  51.0 13.2 %copy-start.16 = (bf16[528,256]{1,0:T(8,128)(2,1)}, bf16[528,256]{1,0:T(8,128)(2,1)S(1)}, u32[]{:S(2)}) copy-start(bf16[528,256]{1,0:T(8,128)(2,1)S(1)} %collective-permute-done.13.refs_2_) | copy-start | bytes 811012
  52.3 12.0 %copy-start.17 = (bf16[528,256]{1,0:T(8,128)(2,1)}, bf16[528,256]{1,0:T(8,128)(2,1)S(1)}, u32[]{:S(2)}) copy-start(bf16[528,256]{1,0:T(8,128)(2,1)S(1)} %collective-permute-done.14.refs_5_) | copy-start | bytes 811012
  52.3 11.8 %collective-permute-start.19 = (bf16[3,256,256]{2,1,0:T(8,128)(2,1)S(1)}, bf16[3,256,256]{2,1,0:T(8,128)(2,1)}, u32[]{:S(2)}, u32[]{:S(2)}) collective-permute-start(bf16[3,256,256]{2,1,0:T(8,128)(2,1)S(1)} %slice.14), channel_id=1, source_target_pairs={{0,64},{32,96},{64,0},{96,32},{128,192},{160,224},{192,128},{224,1... | collective-permute-start | bytes 1179656 | tf_op jit(solution)/shard_map/ppermute | solution.py:31
  53.6 10.6 %collective-permute-start.20 = (bf16[3,256,256]{2,1,0:T(8,128)(2,1)S(1)}, bf16[3,256,256]{2,1,0:T(8,128)(2,1)}, u32[]{:S(2)}, u32[]{:S(2)}) collective-permute-start(bf16[3,256,256]{2,1,0:T(8,128)(2,1)S(1)} %slice.15), channel_id=1, source_target_pairs={{0,192},{32,224},{64,128},{96,160},{128,64},{160,96},{192,0},{224,... | collective-permute-start | bytes 1179656 | tf_op jit(solution)/shard_map/ppermute | solution.py:31
  55.7 6.5 %collective-permute-start.17 = (bf16[528,256]{1,0:T(8,128)(2,1)S(1)}, bf16[528,256]{1,0:T(8,128)(2,1)S(1)}, u32[]{:S(2)}, u32[]{:S(2)}) collective-permute-start(bf16[528,256]{1,0:T(8,128)(2,1)S(1)} %collective-permute-done.14.refs_5_), channel_id=1, source_target_pairs={{0,4},{1,5},{2,6},{3,7},{4,0},{5,1},{6,2},{7,3},{8,12},{9,13},{10,... | collective-permute-start | bytes 811016 | tf_op jit(solution)/shard_map/ppermute | solution.py:40
  56.1 8.0 %collective-permute-start.18 = (bf16[528,256]{1,0:T(8,128)(2,1)S(1)}, bf16[528,256]{1,0:T(8,128)(2,1)}, u32[]{:S(2)}, u32[]{:S(2)}) collective-permute-start(bf16[528,256]{1,0:T(8,128)(2,1)S(1)} %collective-permute-done.13.refs_2_), channel_id=1, source_target_pairs={{0,28},{1,29},{2,30},{3,31},{4,8},{5,9},{6,10},{7,11},{8,4},{9,5},... | collective-permute-start | bytes 811016 | tf_op jit(solution)/shard_map/ppermute | solution.py:40
  64.1 5.0 %collective-permute-start.21 = (bf16[6,256,256]{2,1,0:T(8,128)(2,1)S(1)}, bf16[6,256,256]{2,1,0:T(8,128)(2,1)}, u32[]{:S(2)}, u32[]{:S(2)}) collective-permute-start(bf16[6,256,256]{2,1,0:T(8,128)(2,1)S(1)} %collective-permute-done.15.refs_1_.refs_9_), channel_id=1, source_target_pairs={{0,32},{32,0},{64,96},{96,64},{128,160},{160,128},{192,224},{224,1... | collective-permute-start | bytes 2359304 | tf_op jit(solution)/shard_map/ppermute | solution.py:35
  64.3 4.9 %collective-permute-start.22 = (bf16[6,256,256]{2,1,0:T(8,128)(2,1)S(1)}, bf16[6,256,256]{2,1,0:T(8,128)(2,1)}, u32[]{:S(2)}, u32[]{:S(2)}) collective-permute-start(bf16[6,256,256]{2,1,0:T(8,128)(2,1)S(1)} %collective-permute-done.16.refs_2_.refs_10_), channel_id=1, source_target_pairs={{0,32},{32,0},{64,96},{96,64},{128,160},{160,128},{192,224},{224,1... | collective-permute-start | bytes 2359304 | tf_op jit(solution)/shard_map/ppermute | solution.py:35
  64.7 3.2 %collective-permute-start.23 = (bf16[3,256,256]{2,1,0:T(8,128)(2,1)}, bf16[3,256,256]{2,1,0:T(8,128)(2,1)}, u32[]{:S(2)}, u32[]{:S(2)}) collective-permute-start(bf16[3,256,256]{2,1,0:T(8,128)(2,1)} %collective-permute-done.19.refs_3_.refs_11_), channel_id=1, source_target_pairs={{0,32},{32,0},{64,96},{96,64},{128,160},{160,128},{192,224},{224,1... | collective-permute-start | bytes 1179656 | tf_op jit(solution)/shard_map/ppermute | solution.py:35
  64.9 4.3 %collective-permute-start.24 = (bf16[3,256,256]{2,1,0:T(8,128)(2,1)}, bf16[3,256,256]{2,1,0:T(8,128)(2,1)}, u32[]{:S(2)}, u32[]{:S(2)}) collective-permute-start(bf16[3,256,256]{2,1,0:T(8,128)(2,1)} %collective-permute-done.20.refs_4_.refs_12_), channel_id=1, source_target_pairs={{0,32},{32,0},{64,96},{96,64},{128,160},{160,128},{192,224},{224,1... | collective-permute-start | bytes 1179656 | tf_op jit(solution)/shard_map/ppermute | solution.py:35
  65.3 8.8 %collective-permute-start.25 = (bf16[528,256]{1,0:T(8,128)(2,1)}, bf16[528,256]{1,0:T(8,128)(2,1)}, u32[]{:S(2)}, u32[]{:S(2)}) collective-permute-start(bf16[528,256]{1,0:T(8,128)(2,1)} %collective-permute-done.18.refs_6_), channel_id=1, source_target_pairs={{0,4},{1,5},{2,6},{3,7},{4,0},{5,1},{6,2},{7,3},{8,12},{9,13},{10,... | collective-permute-start | bytes 811016 | tf_op jit(solution)/shard_map/ppermute | solution.py:40
  80.7 14.3 %collective-permute-start.26 = (bf16[640,256]{1,0:T(8,128)(2,1)}, bf16[640,256]{1,0:T(8,128)(2,1)S(1)}, u32[]{:S(2)}, u32[]{:S(2)}) collective-permute-start(bf16[640,256]{1,0:T(8,128)(2,1)} %get-tuple-element.111), channel_id=1, source_target_pairs={{0,2},{1,3},{2,0},{3,1},{4,6},{5,7},{6,4},{7,5},{8,10},{9,11},{10,... | collective-permute-start | bytes 983048 | tf_op jit(solution)/shard_map/ppermute | solution.py:45
  88.2 9.9 %collective-permute-start.27 = (bf16[640,256]{1,0:T(8,128)(2,1)}, bf16[640,256]{1,0:T(8,128)(2,1)S(1)}, u32[]{:S(2)}, u32[]{:S(2)}) collective-permute-start(bf16[640,256]{1,0:T(8,128)(2,1)} %get-tuple-element.109._), channel_id=1, source_target_pairs={{0,1},{1,2},{2,3},{3,0},{4,5},{5,6},{6,7},{7,4},{8,9},{9,10},{10,1... | collective-permute-start | bytes 983048 | tf_op jit(solution)/shard_map/ppermute | solution.py:45
  89.2 9.1 %collective-permute-start.28 = (bf16[640,256]{1,0:T(8,128)(2,1)}, bf16[640,256]{1,0:T(8,128)(2,1)S(1)}, u32[]{:S(2)}, u32[]{:S(2)}) collective-permute-start(bf16[640,256]{1,0:T(8,128)(2,1)} %get-tuple-element.113), channel_id=1, source_target_pairs={{0,3},{1,0},{2,1},{3,2},{4,7},{5,4},{6,5},{7,6},{8,11},{9,8},{10,9... | collective-permute-start | bytes 983048 | tf_op jit(solution)/shard_map/ppermute | solution.py:45
  98.5 10.2 %copy-start.5 = (s32[4]{0:T(128)S(1)}, s32[4]{0:T(128)}, u32[]{:S(2)}) copy-start(s32[4]{0:T(128)} %copy-done.4) | copy-start | bytes 52
  98.5 10.2 %collective-permute-start.29 = (bf16[128,256]{1,0:T(8,128)(2,1)S(1)}, bf16[128,256]{1,0:T(8,128)(2,1)S(1)}, u32[]{:S(2)}, u32[]{:S(2)}) collective-permute-start(bf16[128,256]{1,0:T(8,128)(2,1)S(1)} %fresh.1.f0), channel_id=1, source_target_pairs={{0,1},{1,2},{2,3},{3,0},{4,5},{5,6},{6,7},{7,4},{8,9},{9,10},{10,1... | collective-permute-start | bytes 196616 | tf_op jit(solution)/shard_map/ppermute | solution.py:45
  100.0 8.7 %collective-permute-start.30 = (bf16[128,256]{1,0:T(8,128)(2,1)S(1)}, bf16[128,256]{1,0:T(8,128)(2,1)S(1)}, u32[]{:S(2)}, u32[]{:S(2)}) collective-permute-start(bf16[128,256]{1,0:T(8,128)(2,1)S(1)} %fresh.1.f0), channel_id=1, source_target_pairs={{0,2},{1,3},{2,0},{3,1},{4,6},{5,7},{6,4},{7,5},{8,10},{9,11},{10,... | collective-permute-start | bytes 196616 | tf_op jit(solution)/shard_map/ppermute | solution.py:45
  102.7 5.9 %collective-permute-start.31 = (bf16[128,256]{1,0:T(8,128)(2,1)S(1)}, bf16[128,256]{1,0:T(8,128)(2,1)S(1)}, u32[]{:S(2)}, u32[]{:S(2)}) collective-permute-start(bf16[128,256]{1,0:T(8,128)(2,1)S(1)} %fresh.1.f0), channel_id=1, source_target_pairs={{0,3},{1,0},{2,1},{3,2},{4,7},{5,4},{6,5},{7,6},{8,11},{9,8},{10,9... | collective-permute-start | bytes 196616 | tf_op jit(solution)/shard_map/ppermute | solution.py:45
  (4 other events, 8.8 us)

commit v7 on v6

--- a/solution.py
+++ b/solution.py
@@ -529,7 +529,7 @@
         total_ref[j] = jnp.broadcast_to(total, (2 * ROWS, HEAD_SIZE))
         return 0
 
-    lax.fori_loop(0, OUT_DEV, step, 0)
+    lax.fori_loop(0, OUT_DEV, step, 0, unroll=2)
 
 
 def attend_prompt(own, others, cosine, sine, cache):

time: 111 us -> 110 us (level)
  no operation moved by 1% of the time
where the time goes in v7:
time: 110 us
  starting transfers between devices  45 us (41%)
  Pallas kernels  31.3 us (28%)
  waiting for transfers between devices  29.2 us (27%)
  local copies, waits for them, and re-layouts  3.69 us (3%)
    ppermute x12, starting transfers between devices, send_y(): return lax.ppermute(v, 'fsdp', perm)  20.8 us
    ppermute x7, waiting for transfers between devices, send_z(): return lax.ppermute(v, 'fsdp', perm)  16.9 us
    ppermute x7, starting transfers between devices, send_z(): return lax.ppermute(v, 'fsdp', perm)  13.3 us
    ppermute x7, starting transfers between devices, send_x(): return lax.ppermute(v, 'group', perm)  9.57 us
    pallas_call x1, Pallas kernels, project_first(): pl.pallas_call(first_kernel, out_shape=[shaped((TOTAL, SHARDS * TILE), bf...  6.58 us
    ppermute x7, waiting for transfers between devices, send_x(): return lax.ppermute(v, 'group', perm)  6.47 us
    pallas_call x1, Pallas kernels, project_second(): pl.pallas_call(second_kernel, out_shape=[shaped((TOTAL + ROWS, TILE), bf1...  5.18 us
    pallas_call x1, Pallas kernels, project_third(): pl.pallas_call(third_kernel, out_shape=shaped((TOTAL + ROWS, TILE), jnp.f...  4.19 us
  transfers between devices with their start and end apart: 32, of which 18 were waited for; matrix products, arithmetic and copies ran while one was open for 2% of the time, Pallas kernels for 17%

profile of v7, /device:TPU:8, one launch (start us, length us, event | category | flops | bytes accessed | tf_op | source)
XLA Modules:
  0.0 110.1 jit_solution(6752248417905046759)
XLA Ops:
  0.0 3.4 %pack.1 = (bf16[2,128,256]{2,1,0:T(8,128)(2,1)}, bf16[2,128,256]{2,1,0:T(8,128)(2,1)}, bf16[2,128,256]{2,1,0:T(8,128)(2,1)}, bf16[2,128,256]{2,1,0:T(8,128)(2,1)...) custom-call(s32[64]{0:T(128)} %keep.3, ...), custom_call_target="tpu_custom_call" | custom-call | tf_op jit(solution)/shard_map/pack/pallas_call | solution.py:134
  3.4 1.6 %collective-permute-start = (bf16[2,128,256]{2,1,0:T(8,128)(2,1)}, bf16[2,128,256]{2,1,0:T(8,128)(2,1)S(1)}, u32[]{:S(2)}, u32[]{:S(2)}) collective-permute-start(bf16[2,128,256]{2,1,0:T(8,128)(2,1)} %get-tuple-element.63), channel_id=1, source_target_pairs={{0,64},{32,96},{64,0},{96,32},{128,192},{160,224},{192,128},{224,1... | collective-permute-start | bytes 393224 | tf_op jit(solution)/shard_map/ppermute | solution.py:31
  5.0 2.8 %collective-permute-start.1 = (bf16[2,128,256]{2,1,0:T(8,128)(2,1)}, bf16[2,128,256]{2,1,0:T(8,128)(2,1)S(1)}, u32[]{:S(2)}, u32[]{:S(2)}) collective-permute-start(bf16[2,128,256]{2,1,0:T(8,128)(2,1)} %get-tuple-element.68), channel_id=1, source_target_pairs={{0,128},{32,160},{64,192},{96,224},{128,0},{160,32},{192,64},{224,... | collective-permute-start | bytes 393224 | tf_op jit(solution)/shard_map/ppermute | solution.py:31
  8.2 2.2 %collective-permute-start.3 = (bf16[256,256]{1,0:T(8,128)(2,1)}, bf16[256,256]{1,0:T(8,128)(2,1)S(1)}, u32[]{:S(2)}, u32[]{:S(2)}) collective-permute-start(bf16[256,256]{1,0:T(8,128)(2,1)} %get-tuple-element.70), channel_id=1, source_target_pairs={{0,3},{1,0},{2,1},{3,2},{4,7},{5,4},{6,5},{7,6},{8,11},{9,8},{10,9... | collective-permute-start | bytes 393224 | tf_op jit(solution)/shard_map/ppermute | solution.py:45
  10.5 0.9 copy-done.3
  11.4 1.6 %plan.1 = (s32[16]{0:T(128)S(1)}, bf16[2,128,256]{2,1,0:T(8,128)(2,1)S(1)}) custom-call(s32[4]{0:T(128)S(1)} %pad_add_fusion.place, s32[64]{0:T(128)S(1)} %copy-done.6, s32[64]{0:T(128)S(1)} %copy-done.7, s32[64]{0:T(128)S(1)} %copy-done.8, bf16[2,128,256]{2,1,0:T(8,128)(2,1)S(1)} %copy-done.3), custom_call_target="tpu_custom_call" | custom-call | tf_op jit(solution)/shard_map/plan/pallas_call | solution.py:167
  12.9 1.1 collective-permute-done.1.refs_2_
  14.0 2.0 %collective-permute-done.2.refs_3_ = bf16[2,128,256]{2,1,0:T(8,128)(2,1)S(1)} collective-permute-done((bf16[2,128,256]{2,1,0:T(8,128)(2,1)}, bf16[2,128,256]{2,1,0:T(8,128)(2,1)S(1)}, u32[]{:S(2)}, u32[]{:S(2)}) %collective-permute-start.2) | collective-permute-done | bytes 131104 | tf_op jit(solution)/shard_map/ppermute | solution.py:31
  16.1 0.8 sort.1
  17.0 2.4 %collective-permute-start.8 = (bf16[256,256]{1,0:T(8,128)(2,1)}, bf16[256,256]{1,0:T(8,128)(2,1)S(1)}, u32[]{:S(2)}, u32[]{:S(2)}) collective-permute-start(bf16[256,256]{1,0:T(8,128)(2,1)} %get-tuple-element.80), channel_id=1, source_target_pairs={{0,2},{1,3},{2,0},{3,1},{4,6},{5,7},{6,4},{7,5},{8,10},{9,11},{10,... | collective-permute-start | bytes 393224 | tf_op jit(solution)/shard_map/ppermute | solution.py:45
  19.4 1.1 %unpack.1 = (bf16[512,256]{1,0:T(8,128)(2,1)S(1)}, f32[8,512]{1,0:T(8,128)S(1)}) custom-call(s32[16]{0:T(128)S(1)} %get-tuple-element.65.source.slots, bf16[512,256]{1,0:T(8,128)(2,1)S(1)} %get-tuple-element.75.held, bf16[512,256]{1,0:T(8,128)(2,1)S(1)} %collective-permute-done.4.swapped), custom_call_target="tpu_custom_call" | custom-call | tf_op jit(solution)/shard_map/unpack/pallas_call | solution.py:228
  20.5 1.8 %collective-permute-start.5 = (f32[8,512]{1,0:T(8,128)S(1)}, f32[8,512]{1,0:T(8,128)S(1)}, u32[]{:S(2)}, u32[]{:S(2)}) collective-permute-start(f32[8,512]{1,0:T(8,128)S(1)} %get-tuple-element.82.s0), channel_id=1, source_target_pairs={{0,1},{1,2},{2,3},{3,0},{4,5},{5,6},{6,7},{7,4},{8,9},{9,10},{10,1... | collective-permute-start | bytes 49160 | tf_op jit(solution)/shard_map/ppermute | solution.py:45
  22.3 2.3 %collective-permute-start.6 = (f32[8,512]{1,0:T(8,128)S(1)}, f32[8,512]{1,0:T(8,128)S(1)}, u32[]{:S(2)}, u32[]{:S(2)}) collective-permute-start(f32[8,512]{1,0:T(8,128)S(1)} %get-tuple-element.82.s0), channel_id=1, source_target_pairs={{0,2},{1,3},{2,0},{3,1},{4,6},{5,7},{6,4},{7,5},{8,10},{9,11},{10,... | collective-permute-start | bytes 49160 | tf_op jit(solution)/shard_map/ppermute | solution.py:45
  24.6 1.9 %collective-permute-start.7 = (f32[8,512]{1,0:T(8,128)S(1)}, f32[8,512]{1,0:T(8,128)S(1)}, u32[]{:S(2)}, u32[]{:S(2)}) collective-permute-start(f32[8,512]{1,0:T(8,128)S(1)} %get-tuple-element.82.s0), channel_id=1, source_target_pairs={{0,3},{1,0},{2,1},{3,2},{4,7},{5,4},{6,5},{7,6},{8,11},{9,8},{10,9... | collective-permute-start | bytes 49160 | tf_op jit(solution)/shard_map/ppermute | solution.py:45
  26.6 0.9 slice_dynamic-update-slice_fusion.1
  28.7 1.4 %collective-permute-start.16 = (bf16[6,256,256]{2,1,0:T(8,128)(2,1)S(1)}, bf16[6,256,256]{2,1,0:T(8,128)(2,1)S(1)}, u32[]{:S(2)}, u32[]{:S(2)}) collective-permute-start(bf16[6,256,256]{2,1,0:T(8,128)(2,1)S(1)} %slice_dynamic-update-slice_fusion.refs_0_.refs_8_), channel_id=1, source_target_pairs={{0,192},{32,224},{64,128},{96,160},{128,64},{160,96},{192,0},{224,... | collective-permute-start | bytes 2359304 | tf_op jit(solution)/shard_map/ppermute | solution.py:31
  30.1 1.9 %collective-permute-start.10 = (bf16[528,256]{1,0:T(8,128)(2,1)S(1)}, bf16[528,256]{1,0:T(8,128)(2,1)S(1)}, u32[]{:S(2)}, u32[]{:S(2)}) collective-permute-start(bf16[528,256]{1,0:T(8,128)(2,1)S(1)} %label.1.refs_0_), channel_id=1, source_target_pairs={{0,4},{1,5},{2,6},{3,7},{4,0},{5,1},{6,2},{7,3},{8,12},{9,13},{10,... | collective-permute-start | bytes 811016 | tf_op jit(solution)/shard_map/ppermute | solution.py:40
  32.0 4.9 %collective-permute-start.11 = (bf16[528,256]{1,0:T(8,128)(2,1)S(1)}, bf16[528,256]{1,0:T(8,128)(2,1)S(1)}, u32[]{:S(2)}, u32[]{:S(2)}) collective-permute-start(bf16[528,256]{1,0:T(8,128)(2,1)S(1)} %label.1.refs_0_), channel_id=1, source_target_pairs={{0,28},{1,29},{2,30},{3,31},{4,8},{5,9},{6,10},{7,11},{8,4},{9,5},... | collective-permute-start | bytes 811016 | tf_op jit(solution)/shard_map/ppermute | solution.py:40
  36.9 1.7 %collective-permute-done.10.refs_1_ = bf16[528,256]{1,0:T(8,128)(2,1)S(1)} collective-permute-done((bf16[528,256]{1,0:T(8,128)(2,1)S(1)}, bf16[528,256]{1,0:T(8,128)(2,1)S(1)}, u32[]{:S(2)}, u32[]{:S(2)}) %collective-permute-start.10) | collective-permute-done | bytes 270368 | tf_op jit(solution)/shard_map/ppermute | solution.py:40
  38.6 4.7 %collective-permute-done.11.refs_4_ = bf16[528,256]{1,0:T(8,128)(2,1)S(1)} collective-permute-done((bf16[528,256]{1,0:T(8,128)(2,1)S(1)}, bf16[528,256]{1,0:T(8,128)(2,1)S(1)}, u32[]{:S(2)}, u32[]{:S(2)}) %collective-permute-start.11) | collective-permute-done | bytes 270368 | tf_op jit(solution)/shard_map/ppermute | solution.py:40
  43.4 3.0 %collective-permute-start.14 = (bf16[528,256]{1,0:T(8,128)(2,1)S(1)}, bf16[528,256]{1,0:T(8,128)(2,1)S(1)}, u32[]{:S(2)}, u32[]{:S(2)}) collective-permute-start(bf16[528,256]{1,0:T(8,128)(2,1)S(1)} %collective-permute-done.10.refs_1_), channel_id=1, source_target_pairs={{0,28},{1,29},{2,30},{3,31},{4,8},{5,9},{6,10},{7,11},{8,4},{9,5},... | collective-permute-start | bytes 811016 | tf_op jit(solution)/shard_map/ppermute | solution.py:40
  46.4 2.1 %collective-permute-done.15.refs_1_.refs_9_ = bf16[6,256,256]{2,1,0:T(8,128)(2,1)S(1)} collective-permute-done((bf16[6,256,256]{2,1,0:T(8,128)(2,1)S(1)}, bf16[6,256,256]{2,1,0:T(8,128)(2,1)S(1)}, u32[]{:S(2)}, u32[]{:S(2)}) %collective-permute-start.15) | collective-permute-done | bytes 786464 | tf_op jit(solution)/shard_map/ppermute | solution.py:31
  48.6 1.2 %collective-permute-done.16.refs_2_.refs_10_ = bf16[6,256,256]{2,1,0:T(8,128)(2,1)S(1)} collective-permute-done((bf16[6,256,256]{2,1,0:T(8,128)(2,1)S(1)}, bf16[6,256,256]{2,1,0:T(8,128)(2,1)S(1)}, u32[]{:S(2)}, u32[]{:S(2)}) %collective-permute-start.16) | collective-permute-done | bytes 786464 | tf_op jit(solution)/shard_map/ppermute | solution.py:31
  49.8 1.2 %collective-permute-done.13.refs_2_ = bf16[528,256]{1,0:T(8,128)(2,1)S(1)} collective-permute-done((bf16[528,256]{1,0:T(8,128)(2,1)S(1)}, bf16[528,256]{1,0:T(8,128)(2,1)S(1)}, u32[]{:S(2)}, u32[]{:S(2)}) %collective-permute-start.13) | collective-permute-done | bytes 270368 | tf_op jit(solution)/shard_map/ppermute | solution.py:40
  51.0 1.3 %collective-permute-done.14.refs_5_ = bf16[528,256]{1,0:T(8,128)(2,1)S(1)} collective-permute-done((bf16[528,256]{1,0:T(8,128)(2,1)S(1)}, bf16[528,256]{1,0:T(8,128)(2,1)S(1)}, u32[]{:S(2)}, u32[]{:S(2)}) %collective-permute-start.14) | collective-permute-done | bytes 270368 | tf_op jit(solution)/shard_map/ppermute | solution.py:40
  52.3 1.2 %collective-permute-start.19 = (bf16[3,256,256]{2,1,0:T(8,128)(2,1)S(1)}, bf16[3,256,256]{2,1,0:T(8,128)(2,1)}, u32[]{:S(2)}, u32[]{:S(2)}) collective-permute-start(bf16[3,256,256]{2,1,0:T(8,128)(2,1)S(1)} %slice.14), channel_id=1, source_target_pairs={{0,64},{32,96},{64,0},{96,32},{128,192},{160,224},{192,128},{224,1... | collective-permute-start | bytes 1179656 | tf_op jit(solution)/shard_map/ppermute | solution.py:31
  53.6 2.1 %collective-permute-start.20 = (bf16[3,256,256]{2,1,0:T(8,128)(2,1)S(1)}, bf16[3,256,256]{2,1,0:T(8,128)(2,1)}, u32[]{:S(2)}, u32[]{:S(2)}) collective-permute-start(bf16[3,256,256]{2,1,0:T(8,128)(2,1)S(1)} %slice.15), channel_id=1, source_target_pairs={{0,192},{32,224},{64,128},{96,160},{128,64},{160,96},{192,0},{224,... | collective-permute-start | bytes 1179656 | tf_op jit(solution)/shard_map/ppermute | solution.py:31
  56.1 2.8 %collective-permute-start.18 = (bf16[528,256]{1,0:T(8,128)(2,1)S(1)}, bf16[528,256]{1,0:T(8,128)(2,1)}, u32[]{:S(2)}, u32[]{:S(2)}) collective-permute-start(bf16[528,256]{1,0:T(8,128)(2,1)S(1)} %collective-permute-done.13.refs_2_), channel_id=1, source_target_pairs={{0,28},{1,29},{2,30},{3,31},{4,8},{5,9},{6,10},{7,11},{8,4},{9,5},... | collective-permute-start | bytes 811016 | tf_op jit(solution)/shard_map/ppermute | solution.py:40
  58.9 3.2 %collective-permute-done.17.refs_3_ = bf16[528,256]{1,0:T(8,128)(2,1)S(1)} collective-permute-done((bf16[528,256]{1,0:T(8,128)(2,1)S(1)}, bf16[528,256]{1,0:T(8,128)(2,1)S(1)}, u32[]{:S(2)}, u32[]{:S(2)}) %collective-permute-start.17) | collective-permute-done | bytes 270368 | tf_op jit(solution)/shard_map/ppermute | solution.py:40
  62.1 2.0 %collective-permute-done.18.refs_6_ = bf16[528,256]{1,0:T(8,128)(2,1)} collective-permute-done((bf16[528,256]{1,0:T(8,128)(2,1)S(1)}, bf16[528,256]{1,0:T(8,128)(2,1)}, u32[]{:S(2)}, u32[]{:S(2)}) %collective-permute-start.18) | collective-permute-done | bytes 270368 | tf_op jit(solution)/shard_map/ppermute | solution.py:40
  65.4 0.6 reshape.28.gain
  66.1 1.9 %collective-permute-done.23.refs_8_.refs_16_ = bf16[3,256,256]{2,1,0:T(8,128)(2,1)} collective-permute-done((bf16[3,256,256]{2,1,0:T(8,128)(2,1)}, bf16[3,256,256]{2,1,0:T(8,128)(2,1)}, u32[]{:S(2)}, u32[]{:S(2)}) %collective-permute-start.23) | collective-permute-done | bytes 393248 | tf_op jit(solution)/shard_map/ppermute | solution.py:35
  68.0 1.1 %collective-permute-done.24.refs_9_.refs_17_ = bf16[3,256,256]{2,1,0:T(8,128)(2,1)} collective-permute-done((bf16[3,256,256]{2,1,0:T(8,128)(2,1)}, bf16[3,256,256]{2,1,0:T(8,128)(2,1)}, u32[]{:S(2)}, u32[]{:S(2)}) %collective-permute-start.24) | collective-permute-done | bytes 393248 | tf_op jit(solution)/shard_map/ppermute | solution.py:35
  69.1 2.1 %gather.1.cache_ref = bf16[2048,256]{1,0:T(8,128)(2,1)} custom-call(bf16[6,256,256]{2,1,0:T(8,128)(2,1)} %copy-done.11, bf16[6,256,256]{2,1,0:T(8,128)(2,1)} %copy-done.9, bf16[6,256,256]{2,1,0:T(8,128)(2,1)} %copy-done.10, bf16[3,256,256]{2,1,0:T(8,128)(2,1)} %collective-permute-done.19.refs_3_.refs_11_, ...), custom_call_target="tpu_custom_call" | custom-call | tf_op jit(solution)/shard_map/gather/pallas_call | solution.py:434
  71.3 2.8 %collective-permute-done.25.refs_7_ = bf16[528,256]{1,0:T(8,128)(2,1)} collective-permute-done((bf16[528,256]{1,0:T(8,128)(2,1)}, bf16[528,256]{1,0:T(8,128)(2,1)}, u32[]{:S(2)}, u32[]{:S(2)}) %collective-permute-start.25) | collective-permute-done | bytes 270368 | tf_op jit(solution)/shard_map/ppermute | solution.py:40
  74.1 6.6 %project_first.1 = (bf16[512,2048]{1,0:T(8,128)(2,1)}, bf16[640,256]{1,0:T(8,128)(2,1)}, f32[128,256]{1,0:T(8,128)}, bf16[2,128,256]{2,1,0:T(8,128)(2,1)}) custom-call(s32[4]{0:T(128)} %copy-done.4, f32[32,256]{1,0:T(8,128)} %reshape.28.gain, bf16[528,256]{1,0:T(8,128)(2,1)} %copy-done.2, bf16[528,256]{1,0:T(8,128)(2,1)} %copy-done.14, ...), custom_call_target="tpu_custom_call" | custom-call | flops 1073741824 | bytes 6291456 | tf_op jit(solution)/shard_map/project_first/pallas_call | solution.py:329
  80.7 2.4 %collective-permute-start.26 = (bf16[640,256]{1,0:T(8,128)(2,1)}, bf16[640,256]{1,0:T(8,128)(2,1)S(1)}, u32[]{:S(2)}, u32[]{:S(2)}) collective-permute-start(bf16[640,256]{1,0:T(8,128)(2,1)} %get-tuple-element.111), channel_id=1, source_target_pairs={{0,2},{1,3},{2,0},{3,1},{4,6},{5,7},{6,4},{7,5},{8,10},{9,11},{10,... | collective-permute-start | bytes 983048 | tf_op jit(solution)/shard_map/ppermute | solution.py:45
  83.0 5.2 %project_second.1 = (bf16[640,256]{1,0:T(8,128)(2,1)}, bf16[640,256]{1,0:T(8,128)(2,1)}) custom-call(bf16[512,2048]{1,0:T(8,128)(2,1)} %get-tuple-element.106.normed_ref, bf16[2,128,256]{2,1,0:T(8,128)(2,1)} %get-tuple-element.108.kv_parts, bf16[6,256,256]{2,1,0:T(8,128)(2,1)} %copy-done.11, bf16[6,256,256]{2,1,0:T(8,128)(2,1)} %copy-done.9, ...), custom_call_target="tpu_custom_call" | custom-call | flops 1073741824 | bytes 6291456 | tf_op jit(solution)/shard_map/project_second/pallas_call | solution.py:375
  88.2 1.1 collective-permute-start.27
  89.3 1.0 collective-permute-start.28
  90.7 4.2 %project_third.1.own_ref = f32[640,256]{1,0:T(8,128)} custom-call(bf16[512,2048]{1,0:T(8,128)(2,1)} %get-tuple-element.106.normed_ref, f32[128,256]{1,0:T(8,128)} %get-tuple-element.107.kv_ref, bf16[640,256]{1,0:T(8,128)(2,1)} %get-tuple-element.109._, bf16[6,256,256]{2,1,0:T(8,128)(2,1)} %copy-done.11, bf16[6,256,256]{2,1,0:T(8,128)(2,1)} %copy-done.9, ...), custom_call_target="tpu_custom_call" | custom-call | tf_op jit(solution)/shard_map/project_third/pallas_call | solution.py:407
  95.0 1.1 copy-done.1
  96.4 1.7 %collective-permute-done.27.p1 = bf16[640,256]{1,0:T(8,128)(2,1)S(1)} collective-permute-done((bf16[640,256]{1,0:T(8,128)(2,1)}, bf16[640,256]{1,0:T(8,128)(2,1)S(1)}, u32[]{:S(2)}, u32[]{:S(2)}) %collective-permute-start.27) | collective-permute-done | bytes 327712 | tf_op jit(solution)/shard_map/ppermute | solution.py:45
  98.5 1.6 %collective-permute-start.29 = (bf16[128,256]{1,0:T(8,128)(2,1)S(1)}, bf16[128,256]{1,0:T(8,128)(2,1)S(1)}, u32[]{:S(2)}, u32[]{:S(2)}) collective-permute-start(bf16[128,256]{1,0:T(8,128)(2,1)S(1)} %fresh.1.f0), channel_id=1, source_target_pairs={{0,1},{1,2},{2,3},{3,0},{4,5},{5,6},{6,7},{7,4},{8,9},{9,10},{10,1... | collective-permute-start | bytes 196616 | tf_op jit(solution)/shard_map/ppermute | solution.py:45
  100.0 2.8 %collective-permute-start.30 = (bf16[128,256]{1,0:T(8,128)(2,1)S(1)}, bf16[128,256]{1,0:T(8,128)(2,1)S(1)}, u32[]{:S(2)}, u32[]{:S(2)}) collective-permute-start(bf16[128,256]{1,0:T(8,128)(2,1)S(1)} %fresh.1.f0), channel_id=1, source_target_pairs={{0,2},{1,3},{2,0},{3,1},{4,6},{5,7},{6,4},{7,5},{8,10},{9,11},{10,... | collective-permute-start | bytes 196616 | tf_op jit(solution)/shard_map/ppermute | solution.py:45
  102.8 1.4 %collective-permute-start.31 = (bf16[128,256]{1,0:T(8,128)(2,1)S(1)}, bf16[128,256]{1,0:T(8,128)(2,1)S(1)}, u32[]{:S(2)}, u32[]{:S(2)}) collective-permute-start(bf16[128,256]{1,0:T(8,128)(2,1)S(1)} %fresh.1.f0), channel_id=1, source_target_pairs={{0,3},{1,0},{2,1},{3,2},{4,7},{5,4},{6,5},{7,6},{8,11},{9,8},{10,9... | collective-permute-start | bytes 196616 | tf_op jit(solution)/shard_map/ppermute | solution.py:45
  104.2 3.9 %prompt.1 = (bf16[4,256,128]{2,1,0:T(8,128)(2,1)S(1)}, f32[4,256,128]{2,1,0:T(8,128)S(1)}, f32[4,256,128]{2,1,0:T(8,128)S(1)}, f32[4,256,128]{2,1,0:T(8,128)S(1)}) custom-call(f32[640,256]{1,0:T(8,128)S(1)} %get-tuple-element.112.own, bf16[640,256]{1,0:T(8,128)(2,1)S(1)} %collective-permute-done.27.p1, bf16[640,256]{1,0:T(8,128)(2,1)S(1)} %collective-permute-done.28.p3, ...), custom_call_target="tpu_custom_call" | custom-call | flops 1073741824 | bytes 2097152 | tf_op jit(solution)/shard_map/prompt/pallas_call | solution.py:537
  108.1 2.0 %finish.1 = bf16[4,128,256]{2,1,0:T(8,128)(2,1)} custom-call(s32[4]{0:T(128)S(1)} %copy-done.5, s32[16]{0:T(128)S(1)} %get-tuple-element.65.source.slots, bf16[4,256,128]{2,1,0:T(8,128)(2,1)S(1)} %get-tuple-element.115.q, f32[4,256,128]{2,1,0:T(8,128)S(1)} %get-tuple-element.116.mixed_ref, f32[4,256,128]{2,1,0:T(8,128)S(1)} %get-tuple-element.117.top_ref, ...), custom_call_target="tpu_custom_call" | custom-call | tf_op jit(solution)/shard_map/finish/pallas_call | solution.py:580
  (82 shorter events, 4.7 us)
Async XLA Ops:
  0.0 10.4 %copy-start.6 = (s32[64]{0:T(128)S(1)}, s32[64]{0:T(128)}, u32[]{:S(2)}) copy-start(s32[64]{0:T(128)} %keep.3) | copy-start | bytes 772
  0.0 10.4 %copy-start.7 = (s32[64]{0:T(128)S(1)}, s32[64]{0:T(128)}, u32[]{:S(2)}) copy-start(s32[64]{0:T(128)} %destination.3) | copy-start | bytes 772
  0.0 10.5 %copy-start.8 = (s32[64]{0:T(128)S(1)}, s32[64]{0:T(128)}, u32[]{:S(2)}) copy-start(s32[64]{0:T(128)} %counts.1) | copy-start | bytes 772
  3.4 7.0 %collective-permute-start = (bf16[2,128,256]{2,1,0:T(8,128)(2,1)}, bf16[2,128,256]{2,1,0:T(8,128)(2,1)S(1)}, u32[]{:S(2)}, u32[]{:S(2)}) collective-permute-start(bf16[2,128,256]{2,1,0:T(8,128)(2,1)} %get-tuple-element.63), channel_id=1, source_target_pairs={{0,64},{32,96},{64,0},{96,32},{128,192},{160,224},{192,128},{224,1... | collective-permute-start | bytes 393224 | tf_op jit(solution)/shard_map/ppermute | solution.py:31
  5.0 9.1 %collective-permute-start.1 = (bf16[2,128,256]{2,1,0:T(8,128)(2,1)}, bf16[2,128,256]{2,1,0:T(8,128)(2,1)S(1)}, u32[]{:S(2)}, u32[]{:S(2)}) collective-permute-start(bf16[2,128,256]{2,1,0:T(8,128)(2,1)} %get-tuple-element.68), channel_id=1, source_target_pairs={{0,128},{32,160},{64,192},{96,224},{128,0},{160,32},{192,64},{224,... | collective-permute-start | bytes 393224 | tf_op jit(solution)/shard_map/ppermute | solution.py:31
  7.7 8.3 %collective-permute-start.2 = (bf16[2,128,256]{2,1,0:T(8,128)(2,1)}, bf16[2,128,256]{2,1,0:T(8,128)(2,1)S(1)}, u32[]{:S(2)}, u32[]{:S(2)}) collective-permute-start(bf16[2,128,256]{2,1,0:T(8,128)(2,1)} %get-tuple-element.69), channel_id=1, source_target_pairs={{0,192},{32,224},{64,128},{96,160},{128,64},{160,96},{192,0},{224,... | collective-permute-start | bytes 393224 | tf_op jit(solution)/shard_map/ppermute | solution.py:31
  8.2 7.9 %collective-permute-start.3 = (bf16[256,256]{1,0:T(8,128)(2,1)}, bf16[256,256]{1,0:T(8,128)(2,1)S(1)}, u32[]{:S(2)}, u32[]{:S(2)}) collective-permute-start(bf16[256,256]{1,0:T(8,128)(2,1)} %get-tuple-element.70), channel_id=1, source_target_pairs={{0,3},{1,0},{2,1},{3,2},{4,7},{5,4},{6,5},{7,6},{8,11},{9,8},{10,9... | collective-permute-start | bytes 393224 | tf_op jit(solution)/shard_map/ppermute | solution.py:45
  10.4 43.1 %copy-start.4 = (s32[4]{0:T(128)}, s32[4]{0:T(128)S(1)}, u32[]{:S(2)}) copy-start(s32[4]{0:T(128)S(1)} %pad_add_fusion.place) | copy-start | bytes 52
  11.4 17.0 %copy-start.13 = (bf16[3,256,256]{2,1,0:T(8,128)(2,1)S(1)}, bf16[3,256,256]{2,1,0:T(8,128)(2,1)}, u32[]{:S(2)}) copy-start(bf16[3,256,256]{2,1,0:T(8,128)(2,1)} %get-tuple-element.86) | copy-start | bytes 1179652
  16.9 2.5 %collective-permute-start.4 = (bf16[512,256]{1,0:T(8,128)(2,1)S(1)}, bf16[512,256]{1,0:T(8,128)(2,1)S(1)}, u32[]{:S(2)}, u32[]{:S(2)}) collective-permute-start(bf16[512,256]{1,0:T(8,128)(2,1)S(1)} %get-tuple-element.76), channel_id=1, source_target_pairs={{0,32},{32,0},{64,96},{96,64},{128,160},{160,128},{192,224},{224,1... | collective-permute-start | bytes 786440 | tf_op jit(solution)/shard_map/ppermute | solution.py:35
  17.0 10.5 %collective-permute-start.8 = (bf16[256,256]{1,0:T(8,128)(2,1)}, bf16[256,256]{1,0:T(8,128)(2,1)S(1)}, u32[]{:S(2)}, u32[]{:S(2)}) collective-permute-start(bf16[256,256]{1,0:T(8,128)(2,1)} %get-tuple-element.80), channel_id=1, source_target_pairs={{0,2},{1,3},{2,0},{3,1},{4,6},{5,7},{6,4},{7,5},{8,10},{9,11},{10,... | collective-permute-start | bytes 393224 | tf_op jit(solution)/shard_map/ppermute | solution.py:45
  19.4 8.6 %collective-permute-start.9 = (bf16[256,256]{1,0:T(8,128)(2,1)}, bf16[256,256]{1,0:T(8,128)(2,1)S(1)}, u32[]{:S(2)}, u32[]{:S(2)}) collective-permute-start(bf16[256,256]{1,0:T(8,128)(2,1)} %get-tuple-element.81), channel_id=1, source_target_pairs={{0,1},{1,2},{2,3},{3,0},{4,5},{5,6},{6,7},{7,4},{8,9},{9,10},{10,1... | collective-permute-start | bytes 393224 | tf_op jit(solution)/shard_map/ppermute | solution.py:45
  19.4 46.0 %copy-start.19 = (bf16[8192]{0:T(1024)(128)(2,1)S(1)}, bf16[8192]{0:T(1024)(128)(2,1)}, u32[]{:S(2)}) copy-start(bf16[8192]{0:T(1024)(128)(2,1)} %param.11) | copy-start | bytes 49156
  20.5 7.6 %collective-permute-start.5 = (f32[8,512]{1,0:T(8,128)S(1)}, f32[8,512]{1,0:T(8,128)S(1)}, u32[]{:S(2)}, u32[]{:S(2)}) collective-permute-start(f32[8,512]{1,0:T(8,128)S(1)} %get-tuple-element.82.s0), channel_id=1, source_target_pairs={{0,1},{1,2},{2,3},{3,0},{4,5},{5,6},{6,7},{7,4},{8,9},{9,10},{10,1... | collective-permute-start | bytes 49160 | tf_op jit(solution)/shard_map/ppermute | solution.py:45
  22.3 5.8 %collective-permute-start.6 = (f32[8,512]{1,0:T(8,128)S(1)}, f32[8,512]{1,0:T(8,128)S(1)}, u32[]{:S(2)}, u32[]{:S(2)}) collective-permute-start(f32[8,512]{1,0:T(8,128)S(1)} %get-tuple-element.82.s0), channel_id=1, source_target_pairs={{0,2},{1,3},{2,0},{3,1},{4,6},{5,7},{6,4},{7,5},{8,10},{9,11},{10,... | collective-permute-start | bytes 49160 | tf_op jit(solution)/shard_map/ppermute | solution.py:45
  24.6 3.7 %collective-permute-start.7 = (f32[8,512]{1,0:T(8,128)S(1)}, f32[8,512]{1,0:T(8,128)S(1)}, u32[]{:S(2)}, u32[]{:S(2)}) collective-permute-start(f32[8,512]{1,0:T(8,128)S(1)} %get-tuple-element.82.s0), channel_id=1, source_target_pairs={{0,3},{1,0},{2,1},{3,2},{4,7},{5,4},{6,5},{7,6},{8,11},{9,8},{10,9... | collective-permute-start | bytes 49160 | tf_op jit(solution)/shard_map/ppermute | solution.py:45
  28.4 40.7 %copy-start.11 = (bf16[6,256,256]{2,1,0:T(8,128)(2,1)}, bf16[6,256,256]{2,1,0:T(8,128)(2,1)S(1)}, u32[]{:S(2)}) copy-start(bf16[6,256,256]{2,1,0:T(8,128)(2,1)S(1)} %slice_dynamic-update-slice_fusion.refs_0_.refs_8_) | copy-start | bytes 2359300
  28.5 42.8 %copy-start.2 = (bf16[528,256]{1,0:T(8,128)(2,1)}, bf16[528,256]{1,0:T(8,128)(2,1)S(1)}, u32[]{:S(2)}) copy-start(bf16[528,256]{1,0:T(8,128)(2,1)S(1)} %label.1.refs_0_) | copy-start | bytes 811012
  28.5 14.8 %collective-permute-start.12 = (bf16[6,256,256]{2,1,0:T(8,128)(2,1)S(1)}, bf16[6,256,256]{2,1,0:T(8,128)(2,1)S(1)}, u32[]{:S(2)}, u32[]{:S(2)}) collective-permute-start(bf16[6,256,256]{2,1,0:T(8,128)(2,1)S(1)} %slice_dynamic-update-slice_fusion.refs_0_.refs_8_), channel_id=1, source_target_pairs={{0,32},{32,0},{64,96},{96,64},{128,160},{160,128},{192,224},{224,1... | collective-permute-start | bytes 2359304 | tf_op jit(solution)/shard_map/ppermute | solution.py:35
  28.6 20.0 %collective-permute-start.15 = (bf16[6,256,256]{2,1,0:T(8,128)(2,1)S(1)}, bf16[6,256,256]{2,1,0:T(8,128)(2,1)S(1)}, u32[]{:S(2)}, u32[]{:S(2)}) collective-permute-start(bf16[6,256,256]{2,1,0:T(8,128)(2,1)S(1)} %slice_dynamic-update-slice_fusion.refs_0_.refs_8_), channel_id=1, source_target_pairs={{0,64},{32,96},{64,0},{96,32},{128,192},{160,224},{192,128},{224,1... | collective-permute-start | bytes 2359304 | tf_op jit(solution)/shard_map/ppermute | solution.py:31
  28.7 21.1 %collective-permute-start.16 = (bf16[6,256,256]{2,1,0:T(8,128)(2,1)S(1)}, bf16[6,256,256]{2,1,0:T(8,128)(2,1)S(1)}, u32[]{:S(2)}, u32[]{:S(2)}) collective-permute-start(bf16[6,256,256]{2,1,0:T(8,128)(2,1)S(1)} %slice_dynamic-update-slice_fusion.refs_0_.refs_8_), channel_id=1, source_target_pairs={{0,192},{32,224},{64,128},{96,160},{128,64},{160,96},{192,0},{224,... | collective-permute-start | bytes 2359304 | tf_op jit(solution)/shard_map/ppermute | solution.py:31
  30.1 8.6 %collective-permute-start.10 = (bf16[528,256]{1,0:T(8,128)(2,1)S(1)}, bf16[528,256]{1,0:T(8,128)(2,1)S(1)}, u32[]{:S(2)}, u32[]{:S(2)}) collective-permute-start(bf16[528,256]{1,0:T(8,128)(2,1)S(1)} %label.1.refs_0_), channel_id=1, source_target_pairs={{0,4},{1,5},{2,6},{3,7},{4,0},{5,1},{6,2},{7,3},{8,12},{9,13},{10,... | collective-permute-start | bytes 811016 | tf_op jit(solution)/shard_map/ppermute | solution.py:40
  32.0 11.3 %collective-permute-start.11 = (bf16[528,256]{1,0:T(8,128)(2,1)S(1)}, bf16[528,256]{1,0:T(8,128)(2,1)S(1)}, u32[]{:S(2)}, u32[]{:S(2)}) collective-permute-start(bf16[528,256]{1,0:T(8,128)(2,1)S(1)} %label.1.refs_0_), channel_id=1, source_target_pairs={{0,28},{1,29},{2,30},{3,31},{4,8},{5,9},{6,10},{7,11},{8,4},{9,5},... | collective-permute-start | bytes 811016 | tf_op jit(solution)/shard_map/ppermute | solution.py:40
  38.6 12.3 %copy-start.14 = (bf16[528,256]{1,0:T(8,128)(2,1)}, bf16[528,256]{1,0:T(8,128)(2,1)S(1)}, u32[]{:S(2)}) copy-start(bf16[528,256]{1,0:T(8,128)(2,1)S(1)} %collective-permute-done.10.refs_1_) | copy-start | bytes 811012
  43.3 7.7 %copy-start.15 = (bf16[528,256]{1,0:T(8,128)(2,1)}, bf16[528,256]{1,0:T(8,128)(2,1)S(1)}, u32[]{:S(2)}) copy-start(bf16[528,256]{1,0:T(8,128)(2,1)S(1)} %collective-permute-done.11.refs_4_) | copy-start | bytes 811012
  43.3 25.8 %copy-start.12 = (bf16[6,256,256]{2,1,0:T(8,128)(2,1)}, bf16[6,256,256]{2,1,0:T(8,128)(2,1)S(1)}, u32[]{:S(2)}) copy-start(bf16[6,256,256]{2,1,0:T(8,128)(2,1)S(1)} %collective-permute-done.12.refs_5_.refs_13_) | copy-start | bytes 2359300
  43.3 7.7 %collective-permute-start.13 = (bf16[528,256]{1,0:T(8,128)(2,1)S(1)}, bf16[528,256]{1,0:T(8,128)(2,1)S(1)}, u32[]{:S(2)}, u32[]{:S(2)}) collective-permute-start(bf16[528,256]{1,0:T(8,128)(2,1)S(1)} %collective-permute-done.11.refs_4_), channel_id=1, source_target_pairs={{0,4},{1,5},{2,6},{3,7},{4,0},{5,1},{6,2},{7,3},{8,12},{9,13},{10,... | collective-permute-start | bytes 811016 | tf_op jit(solution)/shard_map/ppermute | solution.py:40
  43.4 8.9 %collective-permute-start.14 = (bf16[528,256]{1,0:T(8,128)(2,1)S(1)}, bf16[528,256]{1,0:T(8,128)(2,1)S(1)}, u32[]{:S(2)}, u32[]{:S(2)}) collective-permute-start(bf16[528,256]{1,0:T(8,128)(2,1)S(1)} %collective-permute-done.10.refs_1_), channel_id=1, source_target_pairs={{0,28},{1,29},{2,30},{3,31},{4,8},{5,9},{6,10},{7,11},{8,4},{9,5},... | collective-permute-start | bytes 811016 | tf_op jit(solution)/shard_map/ppermute | solution.py:40
  48.6 20.6 %copy-start.9 = (bf16[6,256,256]{2,1,0:T(8,128)(2,1)}, bf16[6,256,256]{2,1,0:T(8,128)(2,1)S(1)}, u32[]{:S(2)}) copy-start(bf16[6,256,256]{2,1,0:T(8,128)(2,1)S(1)} %collective-permute-done.15.refs_1_.refs_9_) | copy-start | bytes 2359300
  49.8 19.4 %copy-start.10 = (bf16[6,256,256]{2,1,0:T(8,128)(2,1)}, bf16[6,256,256]{2,1,0:T(8,128)(2,1)S(1)}, u32[]{:S(2)}) copy-start(bf16[6,256,256]{2,1,0:T(8,128)(2,1)S(1)} %collective-permute-done.16.refs_2_.refs_10_) | copy-start | bytes 2359300
  51.0 13.2 %copy-start.16 = (bf16[528,256]{1,0:T(8,128)(2,1)}, bf16[528,256]{1,0:T(8,128)(2,1)S(1)}, u32[]{:S(2)}) copy-start(bf16[528,256]{1,0:T(8,128)(2,1)S(1)} %collective-permute-done.13.refs_2_) | copy-start | bytes 811012
  52.3 12.0 %copy-start.17 = (bf16[528,256]{1,0:T(8,128)(2,1)}, bf16[528,256]{1,0:T(8,128)(2,1)S(1)}, u32[]{:S(2)}) copy-start(bf16[528,256]{1,0:T(8,128)(2,1)S(1)} %collective-permute-done.14.refs_5_) | copy-start | bytes 811012
  52.3 11.8 %collective-permute-start.19 = (bf16[3,256,256]{2,1,0:T(8,128)(2,1)S(1)}, bf16[3,256,256]{2,1,0:T(8,128)(2,1)}, u32[]{:S(2)}, u32[]{:S(2)}) collective-permute-start(bf16[3,256,256]{2,1,0:T(8,128)(2,1)S(1)} %slice.14), channel_id=1, source_target_pairs={{0,64},{32,96},{64,0},{96,32},{128,192},{160,224},{192,128},{224,1... | collective-permute-start | bytes 1179656 | tf_op jit(solution)/shard_map/ppermute | solution.py:31
  53.6 10.6 %collective-permute-start.20 = (bf16[3,256,256]{2,1,0:T(8,128)(2,1)S(1)}, bf16[3,256,256]{2,1,0:T(8,128)(2,1)}, u32[]{:S(2)}, u32[]{:S(2)}) collective-permute-start(bf16[3,256,256]{2,1,0:T(8,128)(2,1)S(1)} %slice.15), channel_id=1, source_target_pairs={{0,192},{32,224},{64,128},{96,160},{128,64},{160,96},{192,0},{224,... | collective-permute-start | bytes 1179656 | tf_op jit(solution)/shard_map/ppermute | solution.py:31
  55.7 6.5 %collective-permute-start.17 = (bf16[528,256]{1,0:T(8,128)(2,1)S(1)}, bf16[528,256]{1,0:T(8,128)(2,1)S(1)}, u32[]{:S(2)}, u32[]{:S(2)}) collective-permute-start(bf16[528,256]{1,0:T(8,128)(2,1)S(1)} %collective-permute-done.14.refs_5_), channel_id=1, source_target_pairs={{0,4},{1,5},{2,6},{3,7},{4,0},{5,1},{6,2},{7,3},{8,12},{9,13},{10,... | collective-permute-start | bytes 811016 | tf_op jit(solution)/shard_map/ppermute | solution.py:40
  56.1 8.0 %collective-permute-start.18 = (bf16[528,256]{1,0:T(8,128)(2,1)S(1)}, bf16[528,256]{1,0:T(8,128)(2,1)}, u32[]{:S(2)}, u32[]{:S(2)}) collective-permute-start(bf16[528,256]{1,0:T(8,128)(2,1)S(1)} %collective-permute-done.13.refs_2_), channel_id=1, source_target_pairs={{0,28},{1,29},{2,30},{3,31},{4,8},{5,9},{6,10},{7,11},{8,4},{9,5},... | collective-permute-start | bytes 811016 | tf_op jit(solution)/shard_map/ppermute | solution.py:40
  64.1 5.0 %collective-permute-start.21 = (bf16[6,256,256]{2,1,0:T(8,128)(2,1)S(1)}, bf16[6,256,256]{2,1,0:T(8,128)(2,1)}, u32[]{:S(2)}, u32[]{:S(2)}) collective-permute-start(bf16[6,256,256]{2,1,0:T(8,128)(2,1)S(1)} %collective-permute-done.15.refs_1_.refs_9_), channel_id=1, source_target_pairs={{0,32},{32,0},{64,96},{96,64},{128,160},{160,128},{192,224},{224,1... | collective-permute-start | bytes 2359304 | tf_op jit(solution)/shard_map/ppermute | solution.py:35
  64.3 4.9 %collective-permute-start.22 = (bf16[6,256,256]{2,1,0:T(8,128)(2,1)S(1)}, bf16[6,256,256]{2,1,0:T(8,128)(2,1)}, u32[]{:S(2)}, u32[]{:S(2)}) collective-permute-start(bf16[6,256,256]{2,1,0:T(8,128)(2,1)S(1)} %collective-permute-done.16.refs_2_.refs_10_), channel_id=1, source_target_pairs={{0,32},{32,0},{64,96},{96,64},{128,160},{160,128},{192,224},{224,1... | collective-permute-start | bytes 2359304 | tf_op jit(solution)/shard_map/ppermute | solution.py:35
  64.7 3.2 %collective-permute-start.23 = (bf16[3,256,256]{2,1,0:T(8,128)(2,1)}, bf16[3,256,256]{2,1,0:T(8,128)(2,1)}, u32[]{:S(2)}, u32[]{:S(2)}) collective-permute-start(bf16[3,256,256]{2,1,0:T(8,128)(2,1)} %collective-permute-done.19.refs_3_.refs_11_), channel_id=1, source_target_pairs={{0,32},{32,0},{64,96},{96,64},{128,160},{160,128},{192,224},{224,1... | collective-permute-start | bytes 1179656 | tf_op jit(solution)/shard_map/ppermute | solution.py:35
  64.9 4.3 %collective-permute-start.24 = (bf16[3,256,256]{2,1,0:T(8,128)(2,1)}, bf16[3,256,256]{2,1,0:T(8,128)(2,1)}, u32[]{:S(2)}, u32[]{:S(2)}) collective-permute-start(bf16[3,256,256]{2,1,0:T(8,128)(2,1)} %collective-permute-done.20.refs_4_.refs_12_), channel_id=1, source_target_pairs={{0,32},{32,0},{64,96},{96,64},{128,160},{160,128},{192,224},{224,1... | collective-permute-start | bytes 1179656 | tf_op jit(solution)/shard_map/ppermute | solution.py:35
  65.3 8.8 %collective-permute-start.25 = (bf16[528,256]{1,0:T(8,128)(2,1)}, bf16[528,256]{1,0:T(8,128)(2,1)}, u32[]{:S(2)}, u32[]{:S(2)}) collective-permute-start(bf16[528,256]{1,0:T(8,128)(2,1)} %collective-permute-done.18.refs_6_), channel_id=1, source_target_pairs={{0,4},{1,5},{2,6},{3,7},{4,0},{5,1},{6,2},{7,3},{8,12},{9,13},{10,... | collective-permute-start | bytes 811016 | tf_op jit(solution)/shard_map/ppermute | solution.py:40
  80.7 14.3 %collective-permute-start.26 = (bf16[640,256]{1,0:T(8,128)(2,1)}, bf16[640,256]{1,0:T(8,128)(2,1)S(1)}, u32[]{:S(2)}, u32[]{:S(2)}) collective-permute-start(bf16[640,256]{1,0:T(8,128)(2,1)} %get-tuple-element.111), channel_id=1, source_target_pairs={{0,2},{1,3},{2,0},{3,1},{4,6},{5,7},{6,4},{7,5},{8,10},{9,11},{10,... | collective-permute-start | bytes 983048 | tf_op jit(solution)/shard_map/ppermute | solution.py:45
  88.2 9.9 %collective-permute-start.27 = (bf16[640,256]{1,0:T(8,128)(2,1)}, bf16[640,256]{1,0:T(8,128)(2,1)S(1)}, u32[]{:S(2)}, u32[]{:S(2)}) collective-permute-start(bf16[640,256]{1,0:T(8,128)(2,1)} %get-tuple-element.109._), channel_id=1, source_target_pairs={{0,1},{1,2},{2,3},{3,0},{4,5},{5,6},{6,7},{7,4},{8,9},{9,10},{10,1... | collective-permute-start | bytes 983048 | tf_op jit(solution)/shard_map/ppermute | solution.py:45
  89.3 9.1 %collective-permute-start.28 = (bf16[640,256]{1,0:T(8,128)(2,1)}, bf16[640,256]{1,0:T(8,128)(2,1)S(1)}, u32[]{:S(2)}, u32[]{:S(2)}) collective-permute-start(bf16[640,256]{1,0:T(8,128)(2,1)} %get-tuple-element.113), channel_id=1, source_target_pairs={{0,3},{1,0},{2,1},{3,2},{4,7},{5,4},{6,5},{7,6},{8,11},{9,8},{10,9... | collective-permute-start | bytes 983048 | tf_op jit(solution)/shard_map/ppermute | solution.py:45
  98.5 9.7 %copy-start.5 = (s32[4]{0:T(128)S(1)}, s32[4]{0:T(128)}, u32[]{:S(2)}) copy-start(s32[4]{0:T(128)} %copy-done.4) | copy-start | bytes 52
  98.5 9.6 %collective-permute-start.29 = (bf16[128,256]{1,0:T(8,128)(2,1)S(1)}, bf16[128,256]{1,0:T(8,128)(2,1)S(1)}, u32[]{:S(2)}, u32[]{:S(2)}) collective-permute-start(bf16[128,256]{1,0:T(8,128)(2,1)S(1)} %fresh.1.f0), channel_id=1, source_target_pairs={{0,1},{1,2},{2,3},{3,0},{4,5},{5,6},{6,7},{7,4},{8,9},{9,10},{10,1... | collective-permute-start | bytes 196616 | tf_op jit(solution)/shard_map/ppermute | solution.py:45
  100.0 8.1 %collective-permute-start.30 = (bf16[128,256]{1,0:T(8,128)(2,1)S(1)}, bf16[128,256]{1,0:T(8,128)(2,1)S(1)}, u32[]{:S(2)}, u32[]{:S(2)}) collective-permute-start(bf16[128,256]{1,0:T(8,128)(2,1)S(1)} %fresh.1.f0), channel_id=1, source_target_pairs={{0,2},{1,3},{2,0},{3,1},{4,6},{5,7},{6,4},{7,5},{8,10},{9,11},{10,... | collective-permute-start | bytes 196616 | tf_op jit(solution)/shard_map/ppermute | solution.py:45
  102.8 5.3 %collective-permute-start.31 = (bf16[128,256]{1,0:T(8,128)(2,1)S(1)}, bf16[128,256]{1,0:T(8,128)(2,1)S(1)}, u32[]{:S(2)}, u32[]{:S(2)}) collective-permute-start(bf16[128,256]{1,0:T(8,128)(2,1)S(1)} %fresh.1.f0), channel_id=1, source_target_pairs={{0,3},{1,0},{2,1},{3,2},{4,7},{5,4},{6,5},{7,6},{8,11},{9,8},{10,9... | collective-permute-start | bytes 196616 | tf_op jit(solution)/shard_map/ppermute | solution.py:45
  (4 other events, 8.8 us)
